TPU v7x, 256 devices: a whole 4x4x8 slice. The times are simulated.
256 devices in a mesh: dp: 8 (over y, z_hi), row: 4 (over x), col: 8 (over z_lo, core).
Axes of the slice: x: 4, y: 4, z: 8 (z_hi: 2, z_lo: 4; z = z_hi * 4 + z_lo), core: 2. Of those that a mesh axis runs over, the one named last changes fastest.
Arguments:
- tokens: bfloat16 [6144, 8192], P('dp', ('row', 'col')), may hold values from -6 to 6
- gate_weight: bfloat16 [8192, 14336], P(('row', 'dp'), 'col'), may hold values from -0.0625 to 0.0625
- up_weight: bfloat16 [8192, 14336], P(('row', 'dp'), 'col'), may hold values from -0.0625 to 0.0625
Outputs:
- hidden: bfloat16 [6144, 14336], P(('dp', 'row'), 'col')
All inputs are finite; a program needn't handle non-finite values.
Results may differ from a plain program's by a relative error of at most 0.0015.
Values may be sent and summed in bfloat16 or wider, within the bound.
No kernel may reach another device: no remote copies, remote signals or barrier semaphores. Data moves between devices by JAX's collectives and lax.ppermute only.
A program may use at most 64 MiB of HBM per device.

v0:
```python
import jax
import jax.numpy as jnp
from jax import lax
from jax.sharding import PartitionSpec as P


def per_device(tokens, gate_weight, up_weight):
    panel = lax.all_gather(tokens, "col", axis=1, tiled=True)
    gate_part = jnp.dot(
        panel,
        lax.all_gather(gate_weight, "dp", axis=0, tiled=True),
        preferred_element_type=jnp.float32,
    )
    up_part = jnp.dot(
        panel,
        lax.all_gather(up_weight, "dp", axis=0, tiled=True),
        preferred_element_type=jnp.float32,
    )
    gate, up = (
        lax.psum_scatter(gate_part, "row", scatter_dimension=0, tiled=True),
        lax.psum_scatter(up_part, "row", scatter_dimension=0, tiled=True),
    )
    return (jax.nn.silu(gate) * up).astype(jnp.bfloat16)


def solution(mesh):
    return jax.shard_map(
        per_device,
        mesh=mesh,
        in_specs=(P("dp", ("row", "col")), P(("row", "dp"), "col"), P(("row", "dp"), "col")),
        out_specs=P(("dp", "row"), "col"),
        check_vma=False,
    )
```

profile of v0, /device:TPU:98, one launch (start us, length us, event | category | flops | bytes accessed | tf_op | source)
XLA Modules:
  0.0 496.7 jit_solution(131031546227514831)
XLA Ops:
  6.5 0.0 all-gather.4.cloned.1.call-start
  6.5 0.7 all-gather.4.cloned.1.call-update
  7.3 0.0 all-gather.6.cloned.1.call-start
  7.3 0.7 all-gather.6.cloned.1.call-update
  8.0 0.0 all-gather.8.cloned.1.call-start
  8.1 0.7 all-gather.8.cloned.1.call-update
  8.7 0.0 reduce-scatter.3.cloned.1.call-start
  8.8 45.0 %all-gather.4.cloned.1.call-done = bf16[768,2048]{1,0:T(8,128)(2,1)} async-done(((bf16[768,256]{1,0:T(8,128)(2,1)}), bf16[768,2048]{1,0:T(8,128)(2,1)}) %all-gather.4.cloned.1.call-update) | async-done | bytes 3145744 | tf_op jit(solution)/shard_map/all_gather | solution.py:8
  53.8 152.4 %all-gather.6.cloned.1.call-done = bf16[2048,1792]{1,0:T(8,128)(2,1)} async-done(((bf16[256,1792]{1,0:T(8,128)(2,1)}), bf16[2048,1792]{1,0:T(8,128)(2,1)}) %all-gather.6.cloned.1.call-update) | async-done | bytes 7340048 | tf_op jit(solution)/shard_map/all_gather | solution.py:11
  206.2 11.1 %fusion = f32[768,1792]{1,0:T(8,128)} fusion(bf16[768,2048]{1,0:T(8,128)(2,1)} %all-gather.4.cloned.1.call-done, bf16[2048,1792]{1,0:T(8,128)(2,1)} %all-gather.6.cloned.1.call-done), kind=kOutput, calls=%fused_computation.1 | convolution fusion | flops 5637144576 | bytes 15990784 | tf_op jit(solution)/shard_map/dot_general | solution.py:9
  217.3 0.0 copy-start
  217.3 0.0 reduce-scatter.3.cloned.1.call-update
  217.3 0.0 reduce-scatter.5.cloned.1.call-start
  217.3 142.8 %all-gather.8.cloned.1.call-done = bf16[2048,1792]{1,0:T(8,128)(2,1)} async-done(((bf16[256,1792]{1,0:T(8,128)(2,1)}), bf16[2048,1792]{1,0:T(8,128)(2,1)}) %all-gather.8.cloned.1.call-update) | async-done | bytes 7340048 | tf_op jit(solution)/shard_map/all_gather | solution.py:16
  360.1 0.0 copy-done
  360.1 10.6 %fusion.1 = f32[768,1792]{1,0:T(8,128)} fusion(bf16[768,2048]{1,0:T(8,128)(2,1)S(1)} %copy-done, bf16[2048,1792]{1,0:T(8,128)(2,1)} %all-gather.8.cloned.1.call-done), kind=kOutput, calls=%fused_computation.2 | convolution fusion | flops 5637144576 | bytes 15990784 | tf_op jit(solution)/shard_map/dot_general | solution.py:14
  370.8 0.0 reduce-scatter.5.cloned.1.call-update
  370.8 54.2 %reduce-scatter.3.cloned.1.call-done = f32[192,1792]{1,0:T(8,128)} async-done(((f32[768,1792]{1,0:T(8,128)}), f32[192,1792]{1,0:T(8,128)}) %reduce-scatter.3.cloned.1.call-update) | async-done | bytes 1376272 | tf_op jit(solution)/shard_map/reduce_scatter | solution.py:20
  425.0 62.2 %reduce-scatter.5.cloned.1.call-done = f32[192,1792]{1,0:T(8,128)} async-done(((f32[768,1792]{1,0:T(8,128)}), f32[192,1792]{1,0:T(8,128)}) %reduce-scatter.5.cloned.1.call-update) | async-done | bytes 1376272 | tf_op jit(solution)/shard_map/reduce_scatter | solution.py:21
  487.2 3.0 multiply_convert_fusion
Async XLA Ops:
  6.5 47.3 %all-gather.4.cloned.1.call-start = ((), (), s32[]{:S(2)}) async-start(), calls=%async_computation.2 | async-start | bytes 3538944 | tf_op jit(solution)/shard_map/all_gather | solution.py:8
  7.3 198.9 %all-gather.6.cloned.1.call-start = ((), (), s32[]{:S(2)}) async-start(), calls=%async_computation.3 | async-start | bytes 8257536 | tf_op jit(solution)/shard_map/all_gather | solution.py:11
  8.0 352.1 %all-gather.8.cloned.1.call-start = ((), (), s32[]{:S(2)}) async-start(), calls=%async_computation.5 | async-start | bytes 8257536 | tf_op jit(solution)/shard_map/all_gather | solution.py:16
  8.7 416.2 %reduce-scatter.3.cloned.1.call-start = ((), (), s32[]{:S(2)}) async-start(), calls=%async_computation.4 | async-start | bytes 6881280 | tf_op jit(solution)/shard_map/reduce_scatter | solution.py:20
  217.3 142.9 %copy-start = (bf16[768,2048]{1,0:T(8,128)(2,1)S(1)}, bf16[768,2048]{1,0:T(8,128)(2,1)}, u32[]{:S(2)}) copy-start(bf16[768,2048]{1,0:T(8,128)(2,1)} %all-gather.4.cloned.1.call-done) | copy-start | bytes 9437188
  217.3 269.9 %reduce-scatter.5.cloned.1.call-start = ((), (), s32[]{:S(2)}) async-start(), calls=%async_computation.6 | async-start | bytes 6881280 | tf_op jit(solution)/shard_map/reduce_scatter | solution.py:21
Sparse Core Ops, SparseCore 0:
  9.1 44.6 all-gather.3
  56.4 149.7 all-gather.5
  208.8 151.2 all-gather.7
  362.5 62.3 reduce-scatter.2
  427.4 59.7 reduce-scatter.4
where the time goes:
time: 500 us; the launch traced here: 497 us
  waiting for transfers between devices  459 us (92%)
  matrix products  21.7 us (4%)
  between operations  13.1 us (3%)
    all_gather x1, waiting for transfers between devices, per_device(): lax.all_gather(gate_weight, 'dp', axis=0, tiled=True)  152 us
    all_gather x1, waiting for transfers between devices, per_device(): lax.all_gather(up_weight, 'dp', axis=0, tiled=True)  143 us
    reduce_scatter x1, waiting for transfers between devices, per_device(): lax.psum_scatter(up_part, 'row', scatter_dimension=0, tiled=True)  62.2 us
    reduce_scatter x1, waiting for transfers between devices, per_device(): lax.psum_scatter(gate_part, 'row', scatter_dimension=0, tiled=True)  54.2 us
    all_gather x1, waiting for transfers between devices, per_device(): panel = lax.all_gather(tokens, 'col', axis=1, tiled=True)  45 us
    dot_general x1, matrix products, per_device(): jnp.dot(panel, lax.all_gather(gate_weight, 'dp', axis=0, tiled=True), pre...  11.1 us
    dot_general x1, matrix products, per_device(): jnp.dot(panel, lax.all_gather(up_weight, 'dp', axis=0, tiled=True), prefe...  10.6 us
  transfers between devices with their start and end apart: 5, of which 5 were waited for; matrix products, arithmetic and copies ran while one was open for 4% of the time, Pallas kernels for 0%

commit v1 on v0

v1 whole, which is shorter than its diff:
```python
import jax
import jax.numpy as jnp
import numpy as np
from jax import lax
from jax.experimental import pallas as pl
from jax.experimental.pallas import tpu as pltpu
from jax.sharding import Mesh
from jax.sharding import PartitionSpec as P

NX, NY, NZ, NC = 4, 4, 8, 2
AXES = ("y", "zh", "x", "zl", "c")
PARTS = 2
TILE = 128
SPLITS = (512, 384)


def device_index(x, y, z, c):
    return ((y * 2 + z // 4) * NX + x) * 8 + (z % 4) * 2 + c


def side(x, c):
    return 1 - 2 * ((x + c) % 2)


def move(value, target):
    pairs = []
    for x in range(NX):
        for y in range(NY):
            for z in range(NZ):
                for c in range(NC):
                    tx, ty, tz, tc = target(x, y, z, c)
                    pairs.append((device_index(x, y, z, c), device_index(tx % NX, ty % NY, tz % NZ, tc)))
    return lax.ppermute(value, AXES, pairs)


def to_partner(x, y, z, c):
    return x + side(x, c), y, z, c


def to_antipode(x, y, z, c):
    return x, y, z + 4, c


def to_both(x, y, z, c):
    return x + side(x, c), y, z + 4, c


def to_summer(x, y, z, c):
    return x - side(x, c), y, z, c


def product_kernel(place, own, partner, *refs):
    weights, (sent, kept, lhs, rhs, lhs_sem, rhs_sem) = refs[:8], refs[8:]
    y, zh = place[0], place[1]
    rows = lhs.shape[2]
    loads = []
    for d in range(4):
        at = lax.rem(y + d, 4) * 2
        for u in range(2):
            for f in range(2):
                k = u * 8 + at + lax.rem(zh + f, 2)
                lo = 0
                for n, width in enumerate(SPLITS):
                    loads.append(
                        pltpu.make_async_copy(
                            weights[n * 4 + d].at[f * 2 + u],
                            rhs.at[pl.ds(pl.multiple_of(k * 256, 256), 256), lo : lo + width],
                            rhs_sem.at[len(loads)],
                        )
                    )
                    lo += width
    shares = [[], []]
    for group in range(2):
        for i in range(2):
            position = group * 2 + i
            for u, source in enumerate((own, partner)):
                for k in range(8):
                    shares[group].append(
                        pltpu.make_async_copy(
                            source.at[:, k, place[2 + position]],
                            lhs.at[position, :, :, (u * 8 + k) * 256 : (u * 8 + k + 1) * 256],
                            lhs_sem.at[group * 32 + len(shares[group])],
                        )
                    )
    for copy in loads + shares[0] + shares[1]:
        copy.start()
    for copy in loads:
        copy.wait()
    for group, out in ((0, sent), (1, kept)):
        for copy in shares[group]:
            copy.wait()
        left = lhs[group * 2 : group * 2 + 2].reshape(4 * rows, lhs.shape[3])
        for lo in range(0, rhs.shape[1], 256):
            hi = min(lo + 256, rhs.shape[1])
            out[:, lo:hi] = jnp.dot(left, rhs[:, lo:hi], preferred_element_type=jnp.float32)


def product(place, own, partner, weights):
    rows, wide, depth = own.shape[3], sum(SPLITS), 4096
    hbm, vmem = pl.BlockSpec(memory_space=pltpu.HBM), pl.BlockSpec(memory_space=pltpu.VMEM)
    return pl.pallas_call(
        product_kernel,
        out_shape=[jax.ShapeDtypeStruct((4 * rows, wide), jnp.float32)] * 2,
        in_specs=[pl.BlockSpec(memory_space=pltpu.SMEM)] + [hbm] * 10,
        out_specs=[vmem] * 2,
        scratch_shapes=[
            pltpu.VMEM((4, 2, rows, depth), jnp.bfloat16),
            pltpu.VMEM((depth, wide), jnp.bfloat16),
            pltpu.SemaphoreType.DMA((64,)),
            pltpu.SemaphoreType.DMA((32,)),
        ],
        compiler_params=pltpu.CompilerParams(vmem_limit_bytes=32 << 20),
        cost_estimate=pl.CostEstimate(flops=16 * rows * depth * wide, bytes_accessed=20 << 20, transcendentals=0),
    )(place, own, partner, *weights)


def gated_kernel(place, kept, received, *outs):
    zh = place[1]
    rows = outs[0].shape[0]
    for n, out in enumerate(outs):
        at = pl.multiple_of((n // 2 * 2 + lax.rem(zh + n, 2)) * rows, rows)
        total = kept[pl.ds(at, rows), :] + received[pl.ds(at, rows), :]
        for t in range(3):
            gate, up = total[:, 2 * t * TILE : (2 * t + 1) * TILE], total[:, (2 * t + 1) * TILE : (2 * t + 2) * TILE]
            out[:, t * TILE : (t + 1) * TILE] = (jax.nn.silu(gate) * up).astype(jnp.bfloat16)
        last = total[:, 6 * TILE :]
        up = pltpu.roll(last, TILE // 2, 1)
        out[:, 3 * TILE :] = (jax.nn.silu(last) * up).astype(jnp.bfloat16)[:, : TILE // 2]


def gated(place, kept, received):
    rows, wide = kept.shape
    vmem = pl.BlockSpec(memory_space=pltpu.VMEM)
    return pl.pallas_call(
        gated_kernel,
        out_shape=[jax.ShapeDtypeStruct((rows // 4, wide // 2), jnp.bfloat16)] * 4,
        in_specs=[pl.BlockSpec(memory_space=pltpu.SMEM), vmem, vmem],
        out_specs=[vmem] * 4,
        compiler_params=pltpu.CompilerParams(vmem_limit_bytes=16 << 20),
        cost_estimate=pl.CostEstimate(flops=8 * rows * wide, bytes_accessed=4 << 20, transcendentals=rows * wide // 2),
    )(place, kept, received)


def column_block(gate, up, zh, q):
    base = zh * 896
    first = base + q * 512
    tiles = []
    for t in range(3):
        cut = slice(first + t * TILE, first + (t + 1) * TILE)
        tiles += [gate[:, cut], up[:, cut]]
    cut = slice(base + 384 + q * 64, base + 448 + q * 64)
    a = jnp.concatenate(tiles[:4], 1)
    b = jnp.concatenate([*tiles[4:], gate[:, cut], up[:, cut]], 1)
    return a, b


def per_device(tokens, gate_weight, up_weight):
    y, zh, x, zl, c = (lax.axis_index(a) for a in AXES)
    ahead = side(x, c)
    partner, summer = (x + ahead + 4) % 4, (x - ahead + 4) % 4
    over = (summer - ahead + 4) % 4
    q = ((x + 1 - c) // 2) % 2
    place = jnp.stack([y, zh, summer, over, x, partner]).astype(jnp.int32)
    rows = tokens.shape[0] // NX // PARTS

    split = tokens.reshape(NX, PARTS, rows, 256)
    own, shared = [], []
    for h in range(PARTS):
        panel = lax.all_gather(split[:, h].reshape(NX * rows, 256), ("zh", "zl", "c"), axis=0)
        own.append(panel.reshape(2, 8, NX, rows, 256))
    for h in range(PARTS):
        shared.append(move(own[h], to_partner))

    weights = []
    blocks = [[column_block(gate_weight, up_weight, a, b) for b in range(2)] for a in range(2)]
    for n in range(len(SPLITS)):
        keep = [jnp.where(q == 0, blocks[a][0][n], blocks[a][1][n]) for a in range(2)]
        give = [jnp.where(q == 0, blocks[a][1][n], blocks[a][0][n]) for a in range(2)]
        got = move(jnp.stack(give), to_partner)
        mine = [jnp.where(zh == 0, keep[0], keep[1]), jnp.where(zh == 0, got[0], got[1])]
        away = jnp.stack([jnp.where(zh == 0, keep[1], keep[0]), jnp.where(zh == 0, got[1], got[0])])
        four = jnp.concatenate([jnp.stack(mine), move(away, to_antipode)])
        weights += [four] + [move(four, lambda x, y, z, c, d=d: (x, y - d, z, c)) for d in range(1, 4)]

    lines = []
    for h in range(PARTS):
        sent, kept = product(place, own[h], shared[h], weights)
        parts = gated(place, kept, move(sent, to_summer))
        parts = [parts[0]] + [move(p, t) for p, t in zip(parts[1:], (to_antipode, to_partner, to_both))]
        halves = []
        for a in range(2):
            low = jnp.where(q == 0, parts[a], parts[2 + a])
            high = jnp.where(q == 0, parts[2 + a], parts[a])
            halves.append(jnp.concatenate([low, high[:, 384:], high[:, :384]], 1))
        lines.append(jnp.where(zh == 0, jnp.concatenate(halves, 1), jnp.concatenate(halves[::-1], 1)))
    return jnp.concatenate(lines, 0)


def solution(mesh):
    fine = Mesh(np.array(mesh.devices).reshape(NY, 2, NX, NZ // 2, NC), AXES)
    rows, cols = ("y", "zh"), ("zl", "c")
    return jax.shard_map(
        per_device,
        mesh=fine,
        in_specs=(P(rows, ("x", *cols)), P(("x", *rows), cols), P(("x", *rows), cols)),
        out_specs=P((*rows, "x"), cols),
        check_vma=False,
    )
```

time: 500 us -> 274 us (0.55)
  waiting for transfers between devices: 459 us -> 175 us
  starting transfers between devices: 0.16 us -> 40.8 us
  Pallas kernels: 0 us -> 23 us
  matrix products: 21.7 us -> 0 us
  local copies, waits for them, and re-layouts: 0.01 us -> 12 us
    all_gather x3 -> x2, waiting for transfers between devices: 340 us -> 80 us  [per_device(): lax.all_gather(split[:, h].reshape(NX * rows, 256), ('zh', 'zl', 'c'), ax...]
    reduce_scatter x2 -> x0, waiting for transfers between devices: 116 us -> none  [the longest x1 62.2 us: per_device(): lax.psum_scatter(up_part, 'row', scatter_dimension=0, tiled=True)]
    ppermute x0 -> x20, waiting for transfers between devices: none -> 94.3 us  [move(): return lax.ppermute(value, AXES, pairs)]
    ppermute x0 -> x20, starting transfers between devices: none -> 40.8 us  [move(): return lax.ppermute(value, AXES, pairs)]
    pallas_call x0 -> x4, Pallas kernels: none -> 23 us  [the longest x2 21.4 us: product(): pl.pallas_call(product_kernel, out_shape=[jax.ShapeDtypeStruct((4 * rows,...]
    dot_general x2 -> x0, matrix products: 21.7 us -> none  [the longest x1 11.1 us: per_device(): jnp.dot(panel, lax.all_gather(gate_weight, 'dp', axis=0, tiled=True), pre...]
    unnamed x2 -> x26, local copies, waits for them, and re-layouts: 0.01 us -> 7.97 us
  transfers between devices with their start and end apart: 5 -> 22, of which waited for: 5 -> 9; matrix products, arithmetic and copies ran while one was open for 4% -> 3% of each run, Pallas kernels for 0% -> 8%
where the time goes in v1:
time: 274 us; the launch traced here: 271 us
  waiting for transfers between devices  175 us (64%)
  starting transfers between devices  40.8 us (15%)
  Pallas kernels  23 us (8%)
  between operations  13.8 us (5%)
  local copies, waits for them, and re-layouts  12 us (4%)
  other arithmetic  6.51 us (2%)
    ppermute x20, waiting for transfers between devices, move(): return lax.ppermute(value, AXES, pairs)  94.3 us
    all_gather x2, waiting for transfers between devices, per_device(): lax.all_gather(split[:, h].reshape(NX * rows, 256), ('zh', 'zl', 'c'), ax...  80 us
    ppermute x20, starting transfers between devices, move(): return lax.ppermute(value, AXES, pairs)  40.8 us
    pallas_call x2, Pallas kernels, product(): pl.pallas_call(product_kernel, out_shape=[jax.ShapeDtypeStruct((4 * rows,...  21.4 us
    unnamed x26, local copies, waits for them, and re-layouts  7.97 us
  transfers between devices with their start and end apart: 22, of which 9 were waited for; matrix products, arithmetic and copies ran while one was open for 3% of the time, Pallas kernels for 8%

profile of v1, /device:TPU:98, one launch (start us, length us, event | category | flops | bytes accessed | tf_op | source)
XLA Modules:
  0.0 271.1 jit_solution(10170692616102480816)
XLA Ops:
  6.5 1.9 fusion
  8.5 0.7 all-gather.5.cloned.1.call-update
  9.4 1.1 slice_bitcast_fusion.12
  10.5 0.2 slice_bitcast_fusion.15
  11.1 0.6 collective-permute-start.6
  11.9 0.8 pad_maximum_fusion.3
  12.8 1.5 collective-permute-start.1
  14.4 37.2 %all-gather.3.cloned.1.call-done = bf16[16,384,256]{2,1,0:T(8,128)(2,1)} async-done(((bf16[1,384,256]{2,1,0:T(8,128)(2,1)}), bf16[16,384,256]{2,1,0:T(8,128)(2,1)}) %all-gather.3.cloned.1.call-update) | async-done | bytes 3145744 | tf_op jit(solution)/shard_map/all_gather | solution.py:169
  51.6 0.6 collective-permute-start
  52.2 0.2 broadcast_select_fusion.15
  52.4 1.1 broadcast_select_fusion.16
  53.5 2.1 collective-permute-start.7
  55.6 42.9 %all-gather.5.cloned.1.call-done = bf16[16,384,256]{2,1,0:T(8,128)(2,1)} async-done(((bf16[1,384,256]{2,1,0:T(8,128)(2,1)}), bf16[16,384,256]{2,1,0:T(8,128)(2,1)}) %all-gather.5.cloned.1.call-update) | async-done | bytes 3145744 | tf_op jit(solution)/shard_map/all_gather | solution.py:169
  98.5 1.8 collective-permute-start.15
  100.3 1.1 broadcast_select_fusion.8
  101.4 2.6 collective-permute-start.2
  104.1 0.2 broadcast_select_fusion.17
  104.3 1.1 pad_maximum_fusion.1.refs_4_
  105.4 1.6 collective-permute-start.10
  107.0 1.7 collective-permute-start.8
  108.7 21.1 %collective-permute-done.2 = bf16[2,256,512]{2,1,0:T(8,128)(2,1)S(1)} collective-permute-done((bf16[2,256,512]{2,1,0:T(8,128)(2,1)S(1)}, bf16[2,256,512]{2,1,0:T(8,128)(2,1)S(1)}, u32[]{:S(2)}, u32[]{:S(2)}) %collective-permute-start.2) | collective-permute-done | bytes 524320 | tf_op jit(solution)/shard_map/ppermute | solution.py:33
  129.9 3.0 %collective-permute-start.9 = (bf16[4,256,384]{2,1,0:T(8,128)(2,1)S(1)}, bf16[4,256,384]{2,1,0:T(8,128)(2,1)S(1)}, u32[]{:S(2)}, u32[]{:S(2)}) collective-permute-start(bf16[4,256,384]{2,1,0:T(8,128)(2,1)S(1)} %pad_maximum_fusion.1.refs_4_), channel_id=1, source_target_pairs={{0,128},{1,129},{2,130},{3,131},{4,132},{5,133},{6,134},{7,135},{3... | collective-permute-start | bytes 2359304 | tf_op jit(solution)/shard_map/ppermute | solution.py:33
  133.2 0.9 copy-done.2
  134.0 1.1 collective-permute-start.3
  135.2 0.9 copy-done.5
  136.1 1.5 collective-permute-start.4
  137.6 14.3 %collective-permute-done.9.refs_6_ = bf16[4,256,384]{2,1,0:T(8,128)(2,1)S(1)} collective-permute-done((bf16[4,256,384]{2,1,0:T(8,128)(2,1)S(1)}, bf16[4,256,384]{2,1,0:T(8,128)(2,1)S(1)}, u32[]{:S(2)}, u32[]{:S(2)}) %collective-permute-start.9) | collective-permute-done | bytes 786464 | tf_op jit(solution)/shard_map/ppermute | solution.py:33
  151.9 0.9 copy-done.8
  152.7 1.5 collective-permute-start.5
  154.4 20.1 %collective-permute-done.3.refs_1_ = bf16[4,256,512]{2,1,0:T(8,128)(2,1)S(1)} collective-permute-done((bf16[4,256,512]{2,1,0:T(8,128)(2,1)S(1)}, bf16[4,256,512]{2,1,0:T(8,128)(2,1)S(1)}, u32[]{:S(2)}, u32[]{:S(2)}) %collective-permute-start.3) | collective-permute-done | bytes 1048608 | tf_op jit(solution)/shard_map/ppermute | solution.py:33
  174.5 19.9 %collective-permute-done.5.refs_3_ = bf16[4,256,512]{2,1,0:T(8,128)(2,1)} collective-permute-done((bf16[4,256,512]{2,1,0:T(8,128)(2,1)S(1)}, bf16[4,256,512]{2,1,0:T(8,128)(2,1)}, u32[]{:S(2)}, u32[]{:S(2)}) %collective-permute-start.5) | collective-permute-done | bytes 1048608 | tf_op jit(solution)/shard_map/ppermute | solution.py:33
  194.4 1.9 copy-done.1
  196.3 1.1 copy-done.3
  197.4 1.1 copy-done.6
  198.6 1.1 copy-done.9
  199.7 10.7 %shard_map.37 = (f32[384,896]{1,0:T(8,128)S(1)}, f32[384,896]{1,0:T(8,128)S(1)}) custom-call(s32[6]{0:T(128)S(1)} %stack.51.place, bf16[2,8,4,96,256]{4,3,2,1,0:T(8,128)(2,1)S(1)} %bitcast.82, bf16[2,8,4,96,256]{4,3,2,1,0:T(8,128)(2,1)} %collective-permute-done.partner, bf16[4,256,512]{2,1,0:T(8,128)(2,1)S(1)} %pad_maximum_fusion.refs_0_, ...), custom_call_target="tpu_custom_call" | custom-call | flops 5637144576 | bytes 20971520 | tf_op jit(solution)/shard_map/pallas_call | solution.py:101
  210.6 10.7 %shard_map.39 = (f32[384,896]{1,0:T(8,128)S(1)}, f32[384,896]{1,0:T(8,128)S(1)}) custom-call(s32[6]{0:T(128)S(1)} %stack.51.place, bf16[2,8,4,96,256]{4,3,2,1,0:T(8,128)(2,1)S(1)} %bitcast.80, bf16[2,8,4,96,256]{4,3,2,1,0:T(8,128)(2,1)} %collective-permute-done.15.partner, bf16[4,256,512]{2,1,0:T(8,128)(2,1)S(1)} %pad_maximum_fusion.refs_0_, ...), custom_call_target="tpu_custom_call" | custom-call | flops 5637144576 | bytes 20971520 | tf_op jit(solution)/shard_map/pallas_call | solution.py:101
  221.3 2.1 collective-permute-start.16
  223.3 5.5 %collective-permute-done.11.received = f32[384,896]{1,0:T(8,128)S(1)} collective-permute-done((f32[384,896]{1,0:T(8,128)S(1)}, f32[384,896]{1,0:T(8,128)S(1)}, u32[]{:S(2)}, u32[]{:S(2)}) %collective-permute-start.11) | collective-permute-done | bytes 1376288 | tf_op jit(solution)/shard_map/ppermute | solution.py:33
  228.8 0.8 shard_map.38
  229.6 3.2 %collective-permute-start.13 = (bf16[96,448]{1,0:T(8,128)(2,1)S(1)}, bf16[96,448]{1,0:T(8,128)(2,1)S(1)}, u32[]{:S(2)}, u32[]{:S(2)}) collective-permute-start(bf16[96,448]{1,0:T(8,128)(2,1)S(1)} %get-tuple-element.21), channel_id=1, source_target_pairs={{0,32},{1,33},{2,34},{3,35},{4,36},{5,37},{6,38},{7,39},{32,0},{33... | collective-permute-start | bytes 258056 | tf_op jit(solution)/shard_map/ppermute | solution.py:33
  232.8 6.2 %collective-permute-start.14 = (bf16[96,448]{1,0:T(8,128)(2,1)S(1)}, bf16[96,448]{1,0:T(8,128)(2,1)S(1)}, u32[]{:S(2)}, u32[]{:S(2)}) collective-permute-start(bf16[96,448]{1,0:T(8,128)(2,1)S(1)} %get-tuple-element.22), channel_id=1, source_target_pairs={{0,40},{1,57},{2,42},{3,59},{4,44},{5,61},{6,46},{7,63},{32,8},{33... | collective-permute-start | bytes 258056 | tf_op jit(solution)/shard_map/ppermute | solution.py:33
  239.0 6.6 %collective-permute-done.16.received = f32[384,896]{1,0:T(8,128)S(1)} collective-permute-done((f32[384,896]{1,0:T(8,128)S(1)}, f32[384,896]{1,0:T(8,128)S(1)}, u32[]{:S(2)}, u32[]{:S(2)}) %collective-permute-start.16) | collective-permute-done | bytes 1376288 | tf_op jit(solution)/shard_map/ppermute | solution.py:33
  245.7 0.8 shard_map.40
  246.5 3.2 %collective-permute-start.18 = (bf16[96,448]{1,0:T(8,128)(2,1)S(1)}, bf16[96,448]{1,0:T(8,128)(2,1)S(1)}, u32[]{:S(2)}, u32[]{:S(2)}) collective-permute-start(bf16[96,448]{1,0:T(8,128)(2,1)S(1)} %get-tuple-element.27), channel_id=1, source_target_pairs={{0,32},{1,33},{2,34},{3,35},{4,36},{5,37},{6,38},{7,39},{32,0},{33... | collective-permute-start | bytes 258056 | tf_op jit(solution)/shard_map/ppermute | solution.py:33
  249.7 6.2 %collective-permute-start.19 = (bf16[96,448]{1,0:T(8,128)(2,1)S(1)}, bf16[96,448]{1,0:T(8,128)(2,1)S(1)}, u32[]{:S(2)}, u32[]{:S(2)}) collective-permute-start(bf16[96,448]{1,0:T(8,128)(2,1)S(1)} %get-tuple-element.28), channel_id=1, source_target_pairs={{0,40},{1,57},{2,42},{3,59},{4,44},{5,61},{6,46},{7,63},{32,8},{33... | collective-permute-start | bytes 258056 | tf_op jit(solution)/shard_map/ppermute | solution.py:33
  256.0 6.7 %collective-permute-done.19 = bf16[96,448]{1,0:T(8,128)(2,1)S(1)} collective-permute-done((bf16[96,448]{1,0:T(8,128)(2,1)S(1)}, bf16[96,448]{1,0:T(8,128)(2,1)S(1)}, u32[]{:S(2)}, u32[]{:S(2)}) %collective-permute-start.19) | collective-permute-done | bytes 86048 | tf_op jit(solution)/shard_map/ppermute | solution.py:33
  263.4 0.9 pad_maximum_fusion.2
  (68 shorter events, 2.2 us)
Async XLA Ops:
  6.5 2.7 copy-start.11
  6.5 45.1 %all-gather.3.cloned.1.call-start = ((), (), s32[]{:S(2)}) async-start(), calls=%async_computation | async-start | bytes 3342336 | tf_op jit(solution)/shard_map/all_gather | solution.py:169
  8.4 90.1 %all-gather.5.cloned.1.call-start = ((), (), s32[]{:S(2)}) async-start(), calls=%async_computation.1 | async-start | bytes 3342336 | tf_op jit(solution)/shard_map/all_gather | solution.py:169
  9.2 1.5 copy-start.12
  11.1 41.2 %collective-permute-start.6 = (bf16[2,256,384]{2,1,0:T(8,128)(2,1)S(1)}, bf16[2,256,384]{2,1,0:T(8,128)(2,1)}, u32[]{:S(2)}, u32[]{:S(2)}) collective-permute-start(bf16[2,256,384]{2,1,0:T(8,128)(2,1)S(1)} %pad_maximum_fusion.5), channel_id=1, source_target_pairs={{0,8},{1,25},{2,10},{3,27},{4,12},{5,29},{6,14},{7,31},{32,40},{33... | collective-permute-start | bytes 1179656 | tf_op jit(solution)/shard_map/ppermute | solution.py:33
  12.8 87.5 %collective-permute-start.1 = (bf16[2,256,512]{2,1,0:T(8,128)(2,1)}, bf16[2,256,512]{2,1,0:T(8,128)(2,1)}, u32[]{:S(2)}, u32[]{:S(2)}) collective-permute-start(bf16[2,256,512]{2,1,0:T(8,128)(2,1)} %pad_maximum_fusion.3), channel_id=1, source_target_pairs={{0,8},{1,25},{2,10},{3,27},{4,12},{5,29},{6,14},{7,31},{32,40},{33... | collective-permute-start | bytes 1572872 | tf_op jit(solution)/shard_map/ppermute | solution.py:33
  51.6 142.8 %collective-permute-start = (bf16[2,8,4,96,256]{4,3,2,1,0:T(8,128)(2,1)}, bf16[2,8,4,96,256]{4,3,2,1,0:T(8,128)(2,1)}, u32[]{:S(2)}, u32[]{:S(2)}) collective-permute-start(bf16[2,8,4,96,256]{4,3,2,1,0:T(8,128)(2,1)} %bitcast.81), channel_id=1, source_target_pairs={{0,8},{1,25},{2,10},{3,27},{4,12},{5,29},{6,14},{7,31},{32,40},{33... | collective-permute-start | bytes 9437192 | tf_op jit(solution)/shard_map/ppermute | solution.py:33
  53.5 50.8 %collective-permute-start.7 = (bf16[2,256,384]{2,1,0:T(8,128)(2,1)S(1)}, bf16[2,256,384]{2,1,0:T(8,128)(2,1)}, u32[]{:S(2)}, u32[]{:S(2)}) collective-permute-start(bf16[2,256,384]{2,1,0:T(8,128)(2,1)S(1)} %pad_maximum_fusion.6), channel_id=1, source_target_pairs={{0,32},{1,33},{2,34},{3,35},{4,36},{5,37},{6,38},{7,39},{32,0},{33... | collective-permute-start | bytes 1179656 | tf_op jit(solution)/shard_map/ppermute | solution.py:33
  98.5 112.0 %collective-permute-start.15 = (bf16[2,8,4,96,256]{4,3,2,1,0:T(8,128)(2,1)}, bf16[2,8,4,96,256]{4,3,2,1,0:T(8,128)(2,1)}, u32[]{:S(2)}, u32[]{:S(2)}) collective-permute-start(bf16[2,8,4,96,256]{4,3,2,1,0:T(8,128)(2,1)} %bitcast.79), channel_id=1, source_target_pairs={{0,8},{1,25},{2,10},{3,27},{4,12},{5,29},{6,14},{7,31},{32,40},{33... | collective-permute-start | bytes 9437192 | tf_op jit(solution)/shard_map/ppermute | solution.py:33
  101.4 28.4 %collective-permute-start.2 = (bf16[2,256,512]{2,1,0:T(8,128)(2,1)S(1)}, bf16[2,256,512]{2,1,0:T(8,128)(2,1)S(1)}, u32[]{:S(2)}, u32[]{:S(2)}) collective-permute-start(bf16[2,256,512]{2,1,0:T(8,128)(2,1)S(1)} %pad_maximum_fusion.4), channel_id=1, source_target_pairs={{0,32},{1,33},{2,34},{3,35},{4,36},{5,37},{6,38},{7,39},{32,0},{33... | collective-permute-start | bytes 1572872 | tf_op jit(solution)/shard_map/ppermute | solution.py:33
  105.4 27.7 %collective-permute-start.10 = (bf16[4,256,384]{2,1,0:T(8,128)(2,1)S(1)}, bf16[4,256,384]{2,1,0:T(8,128)(2,1)S(1)}, u32[]{:S(2)}, u32[]{:S(2)}) collective-permute-start(bf16[4,256,384]{2,1,0:T(8,128)(2,1)S(1)} %pad_maximum_fusion.1.refs_4_), channel_id=1, source_target_pairs={{0,64},{1,65},{2,66},{3,67},{4,68},{5,69},{6,70},{7,71},{32,96},{3... | collective-permute-start | bytes 2359304 | tf_op jit(solution)/shard_map/ppermute | solution.py:33
  107.0 28.2 %collective-permute-start.8 = (bf16[4,256,384]{2,1,0:T(8,128)(2,1)S(1)}, bf16[4,256,384]{2,1,0:T(8,128)(2,1)S(1)}, u32[]{:S(2)}, u32[]{:S(2)}) collective-permute-start(bf16[4,256,384]{2,1,0:T(8,128)(2,1)S(1)} %pad_maximum_fusion.1.refs_4_), channel_id=1, source_target_pairs={{0,192},{1,193},{2,194},{3,195},{4,196},{5,197},{6,198},{7,199},{3... | collective-permute-start | bytes 2359304 | tf_op jit(solution)/shard_map/ppermute | solution.py:33
  129.9 22.0 %collective-permute-start.9 = (bf16[4,256,384]{2,1,0:T(8,128)(2,1)S(1)}, bf16[4,256,384]{2,1,0:T(8,128)(2,1)S(1)}, u32[]{:S(2)}, u32[]{:S(2)}) collective-permute-start(bf16[4,256,384]{2,1,0:T(8,128)(2,1)S(1)} %pad_maximum_fusion.1.refs_4_), channel_id=1, source_target_pairs={{0,128},{1,129},{2,130},{3,131},{4,132},{5,133},{6,134},{7,135},{3... | collective-permute-start | bytes 2359304 | tf_op jit(solution)/shard_map/ppermute | solution.py:33
  133.2 0.9 copy-start.2
  134.0 40.4 %collective-permute-start.3 = (bf16[4,256,512]{2,1,0:T(8,128)(2,1)S(1)}, bf16[4,256,512]{2,1,0:T(8,128)(2,1)S(1)}, u32[]{:S(2)}, u32[]{:S(2)}) collective-permute-start(bf16[4,256,512]{2,1,0:T(8,128)(2,1)S(1)} %pad_maximum_fusion.refs_0_), channel_id=1, source_target_pairs={{0,192},{1,193},{2,194},{3,195},{4,196},{5,197},{6,198},{7,199},{3... | collective-permute-start | bytes 3145736 | tf_op jit(solution)/shard_map/ppermute | solution.py:33
  135.2 0.9 copy-start.5
  136.1 38.4 %collective-permute-start.4 = (bf16[4,256,512]{2,1,0:T(8,128)(2,1)S(1)}, bf16[4,256,512]{2,1,0:T(8,128)(2,1)}, u32[]{:S(2)}, u32[]{:S(2)}) collective-permute-start(bf16[4,256,512]{2,1,0:T(8,128)(2,1)S(1)} %pad_maximum_fusion.refs_0_), channel_id=1, source_target_pairs={{0,128},{1,129},{2,130},{3,131},{4,132},{5,133},{6,134},{7,135},{3... | collective-permute-start | bytes 3145736 | tf_op jit(solution)/shard_map/ppermute | solution.py:33
  151.9 0.9 copy-start.8
  152.7 41.7 %collective-permute-start.5 = (bf16[4,256,512]{2,1,0:T(8,128)(2,1)S(1)}, bf16[4,256,512]{2,1,0:T(8,128)(2,1)}, u32[]{:S(2)}, u32[]{:S(2)}) collective-permute-start(bf16[4,256,512]{2,1,0:T(8,128)(2,1)S(1)} %pad_maximum_fusion.refs_0_), channel_id=1, source_target_pairs={{0,64},{1,65},{2,66},{3,67},{4,68},{5,69},{6,70},{7,71},{32,96},{3... | collective-permute-start | bytes 3145736 | tf_op jit(solution)/shard_map/ppermute | solution.py:33
  154.4 56.2 %copy-start = (bf16[16,384,256]{2,1,0:T(8,128)(2,1)S(1)}, bf16[16,384,256]{2,1,0:T(8,128)(2,1)}, u32[]{:S(2)}) copy-start(bf16[16,384,256]{2,1,0:T(8,128)(2,1)} %all-gather.5.cloned.1.call-done) | copy-start | bytes 9437188
  194.4 1.9 copy-start.1
  196.3 1.1 copy-start.3
  197.4 1.1 copy-start.6
  198.6 1.1 copy-start.9
  199.7 10.8 %copy-start.4 = (bf16[4,256,384]{2,1,0:T(8,128)(2,1)S(1)}, bf16[4,256,384]{2,1,0:T(8,128)(2,1)}, u32[]{:S(2)}) copy-start(bf16[4,256,384]{2,1,0:T(8,128)(2,1)} %copy-done.2) | copy-start | bytes 2359300
  199.7 10.8 %copy-start.7 = (bf16[4,256,384]{2,1,0:T(8,128)(2,1)S(1)}, bf16[4,256,384]{2,1,0:T(8,128)(2,1)}, u32[]{:S(2)}) copy-start(bf16[4,256,384]{2,1,0:T(8,128)(2,1)} %copy-done.5) | copy-start | bytes 2359300
  199.7 10.8 %copy-start.10 = (bf16[4,256,384]{2,1,0:T(8,128)(2,1)S(1)}, bf16[4,256,384]{2,1,0:T(8,128)(2,1)}, u32[]{:S(2)}) copy-start(bf16[4,256,384]{2,1,0:T(8,128)(2,1)} %copy-done.8) | copy-start | bytes 2359300
  210.4 18.4 %collective-permute-start.11 = (f32[384,896]{1,0:T(8,128)S(1)}, f32[384,896]{1,0:T(8,128)S(1)}, u32[]{:S(2)}, u32[]{:S(2)}) collective-permute-start(f32[384,896]{1,0:T(8,128)S(1)} %get-tuple-element.18), channel_id=1, source_target_pairs={{0,24},{1,9},{2,26},{3,11},{4,28},{5,13},{6,30},{7,15},{32,56},{33... | collective-permute-start | bytes 4128776 | tf_op jit(solution)/shard_map/ppermute | solution.py:33
  221.3 24.4 %collective-permute-start.16 = (f32[384,896]{1,0:T(8,128)S(1)}, f32[384,896]{1,0:T(8,128)S(1)}, u32[]{:S(2)}, u32[]{:S(2)}) collective-permute-start(f32[384,896]{1,0:T(8,128)S(1)} %get-tuple-element.24), channel_id=1, source_target_pairs={{0,24},{1,9},{2,26},{3,11},{4,28},{5,13},{6,30},{7,15},{32,56},{33... | collective-permute-start | bytes 4128776 | tf_op jit(solution)/shard_map/ppermute | solution.py:33
  229.6 26.3 %collective-permute-start.13 = (bf16[96,448]{1,0:T(8,128)(2,1)S(1)}, bf16[96,448]{1,0:T(8,128)(2,1)S(1)}, u32[]{:S(2)}, u32[]{:S(2)}) collective-permute-start(bf16[96,448]{1,0:T(8,128)(2,1)S(1)} %get-tuple-element.21), channel_id=1, source_target_pairs={{0,32},{1,33},{2,34},{3,35},{4,36},{5,37},{6,38},{7,39},{32,0},{33... | collective-permute-start | bytes 258056 | tf_op jit(solution)/shard_map/ppermute | solution.py:33
  232.8 23.1 %collective-permute-start.14 = (bf16[96,448]{1,0:T(8,128)(2,1)S(1)}, bf16[96,448]{1,0:T(8,128)(2,1)S(1)}, u32[]{:S(2)}, u32[]{:S(2)}) collective-permute-start(bf16[96,448]{1,0:T(8,128)(2,1)S(1)} %get-tuple-element.22), channel_id=1, source_target_pairs={{0,40},{1,57},{2,42},{3,59},{4,44},{5,61},{6,46},{7,63},{32,8},{33... | collective-permute-start | bytes 258056 | tf_op jit(solution)/shard_map/ppermute | solution.py:33
  239.0 16.9 %collective-permute-start.12 = (bf16[96,448]{1,0:T(8,128)(2,1)S(1)}, bf16[96,448]{1,0:T(8,128)(2,1)S(1)}, u32[]{:S(2)}, u32[]{:S(2)}) collective-permute-start(bf16[96,448]{1,0:T(8,128)(2,1)S(1)} %get-tuple-element.20), channel_id=1, source_target_pairs={{0,8},{1,25},{2,10},{3,27},{4,12},{5,29},{6,14},{7,31},{32,40},{33... | collective-permute-start | bytes 258056 | tf_op jit(solution)/shard_map/ppermute | solution.py:33
  246.5 9.5 %collective-permute-start.18 = (bf16[96,448]{1,0:T(8,128)(2,1)S(1)}, bf16[96,448]{1,0:T(8,128)(2,1)S(1)}, u32[]{:S(2)}, u32[]{:S(2)}) collective-permute-start(bf16[96,448]{1,0:T(8,128)(2,1)S(1)} %get-tuple-element.27), channel_id=1, source_target_pairs={{0,32},{1,33},{2,34},{3,35},{4,36},{5,37},{6,38},{7,39},{32,0},{33... | collective-permute-start | bytes 258056 | tf_op jit(solution)/shard_map/ppermute | solution.py:33
  249.7 13.0 %collective-permute-start.19 = (bf16[96,448]{1,0:T(8,128)(2,1)S(1)}, bf16[96,448]{1,0:T(8,128)(2,1)S(1)}, u32[]{:S(2)}, u32[]{:S(2)}) collective-permute-start(bf16[96,448]{1,0:T(8,128)(2,1)S(1)} %get-tuple-element.28), channel_id=1, source_target_pairs={{0,40},{1,57},{2,42},{3,59},{4,44},{5,61},{6,46},{7,63},{32,8},{33... | collective-permute-start | bytes 258056 | tf_op jit(solution)/shard_map/ppermute | solution.py:33
  255.9 7.1 %collective-permute-start.17 = (bf16[96,448]{1,0:T(8,128)(2,1)S(1)}, bf16[96,448]{1,0:T(8,128)(2,1)S(1)}, u32[]{:S(2)}, u32[]{:S(2)}) collective-permute-start(bf16[96,448]{1,0:T(8,128)(2,1)S(1)} %get-tuple-element.26), channel_id=1, source_target_pairs={{0,8},{1,25},{2,10},{3,27},{4,12},{5,29},{6,14},{7,31},{32,40},{33... | collective-permute-start | bytes 258056 | tf_op jit(solution)/shard_map/ppermute | solution.py:33
Sparse Core Ops, SparseCore 0:
  9.2 42.3 all-gather.2
  53.4 45.0 all-gather.4

commit v2 on v1

v2 whole, which is shorter than its diff:
```python
import functools

import jax
import jax.numpy as jnp
import numpy as np
from jax import lax
from jax.experimental import pallas as pl
from jax.experimental.pallas import tpu as pltpu
from jax.sharding import Mesh
from jax.sharding import PartitionSpec as P

NX, NY, NZ, NC = 4, 4, 8, 2
AXES = ("y", "zh", "x", "zl", "c")
PARTS = 2
TILE = 128


def device_index(x, y, z, c):
    return ((y * 2 + z // 4) * NX + x) * 8 + (z % 4) * 2 + c


def side(x, c):
    return 1 - 2 * ((x + c) % 2)


def move(value, target):
    pairs = []
    for x in range(NX):
        for y in range(NY):
            for z in range(NZ):
                for c in range(NC):
                    tx, ty, tz, tc = target(x, y, z, c)
                    pairs.append((device_index(x, y, z, c), device_index(tx % NX, ty % NY, tz % NZ, tc)))
    return lax.ppermute(value, AXES, pairs)


def to_partner(x, y, z, c):
    return x + side(x, c), y, z, c


def to_crossed(x, y, z, c):
    return x + side(x, 1 - c), y, z, 1 - c


def to_antipode(x, y, z, c):
    return x, y, z + 4, c


def to_both(x, y, z, c):
    return x + side(x, c), y, z + 4, c


def to_summer(x, y, z, c):
    return x - side(x, c), y, z, c


def product_kernel(part, place, own, *refs):
    first, rest, weights, (sent, kept, lhs, rhs, lhs_sem, rhs_sem) = refs[:2], refs[2], refs[3:11], refs[11:]
    y, zh, z, c = place[0], place[1], place[7], place[8]
    rows, wide = lhs.shape[2], rhs.shape[1]
    cuts = [(lo, min(lo + 256, wide)) for lo in range(0, wide, 256)]
    loads = []
    for n, (lo, hi) in enumerate(cuts):
        loads.append([])
        for d in range(4):
            for u in range(2):
                for f in range(2):
                    k = u * 8 + lax.rem(y + d, 4) * 2 + lax.rem(zh + f, 2)
                    source = weights[f * 4 + d].at[u, :, lo:hi]
                    target = rhs.at[pl.ds(pl.multiple_of(k * 256, 256), 256), lo:hi]
                    loads[n].append(pltpu.make_async_copy(source, target, rhs_sem.at[n * 16 + len(loads[n])]))
    shares = [[], []]
    for group in range(2):
        for i in range(2):
            position = group * 2 + i
            share = place[2 + position]
            for k in range(8):
                shares[group].append((own.at[:, k, part, share], lhs.at[position, :, :, k * 256 : (k + 1) * 256]))
            for d in range(8):
                for e in range(2):
                    core = lax.rem(c + e, 2)
                    source = rest.at[d - 1, core, part, share] if d else first[e].at[part, share]
                    at = lax.rem(z + d, 8)
                    k = 8 + lax.rem(at, 4) * 2 + core
                    target = lhs.at[position, at // 4, :, pl.ds(pl.multiple_of(k * 256, 256), 256)]
                    shares[group].append((source, target))
        shares[group] = [
            pltpu.make_async_copy(source, target, lhs_sem.at[group * 48 + n]) for n, (source, target) in enumerate(shares[group])
        ]
    for copies in (shares[0], loads[0], loads[1], shares[1], *loads[2:]):
        for copy in copies:
            copy.start()
    for group, out in ((0, sent), (1, kept)):
        for copy in shares[group]:
            copy.wait()
        left = lhs[group * 2 : group * 2 + 2].reshape(4 * rows, lhs.shape[3])
        for n, (lo, hi) in enumerate(cuts):
            if group == 0:
                for copy in loads[n]:
                    copy.wait()
            out[:, lo:hi] = jnp.dot(left, rhs[:, lo:hi], preferred_element_type=jnp.float32)


def product(part, place, own, partner, weights):
    rows, wide, depth = own.shape[4], weights[0].shape[2], 4096
    hbm, vmem = pl.BlockSpec(memory_space=pltpu.HBM), pl.BlockSpec(memory_space=pltpu.VMEM)
    operands = [own, *partner, *weights]
    return pl.pallas_call(
        functools.partial(product_kernel, part),
        out_shape=[jax.ShapeDtypeStruct((4 * rows, wide), jnp.float32)] * 2,
        in_specs=[pl.BlockSpec(memory_space=pltpu.SMEM)] + [hbm] * len(operands),
        out_specs=[vmem] * 2,
        scratch_shapes=[
            pltpu.VMEM((4, 2, rows, depth), jnp.bfloat16),
            pltpu.VMEM((depth, wide), jnp.bfloat16),
            pltpu.SemaphoreType.DMA((96,)),
            pltpu.SemaphoreType.DMA((64,)),
        ],
        compiler_params=pltpu.CompilerParams(vmem_limit_bytes=56 << 20),
        cost_estimate=pl.CostEstimate(flops=16 * rows * depth * wide, bytes_accessed=20 << 20, transcendentals=0),
    )(place, *operands)


def pick_kernel(place, panel, out, sem):
    copies = [pltpu.make_async_copy(panel.at[lax.rem(place[7] + 1 + d, 8)], out.at[d], sem.at[d]) for d in range(7)]
    for copy in copies:
        copy.start()
    for copy in copies:
        copy.wait()


def pick(place, panel):
    hbm = pl.BlockSpec(memory_space=pltpu.HBM)
    return pl.pallas_call(
        pick_kernel,
        out_shape=jax.ShapeDtypeStruct((7, *panel.shape[1:]), panel.dtype),
        in_specs=[pl.BlockSpec(memory_space=pltpu.SMEM), hbm],
        out_specs=hbm,
        scratch_shapes=[pltpu.SemaphoreType.DMA((7,))],
        compiler_params=pltpu.CompilerParams(vmem_limit_bytes=56 << 20),
        cost_estimate=pl.CostEstimate(flops=0, bytes_accessed=12 << 20, transcendentals=0),
    )(place, panel)


def cut_kernel(place, gate, up, near, away, give_near, give_away):
    for zh in range(2):
        for q in range(2):

            @pl.when((place[1] == zh) & (place[6] == q))
            def _(zh=zh, q=q):
                for out, half, side_q in ((near, zh, q), (away, 1 - zh, q), (give_near, zh, 1 - q), (give_away, 1 - zh, 1 - q)):
                    base = half * 896
                    for t in range(3):
                        lo = base + side_q * 512 + t * TILE
                        out[:, 2 * t * TILE : (2 * t + 1) * TILE] = gate[:, lo : lo + TILE]
                        out[:, (2 * t + 1) * TILE : (2 * t + 2) * TILE] = up[:, lo : lo + TILE]
                    lo = base + 384 + side_q * 64
                    out[:, 6 * TILE :] = jnp.concatenate([gate[:, lo : lo + 64], up[:, lo : lo + 64]], 1)


def cut(place, gate, up):
    vmem = pl.BlockSpec(memory_space=pltpu.VMEM)
    depth, wide = gate.shape[0], gate.shape[1] // 2
    return pl.pallas_call(
        cut_kernel,
        out_shape=[jax.ShapeDtypeStruct((depth, wide), gate.dtype)] * 4,
        in_specs=[pl.BlockSpec(memory_space=pltpu.SMEM), vmem, vmem],
        out_specs=[vmem] * 4,
        compiler_params=pltpu.CompilerParams(vmem_limit_bytes=24 << 20),
        cost_estimate=pl.CostEstimate(flops=0, bytes_accessed=4 << 20, transcendentals=0),
    )(place, gate, up)


def gated_kernel(place, kept, received, *outs):
    zh = place[1]
    rows = outs[0].shape[0]
    for n, out in enumerate(outs):
        at = pl.multiple_of((n // 2 * 2 + lax.rem(zh + n, 2)) * rows, rows)
        total = kept[pl.ds(at, rows), :] + received[pl.ds(at, rows), :]
        for t in range(3):
            gate, up = total[:, 2 * t * TILE : (2 * t + 1) * TILE], total[:, (2 * t + 1) * TILE : (2 * t + 2) * TILE]
            out[:, t * TILE : (t + 1) * TILE] = (jax.nn.silu(gate) * up).astype(jnp.bfloat16)
        last = total[:, 6 * TILE :]
        up = pltpu.roll(last, TILE // 2, 1)
        out[:, 3 * TILE :] = (jax.nn.silu(last) * up).astype(jnp.bfloat16)[:, : TILE // 2]


def gated(place, kept, received):
    rows, wide = kept.shape
    vmem = pl.BlockSpec(memory_space=pltpu.VMEM)
    return pl.pallas_call(
        gated_kernel,
        out_shape=[jax.ShapeDtypeStruct((rows // 4, wide // 2), jnp.bfloat16)] * 4,
        in_specs=[pl.BlockSpec(memory_space=pltpu.SMEM), vmem, vmem],
        out_specs=[vmem] * 4,
        compiler_params=pltpu.CompilerParams(vmem_limit_bytes=16 << 20),
        cost_estimate=pl.CostEstimate(flops=8 * rows * wide, bytes_accessed=4 << 20, transcendentals=rows * wide // 2),
    )(place, kept, received)


def gather_kernel(place, *refs):
    blocks, out = refs[:8], refs[8]
    rows = blocks[0].shape[0]
    for zh in range(2):
        for q in range(2):

            @pl.when((place[1] == zh) & (place[6] == q))
            def _(zh=zh, q=q):
                for n, block in enumerate(blocks):
                    h, other_q, other_half = n // 4, n // 2 % 2, n % 2
                    at, base = slice(h * rows, (h + 1) * rows), (zh ^ other_half) * 896
                    if q ^ other_q:
                        tile = jnp.concatenate([blocks[n ^ 2][:, 384:], block[:, 384:]], 1)
                        out[at, base + 384 : base + 512] = tile
                        out[at, base + 512 : base + 896] = block[:, :384]
                    else:
                        out[at, base : base + 384] = block[:, :384]


def gather(place, blocks):
    rows = blocks[0].shape[0]
    vmem = pl.BlockSpec(memory_space=pltpu.VMEM)
    return pl.pallas_call(
        gather_kernel,
        out_shape=jax.ShapeDtypeStruct((PARTS * rows, 1792), jnp.bfloat16),
        in_specs=[pl.BlockSpec(memory_space=pltpu.SMEM)] + [vmem] * 8,
        out_specs=vmem,
        compiler_params=pltpu.CompilerParams(vmem_limit_bytes=16 << 20),
        cost_estimate=pl.CostEstimate(flops=0, bytes_accessed=2 << 20, transcendentals=0),
    )(place, *blocks)


def per_device(tokens, gate_weight, up_weight):
    y, zh, x, zl, c = (lax.axis_index(a) for a in AXES)
    ahead = side(x, c)
    partner, summer = (x + ahead + 4) % 4, (x - ahead + 4) % 4
    over = (summer - ahead + 4) % 4
    q = ((x + 1 - c) // 2) % 2
    place = jnp.stack([y, zh, summer, over, x, partner, q, zh * 4 + zl, c]).astype(jnp.int32)
    rows = tokens.shape[0] // NX // PARTS

    split = tokens.reshape(NX, PARTS, rows, 256).swapaxes(0, 1)
    panel = lax.all_gather(split.reshape(PARTS * NX * rows, 256), ("zh", "zl", "c"), axis=0)
    first = [move(split, t) for t in (to_partner, to_crossed)]

    near, away, give_near, give_away = cut(place, gate_weight, up_weight)
    got = move(give_near, to_partner)
    far = [move(away, to_antipode), move(give_away, to_both)]
    near, got, *first = lax.optimization_barrier((near, got, *first))
    near = jnp.stack([near, got])
    near = [near] + [move(near, lambda x, y, z, c, d=d: (x, y - d, z, c)) for d in range(1, 4)]

    panel = lax.optimization_barrier((panel, *far, *near[1:]))[0]
    far = jnp.stack(far)
    far = [far] + [move(far, lambda x, y, z, c, d=d: (x, y - d, z, c)) for d in range(1, 4)]
    own = panel.reshape(2, 8, PARTS, NX, rows, 256)
    rest = move(pick(place, panel.reshape(8, 2, PARTS, NX, rows, 256)), to_partner)

    blocks = []
    for h in range(PARTS):
        sent, kept = product(h, place, own, (*first, rest), (*near, *far))
        parts = gated(place, kept, move(sent, to_summer))
        blocks += [parts[0]] + [move(p, t) for p, t in zip(parts[1:], (to_antipode, to_partner, to_both))]
    return gather(place, blocks)


def solution(mesh):
    fine = Mesh(np.array(mesh.devices).reshape(NY, 2, NX, NZ // 2, NC), AXES)
    rows, cols = ("y", "zh"), ("zl", "c")
    return jax.shard_map(
        per_device,
        mesh=fine,
        in_specs=(P(rows, ("x", *cols)), P(("x", *rows), cols), P(("x", *rows), cols)),
        out_specs=P((*rows, "x"), cols),
        check_vma=False,
    )
```

time: 274 us -> 412 us (1.50)
  Pallas kernels: 23 us -> 207 us
  waiting for transfers between devices: 175 us -> 147 us
  local copies, waits for them, and re-layouts: 12 us -> 4.1 us
  other arithmetic: 6.51 us -> 0.19 us
    pallas_call x2 -> x5, Pallas kernels: 21.4 us -> 205 us  [the longest x1 169 us: pick(): pl.pallas_call(pick_kernel, out_shape=jax.ShapeDtypeStruct((7, *panel.sha...]
    all_gather x2 -> x1, waiting for transfers between devices: 80 us -> 0.01 us  [per_device(): lax.all_gather(split.reshape(PARTS * NX * rows, 256), ('zh', 'zl', 'c'),...]
    ppermute x20, waiting for transfers between devices: 94.3 us -> 147 us  [move(): return lax.ppermute(value, AXES, pairs)]
    unnamed x26 -> x32, local copies, waits for them, and re-layouts: 7.97 us -> 2.17 us
  transfers between devices with their start and end apart: 22 -> 21, of which waited for: 9 -> 9; matrix products, arithmetic and copies ran while one was open for 3% -> 0% of each run, Pallas kernels for 8% -> 5%
where the time goes in v2:
time: 412 us; the launch traced here: 410 us
  Pallas kernels  207 us (50%)
  waiting for transfers between devices  147 us (36%)
  starting transfers between devices  37.8 us (9%)
  between operations  13.7 us (3%)
    pallas_call x1, Pallas kernels, pick(): pl.pallas_call(pick_kernel, out_shape=jax.ShapeDtypeStruct((7, *panel.sha...  169 us
    ppermute x20, waiting for transfers between devices, move(): return lax.ppermute(value, AXES, pairs)  147 us
    ppermute x20, starting transfers between devices, move(): return lax.ppermute(value, AXES, pairs)  37.8 us
    pallas_call x2, Pallas kernels, product(): pl.pallas_call(functools.partial(product_kernel, part), out_shape=[jax.Sh...  34.3 us
  transfers between devices with their start and end apart: 21, of which 9 were waited for; matrix products, arithmetic and copies ran while one was open for 0% of the time, Pallas kernels for 5%

profile of v2, /device:TPU:98, one launch (start us, length us, event | category | flops | bytes accessed | tf_op | source)
XLA Modules:
  0.0 410.0 jit_solution(10626354596942770652)
XLA Ops:
  6.5 1.8 copy.8
  8.4 0.0 all-gather.2.cloned.1.call-update
  8.5 0.1 stack.57.place
  8.6 0.0 copy-start.3
  8.6 1.2 copy-done.3
  9.8 0.9 shard_map.37
  10.7 0.6 collective-permute-start.2
  11.3 1.5 collective-permute-start.3
  12.8 0.4 collective-permute-start.4
  13.2 14.5 %collective-permute-done.3.refs_0_ = bf16[2,4,96,256]{3,2,1,0:T(8,128)(2,1)S(1)} collective-permute-done((bf16[2,4,96,256]{3,2,1,0:T(8,128)(2,1)S(1)}, bf16[2,4,96,256]{3,2,1,0:T(8,128)(2,1)S(1)}, u32[]{:S(2)}, u32[]{:S(2)}) %collective-permute-start.3) | collective-permute-done | bytes 393248 | tf_op jit(solution)/shard_map/ppermute | solution.py:34
  27.7 0.0 collective-permute-done.4.refs_1_
  27.7 0.0 collective-permute-done.2
  27.7 0.1 pad_maximum_fusion.refs_3_
  27.8 3.1 collective-permute-start.5
  30.9 0.6 collective-permute-start.6
  31.5 1.0 collective-permute-start.7
  32.5 4.5 %collective-permute-start = (bf16[256,896]{1,0:T(8,128)(2,1)S(1)}, bf16[256,896]{1,0:T(8,128)(2,1)S(1)}, u32[]{:S(2)}, u32[]{:S(2)}) collective-permute-start(bf16[256,896]{1,0:T(8,128)(2,1)S(1)} %get-tuple-element.26), channel_id=1, source_target_pairs={{0,32},{1,33},{2,34},{3,35},{4,36},{5,37},{6,38},{7,39},{32,0},{33... | collective-permute-start | bytes 1376264 | tf_op jit(solution)/shard_map/ppermute | solution.py:34
  37.0 1.4 collective-permute-start.1
  38.4 30.8 %collective-permute-done = bf16[256,896]{1,0:T(8,128)(2,1)S(1)} collective-permute-done((bf16[256,896]{1,0:T(8,128)(2,1)S(1)}, bf16[256,896]{1,0:T(8,128)(2,1)S(1)}, u32[]{:S(2)}, u32[]{:S(2)}) %collective-permute-start) | collective-permute-done | bytes 458784 | tf_op jit(solution)/shard_map/ppermute | solution.py:34
  69.2 25.3 %collective-permute-done.1 = bf16[256,896]{1,0:T(8,128)(2,1)S(1)} collective-permute-done((bf16[256,896]{1,0:T(8,128)(2,1)S(1)}, bf16[256,896]{1,0:T(8,128)(2,1)S(1)}, u32[]{:S(2)}, u32[]{:S(2)}) %collective-permute-start.1) | collective-permute-done | bytes 458784 | tf_op jit(solution)/shard_map/ppermute | solution.py:34
  94.5 0.0 collective-permute-done.5.refs_4_
  94.5 0.0 collective-permute-done.6.refs_5_
  94.5 0.9 copy-done.10
  95.5 168.6 %shard_map.38 = bf16[7,2,2,4,96,256]{5,4,3,2,1,0:T(8,128)(2,1)} custom-call(s32[9]{0:T(128)} %copy-done.4, bf16[8,2,2,4,96,256]{5,4,3,2,1,0:T(8,128)(2,1)} %bitcast.22), custom_call_target="tpu_custom_call" | custom-call | bytes 12582912 | tf_op jit(solution)/shard_map/pallas_call | solution.py:134
  264.1 1.6 collective-permute-start.8
  265.7 0.1 pad_maximum_fusion.1.refs_7_
  265.8 2.8 collective-permute-start.9
  268.6 0.8 collective-permute-start.10
  269.4 0.9 collective-permute-start.11
  270.3 36.6 %collective-permute-done.9.refs_8_ = bf16[2,256,896]{2,1,0:T(8,128)(2,1)S(1)} collective-permute-done((bf16[2,256,896]{2,1,0:T(8,128)(2,1)S(1)}, bf16[2,256,896]{2,1,0:T(8,128)(2,1)S(1)}, u32[]{:S(2)}, u32[]{:S(2)}) %collective-permute-start.9) | collective-permute-done | bytes 917536 | tf_op jit(solution)/shard_map/ppermute | solution.py:34
  306.9 3.7 collective-permute-done.11.refs_10_
  310.6 16.5 %collective-permute-done.8.refs_2_ = bf16[7,2,2,4,96,256]{5,4,3,2,1,0:T(8,128)(2,1)} collective-permute-done((bf16[7,2,2,4,96,256]{5,4,3,2,1,0:T(8,128)(2,1)}, bf16[7,2,2,4,96,256]{5,4,3,2,1,0:T(8,128)(2,1)}, u32[]{:S(2)}, u32[]{:S(2)}) %collective-permute-start.8) | collective-permute-done | bytes 5505056 | tf_op jit(solution)/shard_map/ppermute | solution.py:34
  327.1 17.2 %shard_map.39 = (f32[384,896]{1,0:T(8,128)}, f32[384,896]{1,0:T(8,128)}) custom-call(s32[9]{0:T(128)} %copy-done.4, bf16[2,8,2,4,96,256]{5,4,3,2,1,0:T(8,128)(2,1)} %bitcast.23, bf16[2,4,96,256]{3,2,1,0:T(8,128)(2,1)} %copy-done.14, bf16[2,4,96,256]{3,2,1,0:T(8,128)(2,1)} %copy-done.15, bf16[7,2,2,4,96,256]{5,4,3,2,1,0:T(8,128)(2,1)} %collective-permute-done.8.refs_2_, ...), custom_call_target="tpu_custom_call" | custom-call | flops 5637144576 | bytes 20971520 | tf_op jit(solution)/shard_map/pallas_call | solution.py:108
  344.3 2.4 collective-permute-start.12
  346.7 17.2 %shard_map.41 = (f32[384,896]{1,0:T(8,128)}, f32[384,896]{1,0:T(8,128)}) custom-call(s32[9]{0:T(128)} %copy-done.4, bf16[2,8,2,4,96,256]{5,4,3,2,1,0:T(8,128)(2,1)} %bitcast.24, bf16[2,4,96,256]{3,2,1,0:T(8,128)(2,1)} %copy-done.14, bf16[2,4,96,256]{3,2,1,0:T(8,128)(2,1)} %copy-done.15, bf16[7,2,2,4,96,256]{5,4,3,2,1,0:T(8,128)(2,1)} %collective-permute-done.8.refs_2_, ...), custom_call_target="tpu_custom_call" | custom-call | flops 5637144576 | bytes 20971520 | tf_op jit(solution)/shard_map/pallas_call | solution.py:108
  363.8 0.2 collective-permute-start.16
  364.1 0.8 shard_map.40
  364.9 4.2 %collective-permute-start.13 = (bf16[96,448]{1,0:T(8,128)(2,1)S(1)}, bf16[96,448]{1,0:T(8,128)(2,1)S(1)}, u32[]{:S(2)}, u32[]{:S(2)}) collective-permute-start(bf16[96,448]{1,0:T(8,128)(2,1)S(1)} %get-tuple-element.38), channel_id=1, source_target_pairs={{0,32},{1,33},{2,34},{3,35},{4,36},{5,37},{6,38},{7,39},{32,0},{33... | collective-permute-start | bytes 258056 | tf_op jit(solution)/shard_map/ppermute | solution.py:34
  369.1 2.5 collective-permute-start.14
  371.5 1.3 collective-permute-start.15
  372.8 11.7 %collective-permute-done.16.received = f32[384,896]{1,0:T(8,128)S(1)} collective-permute-done((f32[384,896]{1,0:T(8,128)}, f32[384,896]{1,0:T(8,128)S(1)}, u32[]{:S(2)}, u32[]{:S(2)}) %collective-permute-start.16) | collective-permute-done | bytes 1376288 | tf_op jit(solution)/shard_map/ppermute | solution.py:34
  384.6 0.8 shard_map.42
  385.4 4.2 %collective-permute-start.17 = (bf16[96,448]{1,0:T(8,128)(2,1)S(1)}, bf16[96,448]{1,0:T(8,128)(2,1)S(1)}, u32[]{:S(2)}, u32[]{:S(2)}) collective-permute-start(bf16[96,448]{1,0:T(8,128)(2,1)S(1)} %get-tuple-element.44), channel_id=1, source_target_pairs={{0,32},{1,33},{2,34},{3,35},{4,36},{5,37},{6,38},{7,39},{32,0},{33... | collective-permute-start | bytes 258056 | tf_op jit(solution)/shard_map/ppermute | solution.py:34
  389.5 2.7 collective-permute-start.18
  392.2 1.3 collective-permute-start.19
  393.5 1.9 collective-permute-done.17.refs_5_
  395.4 6.2 %collective-permute-done.19.refs_7_ = bf16[96,448]{1,0:T(8,128)(2,1)S(1)} collective-permute-done((bf16[96,448]{1,0:T(8,128)(2,1)S(1)}, bf16[96,448]{1,0:T(8,128)(2,1)S(1)}, u32[]{:S(2)}, u32[]{:S(2)}) %collective-permute-start.19) | collective-permute-done | bytes 86048 | tf_op jit(solution)/shard_map/ppermute | solution.py:34
  401.6 1.5 shard_map.43
  (38 shorter events, 0.1 us)
Async XLA Ops:
  6.5 2.0 copy-start.2
  6.5 88.9 %all-gather.2.cloned.1.call-start = ((), (), s32[]{:S(2)}) async-start(), calls=%async_computation | async-start | bytes 6684672 | tf_op jit(solution)/shard_map/all_gather | solution.py:243
  8.4 2.9 copy-start.6
  8.6 1.2 copy-start.3
  9.8 18.0 %copy-start.4 = (s32[9]{0:T(128)}, s32[9]{0:T(128)S(1)}, u32[]{:S(2)}) copy-start(s32[9]{0:T(128)S(1)} %stack.57.place) | copy-start | bytes 112
  10.7 17.0 %collective-permute-start.2 = (bf16[256,896]{1,0:T(8,128)(2,1)S(1)}, bf16[256,896]{1,0:T(8,128)(2,1)S(1)}, u32[]{:S(2)}, u32[]{:S(2)}) collective-permute-start(bf16[256,896]{1,0:T(8,128)(2,1)S(1)} %get-tuple-element.29), channel_id=1, source_target_pairs={{0,8},{1,25},{2,10},{3,27},{4,12},{5,29},{6,14},{7,31},{32,40},{33... | collective-permute-start | bytes 1376264 | tf_op jit(solution)/shard_map/ppermute | solution.py:34
  11.3 16.4 %collective-permute-start.3 = (bf16[2,4,96,256]{3,2,1,0:T(8,128)(2,1)S(1)}, bf16[2,4,96,256]{3,2,1,0:T(8,128)(2,1)S(1)}, u32[]{:S(2)}, u32[]{:S(2)}) collective-permute-start(bf16[2,4,96,256]{3,2,1,0:T(8,128)(2,1)S(1)} %bitcast.26), channel_id=1, source_target_pairs={{0,8},{1,25},{2,10},{3,27},{4,12},{5,29},{6,14},{7,31},{32,40},{33... | collective-permute-start | bytes 1179656 | tf_op jit(solution)/shard_map/ppermute | solution.py:34
  12.8 14.9 %collective-permute-start.4 = (bf16[2,4,96,256]{3,2,1,0:T(8,128)(2,1)S(1)}, bf16[2,4,96,256]{3,2,1,0:T(8,128)(2,1)S(1)}, u32[]{:S(2)}, u32[]{:S(2)}) collective-permute-start(bf16[2,4,96,256]{3,2,1,0:T(8,128)(2,1)S(1)} %bitcast.27), channel_id=1, source_target_pairs={{0,25},{1,8},{2,27},{3,10},{4,29},{5,12},{6,31},{7,14},{32,57},{33... | collective-permute-start | bytes 1179656 | tf_op jit(solution)/shard_map/ppermute | solution.py:34
  27.7 236.4 %copy-start.14 = (bf16[2,4,96,256]{3,2,1,0:T(8,128)(2,1)}, bf16[2,4,96,256]{3,2,1,0:T(8,128)(2,1)S(1)}, u32[]{:S(2)}) copy-start(bf16[2,4,96,256]{3,2,1,0:T(8,128)(2,1)S(1)} %collective-permute-done.3.refs_0_) | copy-start | bytes 1179652
  27.7 236.4 %copy-start.15 = (bf16[2,4,96,256]{3,2,1,0:T(8,128)(2,1)}, bf16[2,4,96,256]{3,2,1,0:T(8,128)(2,1)S(1)}, u32[]{:S(2)}) copy-start(bf16[2,4,96,256]{3,2,1,0:T(8,128)(2,1)S(1)} %collective-permute-done.4.refs_1_) | copy-start | bytes 1179652
  27.8 236.3 %copy-start.7 = (bf16[2,256,896]{2,1,0:T(8,128)(2,1)}, bf16[2,256,896]{2,1,0:T(8,128)(2,1)S(1)}, u32[]{:S(2)}) copy-start(bf16[2,256,896]{2,1,0:T(8,128)(2,1)S(1)} %pad_maximum_fusion.refs_3_) | copy-start | bytes 2752516
  27.8 66.7 %collective-permute-start.5 = (bf16[2,256,896]{2,1,0:T(8,128)(2,1)S(1)}, bf16[2,256,896]{2,1,0:T(8,128)(2,1)S(1)}, u32[]{:S(2)}, u32[]{:S(2)}) collective-permute-start(bf16[2,256,896]{2,1,0:T(8,128)(2,1)S(1)} %pad_maximum_fusion.refs_3_), channel_id=1, source_target_pairs={{0,192},{1,193},{2,194},{3,195},{4,196},{5,197},{6,198},{7,199},{3... | collective-permute-start | bytes 2752520 | tf_op jit(solution)/shard_map/ppermute | solution.py:34
  30.9 63.6 %collective-permute-start.6 = (bf16[2,256,896]{2,1,0:T(8,128)(2,1)S(1)}, bf16[2,256,896]{2,1,0:T(8,128)(2,1)S(1)}, u32[]{:S(2)}, u32[]{:S(2)}) collective-permute-start(bf16[2,256,896]{2,1,0:T(8,128)(2,1)S(1)} %pad_maximum_fusion.refs_3_), channel_id=1, source_target_pairs={{0,128},{1,129},{2,130},{3,131},{4,132},{5,133},{6,134},{7,135},{3... | collective-permute-start | bytes 2752520 | tf_op jit(solution)/shard_map/ppermute | solution.py:34
  31.5 63.9 %collective-permute-start.7 = (bf16[2,256,896]{2,1,0:T(8,128)(2,1)S(1)}, bf16[2,256,896]{2,1,0:T(8,128)(2,1)}, u32[]{:S(2)}, u32[]{:S(2)}) collective-permute-start(bf16[2,256,896]{2,1,0:T(8,128)(2,1)S(1)} %pad_maximum_fusion.refs_3_), channel_id=1, source_target_pairs={{0,64},{1,65},{2,66},{3,67},{4,68},{5,69},{6,70},{7,71},{32,96},{3... | collective-permute-start | bytes 2752520 | tf_op jit(solution)/shard_map/ppermute | solution.py:34
  32.5 36.7 %collective-permute-start = (bf16[256,896]{1,0:T(8,128)(2,1)S(1)}, bf16[256,896]{1,0:T(8,128)(2,1)S(1)}, u32[]{:S(2)}, u32[]{:S(2)}) collective-permute-start(bf16[256,896]{1,0:T(8,128)(2,1)S(1)} %get-tuple-element.26), channel_id=1, source_target_pairs={{0,32},{1,33},{2,34},{3,35},{4,36},{5,37},{6,38},{7,39},{32,0},{33... | collective-permute-start | bytes 1376264 | tf_op jit(solution)/shard_map/ppermute | solution.py:34
  37.0 57.5 %collective-permute-start.1 = (bf16[256,896]{1,0:T(8,128)(2,1)S(1)}, bf16[256,896]{1,0:T(8,128)(2,1)S(1)}, u32[]{:S(2)}, u32[]{:S(2)}) collective-permute-start(bf16[256,896]{1,0:T(8,128)(2,1)S(1)} %get-tuple-element.27), channel_id=1, source_target_pairs={{0,40},{1,57},{2,42},{3,59},{4,44},{5,61},{6,46},{7,63},{32,8},{33... | collective-permute-start | bytes 1376264 | tf_op jit(solution)/shard_map/ppermute | solution.py:34
  94.5 169.6 %copy-start.9 = (bf16[2,256,896]{2,1,0:T(8,128)(2,1)}, bf16[2,256,896]{2,1,0:T(8,128)(2,1)S(1)}, u32[]{:S(2)}) copy-start(bf16[2,256,896]{2,1,0:T(8,128)(2,1)S(1)} %collective-permute-done.5.refs_4_) | copy-start | bytes 2752516
  94.5 0.9 copy-start.10
  264.1 63.0 %collective-permute-start.8 = (bf16[7,2,2,4,96,256]{5,4,3,2,1,0:T(8,128)(2,1)}, bf16[7,2,2,4,96,256]{5,4,3,2,1,0:T(8,128)(2,1)}, u32[]{:S(2)}, u32[]{:S(2)}) collective-permute-start(bf16[7,2,2,4,96,256]{5,4,3,2,1,0:T(8,128)(2,1)} %shard_map.38), channel_id=1, source_target_pairs={{0,8},{1,25},{2,10},{3,27},{4,12},{5,29},{6,14},{7,31},{32,40},{33... | collective-permute-start | bytes 16515080 | tf_op jit(solution)/shard_map/ppermute | solution.py:34
  265.8 61.3 %copy-start.8 = (bf16[2,256,896]{2,1,0:T(8,128)(2,1)}, bf16[2,256,896]{2,1,0:T(8,128)(2,1)S(1)}, u32[]{:S(2)}) copy-start(bf16[2,256,896]{2,1,0:T(8,128)(2,1)S(1)} %pad_maximum_fusion.1.refs_7_) | copy-start | bytes 2752516
  265.8 41.1 %collective-permute-start.9 = (bf16[2,256,896]{2,1,0:T(8,128)(2,1)S(1)}, bf16[2,256,896]{2,1,0:T(8,128)(2,1)S(1)}, u32[]{:S(2)}, u32[]{:S(2)}) collective-permute-start(bf16[2,256,896]{2,1,0:T(8,128)(2,1)S(1)} %pad_maximum_fusion.1.refs_7_), channel_id=1, source_target_pairs={{0,192},{1,193},{2,194},{3,195},{4,196},{5,197},{6,198},{7,199},{3... | collective-permute-start | bytes 2752520 | tf_op jit(solution)/shard_map/ppermute | solution.py:34
  268.6 38.3 %collective-permute-start.10 = (bf16[2,256,896]{2,1,0:T(8,128)(2,1)S(1)}, bf16[2,256,896]{2,1,0:T(8,128)(2,1)S(1)}, u32[]{:S(2)}, u32[]{:S(2)}) collective-permute-start(bf16[2,256,896]{2,1,0:T(8,128)(2,1)S(1)} %pad_maximum_fusion.1.refs_7_), channel_id=1, source_target_pairs={{0,128},{1,129},{2,130},{3,131},{4,132},{5,133},{6,134},{7,135},{3... | collective-permute-start | bytes 2752520 | tf_op jit(solution)/shard_map/ppermute | solution.py:34
  269.4 41.2 %collective-permute-start.11 = (bf16[2,256,896]{2,1,0:T(8,128)(2,1)S(1)}, bf16[2,256,896]{2,1,0:T(8,128)(2,1)S(1)}, u32[]{:S(2)}, u32[]{:S(2)}) collective-permute-start(bf16[2,256,896]{2,1,0:T(8,128)(2,1)S(1)} %pad_maximum_fusion.1.refs_7_), channel_id=1, source_target_pairs={{0,64},{1,65},{2,66},{3,67},{4,68},{5,69},{6,70},{7,71},{32,96},{3... | collective-permute-start | bytes 2752520 | tf_op jit(solution)/shard_map/ppermute | solution.py:34
  306.9 20.2 %copy-start.11 = (bf16[2,256,896]{2,1,0:T(8,128)(2,1)}, bf16[2,256,896]{2,1,0:T(8,128)(2,1)S(1)}, u32[]{:S(2)}) copy-start(bf16[2,256,896]{2,1,0:T(8,128)(2,1)S(1)} %collective-permute-done.9.refs_8_) | copy-start | bytes 2752516
  306.9 20.2 %copy-start.12 = (bf16[2,256,896]{2,1,0:T(8,128)(2,1)}, bf16[2,256,896]{2,1,0:T(8,128)(2,1)S(1)}, u32[]{:S(2)}) copy-start(bf16[2,256,896]{2,1,0:T(8,128)(2,1)S(1)} %collective-permute-done.10.refs_9_) | copy-start | bytes 2752516
  310.6 16.5 %copy-start.13 = (bf16[2,256,896]{2,1,0:T(8,128)(2,1)}, bf16[2,256,896]{2,1,0:T(8,128)(2,1)S(1)}, u32[]{:S(2)}) copy-start(bf16[2,256,896]{2,1,0:T(8,128)(2,1)S(1)} %collective-permute-done.11.refs_10_) | copy-start | bytes 2752516
  344.3 19.8 %copy-start.1 = (f32[384,896]{1,0:T(8,128)S(1)}, f32[384,896]{1,0:T(8,128)}, u32[]{:S(2)}) copy-start(f32[384,896]{1,0:T(8,128)} %get-tuple-element.35.kept) | copy-start | bytes 4128772
  344.3 19.8 %copy-start.5 = (s32[9]{0:T(128)S(1)}, s32[9]{0:T(128)}, u32[]{:S(2)}) copy-start(s32[9]{0:T(128)} %copy-done.4) | copy-start | bytes 112
  344.3 19.8 %collective-permute-start.12 = (f32[384,896]{1,0:T(8,128)}, f32[384,896]{1,0:T(8,128)S(1)}, u32[]{:S(2)}, u32[]{:S(2)}) collective-permute-start(f32[384,896]{1,0:T(8,128)} %get-tuple-element.36), channel_id=1, source_target_pairs={{0,24},{1,9},{2,26},{3,11},{4,28},{5,13},{6,30},{7,15},{32,56},{33... | collective-permute-start | bytes 4128776 | tf_op jit(solution)/shard_map/ppermute | solution.py:34
  363.8 20.7 %collective-permute-start.16 = (f32[384,896]{1,0:T(8,128)}, f32[384,896]{1,0:T(8,128)S(1)}, u32[]{:S(2)}, u32[]{:S(2)}) collective-permute-start(f32[384,896]{1,0:T(8,128)} %get-tuple-element.42), channel_id=1, source_target_pairs={{0,24},{1,9},{2,26},{3,11},{4,28},{5,13},{6,30},{7,15},{32,56},{33... | collective-permute-start | bytes 4128776 | tf_op jit(solution)/shard_map/ppermute | solution.py:34
  364.1 20.5 %copy-start = (f32[384,896]{1,0:T(8,128)S(1)}, f32[384,896]{1,0:T(8,128)}, u32[]{:S(2)}) copy-start(f32[384,896]{1,0:T(8,128)} %get-tuple-element.41.kept) | copy-start | bytes 4128772
  364.9 27.3 %collective-permute-start.13 = (bf16[96,448]{1,0:T(8,128)(2,1)S(1)}, bf16[96,448]{1,0:T(8,128)(2,1)S(1)}, u32[]{:S(2)}, u32[]{:S(2)}) collective-permute-start(bf16[96,448]{1,0:T(8,128)(2,1)S(1)} %get-tuple-element.38), channel_id=1, source_target_pairs={{0,32},{1,33},{2,34},{3,35},{4,36},{5,37},{6,38},{7,39},{32,0},{33... | collective-permute-start | bytes 258056 | tf_op jit(solution)/shard_map/ppermute | solution.py:34
  369.1 24.4 %collective-permute-start.14 = (bf16[96,448]{1,0:T(8,128)(2,1)S(1)}, bf16[96,448]{1,0:T(8,128)(2,1)S(1)}, u32[]{:S(2)}, u32[]{:S(2)}) collective-permute-start(bf16[96,448]{1,0:T(8,128)(2,1)S(1)} %get-tuple-element.39), channel_id=1, source_target_pairs={{0,8},{1,25},{2,10},{3,27},{4,12},{5,29},{6,14},{7,31},{32,40},{33... | collective-permute-start | bytes 258056 | tf_op jit(solution)/shard_map/ppermute | solution.py:34
  371.5 22.0 %collective-permute-start.15 = (bf16[96,448]{1,0:T(8,128)(2,1)S(1)}, bf16[96,448]{1,0:T(8,128)(2,1)S(1)}, u32[]{:S(2)}, u32[]{:S(2)}) collective-permute-start(bf16[96,448]{1,0:T(8,128)(2,1)S(1)} %get-tuple-element.40), channel_id=1, source_target_pairs={{0,40},{1,57},{2,42},{3,59},{4,44},{5,61},{6,46},{7,63},{32,8},{33... | collective-permute-start | bytes 258056 | tf_op jit(solution)/shard_map/ppermute | solution.py:34
  385.4 10.0 %collective-permute-start.17 = (bf16[96,448]{1,0:T(8,128)(2,1)S(1)}, bf16[96,448]{1,0:T(8,128)(2,1)S(1)}, u32[]{:S(2)}, u32[]{:S(2)}) collective-permute-start(bf16[96,448]{1,0:T(8,128)(2,1)S(1)} %get-tuple-element.44), channel_id=1, source_target_pairs={{0,32},{1,33},{2,34},{3,35},{4,36},{5,37},{6,38},{7,39},{32,0},{33... | collective-permute-start | bytes 258056 | tf_op jit(solution)/shard_map/ppermute | solution.py:34
  389.5 5.9 %collective-permute-start.18 = (bf16[96,448]{1,0:T(8,128)(2,1)S(1)}, bf16[96,448]{1,0:T(8,128)(2,1)S(1)}, u32[]{:S(2)}, u32[]{:S(2)}) collective-permute-start(bf16[96,448]{1,0:T(8,128)(2,1)S(1)} %get-tuple-element.45), channel_id=1, source_target_pairs={{0,8},{1,25},{2,10},{3,27},{4,12},{5,29},{6,14},{7,31},{32,40},{33... | collective-permute-start | bytes 258056 | tf_op jit(solution)/shard_map/ppermute | solution.py:34
  392.2 9.4 %collective-permute-start.19 = (bf16[96,448]{1,0:T(8,128)(2,1)S(1)}, bf16[96,448]{1,0:T(8,128)(2,1)S(1)}, u32[]{:S(2)}, u32[]{:S(2)}) collective-permute-start(bf16[96,448]{1,0:T(8,128)(2,1)S(1)} %get-tuple-element.46), channel_id=1, source_target_pairs={{0,40},{1,57},{2,42},{3,59},{4,44},{5,61},{6,46},{7,63},{32,8},{33... | collective-permute-start | bytes 258056 | tf_op jit(solution)/shard_map/ppermute | solution.py:34
Sparse Core Ops, SparseCore 0:
  9.2 84.0 all-gather.1

commit v3 on v2

v3 whole, which is shorter than its diff:
```python
import functools

import jax
import jax.numpy as jnp
import numpy as np
from jax import lax
from jax.experimental import pallas as pl
from jax.experimental.pallas import tpu as pltpu
from jax.sharding import Mesh
from jax.sharding import PartitionSpec as P

NX, NY, NZ, NC = 4, 4, 8, 2
AXES = ("y", "zh", "x", "zl", "c")
TILE = 128
PARTS = ((0, 512), (512, 896))


def device_index(x, y, z, c):
    return ((y * 2 + z // 4) * NX + x) * 8 + (z % 4) * 2 + c


def side(x, c):
    return 1 - 2 * ((x + c) % 2)


def move(value, target):
    pairs = []
    for x in range(NX):
        for y in range(NY):
            for z in range(NZ):
                for c in range(NC):
                    tx, ty, tz, tc = target(x, y, z, c)
                    pairs.append((device_index(x, y, z, c), device_index(tx % NX, ty % NY, tz % NZ, tc)))
    return lax.ppermute(value, AXES, pairs)


def to_partner(x, y, z, c):
    return x + side(x, c), y, z, c


def to_crossed(x, y, z, c):
    return x + side(x, 1 - c), y, z, 1 - c


def to_antipode(x, y, z, c):
    return x, y, z + 4, c


def to_both(x, y, z, c):
    return x + side(x, c), y, z + 4, c


def to_summer(x, y, z, c):
    return x - side(x, c), y, z, c


def product_kernel(lo, hi, place, own, *refs):
    first, beside, rest, near, far, (out, pieces, lhs, rhs, lhs_sem, rhs_sem) = refs[:2], refs[2:4], refs[4], refs[5:9], refs[9:13], refs[13:]
    y, zh, z, c = place[0], place[1], place[2], place[3]
    rows = pieces.shape[3]
    shares = []
    for i in range(2):
        share, loads = place[6 + i], []
        for k in range(8):
            loads.append((own.at[:, k, share], pieces.at[i, k]))
        for d in range(8):
            for e in range(2):
                core, at = lax.rem(c + e, 2), lax.rem(z + d, 8)
                if d == 0:
                    source = first[e].at[share]
                elif d in (1, 7):
                    source = beside[e].at[d // 7, share]
                else:
                    source = rest.at[d - 2, core, share]
                loads.append((source, pieces.at[i, 8 + lax.rem(at, 4) * 2 + core, at // 4]))
        shares.append([pltpu.make_async_copy(a, b, lhs_sem.at[i * 24 + n]) for n, (a, b) in enumerate(loads)])
    weights = []
    for d in range(4):
        for u in range(2):
            for f in range(2):
                k = u * 8 + lax.rem(y + d, 4) * 2 + lax.rem(zh + f, 2)
                source = far[d].at[u] if f else near[d].at[u, :, lo:hi]
                target = rhs.at[pl.ds(pl.multiple_of(k * 256, 256), 256)]
                weights.append(pltpu.make_async_copy(source, target, rhs_sem.at[len(weights)]))
    for copy in (*shares[0], *weights, *shares[1]):
        copy.start()
    for i in range(2):
        for copy in shares[i]:
            copy.wait()
        for k in range(16):
            lhs[:, k * 256 : (k + 1) * 256] = pieces[i, k].reshape(2 * rows, 256)
        if i == 0:
            for copy in weights:
                copy.wait()
        for at in range(0, hi - lo, 256):
            to = min(at + 256, hi - lo)
            out[i * 2 * rows : (i + 1) * 2 * rows, at:to] = jnp.dot(lhs[...], rhs[:, at:to], preferred_element_type=jnp.float32)


def product(part, place, own, partner, near, far):
    lo, hi = part
    rows, depth = own.shape[3], 4096
    hbm, vmem = pl.BlockSpec(memory_space=pltpu.HBM), pl.BlockSpec(memory_space=pltpu.VMEM)
    operands = [own, *partner, *near, *far]
    return pl.pallas_call(
        functools.partial(product_kernel, lo, hi),
        out_shape=jax.ShapeDtypeStruct((4 * rows, hi - lo), jnp.float32),
        in_specs=[pl.BlockSpec(memory_space=pltpu.SMEM)] + [hbm] * len(operands),
        out_specs=vmem,
        scratch_shapes=[
            pltpu.VMEM((2, 16, 2, rows, 256), jnp.bfloat16),
            pltpu.VMEM((2 * rows, depth), jnp.bfloat16),
            pltpu.VMEM((depth, hi - lo), jnp.bfloat16),
            pltpu.SemaphoreType.DMA((48,)),
            pltpu.SemaphoreType.DMA((16,)),
        ],
        compiler_params=pltpu.CompilerParams(vmem_limit_bytes=48 << 20),
        cost_estimate=pl.CostEstimate(flops=8 * rows * depth * (hi - lo), bytes_accessed=12 << 20, transcendentals=0),
    )(place, *operands)


def pick_kernel(place, panel, out, sem):
    copies = [pltpu.make_async_copy(panel.at[lax.rem(place[2] + 2 + d, 8)], out.at[d], sem.at[d]) for d in range(5)]
    for copy in copies:
        copy.start()
    for copy in copies:
        copy.wait()


def pick(place, panel):
    return pl.pallas_call(
        pick_kernel,
        out_shape=jax.ShapeDtypeStruct((5, *panel.shape[1:]), panel.dtype),
        in_specs=[pl.BlockSpec(memory_space=pltpu.SMEM), pl.BlockSpec(memory_space=pltpu.HBM)],
        out_specs=pl.BlockSpec(memory_space=pltpu.VMEM),
        scratch_shapes=[pltpu.SemaphoreType.DMA((5,))],
        compiler_params=pltpu.CompilerParams(vmem_limit_bytes=16 << 20),
        cost_estimate=pl.CostEstimate(flops=0, bytes_accessed=8 << 20, transcendentals=0),
    )(place, panel)


def cut_kernel(place, gate, up, near, away, give):
    for zh in range(2):
        for q in range(2):

            @pl.when((place[1] == zh) & (place[8] == q))
            def _(zh=zh, q=q):
                for out, half, side_q in ((near, zh, q), (away, 1 - zh, q), (give.at[0], zh, 1 - q), (give.at[1], 1 - zh, 1 - q)):
                    base = half * 896
                    for t in range(3):
                        lo = base + side_q * 512 + t * TILE
                        out[:, 2 * t * TILE : (2 * t + 1) * TILE] = gate[:, lo : lo + TILE]
                        out[:, (2 * t + 1) * TILE : (2 * t + 2) * TILE] = up[:, lo : lo + TILE]
                    lo = base + 384 + side_q * 64
                    out[:, 6 * TILE :] = jnp.concatenate([gate[:, lo : lo + 64], up[:, lo : lo + 64]], 1)


def cut(place, gate, up):
    vmem = pl.BlockSpec(memory_space=pltpu.VMEM)
    depth, wide = gate.shape[0], gate.shape[1] // 2
    return pl.pallas_call(
        cut_kernel,
        out_shape=[jax.ShapeDtypeStruct((depth, wide), gate.dtype)] * 2 + [jax.ShapeDtypeStruct((2, depth, wide), gate.dtype)],
        in_specs=[pl.BlockSpec(memory_space=pltpu.SMEM), vmem, vmem],
        out_specs=[vmem] * 3,
        compiler_params=pltpu.CompilerParams(vmem_limit_bytes=24 << 20),
        cost_estimate=pl.CostEstimate(flops=0, bytes_accessed=4 << 20, transcendentals=0),
    )(place, gate, up)


def gated_kernel(place, kept, received, *outs):
    zh = place[1]
    rows = outs[0].shape[0]
    for n, out in enumerate(outs):
        at = pl.multiple_of((n // 2 * 2 + lax.rem(zh + n, 2)) * rows, rows)
        total = kept[pl.ds(at, rows), :] + received[pl.ds(at, rows), :]
        whole = total.shape[1] // (2 * TILE)
        for t in range(whole):
            gate, up = total[:, 2 * t * TILE : (2 * t + 1) * TILE], total[:, (2 * t + 1) * TILE : (2 * t + 2) * TILE]
            out[:, t * TILE : (t + 1) * TILE] = (jax.nn.silu(gate) * up).astype(jnp.bfloat16)
        if total.shape[1] % (2 * TILE):
            last = total[:, 2 * whole * TILE :]
            up = pltpu.roll(last, TILE // 2, 1)
            out[:, whole * TILE :] = (jax.nn.silu(last) * up).astype(jnp.bfloat16)[:, : TILE // 2]


def gated(place, kept, received):
    rows, wide = kept.shape
    vmem = pl.BlockSpec(memory_space=pltpu.VMEM)
    return pl.pallas_call(
        gated_kernel,
        out_shape=[jax.ShapeDtypeStruct((rows // 4, wide // 2), jnp.bfloat16)] * 4,
        in_specs=[pl.BlockSpec(memory_space=pltpu.SMEM), vmem, vmem],
        out_specs=[vmem] * 4,
        compiler_params=pltpu.CompilerParams(vmem_limit_bytes=16 << 20),
        cost_estimate=pl.CostEstimate(flops=8 * rows * wide, bytes_accessed=4 << 20, transcendentals=rows * wide // 2),
    )(place, kept, received)


def gather_kernel(place, *refs):
    blocks, out = refs[:8], refs[8]
    for zh in range(2):
        for q in range(2):

            @pl.when((place[1] == zh) & (place[8] == q))
            def _(zh=zh, q=q):
                for other in range(2):
                    base = (zh ^ other) * 896
                    for side_q in range(2):
                        n = 2 * (q ^ side_q) + other
                        at = base + side_q * 512
                        out[:, at : at + 256] = blocks[n][...]
                        out[:, at + 256 : at + 384] = blocks[4 + n][:, :TILE]
                    halves = [blocks[4 + 2 * (q ^ side_q) + other][:, TILE:] for side_q in range(2)]
                    out[:, base + 384 : base + 512] = jnp.concatenate(halves, 1)


def gather(place, blocks):
    vmem = pl.BlockSpec(memory_space=pltpu.VMEM)
    return pl.pallas_call(
        gather_kernel,
        out_shape=jax.ShapeDtypeStruct((blocks[0].shape[0], 1792), jnp.bfloat16),
        in_specs=[pl.BlockSpec(memory_space=pltpu.SMEM)] + [vmem] * 8,
        out_specs=vmem,
        compiler_params=pltpu.CompilerParams(vmem_limit_bytes=16 << 20),
        cost_estimate=pl.CostEstimate(flops=0, bytes_accessed=2 << 20, transcendentals=0),
    )(place, *blocks)


def along_y(value):
    return [value] + [move(value, lambda x, y, z, c, d=d: (x, y - d, z, c)) for d in range(1, 4)]


def after(value, *others):
    return lax.optimization_barrier((value, *others))[0]


def per_device(tokens, gate_weight, up_weight):
    y, zh, x, zl, c = (lax.axis_index(a) for a in AXES)
    ahead = side(x, c)
    partner, summer = (x + ahead + 4) % 4, (x - ahead + 4) % 4
    over = (summer - ahead + 4) % 4
    q = ((x + 1 - c) // 2) % 2
    rows = tokens.shape[0] // NX

    def places(a, b):
        return jnp.stack([y, zh, zh * 4 + zl, c, x, partner, a, b, q]).astype(jnp.int32)

    send_place, keep_place = places(summer, over), places(x, partner)

    panel = lax.all_gather(tokens, ("zh", "zl", "c"), axis=0)
    split = tokens.reshape(NX, rows, 256)
    around = [move(split, lambda x, y, z, c: (x, y, z - 1, c)), move(split, lambda x, y, z, c: (x, y, z + 1, c))]
    first = [move(split, t) for t in (to_partner, to_crossed)]
    near, away, give = cut(keep_place, gate_weight, up_weight)
    got = move(give, to_partner)

    near, away, got, around, first = lax.optimization_barrier((near, away, got, around, first))
    far = [jnp.stack([away[:, lo:hi], got[1, :, lo:hi]]) for lo, hi in PARTS]
    far[0] = move(far[0], to_antipode)
    near = along_y(jnp.stack([near, got[0]]))
    around = jnp.stack(around)
    beside = [move(around, t) for t in (to_partner, to_crossed)]

    panel = after(panel, far[0], *near[1:], *beside)
    own = panel.reshape(2, 8, NX, rows, 256)
    rest = move(pick(keep_place, panel.reshape(8, 2, NX, rows, 256)), to_partner)
    far[1] = move(after(far[1], panel), to_antipode)
    far = [along_y(f) for f in far]

    held = (*first, *beside, rest)
    sums = [move(product(p, send_place, own, held, near, f), to_summer) for p, f in zip(PARTS, far)]
    blocks = []
    for p, f, received in zip(PARTS, far, sums):
        turn = after(keep_place, *blocks[:1])
        parts = gated(keep_place, product(p, turn, own, held, near, f), received)
        blocks += [parts[0]] + [move(b, t) for b, t in zip(parts[1:], (to_antipode, to_partner, to_both))]
    return gather(keep_place, blocks)


def solution(mesh):
    fine = Mesh(np.array(mesh.devices).reshape(NY, 2, NX, NZ // 2, NC), AXES)
    rows, cols = ("y", "zh"), ("zl", "c")
    return jax.shard_map(
        per_device,
        mesh=fine,
        in_specs=(P(rows, ("x", *cols)), P(("x", *rows), cols), P(("x", *rows), cols)),
        out_specs=P((*rows, "x"), cols),
        check_vma=False,
    )
```

time: 412 us -> 246 us (0.60)
  Pallas kernels: 207 us -> 45.1 us
  waiting for transfers between devices: 147 us -> 119 us
  starting transfers between devices: 37.8 us -> 49.8 us
  local copies, waits for them, and re-layouts: 4.1 us -> 12.5 us
    pallas_call x4 -> x6, Pallas kernels: 204 us -> 42.6 us  [the longest x4 38.3 us: product(): pl.pallas_call(functools.partial(product_kernel, lo, hi), out_shape=jax.S...]
    ppermute x20 -> x27, waiting for transfers between devices: 147 us -> 119 us  [move(): return lax.ppermute(value, AXES, pairs)]
    ppermute x20 -> x27, starting transfers between devices: 37.8 us -> 49.8 us  [move(): return lax.ppermute(value, AXES, pairs)]
    unnamed x32, local copies, waits for them, and re-layouts: 2.17 us -> 10.4 us
  transfers between devices with their start and end apart: 21 -> 28, of which waited for: 9 -> 12; matrix products, arithmetic and copies ran while one was open for 0% -> 1% of each run, Pallas kernels for 5% -> 17%
where the time goes in v3:
time: 246 us; the launch traced here: 241 us
  waiting for transfers between devices  119 us (48%)
  starting transfers between devices  49.8 us (20%)
  Pallas kernels  45.1 us (18%)
  between operations  13.7 us (6%)
  local copies, waits for them, and re-layouts  12.5 us (5%)
    ppermute x27, waiting for transfers between devices, move(): return lax.ppermute(value, AXES, pairs)  119 us
    ppermute x27, starting transfers between devices, move(): return lax.ppermute(value, AXES, pairs)  49.8 us
    pallas_call x4, Pallas kernels, product(): pl.pallas_call(functools.partial(product_kernel, lo, hi), out_shape=jax.S...  38.3 us
    unnamed x32, local copies, waits for them, and re-layouts  10.4 us
  transfers between devices with their start and end apart: 28, of which 12 were waited for; matrix products, arithmetic and copies ran while one was open for 1% of the time, Pallas kernels for 17%

profile of v3, /device:TPU:98, one launch (start us, length us, event | category | flops | bytes accessed | tf_op | source)
XLA Modules:
  0.0 241.4 jit_solution(10682287169290476310)
XLA Ops:
  7.4 1.2 copy-done.10
  8.6 1.2 copy-done.11
  9.8 0.9 shard_map.37
  11.4 3.1 %collective-permute-start.2 = (bf16[4,192,256]{2,1,0:T(8,128)(2,1)S(1)}, bf16[4,192,256]{2,1,0:T(8,128)(2,1)S(1)}, u32[]{:S(2)}, u32[]{:S(2)}) collective-permute-start(bf16[4,192,256]{2,1,0:T(8,128)(2,1)S(1)} %bitcast.27), channel_id=1, source_target_pairs={{0,2},{1,3},{2,4},{3,5},{4,6},{5,7},{6,32},{7,33},{32,34},{33,35},... | collective-permute-start | bytes 1179656 | tf_op jit(solution)/shard_map/ppermute | solution.py:34
  14.6 1.5 collective-permute-start.3
  16.1 8.2 %collective-permute-done.1 = bf16[4,192,256]{2,1,0:T(8,128)(2,1)S(1)} collective-permute-done((bf16[4,192,256]{2,1,0:T(8,128)(2,1)S(1)}, bf16[4,192,256]{2,1,0:T(8,128)(2,1)S(1)}, u32[]{:S(2)}, u32[]{:S(2)}) %collective-permute-start.1) | collective-permute-done | bytes 393248 | tf_op jit(solution)/shard_map/ppermute | solution.py:34
  24.2 1.0 collective-permute-done.2
  25.2 7.4 %collective-permute-done.3.refs_0_ = bf16[4,192,256]{2,1,0:T(8,128)(2,1)S(1)} collective-permute-done((bf16[4,192,256]{2,1,0:T(8,128)(2,1)S(1)}, bf16[4,192,256]{2,1,0:T(8,128)(2,1)S(1)}, u32[]{:S(2)}, u32[]{:S(2)}) %collective-permute-start.3) | collective-permute-done | bytes 393248 | tf_op jit(solution)/shard_map/ppermute | solution.py:34
  34.2 4.6 %collective-permute-start.5 = (bf16[2,256,512]{2,1,0:T(8,128)(2,1)S(1)}, bf16[2,256,512]{2,1,0:T(8,128)(2,1)}, u32[]{:S(2)}, u32[]{:S(2)}) collective-permute-start(bf16[2,256,512]{2,1,0:T(8,128)(2,1)S(1)} %pad_maximum_fusion.2), channel_id=1, source_target_pairs={{0,32},{1,33},{2,34},{3,35},{4,36},{5,37},{6,38},{7,39},{32,0},{33... | collective-permute-start | bytes 1572872 | tf_op jit(solution)/shard_map/ppermute | solution.py:34
  39.0 3.1 %collective-permute-start.6 = (bf16[2,256,896]{2,1,0:T(8,128)(2,1)S(1)}, bf16[2,256,896]{2,1,0:T(8,128)(2,1)S(1)}, u32[]{:S(2)}, u32[]{:S(2)}) collective-permute-start(bf16[2,256,896]{2,1,0:T(8,128)(2,1)S(1)} %pad_maximum_fusion.refs_5_), channel_id=1, source_target_pairs={{0,192},{1,193},{2,194},{3,195},{4,196},{5,197},{6,198},{7,199},{3... | collective-permute-start | bytes 2752520 | tf_op jit(solution)/shard_map/ppermute | solution.py:34
  42.7 1.0 collective-permute-start.8
  44.3 29.3 %collective-permute-done.5.refs_9_ = bf16[2,256,512]{2,1,0:T(8,128)(2,1)} collective-permute-done((bf16[2,256,512]{2,1,0:T(8,128)(2,1)S(1)}, bf16[2,256,512]{2,1,0:T(8,128)(2,1)}, u32[]{:S(2)}, u32[]{:S(2)}) %collective-permute-start.5) | collective-permute-done | bytes 524320 | tf_op jit(solution)/shard_map/ppermute | solution.py:34
  73.6 11.4 %collective-permute-done.10.refs_3_ = bf16[2,4,192,256]{3,2,1,0:T(8,128)(2,1)S(1)} collective-permute-done((bf16[2,4,192,256]{3,2,1,0:T(8,128)(2,1)S(1)}, bf16[2,4,192,256]{3,2,1,0:T(8,128)(2,1)S(1)}, u32[]{:S(2)}, u32[]{:S(2)}) %collective-permute-start.10) | collective-permute-done | bytes 786464 | tf_op jit(solution)/shard_map/ppermute | solution.py:34
  85.1 1.0 copy-done.13
  86.0 2.8 %copy-done = bf16[12288,256]{1,0:T(8,128)(2,1)S(1)} copy-done((bf16[12288,256]{1,0:T(8,128)(2,1)S(1)}, bf16[12288,256]{1,0:T(8,128)(2,1)}, u32[]{:S(2)}) %copy-start) | copy-done | bytes 6291480
  88.8 2.9 %shard_map.38 = bf16[5,2,4,192,256]{4,3,2,1,0:T(8,128)(2,1)} custom-call(s32[9]{0:T(128)S(1)} %stack.76.place, bf16[8,2,4,192,256]{4,3,2,1,0:T(8,128)(2,1)S(1)} %bitcast.24), custom_call_target="tpu_custom_call" | custom-call | bytes 8388608 | tf_op jit(solution)/shard_map/pallas_call | solution.py:131
  91.7 0.9 collective-permute-start.11
  92.6 3.0 %collective-permute-start.12 = (bf16[2,256,512]{2,1,0:T(8,128)(2,1)}, bf16[2,256,512]{2,1,0:T(8,128)(2,1)}, u32[]{:S(2)}, u32[]{:S(2)}) collective-permute-start(bf16[2,256,512]{2,1,0:T(8,128)(2,1)} %collective-permute-done.5.refs_9_), channel_id=1, source_target_pairs={{0,192},{1,193},{2,194},{3,195},{4,196},{5,197},{6,198},{7,199},{3... | collective-permute-start | bytes 1572872 | tf_op jit(solution)/shard_map/ppermute | solution.py:34
  96.2 1.0 collective-permute-start.14
  97.2 0.9 slice.19
  98.2 1.0 slice_bitcast_fusion.1
  99.1 0.8 pad_maximum_fusion.3
  99.9 5.1 %collective-permute-start.19 = (bf16[2,256,384]{2,1,0:T(8,128)(2,1)}, bf16[2,256,384]{2,1,0:T(8,128)(2,1)}, u32[]{:S(2)}, u32[]{:S(2)}) collective-permute-start(bf16[2,256,384]{2,1,0:T(8,128)(2,1)} %pad_maximum_fusion.3), channel_id=1, source_target_pairs={{0,32},{1,33},{2,34},{3,35},{4,36},{5,37},{6,38},{7,39},{32,0},{33... | collective-permute-start | bytes 1179656 | tf_op jit(solution)/shard_map/ppermute | solution.py:34
  105.1 13.3 %collective-permute-done.12.refs_10_ = bf16[2,256,512]{2,1,0:T(8,128)(2,1)} collective-permute-done((bf16[2,256,512]{2,1,0:T(8,128)(2,1)}, bf16[2,256,512]{2,1,0:T(8,128)(2,1)}, u32[]{:S(2)}, u32[]{:S(2)}) %collective-permute-start.12) | collective-permute-done | bytes 524320 | tf_op jit(solution)/shard_map/ppermute | solution.py:34
  118.4 3.7 %collective-permute-done.14.refs_12_ = bf16[2,256,512]{2,1,0:T(8,128)(2,1)} collective-permute-done((bf16[2,256,512]{2,1,0:T(8,128)(2,1)}, bf16[2,256,512]{2,1,0:T(8,128)(2,1)}, u32[]{:S(2)}, u32[]{:S(2)}) %collective-permute-start.14) | collective-permute-done | bytes 524320 | tf_op jit(solution)/shard_map/ppermute | solution.py:34
  122.2 15.6 %collective-permute-done.11.refs_4_ = bf16[5,2,4,192,256]{4,3,2,1,0:T(8,128)(2,1)} collective-permute-done((bf16[5,2,4,192,256]{4,3,2,1,0:T(8,128)(2,1)}, bf16[5,2,4,192,256]{4,3,2,1,0:T(8,128)(2,1)}, u32[]{:S(2)}, u32[]{:S(2)}) %collective-permute-start.11) | collective-permute-done | bytes 3932192 | tf_op jit(solution)/shard_map/ppermute | solution.py:34
  137.8 9.4 %shard_map.40 = f32[768,512]{1,0:T(8,128)} custom-call(s32[9]{0:T(128)S(1)} %stack.86.place, bf16[2,8,4,192,256]{4,3,2,1,0:T(8,128)(2,1)} %bitcast.20, bf16[4,192,256]{2,1,0:T(8,128)(2,1)S(1)} %copy-done.6, bf16[4,192,256]{2,1,0:T(8,128)(2,1)S(1)} %copy-done.8, bf16[2,4,192,256]{3,2,1,0:T(8,128)(2,1)S(1)} %collective-permute-done.9.refs_2_, ...), custom_call_target="tpu_custom_call" | custom-call | flops 3221225472 | bytes 12582912 | tf_op jit(solution)/shard_map/pallas_call | solution.py:105
  147.2 1.8 collective-permute-start.15
  148.9 3.0 %collective-permute-start.20 = (bf16[2,256,384]{2,1,0:T(8,128)(2,1)}, bf16[2,256,384]{2,1,0:T(8,128)(2,1)S(1)}, u32[]{:S(2)}, u32[]{:S(2)}) collective-permute-start(bf16[2,256,384]{2,1,0:T(8,128)(2,1)} %collective-permute-done.19.refs_9_), channel_id=1, source_target_pairs={{0,192},{1,193},{2,194},{3,195},{4,196},{5,197},{6,198},{7,199},{3... | collective-permute-start | bytes 1179656 | tf_op jit(solution)/shard_map/ppermute | solution.py:34
  152.6 1.0 collective-permute-start.22
  153.5 16.2 %collective-permute-done.20.refs_10_ = bf16[2,256,384]{2,1,0:T(8,128)(2,1)S(1)} collective-permute-done((bf16[2,256,384]{2,1,0:T(8,128)(2,1)}, bf16[2,256,384]{2,1,0:T(8,128)(2,1)S(1)}, u32[]{:S(2)}, u32[]{:S(2)}) %collective-permute-start.20) | collective-permute-done | bytes 393248 | tf_op jit(solution)/shard_map/ppermute | solution.py:34
  169.7 3.6 %collective-permute-done.22.refs_12_ = bf16[2,256,384]{2,1,0:T(8,128)(2,1)S(1)} collective-permute-done((bf16[2,256,384]{2,1,0:T(8,128)(2,1)}, bf16[2,256,384]{2,1,0:T(8,128)(2,1)S(1)}, u32[]{:S(2)}, u32[]{:S(2)}) %collective-permute-start.22) | collective-permute-done | bytes 393248 | tf_op jit(solution)/shard_map/ppermute | solution.py:34
  173.3 9.8 %shard_map.43 = f32[768,384]{1,0:T(8,128)} custom-call(s32[9]{0:T(128)S(1)} %stack.86.place, bf16[2,8,4,192,256]{4,3,2,1,0:T(8,128)(2,1)} %bitcast.21, bf16[4,192,256]{2,1,0:T(8,128)(2,1)S(1)} %copy-done.6, bf16[4,192,256]{2,1,0:T(8,128)(2,1)S(1)} %copy-done.8, bf16[2,4,192,256]{3,2,1,0:T(8,128)(2,1)S(1)} %collective-permute-done.9.refs_2_, ...), custom_call_target="tpu_custom_call" | custom-call | flops 2415919104 | bytes 12582912 | tf_op jit(solution)/shard_map/pallas_call | solution.py:105
  183.1 1.4 collective-permute-start.23
  184.5 9.4 %shard_map.39.kept = f32[768,512]{1,0:T(8,128)} custom-call(s32[9]{0:T(128)S(1)} %stack.76.place, bf16[2,8,4,192,256]{4,3,2,1,0:T(8,128)(2,1)} %bitcast.22, bf16[4,192,256]{2,1,0:T(8,128)(2,1)S(1)} %copy-done.6, bf16[4,192,256]{2,1,0:T(8,128)(2,1)S(1)} %copy-done.8, bf16[2,4,192,256]{3,2,1,0:T(8,128)(2,1)S(1)} %collective-permute-done.9.refs_2_, ...), custom_call_target="tpu_custom_call" | custom-call | flops 3221225472 | bytes 12582912 | tf_op jit(solution)/shard_map/pallas_call | solution.py:105
  193.9 1.5 copy-done.4
  196.2 9.8 %shard_map.42.kept = f32[768,384]{1,0:T(8,128)} custom-call(s32[9]{0:T(128)S(1)} %stack.76.place, bf16[2,8,4,192,256]{4,3,2,1,0:T(8,128)(2,1)} %bitcast.23, bf16[4,192,256]{2,1,0:T(8,128)(2,1)S(1)} %copy-done.6, bf16[4,192,256]{2,1,0:T(8,128)(2,1)S(1)} %copy-done.8, bf16[2,4,192,256]{3,2,1,0:T(8,128)(2,1)S(1)} %collective-permute-done.9.refs_2_, ...), custom_call_target="tpu_custom_call" | custom-call | flops 2415919104 | bytes 12582912 | tf_op jit(solution)/shard_map/pallas_call | solution.py:105
  206.0 1.3 copy-done.9
  207.2 0.8 shard_map.44
  208.0 5.0 %collective-permute-start.24 = (bf16[192,192]{1,0:T(8,128)(2,1)S(1)}, bf16[192,192]{1,0:T(8,128)(2,1)S(1)}, u32[]{:S(2)}, u32[]{:S(2)}) collective-permute-start(bf16[192,192]{1,0:T(8,128)(2,1)S(1)} %get-tuple-element.44), channel_id=1, source_target_pairs={{0,32},{1,33},{2,34},{3,35},{4,36},{5,37},{6,38},{7,39},{32,0},{33... | collective-permute-start | bytes 221192 | tf_op jit(solution)/shard_map/ppermute | solution.py:34
  213.0 1.0 collective-permute-start.16
  214.0 1.2 collective-permute-start.17
  215.2 5.2 %collective-permute-start.18 = (bf16[192,256]{1,0:T(8,128)(2,1)S(1)}, bf16[192,256]{1,0:T(8,128)(2,1)S(1)}, u32[]{:S(2)}, u32[]{:S(2)}) collective-permute-start(bf16[192,256]{1,0:T(8,128)(2,1)S(1)} %get-tuple-element.40), channel_id=1, source_target_pairs={{0,40},{1,57},{2,42},{3,59},{4,44},{5,61},{6,46},{7,63},{32,8},{33... | collective-permute-start | bytes 294920 | tf_op jit(solution)/shard_map/ppermute | solution.py:34
  220.4 1.4 collective-permute-start.25
  221.8 2.3 collective-permute-start.26
  224.1 1.7 collective-permute-done.25.refs_6_
  225.8 7.2 %collective-permute-done.26.refs_7_ = bf16[192,192]{1,0:T(8,128)(2,1)S(1)} collective-permute-done((bf16[192,192]{1,0:T(8,128)(2,1)S(1)}, bf16[192,192]{1,0:T(8,128)(2,1)S(1)}, u32[]{:S(2)}, u32[]{:S(2)}) %collective-permute-start.26) | collective-permute-done | bytes 73760 | tf_op jit(solution)/shard_map/ppermute | solution.py:34
  233.0 1.5 shard_map.45
  (61 shorter events, 6.7 us)
Async XLA Ops:
  6.5 4.8 %copy-start.15 = (bf16[768,256]{1,0:T(8,128)(2,1)S(1)}, bf16[768,256]{1,0:T(8,128)(2,1)}, u32[]{:S(2)}) copy-start(bf16[768,256]{1,0:T(8,128)(2,1)} %param.3) | copy-start | bytes 1179652
  6.5 79.5 %all-gather.3.cloned.1.call-start = ((), (), s32[]{:S(2)}) async-start(), calls=%async_computation | async-start | bytes 6684672 | tf_op jit(solution)/shard_map/all_gather | solution.py:251
  7.4 1.2 copy-start.10
  8.6 1.2 copy-start.11
  10.7 74.4 %copy-start.12 = (bf16[256,896]{1,0:T(8,128)(2,1)}, bf16[256,896]{1,0:T(8,128)(2,1)S(1)}, u32[]{:S(2)}) copy-start(bf16[256,896]{1,0:T(8,128)(2,1)S(1)} %get-tuple-element.29) | copy-start | bytes 1376260
  10.7 23.4 %collective-permute-start = (bf16[2,256,896]{2,1,0:T(8,128)(2,1)S(1)}, bf16[2,256,896]{2,1,0:T(8,128)(2,1)S(1)}, u32[]{:S(2)}, u32[]{:S(2)}) collective-permute-start(bf16[2,256,896]{2,1,0:T(8,128)(2,1)S(1)} %get-tuple-element.28), channel_id=1, source_target_pairs={{0,8},{1,25},{2,10},{3,27},{4,12},{5,29},{6,14},{7,31},{32,40},{33... | collective-permute-start | bytes 2752520 | tf_op jit(solution)/shard_map/ppermute | solution.py:34
  11.3 12.9 %collective-permute-start.1 = (bf16[4,192,256]{2,1,0:T(8,128)(2,1)S(1)}, bf16[4,192,256]{2,1,0:T(8,128)(2,1)S(1)}, u32[]{:S(2)}, u32[]{:S(2)}) collective-permute-start(bf16[4,192,256]{2,1,0:T(8,128)(2,1)S(1)} %bitcast.26), channel_id=1, source_target_pairs={{0,38},{1,39},{2,0},{3,1},{4,2},{5,3},{6,4},{7,5},{32,6},{33,7},{3... | collective-permute-start | bytes 1179656 | tf_op jit(solution)/shard_map/ppermute | solution.py:34
  11.4 13.8 %collective-permute-start.2 = (bf16[4,192,256]{2,1,0:T(8,128)(2,1)S(1)}, bf16[4,192,256]{2,1,0:T(8,128)(2,1)S(1)}, u32[]{:S(2)}, u32[]{:S(2)}) collective-permute-start(bf16[4,192,256]{2,1,0:T(8,128)(2,1)S(1)} %bitcast.27), channel_id=1, source_target_pairs={{0,2},{1,3},{2,4},{3,5},{4,6},{5,7},{6,32},{7,33},{32,34},{33,35},... | collective-permute-start | bytes 1179656 | tf_op jit(solution)/shard_map/ppermute | solution.py:34
  14.6 18.0 %collective-permute-start.3 = (bf16[4,192,256]{2,1,0:T(8,128)(2,1)S(1)}, bf16[4,192,256]{2,1,0:T(8,128)(2,1)S(1)}, u32[]{:S(2)}, u32[]{:S(2)}) collective-permute-start(bf16[4,192,256]{2,1,0:T(8,128)(2,1)S(1)} %bitcast.28), channel_id=1, source_target_pairs={{0,8},{1,25},{2,10},{3,27},{4,12},{5,29},{6,14},{7,31},{32,40},{33... | collective-permute-start | bytes 1179656 | tf_op jit(solution)/shard_map/ppermute | solution.py:34
  16.1 17.3 %collective-permute-start.4 = (bf16[4,192,256]{2,1,0:T(8,128)(2,1)S(1)}, bf16[4,192,256]{2,1,0:T(8,128)(2,1)S(1)}, u32[]{:S(2)}, u32[]{:S(2)}) collective-permute-start(bf16[4,192,256]{2,1,0:T(8,128)(2,1)S(1)} %bitcast.29), channel_id=1, source_target_pairs={{0,25},{1,8},{2,27},{3,10},{4,29},{5,12},{6,31},{7,14},{32,57},{33... | collective-permute-start | bytes 1179656 | tf_op jit(solution)/shard_map/ppermute | solution.py:34
  32.6 0.7 copy-start.5
  33.4 0.7 copy-start.7
  34.1 4.7 %copy-start.14 = (bf16[2,256,896]{2,1,0:T(8,128)(2,1)}, bf16[2,256,896]{2,1,0:T(8,128)(2,1)S(1)}, u32[]{:S(2)}) copy-start(bf16[2,256,896]{2,1,0:T(8,128)(2,1)S(1)} %collective-permute-done) | copy-start | bytes 2752516
  34.2 39.4 %collective-permute-start.5 = (bf16[2,256,512]{2,1,0:T(8,128)(2,1)S(1)}, bf16[2,256,512]{2,1,0:T(8,128)(2,1)}, u32[]{:S(2)}, u32[]{:S(2)}) collective-permute-start(bf16[2,256,512]{2,1,0:T(8,128)(2,1)S(1)} %pad_maximum_fusion.2), channel_id=1, source_target_pairs={{0,32},{1,33},{2,34},{3,35},{4,36},{5,37},{6,38},{7,39},{32,0},{33... | collective-permute-start | bytes 1572872 | tf_op jit(solution)/shard_map/ppermute | solution.py:34
  39.0 46.1 %collective-permute-start.6 = (bf16[2,256,896]{2,1,0:T(8,128)(2,1)S(1)}, bf16[2,256,896]{2,1,0:T(8,128)(2,1)S(1)}, u32[]{:S(2)}, u32[]{:S(2)}) collective-permute-start(bf16[2,256,896]{2,1,0:T(8,128)(2,1)S(1)} %pad_maximum_fusion.refs_5_), channel_id=1, source_target_pairs={{0,192},{1,193},{2,194},{3,195},{4,196},{5,197},{6,198},{7,199},{3... | collective-permute-start | bytes 2752520 | tf_op jit(solution)/shard_map/ppermute | solution.py:34
  42.0 43.0 %collective-permute-start.7 = (bf16[2,256,896]{2,1,0:T(8,128)(2,1)S(1)}, bf16[2,256,896]{2,1,0:T(8,128)(2,1)S(1)}, u32[]{:S(2)}, u32[]{:S(2)}) collective-permute-start(bf16[2,256,896]{2,1,0:T(8,128)(2,1)S(1)} %pad_maximum_fusion.refs_5_), channel_id=1, source_target_pairs={{0,128},{1,129},{2,130},{3,131},{4,132},{5,133},{6,134},{7,135},{3... | collective-permute-start | bytes 2752520 | tf_op jit(solution)/shard_map/ppermute | solution.py:34
  42.7 43.4 %collective-permute-start.8 = (bf16[2,256,896]{2,1,0:T(8,128)(2,1)S(1)}, bf16[2,256,896]{2,1,0:T(8,128)(2,1)}, u32[]{:S(2)}, u32[]{:S(2)}) collective-permute-start(bf16[2,256,896]{2,1,0:T(8,128)(2,1)S(1)} %pad_maximum_fusion.refs_5_), channel_id=1, source_target_pairs={{0,64},{1,65},{2,66},{3,67},{4,68},{5,69},{6,70},{7,71},{32,96},{3... | collective-permute-start | bytes 2752520 | tf_op jit(solution)/shard_map/ppermute | solution.py:34
  43.7 29.9 %collective-permute-start.9 = (bf16[2,4,192,256]{3,2,1,0:T(8,128)(2,1)S(1)}, bf16[2,4,192,256]{3,2,1,0:T(8,128)(2,1)S(1)}, u32[]{:S(2)}, u32[]{:S(2)}) collective-permute-start(bf16[2,4,192,256]{3,2,1,0:T(8,128)(2,1)S(1)} %pad_maximum_fusion.1), channel_id=1, source_target_pairs={{0,8},{1,25},{2,10},{3,27},{4,12},{5,29},{6,14},{7,31},{32,40},{33... | collective-permute-start | bytes 2359304 | tf_op jit(solution)/shard_map/ppermute | solution.py:34
  73.6 11.4 %collective-permute-start.10 = (bf16[2,4,192,256]{3,2,1,0:T(8,128)(2,1)S(1)}, bf16[2,4,192,256]{3,2,1,0:T(8,128)(2,1)S(1)}, u32[]{:S(2)}, u32[]{:S(2)}) collective-permute-start(bf16[2,4,192,256]{3,2,1,0:T(8,128)(2,1)S(1)} %pad_maximum_fusion.1), channel_id=1, source_target_pairs={{0,25},{1,8},{2,27},{3,10},{4,29},{5,12},{6,31},{7,14},{32,57},{33... | collective-permute-start | bytes 2359304 | tf_op jit(solution)/shard_map/ppermute | solution.py:34
  85.0 6.6 %copy-start.1 = (bf16[2,256,896]{2,1,0:T(8,128)(2,1)}, bf16[2,256,896]{2,1,0:T(8,128)(2,1)S(1)}, u32[]{:S(2)}) copy-start(bf16[2,256,896]{2,1,0:T(8,128)(2,1)S(1)} %collective-permute-done.6.refs_6_) | copy-start | bytes 2752516
  85.1 1.0 copy-start.13
  86.0 2.8 %copy-start = (bf16[12288,256]{1,0:T(8,128)(2,1)S(1)}, bf16[12288,256]{1,0:T(8,128)(2,1)}, u32[]{:S(2)}) copy-start(bf16[12288,256]{1,0:T(8,128)(2,1)} %all-gather.3.cloned.1.call-done) | copy-start | bytes 18874372
  91.7 46.1 %collective-permute-start.11 = (bf16[5,2,4,192,256]{4,3,2,1,0:T(8,128)(2,1)}, bf16[5,2,4,192,256]{4,3,2,1,0:T(8,128)(2,1)}, u32[]{:S(2)}, u32[]{:S(2)}) collective-permute-start(bf16[5,2,4,192,256]{4,3,2,1,0:T(8,128)(2,1)} %shard_map.38), channel_id=1, source_target_pairs={{0,8},{1,25},{2,10},{3,27},{4,12},{5,29},{6,14},{7,31},{32,40},{33... | collective-permute-start | bytes 11796488 | tf_op jit(solution)/shard_map/ppermute | solution.py:34
  92.6 45.2 %copy-start.6 = (bf16[4,192,256]{2,1,0:T(8,128)(2,1)S(1)}, bf16[4,192,256]{2,1,0:T(8,128)(2,1)}, u32[]{:S(2)}) copy-start(bf16[4,192,256]{2,1,0:T(8,128)(2,1)} %copy-done.5) | copy-start | bytes 1179652
  92.6 45.2 %copy-start.8 = (bf16[4,192,256]{2,1,0:T(8,128)(2,1)S(1)}, bf16[4,192,256]{2,1,0:T(8,128)(2,1)}, u32[]{:S(2)}) copy-start(bf16[4,192,256]{2,1,0:T(8,128)(2,1)} %copy-done.7) | copy-start | bytes 1179652
  92.6 25.9 %collective-permute-start.12 = (bf16[2,256,512]{2,1,0:T(8,128)(2,1)}, bf16[2,256,512]{2,1,0:T(8,128)(2,1)}, u32[]{:S(2)}, u32[]{:S(2)}) collective-permute-start(bf16[2,256,512]{2,1,0:T(8,128)(2,1)} %collective-permute-done.5.refs_9_), channel_id=1, source_target_pairs={{0,192},{1,193},{2,194},{3,195},{4,196},{5,197},{6,198},{7,199},{3... | collective-permute-start | bytes 1572872 | tf_op jit(solution)/shard_map/ppermute | solution.py:34
  95.6 22.8 %collective-permute-start.13 = (bf16[2,256,512]{2,1,0:T(8,128)(2,1)}, bf16[2,256,512]{2,1,0:T(8,128)(2,1)}, u32[]{:S(2)}, u32[]{:S(2)}) collective-permute-start(bf16[2,256,512]{2,1,0:T(8,128)(2,1)} %collective-permute-done.5.refs_9_), channel_id=1, source_target_pairs={{0,128},{1,129},{2,130},{3,131},{4,132},{5,133},{6,134},{7,135},{3... | collective-permute-start | bytes 1572872 | tf_op jit(solution)/shard_map/ppermute | solution.py:34
  96.2 25.9 %collective-permute-start.14 = (bf16[2,256,512]{2,1,0:T(8,128)(2,1)}, bf16[2,256,512]{2,1,0:T(8,128)(2,1)}, u32[]{:S(2)}, u32[]{:S(2)}) collective-permute-start(bf16[2,256,512]{2,1,0:T(8,128)(2,1)} %collective-permute-done.5.refs_9_), channel_id=1, source_target_pairs={{0,64},{1,65},{2,66},{3,67},{4,68},{5,69},{6,70},{7,71},{32,96},{3... | collective-permute-start | bytes 1572872 | tf_op jit(solution)/shard_map/ppermute | solution.py:34
  99.9 49.0 %collective-permute-start.19 = (bf16[2,256,384]{2,1,0:T(8,128)(2,1)}, bf16[2,256,384]{2,1,0:T(8,128)(2,1)}, u32[]{:S(2)}, u32[]{:S(2)}) collective-permute-start(bf16[2,256,384]{2,1,0:T(8,128)(2,1)} %pad_maximum_fusion.3), channel_id=1, source_target_pairs={{0,32},{1,33},{2,34},{3,35},{4,36},{5,37},{6,38},{7,39},{32,0},{33... | collective-permute-start | bytes 1179656 | tf_op jit(solution)/shard_map/ppermute | solution.py:34
  137.8 35.5 %copy-start.2 = (bf16[2,256,896]{2,1,0:T(8,128)(2,1)S(1)}, bf16[2,256,896]{2,1,0:T(8,128)(2,1)}, u32[]{:S(2)}) copy-start(bf16[2,256,896]{2,1,0:T(8,128)(2,1)} %copy-done.1) | copy-start | bytes 2752516
  147.2 46.8 %collective-permute-start.15 = (f32[768,512]{1,0:T(8,128)}, f32[768,512]{1,0:T(8,128)S(1)}, u32[]{:S(2)}, u32[]{:S(2)}) collective-permute-start(f32[768,512]{1,0:T(8,128)} %shard_map.40), channel_id=1, source_target_pairs={{0,24},{1,9},{2,26},{3,11},{4,28},{5,13},{6,30},{7,15},{32,56},{33... | collective-permute-start | bytes 4718600 | tf_op jit(solution)/shard_map/ppermute | solution.py:34
  148.9 20.8 %collective-permute-start.20 = (bf16[2,256,384]{2,1,0:T(8,128)(2,1)}, bf16[2,256,384]{2,1,0:T(8,128)(2,1)S(1)}, u32[]{:S(2)}, u32[]{:S(2)}) collective-permute-start(bf16[2,256,384]{2,1,0:T(8,128)(2,1)} %collective-permute-done.19.refs_9_), channel_id=1, source_target_pairs={{0,192},{1,193},{2,194},{3,195},{4,196},{5,197},{6,198},{7,199},{3... | collective-permute-start | bytes 1179656 | tf_op jit(solution)/shard_map/ppermute | solution.py:34
  151.9 17.8 %collective-permute-start.21 = (bf16[2,256,384]{2,1,0:T(8,128)(2,1)}, bf16[2,256,384]{2,1,0:T(8,128)(2,1)S(1)}, u32[]{:S(2)}, u32[]{:S(2)}) collective-permute-start(bf16[2,256,384]{2,1,0:T(8,128)(2,1)} %collective-permute-done.19.refs_9_), channel_id=1, source_target_pairs={{0,128},{1,129},{2,130},{3,131},{4,132},{5,133},{6,134},{7,135},{3... | collective-permute-start | bytes 1179656 | tf_op jit(solution)/shard_map/ppermute | solution.py:34
  152.6 20.7 %collective-permute-start.22 = (bf16[2,256,384]{2,1,0:T(8,128)(2,1)}, bf16[2,256,384]{2,1,0:T(8,128)(2,1)S(1)}, u32[]{:S(2)}, u32[]{:S(2)}) collective-permute-start(bf16[2,256,384]{2,1,0:T(8,128)(2,1)} %collective-permute-done.19.refs_9_), channel_id=1, source_target_pairs={{0,64},{1,65},{2,66},{3,67},{4,68},{5,69},{6,70},{7,71},{32,96},{3... | collective-permute-start | bytes 1179656 | tf_op jit(solution)/shard_map/ppermute | solution.py:34
  183.1 22.9 %collective-permute-start.23 = (f32[768,384]{1,0:T(8,128)}, f32[768,384]{1,0:T(8,128)S(1)}, u32[]{:S(2)}, u32[]{:S(2)}) collective-permute-start(f32[768,384]{1,0:T(8,128)} %shard_map.43), channel_id=1, source_target_pairs={{0,24},{1,9},{2,26},{3,11},{4,28},{5,13},{6,30},{7,15},{32,56},{33... | collective-permute-start | bytes 3538952 | tf_op jit(solution)/shard_map/ppermute | solution.py:34
  193.9 2.3 copy-start.3
  193.9 1.5 copy-start.4
  206.0 1.3 copy-start.9
  208.0 13.8 %collective-permute-start.24 = (bf16[192,192]{1,0:T(8,128)(2,1)S(1)}, bf16[192,192]{1,0:T(8,128)(2,1)S(1)}, u32[]{:S(2)}, u32[]{:S(2)}) collective-permute-start(bf16[192,192]{1,0:T(8,128)(2,1)S(1)} %get-tuple-element.44), channel_id=1, source_target_pairs={{0,32},{1,33},{2,34},{3,35},{4,36},{5,37},{6,38},{7,39},{32,0},{33... | collective-permute-start | bytes 221192 | tf_op jit(solution)/shard_map/ppermute | solution.py:34
  213.0 20.0 %collective-permute-start.16 = (bf16[192,256]{1,0:T(8,128)(2,1)S(1)}, bf16[192,256]{1,0:T(8,128)(2,1)S(1)}, u32[]{:S(2)}, u32[]{:S(2)}) collective-permute-start(bf16[192,256]{1,0:T(8,128)(2,1)S(1)} %get-tuple-element.38), channel_id=1, source_target_pairs={{0,32},{1,33},{2,34},{3,35},{4,36},{5,37},{6,38},{7,39},{32,0},{33... | collective-permute-start | bytes 294920 | tf_op jit(solution)/shard_map/ppermute | solution.py:34
  214.0 19.0 %collective-permute-start.17 = (bf16[192,256]{1,0:T(8,128)(2,1)S(1)}, bf16[192,256]{1,0:T(8,128)(2,1)S(1)}, u32[]{:S(2)}, u32[]{:S(2)}) collective-permute-start(bf16[192,256]{1,0:T(8,128)(2,1)S(1)} %get-tuple-element.39), channel_id=1, source_target_pairs={{0,8},{1,25},{2,10},{3,27},{4,12},{5,29},{6,14},{7,31},{32,40},{33... | collective-permute-start | bytes 294920 | tf_op jit(solution)/shard_map/ppermute | solution.py:34
  215.2 17.8 %collective-permute-start.18 = (bf16[192,256]{1,0:T(8,128)(2,1)S(1)}, bf16[192,256]{1,0:T(8,128)(2,1)S(1)}, u32[]{:S(2)}, u32[]{:S(2)}) collective-permute-start(bf16[192,256]{1,0:T(8,128)(2,1)S(1)} %get-tuple-element.40), channel_id=1, source_target_pairs={{0,40},{1,57},{2,42},{3,59},{4,44},{5,61},{6,46},{7,63},{32,8},{33... | collective-permute-start | bytes 294920 | tf_op jit(solution)/shard_map/ppermute | solution.py:34
  220.4 5.4 %collective-permute-start.25 = (bf16[192,192]{1,0:T(8,128)(2,1)S(1)}, bf16[192,192]{1,0:T(8,128)(2,1)S(1)}, u32[]{:S(2)}, u32[]{:S(2)}) collective-permute-start(bf16[192,192]{1,0:T(8,128)(2,1)S(1)} %get-tuple-element.45), channel_id=1, source_target_pairs={{0,8},{1,25},{2,10},{3,27},{4,12},{5,29},{6,14},{7,31},{32,40},{33... | collective-permute-start | bytes 221192 | tf_op jit(solution)/shard_map/ppermute | solution.py:34
  221.8 11.2 %collective-permute-start.26 = (bf16[192,192]{1,0:T(8,128)(2,1)S(1)}, bf16[192,192]{1,0:T(8,128)(2,1)S(1)}, u32[]{:S(2)}, u32[]{:S(2)}) collective-permute-start(bf16[192,192]{1,0:T(8,128)(2,1)S(1)} %get-tuple-element.46), channel_id=1, source_target_pairs={{0,40},{1,57},{2,42},{3,59},{4,44},{5,61},{6,46},{7,63},{32,8},{33... | collective-permute-start | bytes 221192 | tf_op jit(solution)/shard_map/ppermute | solution.py:34
Sparse Core Ops, SparseCore 0:
  9.2 69.8 all-gather.2

commit v4 on v3

v4 whole, which is shorter than its diff:
```python
import functools

import jax
import jax.numpy as jnp
import numpy as np
from jax import lax
from jax.experimental import pallas as pl
from jax.experimental.pallas import tpu as pltpu
from jax.sharding import Mesh
from jax.sharding import PartitionSpec as P

NX, NY, NZ, NC = 4, 4, 8, 2
AXES = ("y", "zh", "x", "zl", "c")
TILE = 128
PARTS = ((0, 512), (512, 896))


def device_index(x, y, z, c):
    return ((y * 2 + z // 4) * NX + x) * 8 + (z % 4) * 2 + c


def side(x, c):
    return 1 - 2 * ((x + c) % 2)


def move(value, target):
    pairs = []
    for x in range(NX):
        for y in range(NY):
            for z in range(NZ):
                for c in range(NC):
                    tx, ty, tz, tc = target(x, y, z, c)
                    pairs.append((device_index(x, y, z, c), device_index(tx % NX, ty % NY, tz % NZ, tc)))
    return lax.ppermute(value, AXES, pairs)


def to_partner(x, y, z, c):
    return x + side(x, c), y, z, c


def to_crossed(x, y, z, c):
    return x + side(x, 1 - c), y, z, 1 - c


def to_antipode(x, y, z, c):
    return x, y, z + 4, c


def to_both(x, y, z, c):
    return x + side(x, c), y, z + 4, c


def to_summer(x, y, z, c):
    return x - side(x, c), y, z, c


def product_kernel(place, own, partner, *refs):
    near, far, (outs, lhs, rhs) = refs[:4], (refs[4:8], refs[8:12]), (refs[12:14], *refs[14:])
    y, zh = place[0], place[1]
    rows = own.shape[3]
    for d in range(4):
        for u in range(2):
            k = u * 8 + lax.rem(y + d, 4) * 2
            at = pl.ds(pl.multiple_of((k + zh) * 256, 256), 256)
            rhs[at, :] = near[d][u]
            at = pl.ds(pl.multiple_of((k + 1 - zh) * 256, 256), 256)
            for (lo, hi), part in zip(PARTS, far):
                rhs[at, lo:hi] = part[d][u]
    for i, out in enumerate(outs):
        for k in range(16):
            source = own if k < 8 else partner
            lhs[:, k * 256 : (k + 1) * 256] = source[:, k % 8, place[4 + i]].reshape(2 * rows, 256)
        for at in range(0, rhs.shape[1], 256):
            to = min(at + 256, rhs.shape[1])
            out[:, at:to] = jnp.dot(lhs[...], rhs[:, at:to], preferred_element_type=jnp.float32)


def product(place, own, partner, near, far):
    rows, depth, wide = own.shape[3], 4096, near[0].shape[2]
    vmem = pl.BlockSpec(memory_space=pltpu.VMEM)
    operands = [own, partner, *near, *far[0], *far[1]]
    return pl.pallas_call(
        product_kernel,
        out_shape=[jax.ShapeDtypeStruct((2 * rows, wide), jnp.float32)] * 2,
        in_specs=[pl.BlockSpec(memory_space=pltpu.SMEM)] + [vmem] * len(operands),
        out_specs=[vmem] * 2,
        scratch_shapes=[pltpu.VMEM((2 * rows, depth), jnp.bfloat16), pltpu.VMEM((depth, wide), jnp.bfloat16)],
        compiler_params=pltpu.CompilerParams(vmem_limit_bytes=40 << 20),
        cost_estimate=pl.CostEstimate(flops=8 * rows * depth * wide, bytes_accessed=24 << 20, transcendentals=0),
    )(place, *operands)


def cut_kernel(place, gate, up, near, away, give_near, give_away):
    for zh in range(2):
        for q in range(2):

            @pl.when((place[1] == zh) & (place[6] == q))
            def _(zh=zh, q=q):
                for out, half, side_q in ((near, zh, q), (away, 1 - zh, q), (give_near, zh, 1 - q), (give_away, 1 - zh, 1 - q)):
                    base = half * 896
                    for t in range(3):
                        lo = base + side_q * 512 + t * TILE
                        out[:, 2 * t * TILE : (2 * t + 1) * TILE] = gate[:, lo : lo + TILE]
                        out[:, (2 * t + 1) * TILE : (2 * t + 2) * TILE] = up[:, lo : lo + TILE]
                    lo = base + 384 + side_q * 64
                    out[:, 6 * TILE :] = jnp.concatenate([gate[:, lo : lo + 64], up[:, lo : lo + 64]], 1)


def cut(place, gate, up):
    vmem = pl.BlockSpec(memory_space=pltpu.VMEM)
    depth, wide = gate.shape[0], gate.shape[1] // 2
    return pl.pallas_call(
        cut_kernel,
        out_shape=[jax.ShapeDtypeStruct((depth, wide), gate.dtype)] * 4,
        in_specs=[pl.BlockSpec(memory_space=pltpu.SMEM), vmem, vmem],
        out_specs=[vmem] * 4,
        compiler_params=pltpu.CompilerParams(vmem_limit_bytes=24 << 20),
        cost_estimate=pl.CostEstimate(flops=0, bytes_accessed=4 << 20, transcendentals=0),
    )(place, gate, up)


def gated_kernel(place, kept, received, *outs):
    zh = place[1]
    rows, whole = outs[0].shape[0], kept.shape[1] // (2 * TILE)
    for n, out in enumerate(outs):
        at = pl.ds(pl.multiple_of(lax.rem(zh + n, 2) * rows, rows), rows)
        total = kept[at, :] + received[at, :]
        for t in range(whole):
            gate, up = total[:, 2 * t * TILE : (2 * t + 1) * TILE], total[:, (2 * t + 1) * TILE : (2 * t + 2) * TILE]
            out[:, t * TILE : (t + 1) * TILE] = (jax.nn.silu(gate) * up).astype(jnp.bfloat16)
        last = total[:, 2 * whole * TILE :]
        up = pltpu.roll(last, TILE // 2, 1)
        out[:, whole * TILE :] = (jax.nn.silu(last) * up).astype(jnp.bfloat16)[:, : TILE // 2]


def gated(place, kept, received):
    rows, wide = kept.shape
    vmem = pl.BlockSpec(memory_space=pltpu.VMEM)
    return pl.pallas_call(
        gated_kernel,
        out_shape=[jax.ShapeDtypeStruct((rows // 2, wide // 2), jnp.bfloat16)] * 2,
        in_specs=[pl.BlockSpec(memory_space=pltpu.SMEM), vmem, vmem],
        out_specs=[vmem] * 2,
        compiler_params=pltpu.CompilerParams(vmem_limit_bytes=16 << 20),
        cost_estimate=pl.CostEstimate(flops=8 * rows * wide, bytes_accessed=4 << 20, transcendentals=rows * wide // 2),
    )(place, kept, received)


def gather_kernel(place, *refs):
    blocks, out = refs[:4], refs[4]
    for zh in range(2):
        for q in range(2):

            @pl.when((place[1] == zh) & (place[6] == q))
            def _(zh=zh, q=q):
                for other in range(2):
                    base = (zh ^ other) * 896
                    low, high = blocks[2 * q + other], blocks[2 * (1 - q) + other]
                    out[:, base : base + 384] = low[:, :384]
                    out[:, base + 384 : base + 512] = jnp.concatenate([low[:, 384:], high[:, 384:]], 1)
                    out[:, base + 512 : base + 896] = high[:, :384]


def gather(place, blocks):
    vmem = pl.BlockSpec(memory_space=pltpu.VMEM)
    return pl.pallas_call(
        gather_kernel,
        out_shape=jax.ShapeDtypeStruct((blocks[0].shape[0], 1792), jnp.bfloat16),
        in_specs=[pl.BlockSpec(memory_space=pltpu.SMEM)] + [vmem] * 4,
        out_specs=vmem,
        compiler_params=pltpu.CompilerParams(vmem_limit_bytes=16 << 20),
        cost_estimate=pl.CostEstimate(flops=0, bytes_accessed=2 << 20, transcendentals=0),
    )(place, *blocks)


def along_y(value):
    return [value] + [move(value, lambda x, y, z, c, d=d: (x, y - d, z, c)) for d in range(1, 4)]


def after(value, *others):
    return lax.optimization_barrier((value, *others))[0]


def per_device(tokens, gate_weight, up_weight):
    y, zh, x, zl, c = (lax.axis_index(a) for a in AXES)
    ahead = side(x, c)
    partner, summer = (x + ahead + 4) % 4, (x - ahead + 4) % 4
    over = (summer - ahead + 4) % 4
    q = ((x + 1 - c) // 2) % 2
    rows = tokens.shape[0] // NX

    def places(a, b):
        return jnp.stack([y, zh, zl, c, a, b, q]).astype(jnp.int32)

    send_place, keep_place = places(summer, over), places(x, partner)

    panel = lax.all_gather(tokens, ("zh", "zl", "c"), axis=0)
    near, away, give_near, give_away = cut(keep_place, gate_weight, up_weight)
    got_near, got_away = move(give_near, to_partner), move(give_away, to_partner)
    near = along_y(jnp.stack([near, got_near]))

    panel = after(panel, got_away, *near[1:])
    partner_panel = move(panel, to_partner).reshape(2, 8, NX, rows, 256)
    own = panel.reshape(2, 8, NX, rows, 256)
    away, got_away = lax.optimization_barrier((away, got_away, panel))[:2]
    far = [jnp.stack([away[:, lo:hi], got_away[:, lo:hi]]) for lo, hi in PARTS]
    far[0] = move(far[0], to_antipode)
    far[1] = move(after(far[1], far[0]), to_antipode)
    far = [along_y(f) for f in far]

    sent = product(send_place, own, partner_panel, near, far)
    sums = [move(sent[0], to_summer), move(sent[1], to_summer)]
    kept = product(after(keep_place, *sent), own, partner_panel, near, far)
    mine, over_z = gated(keep_place, kept[0], sums[0])
    over_x, over_both = gated(keep_place, kept[1], sums[1])
    blocks = [mine, move(over_z, to_antipode), move(over_x, to_partner), move(over_both, to_both)]
    return gather(keep_place, blocks)


def solution(mesh):
    fine = Mesh(np.array(mesh.devices).reshape(NY, 2, NX, NZ // 2, NC), AXES)
    rows, cols = ("y", "zh"), ("zl", "c")
    return jax.shard_map(
        per_device,
        mesh=fine,
        in_specs=(P(rows, ("x", *cols)), P(("x", *rows), cols), P(("x", *rows), cols)),
        out_specs=P((*rows, "x"), cols),
        check_vma=False,
    )
```

time: 246 us -> 221 us (0.90)
  the two profiles are of different devices: /device:TPU:98 before, /device:TPU:24 now
where the time goes in v4:
time: 221 us
  waiting for transfers between devices  95.5 us (43%)
  starting transfers between devices  72.3 us (33%)
  Pallas kernels  28.7 us (13%)
  between operations  13.6 us (6%)
  local copies, waits for them, and re-layouts  10.3 us (5%)
    ppermute x19, waiting for transfers between devices, move(): return lax.ppermute(value, AXES, pairs)  94.8 us
    ppermute x19, starting transfers between devices, move(): return lax.ppermute(value, AXES, pairs)  72.3 us
    pallas_call x2, Pallas kernels, product(): pl.pallas_call(product_kernel, out_shape=[jax.ShapeDtypeStruct((2 * rows,...  24.7 us
    unnamed x22, local copies, waits for them, and re-layouts  8.16 us
  transfers between devices with their start and end apart: 20, of which 13 were waited for; matrix products, arithmetic and copies ran while one was open for 1% of the time, Pallas kernels for 7%

profile of v4, /device:TPU:24, one launch (start us, length us, event | category | flops | bytes accessed | tf_op | source)
XLA Modules:
  0.0 220.6 jit_solution(17977106347689286720)
XLA Ops:
  6.5 0.7 all-gather.3.cloned.1.call-update
  7.4 1.2 copy-done
  8.6 1.2 copy-done.1
  9.8 0.9 shard_map.37
  10.7 1.6 collective-permute-start.1
  12.3 7.0 %collective-permute-done.1 = bf16[256,896]{1,0:T(8,128)(2,1)S(1)} collective-permute-done((bf16[256,896]{1,0:T(8,128)(2,1)S(1)}, bf16[256,896]{1,0:T(8,128)(2,1)S(1)}, u32[]{:S(2)}, u32[]{:S(2)}) %collective-permute-start.1) | collective-permute-done | bytes 458784 | tf_op jit(solution)/shard_map/ppermute | solution.py:34
  19.3 0.1 pad_maximum_fusion.refs_0_
  19.4 2.0 collective-permute-start.4
  21.4 0.9 collective-permute-start.3
  22.2 0.1 collective-permute-start.2
  22.3 1.4 collective-permute-start
  23.7 7.1 %collective-permute-done = bf16[256,896]{1,0:T(8,128)(2,1)S(1)} collective-permute-done((bf16[256,896]{1,0:T(8,128)(2,1)S(1)}, bf16[256,896]{1,0:T(8,128)(2,1)S(1)}, u32[]{:S(2)}, u32[]{:S(2)}) %collective-permute-start) | collective-permute-done | bytes 458784 | tf_op jit(solution)/shard_map/ppermute | solution.py:34
  30.8 11.8 %collective-permute-done.4.refs_3_ = bf16[2,256,896]{2,1,0:T(8,128)(2,1)S(1)} collective-permute-done((bf16[2,256,896]{2,1,0:T(8,128)(2,1)S(1)}, bf16[2,256,896]{2,1,0:T(8,128)(2,1)S(1)}, u32[]{:S(2)}, u32[]{:S(2)}) %collective-permute-start.4) | collective-permute-done | bytes 917536 | tf_op jit(solution)/shard_map/ppermute | solution.py:34
  42.7 3.6 %collective-permute-done.3.refs_2_ = bf16[2,256,896]{2,1,0:T(8,128)(2,1)S(1)} collective-permute-done((bf16[2,256,896]{2,1,0:T(8,128)(2,1)S(1)}, bf16[2,256,896]{2,1,0:T(8,128)(2,1)S(1)}, u32[]{:S(2)}, u32[]{:S(2)}) %collective-permute-start.3) | collective-permute-done | bytes 917536 | tf_op jit(solution)/shard_map/ppermute | solution.py:34
  46.2 16.6 %collective-permute-done.2.refs_1_ = bf16[2,256,896]{2,1,0:T(8,128)(2,1)S(1)} collective-permute-done((bf16[2,256,896]{2,1,0:T(8,128)(2,1)S(1)}, bf16[2,256,896]{2,1,0:T(8,128)(2,1)S(1)}, u32[]{:S(2)}, u32[]{:S(2)}) %collective-permute-start.2) | collective-permute-done | bytes 917536 | tf_op jit(solution)/shard_map/ppermute | solution.py:34
  62.9 0.9 copy-done.2
  63.8 0.6 collective-permute-start.5
  64.4 1.0 slice_bitcast_fusion
  65.4 7.3 %collective-permute-start.6 = (bf16[2,256,512]{2,1,0:T(8,128)(2,1)S(1)}, bf16[2,256,512]{2,1,0:T(8,128)(2,1)}, u32[]{:S(2)}, u32[]{:S(2)}) collective-permute-start(bf16[2,256,512]{2,1,0:T(8,128)(2,1)S(1)} %pad_maximum_fusion.1), channel_id=1, source_target_pairs={{0,32},{1,33},{2,34},{3,35},{4,36},{5,37},{6,38},{7,39},{32,0},{33... | collective-permute-start | bytes 1572872 | tf_op jit(solution)/shard_map/ppermute | solution.py:34
  72.7 13.9 %collective-permute-done.6.refs_4_ = bf16[2,256,512]{2,1,0:T(8,128)(2,1)} collective-permute-done((bf16[2,256,512]{2,1,0:T(8,128)(2,1)S(1)}, bf16[2,256,512]{2,1,0:T(8,128)(2,1)}, u32[]{:S(2)}, u32[]{:S(2)}) %collective-permute-start.6) | collective-permute-done | bytes 524320 | tf_op jit(solution)/shard_map/ppermute | solution.py:34
  86.6 10.3 %collective-permute-start.9 = (bf16[2,256,512]{2,1,0:T(8,128)(2,1)}, bf16[2,256,512]{2,1,0:T(8,128)(2,1)S(1)}, u32[]{:S(2)}, u32[]{:S(2)}) collective-permute-start(bf16[2,256,512]{2,1,0:T(8,128)(2,1)} %collective-permute-done.6.refs_4_), channel_id=1, source_target_pairs={{0,64},{1,65},{2,66},{3,67},{4,68},{5,69},{6,70},{7,71},{32,96},{3... | collective-permute-start | bytes 1572872 | tf_op jit(solution)/shard_map/ppermute | solution.py:34
  96.9 1.0 slice_bitcast_fusion.2
  97.9 8.0 %collective-permute-start.10 = (bf16[2,256,384]{2,1,0:T(8,128)(2,1)S(1)}, bf16[2,256,384]{2,1,0:T(8,128)(2,1)S(1)}, u32[]{:S(2)}, u32[]{:S(2)}) collective-permute-start(bf16[2,256,384]{2,1,0:T(8,128)(2,1)S(1)} %pad_maximum_fusion.2), channel_id=1, source_target_pairs={{0,32},{1,33},{2,34},{3,35},{4,36},{5,37},{6,38},{7,39},{32,0},{33... | collective-permute-start | bytes 1179656 | tf_op jit(solution)/shard_map/ppermute | solution.py:34
  106.0 0.5 collective-permute-start.7
  106.5 7.9 %collective-permute-done.10.refs_8_ = bf16[2,256,384]{2,1,0:T(8,128)(2,1)S(1)} collective-permute-done((bf16[2,256,384]{2,1,0:T(8,128)(2,1)S(1)}, bf16[2,256,384]{2,1,0:T(8,128)(2,1)S(1)}, u32[]{:S(2)}, u32[]{:S(2)}) %collective-permute-start.10) | collective-permute-done | bytes 393248 | tf_op jit(solution)/shard_map/ppermute | solution.py:34
  114.4 10.1 %collective-permute-start.13 = (bf16[2,256,384]{2,1,0:T(8,128)(2,1)S(1)}, bf16[2,256,384]{2,1,0:T(8,128)(2,1)}, u32[]{:S(2)}, u32[]{:S(2)}) collective-permute-start(bf16[2,256,384]{2,1,0:T(8,128)(2,1)S(1)} %collective-permute-done.10.refs_8_), channel_id=1, source_target_pairs={{0,64},{1,65},{2,66},{3,67},{4,68},{5,69},{6,70},{7,71},{32,96},{3... | collective-permute-start | bytes 1179656 | tf_op jit(solution)/shard_map/ppermute | solution.py:34
  124.5 0.8 copy-done.4
  125.3 0.8 copy-done.7
  126.1 0.9 collective-permute-start.11
  127.0 9.4 %collective-permute-done.13.refs_11_ = bf16[2,256,384]{2,1,0:T(8,128)(2,1)} collective-permute-done((bf16[2,256,384]{2,1,0:T(8,128)(2,1)S(1)}, bf16[2,256,384]{2,1,0:T(8,128)(2,1)}, u32[]{:S(2)}, u32[]{:S(2)}) %collective-permute-start.13) | collective-permute-done | bytes 393248 | tf_op jit(solution)/shard_map/ppermute | solution.py:34
  136.5 0.1 collective-permute-done.12.refs_10_
  136.5 4.1 %collective-permute-done.11.refs_9_ = bf16[2,256,384]{2,1,0:T(8,128)(2,1)} collective-permute-done((bf16[2,256,384]{2,1,0:T(8,128)(2,1)S(1)}, bf16[2,256,384]{2,1,0:T(8,128)(2,1)}, u32[]{:S(2)}, u32[]{:S(2)}) %collective-permute-start.11) | collective-permute-done | bytes 393248 | tf_op jit(solution)/shard_map/ppermute | solution.py:34
  140.6 1.2 copy-done.3
  141.8 1.0 copy-done.5
  142.8 1.0 copy-done.8
  143.9 12.4 %shard_map.38 = (f32[384,896]{1,0:T(8,128)S(1)}, f32[384,896]{1,0:T(8,128)S(1)}) custom-call(s32[7]{0:T(128)S(1)} %stack.75.place, bf16[2,8,4,192,256]{4,3,2,1,0:T(8,128)(2,1)} %bitcast.25, bf16[2,8,4,192,256]{4,3,2,1,0:T(8,128)(2,1)} %bitcast.13.partner, bf16[2,256,896]{2,1,0:T(8,128)(2,1)S(1)} %pad_maximum_fusion.refs_0_, ...), custom_call_target="tpu_custom_call" | custom-call | flops 5637144576 | bytes 25165824 | tf_op jit(solution)/shard_map/pallas_call | solution.py:82
  156.3 0.1 collective-permute-start.14
  156.4 3.2 %collective-permute-start.16 = (f32[384,896]{1,0:T(8,128)S(1)}, f32[384,896]{1,0:T(8,128)S(1)}, u32[]{:S(2)}, u32[]{:S(2)}) collective-permute-start(f32[384,896]{1,0:T(8,128)S(1)} %get-tuple-element.31), channel_id=1, source_target_pairs={{0,24},{1,9},{2,26},{3,11},{4,28},{5,13},{6,30},{7,15},{32,56},{33... | collective-permute-start | bytes 4128776 | tf_op jit(solution)/shard_map/ppermute | solution.py:34
  159.6 12.3 %shard_map.39 = (f32[384,896]{1,0:T(8,128)S(1)}, f32[384,896]{1,0:T(8,128)S(1)}) custom-call(s32[7]{0:T(128)S(1)} %stack.72.place, bf16[2,8,4,192,256]{4,3,2,1,0:T(8,128)(2,1)} %bitcast.26, bf16[2,8,4,192,256]{4,3,2,1,0:T(8,128)(2,1)} %bitcast.13.partner, bf16[2,256,896]{2,1,0:T(8,128)(2,1)S(1)} %pad_maximum_fusion.refs_0_, ...), custom_call_target="tpu_custom_call" | custom-call | flops 5637144576 | bytes 25165824 | tf_op jit(solution)/shard_map/pallas_call | solution.py:82
  171.9 4.0 %collective-permute-done.14.received = f32[384,896]{1,0:T(8,128)S(1)} collective-permute-done((f32[384,896]{1,0:T(8,128)S(1)}, f32[384,896]{1,0:T(8,128)S(1)}, u32[]{:S(2)}, u32[]{:S(2)}) %collective-permute-start.14) | collective-permute-done | bytes 1376288 | tf_op jit(solution)/shard_map/ppermute | solution.py:34
  175.9 0.8 shard_map.40
  176.7 11.9 %collective-permute-start.15 = (bf16[192,448]{1,0:T(8,128)(2,1)S(1)}, bf16[192,448]{1,0:T(8,128)(2,1)S(1)}, u32[]{:S(2)}, u32[]{:S(2)}) collective-permute-start(bf16[192,448]{1,0:T(8,128)(2,1)S(1)} %get-tuple-element.35), channel_id=1, source_target_pairs={{0,32},{1,33},{2,34},{3,35},{4,36},{5,37},{6,38},{7,39},{32,0},{33... | collective-permute-start | bytes 516104 | tf_op jit(solution)/shard_map/ppermute | solution.py:34
  188.6 2.0 collective-permute-done.16.received
  190.7 0.8 shard_map.41
  191.4 0.1 collective-permute-start.17
  191.5 13.3 %collective-permute-start.18 = (bf16[192,448]{1,0:T(8,128)(2,1)S(1)}, bf16[192,448]{1,0:T(8,128)(2,1)S(1)}, u32[]{:S(2)}, u32[]{:S(2)}) collective-permute-start(bf16[192,448]{1,0:T(8,128)(2,1)S(1)} %get-tuple-element.38), channel_id=1, source_target_pairs={{0,40},{1,57},{2,42},{3,59},{4,44},{5,61},{6,46},{7,63},{32,8},{33... | collective-permute-start | bytes 516104 | tf_op jit(solution)/shard_map/ppermute | solution.py:34
  204.8 7.4 %collective-permute-done.18.refs_3_ = bf16[192,448]{1,0:T(8,128)(2,1)S(1)} collective-permute-done((bf16[192,448]{1,0:T(8,128)(2,1)S(1)}, bf16[192,448]{1,0:T(8,128)(2,1)S(1)}, u32[]{:S(2)}, u32[]{:S(2)}) %collective-permute-start.18) | collective-permute-done | bytes 172064 | tf_op jit(solution)/shard_map/ppermute | solution.py:34
  212.2 1.5 shard_map.42
  (28 shorter events, 0.3 us)
Async XLA Ops:
  6.5 57.2 %all-gather.3.cloned.1.call-start = ((), (), s32[]{:S(2)}) async-start(), calls=%async_computation | async-start | bytes 6684672 | tf_op jit(solution)/shard_map/all_gather | solution.py:197
  7.4 1.2 copy-start
  8.6 1.2 copy-start.1
  10.7 8.6 %collective-permute-start.1 = (bf16[256,896]{1,0:T(8,128)(2,1)S(1)}, bf16[256,896]{1,0:T(8,128)(2,1)S(1)}, u32[]{:S(2)}, u32[]{:S(2)}) collective-permute-start(bf16[256,896]{1,0:T(8,128)(2,1)S(1)} %get-tuple-element.24), channel_id=1, source_target_pairs={{0,8},{1,25},{2,10},{3,27},{4,12},{5,29},{6,14},{7,31},{32,40},{33... | collective-permute-start | bytes 1376264 | tf_op jit(solution)/shard_map/ppermute | solution.py:34
  19.4 23.3 %collective-permute-start.4 = (bf16[2,256,896]{2,1,0:T(8,128)(2,1)S(1)}, bf16[2,256,896]{2,1,0:T(8,128)(2,1)S(1)}, u32[]{:S(2)}, u32[]{:S(2)}) collective-permute-start(bf16[2,256,896]{2,1,0:T(8,128)(2,1)S(1)} %pad_maximum_fusion.refs_0_), channel_id=1, source_target_pairs={{0,64},{1,65},{2,66},{3,67},{4,68},{5,69},{6,70},{7,71},{32,96},{3... | collective-permute-start | bytes 2752520 | tf_op jit(solution)/shard_map/ppermute | solution.py:34
  21.4 24.8 %collective-permute-start.3 = (bf16[2,256,896]{2,1,0:T(8,128)(2,1)S(1)}, bf16[2,256,896]{2,1,0:T(8,128)(2,1)S(1)}, u32[]{:S(2)}, u32[]{:S(2)}) collective-permute-start(bf16[2,256,896]{2,1,0:T(8,128)(2,1)S(1)} %pad_maximum_fusion.refs_0_), channel_id=1, source_target_pairs={{0,128},{1,129},{2,130},{3,131},{4,132},{5,133},{6,134},{7,135},{3... | collective-permute-start | bytes 2752520 | tf_op jit(solution)/shard_map/ppermute | solution.py:34
  22.2 40.6 %collective-permute-start.2 = (bf16[2,256,896]{2,1,0:T(8,128)(2,1)S(1)}, bf16[2,256,896]{2,1,0:T(8,128)(2,1)S(1)}, u32[]{:S(2)}, u32[]{:S(2)}) collective-permute-start(bf16[2,256,896]{2,1,0:T(8,128)(2,1)S(1)} %pad_maximum_fusion.refs_0_), channel_id=1, source_target_pairs={{0,192},{1,193},{2,194},{3,195},{4,196},{5,197},{6,198},{7,199},{3... | collective-permute-start | bytes 2752520 | tf_op jit(solution)/shard_map/ppermute | solution.py:34
  22.3 8.5 %collective-permute-start = (bf16[256,896]{1,0:T(8,128)(2,1)S(1)}, bf16[256,896]{1,0:T(8,128)(2,1)S(1)}, u32[]{:S(2)}, u32[]{:S(2)}) collective-permute-start(bf16[256,896]{1,0:T(8,128)(2,1)S(1)} %get-tuple-element.22), channel_id=1, source_target_pairs={{0,8},{1,25},{2,10},{3,27},{4,12},{5,29},{6,14},{7,31},{32,40},{33... | collective-permute-start | bytes 1376264 | tf_op jit(solution)/shard_map/ppermute | solution.py:34
  30.8 15.4 %copy-start.10 = (bf16[256,896]{1,0:T(8,128)(2,1)}, bf16[256,896]{1,0:T(8,128)(2,1)S(1)}, u32[]{:S(2)}) copy-start(bf16[256,896]{1,0:T(8,128)(2,1)S(1)} %collective-permute-done) | copy-start | bytes 1376260
  62.8 0.9 copy-start.2
  63.8 76.8 %collective-permute-start.5 = (bf16[16,768,256]{2,1,0:T(8,128)(2,1)}, bf16[16,768,256]{2,1,0:T(8,128)(2,1)}, u32[]{:S(2)}, u32[]{:S(2)}) collective-permute-start(bf16[16,768,256]{2,1,0:T(8,128)(2,1)} %bitcast.24), channel_id=1, source_target_pairs={{0,8},{1,25},{2,10},{3,27},{4,12},{5,29},{6,14},{7,31},{32,40},{33... | collective-permute-start | bytes 18874376 | tf_op jit(solution)/shard_map/ppermute | solution.py:34
  65.4 21.2 %collective-permute-start.6 = (bf16[2,256,512]{2,1,0:T(8,128)(2,1)S(1)}, bf16[2,256,512]{2,1,0:T(8,128)(2,1)}, u32[]{:S(2)}, u32[]{:S(2)}) collective-permute-start(bf16[2,256,512]{2,1,0:T(8,128)(2,1)S(1)} %pad_maximum_fusion.1), channel_id=1, source_target_pairs={{0,32},{1,33},{2,34},{3,35},{4,36},{5,37},{6,38},{7,39},{32,0},{33... | collective-permute-start | bytes 1572872 | tf_op jit(solution)/shard_map/ppermute | solution.py:34
  86.6 37.9 %collective-permute-start.9 = (bf16[2,256,512]{2,1,0:T(8,128)(2,1)}, bf16[2,256,512]{2,1,0:T(8,128)(2,1)S(1)}, u32[]{:S(2)}, u32[]{:S(2)}) collective-permute-start(bf16[2,256,512]{2,1,0:T(8,128)(2,1)} %collective-permute-done.6.refs_4_), channel_id=1, source_target_pairs={{0,64},{1,65},{2,66},{3,67},{4,68},{5,69},{6,70},{7,71},{32,96},{3... | collective-permute-start | bytes 1572872 | tf_op jit(solution)/shard_map/ppermute | solution.py:34
  96.9 28.4 %collective-permute-start.8 = (bf16[2,256,512]{2,1,0:T(8,128)(2,1)}, bf16[2,256,512]{2,1,0:T(8,128)(2,1)S(1)}, u32[]{:S(2)}, u32[]{:S(2)}) collective-permute-start(bf16[2,256,512]{2,1,0:T(8,128)(2,1)} %collective-permute-done.6.refs_4_), channel_id=1, source_target_pairs={{0,128},{1,129},{2,130},{3,131},{4,132},{5,133},{6,134},{7,135},{3... | collective-permute-start | bytes 1572872 | tf_op jit(solution)/shard_map/ppermute | solution.py:34
  97.9 16.4 %collective-permute-start.10 = (bf16[2,256,384]{2,1,0:T(8,128)(2,1)S(1)}, bf16[2,256,384]{2,1,0:T(8,128)(2,1)S(1)}, u32[]{:S(2)}, u32[]{:S(2)}) collective-permute-start(bf16[2,256,384]{2,1,0:T(8,128)(2,1)S(1)} %pad_maximum_fusion.2), channel_id=1, source_target_pairs={{0,32},{1,33},{2,34},{3,35},{4,36},{5,37},{6,38},{7,39},{32,0},{33... | collective-permute-start | bytes 1179656 | tf_op jit(solution)/shard_map/ppermute | solution.py:34
  106.0 21.0 %collective-permute-start.7 = (bf16[2,256,512]{2,1,0:T(8,128)(2,1)}, bf16[2,256,512]{2,1,0:T(8,128)(2,1)}, u32[]{:S(2)}, u32[]{:S(2)}) collective-permute-start(bf16[2,256,512]{2,1,0:T(8,128)(2,1)} %collective-permute-done.6.refs_4_), channel_id=1, source_target_pairs={{0,192},{1,193},{2,194},{3,195},{4,196},{5,197},{6,198},{7,199},{3... | collective-permute-start | bytes 1572872 | tf_op jit(solution)/shard_map/ppermute | solution.py:34
  114.4 22.1 %collective-permute-start.13 = (bf16[2,256,384]{2,1,0:T(8,128)(2,1)S(1)}, bf16[2,256,384]{2,1,0:T(8,128)(2,1)}, u32[]{:S(2)}, u32[]{:S(2)}) collective-permute-start(bf16[2,256,384]{2,1,0:T(8,128)(2,1)S(1)} %collective-permute-done.10.refs_8_), channel_id=1, source_target_pairs={{0,64},{1,65},{2,66},{3,67},{4,68},{5,69},{6,70},{7,71},{32,96},{3... | collective-permute-start | bytes 1179656 | tf_op jit(solution)/shard_map/ppermute | solution.py:34
  124.5 0.8 copy-start.4
  125.3 11.3 %collective-permute-start.12 = (bf16[2,256,384]{2,1,0:T(8,128)(2,1)S(1)}, bf16[2,256,384]{2,1,0:T(8,128)(2,1)}, u32[]{:S(2)}, u32[]{:S(2)}) collective-permute-start(bf16[2,256,384]{2,1,0:T(8,128)(2,1)S(1)} %collective-permute-done.10.refs_8_), channel_id=1, source_target_pairs={{0,128},{1,129},{2,130},{3,131},{4,132},{5,133},{6,134},{7,135},{3... | collective-permute-start | bytes 1179656 | tf_op jit(solution)/shard_map/ppermute | solution.py:34
  125.3 0.8 copy-start.7
  126.1 14.5 %collective-permute-start.11 = (bf16[2,256,384]{2,1,0:T(8,128)(2,1)S(1)}, bf16[2,256,384]{2,1,0:T(8,128)(2,1)}, u32[]{:S(2)}, u32[]{:S(2)}) collective-permute-start(bf16[2,256,384]{2,1,0:T(8,128)(2,1)S(1)} %collective-permute-done.10.refs_8_), channel_id=1, source_target_pairs={{0,192},{1,193},{2,194},{3,195},{4,196},{5,197},{6,198},{7,199},{3... | collective-permute-start | bytes 1179656 | tf_op jit(solution)/shard_map/ppermute | solution.py:34
  140.6 1.2 copy-start.3
  141.8 1.0 copy-start.5
  142.8 1.0 copy-start.8
  143.9 15.7 %copy-start.6 = (bf16[2,256,512]{2,1,0:T(8,128)(2,1)S(1)}, bf16[2,256,512]{2,1,0:T(8,128)(2,1)}, u32[]{:S(2)}) copy-start(bf16[2,256,512]{2,1,0:T(8,128)(2,1)} %copy-done.4) | copy-start | bytes 1572868
  143.9 15.7 %copy-start.9 = (bf16[2,256,512]{2,1,0:T(8,128)(2,1)S(1)}, bf16[2,256,512]{2,1,0:T(8,128)(2,1)}, u32[]{:S(2)}) copy-start(bf16[2,256,512]{2,1,0:T(8,128)(2,1)} %copy-done.7) | copy-start | bytes 1572868
  156.3 19.6 %collective-permute-start.14 = (f32[384,896]{1,0:T(8,128)S(1)}, f32[384,896]{1,0:T(8,128)S(1)}, u32[]{:S(2)}, u32[]{:S(2)}) collective-permute-start(f32[384,896]{1,0:T(8,128)S(1)} %get-tuple-element.30), channel_id=1, source_target_pairs={{0,24},{1,9},{2,26},{3,11},{4,28},{5,13},{6,30},{7,15},{32,56},{33... | collective-permute-start | bytes 4128776 | tf_op jit(solution)/shard_map/ppermute | solution.py:34
  156.4 34.3 %collective-permute-start.16 = (f32[384,896]{1,0:T(8,128)S(1)}, f32[384,896]{1,0:T(8,128)S(1)}, u32[]{:S(2)}, u32[]{:S(2)}) collective-permute-start(f32[384,896]{1,0:T(8,128)S(1)} %get-tuple-element.31), channel_id=1, source_target_pairs={{0,24},{1,9},{2,26},{3,11},{4,28},{5,13},{6,30},{7,15},{32,56},{33... | collective-permute-start | bytes 4128776 | tf_op jit(solution)/shard_map/ppermute | solution.py:34
  176.7 28.1 %collective-permute-start.15 = (bf16[192,448]{1,0:T(8,128)(2,1)S(1)}, bf16[192,448]{1,0:T(8,128)(2,1)S(1)}, u32[]{:S(2)}, u32[]{:S(2)}) collective-permute-start(bf16[192,448]{1,0:T(8,128)(2,1)S(1)} %get-tuple-element.35), channel_id=1, source_target_pairs={{0,32},{1,33},{2,34},{3,35},{4,36},{5,37},{6,38},{7,39},{32,0},{33... | collective-permute-start | bytes 516104 | tf_op jit(solution)/shard_map/ppermute | solution.py:34
  191.4 13.4 %collective-permute-start.17 = (bf16[192,448]{1,0:T(8,128)(2,1)S(1)}, bf16[192,448]{1,0:T(8,128)(2,1)S(1)}, u32[]{:S(2)}, u32[]{:S(2)}) collective-permute-start(bf16[192,448]{1,0:T(8,128)(2,1)S(1)} %get-tuple-element.37), channel_id=1, source_target_pairs={{0,8},{1,25},{2,10},{3,27},{4,12},{5,29},{6,14},{7,31},{32,40},{33... | collective-permute-start | bytes 516104 | tf_op jit(solution)/shard_map/ppermute | solution.py:34
  191.5 20.7 %collective-permute-start.18 = (bf16[192,448]{1,0:T(8,128)(2,1)S(1)}, bf16[192,448]{1,0:T(8,128)(2,1)S(1)}, u32[]{:S(2)}, u32[]{:S(2)}) collective-permute-start(bf16[192,448]{1,0:T(8,128)(2,1)S(1)} %get-tuple-element.38), channel_id=1, source_target_pairs={{0,40},{1,57},{2,42},{3,59},{4,44},{5,61},{6,46},{7,63},{32,8},{33... | collective-permute-start | bytes 516104 | tf_op jit(solution)/shard_map/ppermute | solution.py:34
Sparse Core Ops, SparseCore 0:
  9.2 48.7 all-gather.2

commit v5 on v4

--- a/solution.py
+++ b/solution.py
@@ -12,6 +12,7 @@
 NX, NY, NZ, NC = 4, 4, 8, 2
 AXES = ("y", "zh", "x", "zl", "c")
 TILE = 128
+STEPS = ((0,), (1, 7), (2, 6), (3, 5), (4,))
 PARTS = ((0, 512), (512, 896))
 
 
@@ -54,38 +55,63 @@
     return x - side(x, c), y, z, c
 
 
-def product_kernel(place, own, partner, *refs):
-    near, far, (outs, lhs, rhs) = refs[:4], (refs[4:8], refs[8:12]), (refs[12:14], *refs[14:])
-    y, zh = place[0], place[1]
-    rows = own.shape[3]
+def product_kernel(place, *refs):
+    tokens, near, far = refs[:20], refs[20], (refs[21:25], refs[25:29])
+    outs, (pieces, lhs, rhs, lhs_sem, rhs_sem) = refs[29:31], refs[31:]
+    y, zh, zl, c = place[0], place[1], place[2], place[3]
+    rows = pieces.shape[3]
+    shares = []
+    for i in range(2):
+        loads = []
+        for s, offsets in enumerate(STEPS):
+            for j, d in enumerate(offsets):
+                z = lax.rem(zh * 4 + zl + d, 8)
+                for t in range(4):
+                    k = t // 2 * 8 + lax.rem(z, 4) * 2 + lax.rem(c + t, 2)
+                    source, target = tokens[4 * s + t].at[j, place[4 + i]], pieces.at[i, k, z // 4]
+                    loads.append(pltpu.make_async_copy(source, target, lhs_sem.at[i * 32 + len(loads)]))
+        shares.append(loads)
+    weights = []
     for d in range(4):
         for u in range(2):
-            k = u * 8 + lax.rem(y + d, 4) * 2
-            at = pl.ds(pl.multiple_of((k + zh) * 256, 256), 256)
-            rhs[at, :] = near[d][u]
-            at = pl.ds(pl.multiple_of((k + 1 - zh) * 256, 256), 256)
+            at = pl.multiple_of((u * 8 + d * 2 + zh) * 256, 256)
+            weights.append(pltpu.make_async_copy(near.at[d, u], rhs.at[pl.ds(at, 256)], rhs_sem.at[len(weights)]))
+            at = pl.multiple_of((u * 8 + lax.rem(y + d, 4) * 2 + 1 - zh) * 256, 256)
             for (lo, hi), part in zip(PARTS, far):
-                rhs[at, lo:hi] = part[d][u]
+                target = rhs.at[pl.ds(at, 256), lo:hi]
+                weights.append(pltpu.make_async_copy(part[d].at[u], target, rhs_sem.at[len(weights)]))
+    for copy in (*shares[0], *weights, *shares[1]):
+        copy.start()
     for i, out in enumerate(outs):
+        for copy in shares[i]:
+            copy.wait()
         for k in range(16):
-            source = own if k < 8 else partner
-            lhs[:, k * 256 : (k + 1) * 256] = source[:, k % 8, place[4 + i]].reshape(2 * rows, 256)
+            lhs[:, k * 256 : (k + 1) * 256] = pieces[i, k].reshape(2 * rows, 256)
+        if i == 0:
+            for copy in weights:
+                copy.wait()
         for at in range(0, rhs.shape[1], 256):
             to = min(at + 256, rhs.shape[1])
             out[:, at:to] = jnp.dot(lhs[...], rhs[:, at:to], preferred_element_type=jnp.float32)
 
 
-def product(place, own, partner, near, far):
-    rows, depth, wide = own.shape[3], 4096, near[0].shape[2]
-    vmem = pl.BlockSpec(memory_space=pltpu.VMEM)
-    operands = [own, partner, *near, *far[0], *far[1]]
+def product(place, tokens, near, far):
+    rows, depth, wide = tokens[0].shape[2], 4096, near.shape[3]
+    hbm, vmem = pl.BlockSpec(memory_space=pltpu.HBM), pl.BlockSpec(memory_space=pltpu.VMEM)
+    operands = [*tokens, near, *far[0], *far[1]]
     return pl.pallas_call(
         product_kernel,
         out_shape=[jax.ShapeDtypeStruct((2 * rows, wide), jnp.float32)] * 2,
-        in_specs=[pl.BlockSpec(memory_space=pltpu.SMEM)] + [vmem] * len(operands),
+        in_specs=[pl.BlockSpec(memory_space=pltpu.SMEM)] + [hbm] * len(operands),
         out_specs=[vmem] * 2,
-        scratch_shapes=[pltpu.VMEM((2 * rows, depth), jnp.bfloat16), pltpu.VMEM((depth, wide), jnp.bfloat16)],
-        compiler_params=pltpu.CompilerParams(vmem_limit_bytes=40 << 20),
+        scratch_shapes=[
+            pltpu.VMEM((2, 16, 2, rows, 256), jnp.bfloat16),
+            pltpu.VMEM((2 * rows, depth), jnp.bfloat16),
+            pltpu.VMEM((depth, wide), jnp.bfloat16),
+            pltpu.SemaphoreType.DMA((64,)),
+            pltpu.SemaphoreType.DMA((24,)),
+        ],
+        compiler_params=pltpu.CompilerParams(vmem_limit_bytes=60 << 20),
         cost_estimate=pl.CostEstimate(flops=8 * rows * depth * wide, bytes_accessed=24 << 20, transcendentals=0),
     )(place, *operands)
 
@@ -194,23 +220,32 @@
 
     send_place, keep_place = places(summer, over), places(x, partner)
 
-    panel = lax.all_gather(tokens, ("zh", "zl", "c"), axis=0)
     near, away, give_near, give_away = cut(keep_place, gate_weight, up_weight)
     got_near, got_away = move(give_near, to_partner), move(give_away, to_partner)
-    near = along_y(jnp.stack([near, got_near]))
-
-    panel = after(panel, got_away, *near[1:])
-    partner_panel = move(panel, to_partner).reshape(2, 8, NX, rows, 256)
-    own = panel.reshape(2, 8, NX, rows, 256)
-    away, got_away = lax.optimization_barrier((away, got_away, panel))[:2]
     far = [jnp.stack([away[:, lo:hi], got_away[:, lo:hi]]) for lo, hi in PARTS]
     far[0] = move(far[0], to_antipode)
+
+    block = tokens.reshape(1, NX, rows, 256)
+    held, sent_on = [], ()
+    behind = before = block
+    for s in range(5):
+        if s in (1, 2, 3):
+            behind = move(behind, lambda x, y, z, c: (x, y, z - 1, c))
+            before = move(before, lambda x, y, z, c: (x, y, z + 1, c))
+            block = jnp.concatenate([behind, before])
+        elif s == 4:
+            block = move(jnp.where(c == 0, before, behind), lambda x, y, z, c: (x, y, z + 1 - 2 * c, c))
+        ready = after(block, *sent_on, *far[: s // 3])
+        sent_on = [move(ready, to_partner), move(ready, to_crossed)]
+        held += [block, move(ready, lambda x, y, z, c: (x, y, z, 1 - c)), *sent_on]
+
+    near = lax.all_gather(jnp.stack([near, got_near]), "y", axis=0)
     far[1] = move(after(far[1], far[0]), to_antipode)
     far = [along_y(f) for f in far]
 
-    sent = product(send_place, own, partner_panel, near, far)
+    sent = product(send_place, held, near, far)
     sums = [move(sent[0], to_summer), move(sent[1], to_summer)]
-    kept = product(after(keep_place, *sent), own, partner_panel, near, far)
+    kept = product(after(keep_place, *sent), held, near, far)
     mine, over_z = gated(keep_place, kept[0], sums[0])
     over_x, over_both = gated(keep_place, kept[1], sums[1])
     blocks = [mine, move(over_z, to_antipode), move(over_x, to_partner), move(over_both, to_both)]

time: 221 us -> 231 us (1.045)
  the two profiles are of different devices: /device:TPU:24 before, /device:TPU:17 now
where the time goes in v5:
time: 231 us
  waiting for transfers between devices  121 us (52%)
  starting transfers between devices  54.8 us (24%)
  Pallas kernels  33 us (14%)
  between operations  13.6 us (6%)
  local copies, waits for them, and re-layouts  7.66 us (3%)
    ppermute x37, waiting for transfers between devices, move(): return lax.ppermute(value, AXES, pairs)  121 us
    ppermute x37, starting transfers between devices, move(): return lax.ppermute(value, AXES, pairs)  54.8 us
    pallas_call x2, Pallas kernels, product(): pl.pallas_call(product_kernel, out_shape=[jax.ShapeDtypeStruct((2 * rows,...  28.9 us
    unnamed x46, local copies, waits for them, and re-layouts  6.07 us
  transfers between devices with their start and end apart: 38, of which 21 were waited for; matrix products, arithmetic and copies ran while one was open for 1% of the time, Pallas kernels for 7%

profile of v5, /device:TPU:17, one launch (start us, length us, event | category | flops | bytes accessed | tf_op | source)
XLA Modules:
  0.0 231.2 jit_solution(7606050219072266690)
XLA Ops:
  6.6 1.2 copy-done.2
  7.8 1.2 copy-done.3
  9.0 0.9 shard_map.37
  9.9 2.6 %collective-permute-start.24 = (bf16[256,896]{1,0:T(8,128)(2,1)S(1)}, bf16[256,896]{1,0:T(8,128)(2,1)S(1)}, u32[]{:S(2)}, u32[]{:S(2)}) collective-permute-start(bf16[256,896]{1,0:T(8,128)(2,1)S(1)} %get-tuple-element.30), channel_id=1, source_target_pairs={{0,8},{1,25},{2,10},{3,27},{4,12},{5,29},{6,14},{7,31},{32,40},{33... | collective-permute-start | bytes 1376264 | tf_op jit(solution)/shard_map/ppermute | solution.py:35
  12.5 6.1 %collective-permute-done.24 = bf16[256,896]{1,0:T(8,128)(2,1)S(1)} collective-permute-done((bf16[256,896]{1,0:T(8,128)(2,1)S(1)}, bf16[256,896]{1,0:T(8,128)(2,1)S(1)}, u32[]{:S(2)}, u32[]{:S(2)}) %collective-permute-start.24) | collective-permute-done | bytes 458784 | tf_op jit(solution)/shard_map/ppermute | solution.py:35
  18.5 1.1 pad_maximum_fusion
  19.6 5.7 %collective-permute-start.3 = (bf16[1,4,192,256]{3,2,1,0:T(8,128)(2,1)S(1)}, bf16[1,4,192,256]{3,2,1,0:T(8,128)(2,1)S(1)}, u32[]{:S(2)}, u32[]{:S(2)}) collective-permute-start(bf16[1,4,192,256]{3,2,1,0:T(8,128)(2,1)S(1)} %bitcast.28), channel_id=1, source_target_pairs={{0,38},{1,39},{2,0},{3,1},{4,2},{5,3},{6,4},{7,5},{32,6},{33,7},{3... | collective-permute-start | bytes 1179656 | tf_op jit(solution)/shard_map/ppermute | solution.py:35
  25.3 2.0 collective-permute-start.2
  27.3 1.8 collective-permute-start.1
  29.1 0.9 collective-permute-start.15
  30.0 3.2 %collective-permute-done.3 = bf16[1,4,192,256]{3,2,1,0:T(8,128)(2,1)S(1)} collective-permute-done((bf16[1,4,192,256]{3,2,1,0:T(8,128)(2,1)S(1)}, bf16[1,4,192,256]{3,2,1,0:T(8,128)(2,1)S(1)}, u32[]{:S(2)}, u32[]{:S(2)}) %collective-permute-start.3) | collective-permute-done | bytes 393248 | tf_op jit(solution)/shard_map/ppermute | solution.py:35
  33.2 3.1 %collective-permute-done.4 = bf16[1,4,192,256]{3,2,1,0:T(8,128)(2,1)S(1)} collective-permute-done((bf16[1,4,192,256]{3,2,1,0:T(8,128)(2,1)S(1)}, bf16[1,4,192,256]{3,2,1,0:T(8,128)(2,1)S(1)}, u32[]{:S(2)}, u32[]{:S(2)}) %collective-permute-start.4) | collective-permute-done | bytes 393248 | tf_op jit(solution)/shard_map/ppermute | solution.py:35
  36.3 1.1 collective-permute-done.2.refs_3_
  39.1 1.8 collective-permute-start.6
  40.9 2.8 %collective-permute-start.8 = (bf16[1,4,192,256]{3,2,1,0:T(8,128)(2,1)S(1)}, bf16[1,4,192,256]{3,2,1,0:T(8,128)(2,1)S(1)}, u32[]{:S(2)}, u32[]{:S(2)}) collective-permute-start(bf16[1,4,192,256]{3,2,1,0:T(8,128)(2,1)S(1)} %collective-permute-done.3), channel_id=1, source_target_pairs={{0,38},{1,39},{2,0},{3,1},{4,2},{5,3},{6,4},{7,5},{32,6},{33,7},{3... | collective-permute-start | bytes 1179656 | tf_op jit(solution)/shard_map/ppermute | solution.py:35
  43.9 3.0 %collective-permute-start.16 = (bf16[2,256,512]{2,1,0:T(8,128)(2,1)S(1)}, bf16[2,256,512]{2,1,0:T(8,128)(2,1)}, u32[]{:S(2)}, u32[]{:S(2)}) collective-permute-start(bf16[2,256,512]{2,1,0:T(8,128)(2,1)S(1)} %pad_maximum_fusion.1), channel_id=1, source_target_pairs={{0,32},{1,33},{2,34},{3,35},{4,36},{5,37},{6,38},{7,39},{32,0},{33... | collective-permute-start | bytes 1572872 | tf_op jit(solution)/shard_map/ppermute | solution.py:35
  46.9 27.8 %collective-permute-done.8 = bf16[1,4,192,256]{3,2,1,0:T(8,128)(2,1)S(1)} collective-permute-done((bf16[1,4,192,256]{3,2,1,0:T(8,128)(2,1)S(1)}, bf16[1,4,192,256]{3,2,1,0:T(8,128)(2,1)S(1)}, u32[]{:S(2)}, u32[]{:S(2)}) %collective-permute-start.8) | collective-permute-done | bytes 393248 | tf_op jit(solution)/shard_map/ppermute | solution.py:35
  75.5 2.5 %collective-permute-done.9 = bf16[1,4,192,256]{3,2,1,0:T(8,128)(2,1)S(1)} collective-permute-done((bf16[1,4,192,256]{3,2,1,0:T(8,128)(2,1)S(1)}, bf16[1,4,192,256]{3,2,1,0:T(8,128)(2,1)S(1)}, u32[]{:S(2)}, u32[]{:S(2)}) %collective-permute-start.9) | collective-permute-done | bytes 393248 | tf_op jit(solution)/shard_map/ppermute | solution.py:35
  78.8 1.3 collective-permute-start.12
  80.1 2.7 %collective-permute-start.13 = (bf16[1,4,192,256]{3,2,1,0:T(8,128)(2,1)S(1)}, bf16[1,4,192,256]{3,2,1,0:T(8,128)(2,1)S(1)}, u32[]{:S(2)}, u32[]{:S(2)}) collective-permute-start(bf16[1,4,192,256]{3,2,1,0:T(8,128)(2,1)S(1)} %collective-permute-done.8), channel_id=1, source_target_pairs={{0,38},{1,39},{2,0},{3,1},{4,2},{5,3},{6,4},{7,5},{32,6},{33,7},{3... | collective-permute-start | bytes 1179656 | tf_op jit(solution)/shard_map/ppermute | solution.py:35
  83.9 8.2 %collective-permute-done.14 = bf16[1,4,192,256]{3,2,1,0:T(8,128)(2,1)S(1)} collective-permute-done((bf16[1,4,192,256]{3,2,1,0:T(8,128)(2,1)S(1)}, bf16[1,4,192,256]{3,2,1,0:T(8,128)(2,1)S(1)}, u32[]{:S(2)}, u32[]{:S(2)}) %collective-permute-start.14) | collective-permute-done | bytes 393248 | tf_op jit(solution)/shard_map/ppermute | solution.py:35
  93.0 3.9 %collective-permute-done.12.refs_11_ = bf16[2,4,192,256]{3,2,1,0:T(8,128)(2,1)} collective-permute-done((bf16[2,4,192,256]{3,2,1,0:T(8,128)(2,1)}, bf16[2,4,192,256]{3,2,1,0:T(8,128)(2,1)}, u32[]{:S(2)}, u32[]{:S(2)}) %collective-permute-start.12) | collective-permute-done | bytes 786464 | tf_op jit(solution)/shard_map/ppermute | solution.py:35
  96.9 1.0 collective-permute-start.27
  98.0 2.2 collective-permute-done.11.refs_10_
  100.9 15.1 %collective-permute-done.28.refs_25_ = bf16[2,256,384]{2,1,0:T(8,128)(2,1)S(1)} collective-permute-done((bf16[2,256,384]{2,1,0:T(8,128)(2,1)S(1)}, bf16[2,256,384]{2,1,0:T(8,128)(2,1)S(1)}, u32[]{:S(2)}, u32[]{:S(2)}) %collective-permute-start.28) | collective-permute-done | bytes 393248 | tf_op jit(solution)/shard_map/ppermute | solution.py:35
  116.2 5.8 %collective-permute-done.27.refs_24_ = bf16[2,256,512]{2,1,0:T(8,128)(2,1)S(1)} collective-permute-done((bf16[2,256,512]{2,1,0:T(8,128)(2,1)}, bf16[2,256,512]{2,1,0:T(8,128)(2,1)S(1)}, u32[]{:S(2)}, u32[]{:S(2)}) %collective-permute-start.27) | collective-permute-done | bytes 524320 | tf_op jit(solution)/shard_map/ppermute | solution.py:35
  122.0 1.6 collective-permute-start.20
  123.6 5.4 %collective-permute-done.25.refs_22_ = bf16[2,256,512]{2,1,0:T(8,128)(2,1)S(1)} collective-permute-done((bf16[2,256,512]{2,1,0:T(8,128)(2,1)}, bf16[2,256,512]{2,1,0:T(8,128)(2,1)S(1)}, u32[]{:S(2)}, u32[]{:S(2)}) %collective-permute-start.25) | collective-permute-done | bytes 524320 | tf_op jit(solution)/shard_map/ppermute | solution.py:35
  129.0 2.2 collective-permute-start.31
  131.2 2.0 collective-permute-start.17
  133.2 1.2 collective-permute-start.29
  134.5 3.7 %collective-permute-done.31.refs_28_ = bf16[2,256,384]{2,1,0:T(8,128)(2,1)S(1)} collective-permute-done((bf16[2,256,384]{2,1,0:T(8,128)(2,1)S(1)}, bf16[2,256,384]{2,1,0:T(8,128)(2,1)S(1)}, u32[]{:S(2)}, u32[]{:S(2)}) %collective-permute-start.31) | collective-permute-done | bytes 393248 | tf_op jit(solution)/shard_map/ppermute | solution.py:35
  138.1 10.3 %collective-permute-start.23 = (bf16[1,4,192,256]{3,2,1,0:T(8,128)(2,1)}, bf16[1,4,192,256]{3,2,1,0:T(8,128)(2,1)}, u32[]{:S(2)}, u32[]{:S(2)}) collective-permute-start(bf16[1,4,192,256]{3,2,1,0:T(8,128)(2,1)} %collective-permute-done.20.refs_16_), channel_id=1, source_target_pairs={{0,25},{1,8},{2,27},{3,10},{4,29},{5,12},{6,31},{7,14},{32,57},{33... | collective-permute-start | bytes 1179656 | tf_op jit(solution)/shard_map/ppermute | solution.py:35
  150.1 1.5 collective-permute-start.21
  152.2 4.8 %collective-permute-done.23.refs_19_ = bf16[1,4,192,256]{3,2,1,0:T(8,128)(2,1)} collective-permute-done((bf16[1,4,192,256]{3,2,1,0:T(8,128)(2,1)}, bf16[1,4,192,256]{3,2,1,0:T(8,128)(2,1)}, u32[]{:S(2)}, u32[]{:S(2)}) %collective-permute-start.23) | collective-permute-done | bytes 393248 | tf_op jit(solution)/shard_map/ppermute | solution.py:35
  157.2 14.5 %shard_map.38 = (f32[384,896]{1,0:T(8,128)}, f32[384,896]{1,0:T(8,128)}) custom-call(s32[7]{0:T(128)} %stack.75.place, bf16[1,4,192,256]{3,2,1,0:T(8,128)(2,1)} %bitcast.26, bf16[1,4,192,256]{3,2,1,0:T(8,128)(2,1)} %collective-permute-done.refs_1_, bf16[1,4,192,256]{3,2,1,0:T(8,128)(2,1)} %collective-permute-done.1.refs_2_, ...), custom_call_target="tpu_custom_call" | custom-call | flops 5637144576 | bytes 25165824 | tf_op jit(solution)/shard_map/pallas_call | solution.py:102
  171.7 1.9 collective-permute-start.32
  173.7 14.4 %shard_map.39 = (f32[384,896]{1,0:T(8,128)}, f32[384,896]{1,0:T(8,128)}) custom-call(s32[7]{0:T(128)} %copy-done.4, bf16[1,4,192,256]{3,2,1,0:T(8,128)(2,1)} %bitcast.27, bf16[1,4,192,256]{3,2,1,0:T(8,128)(2,1)} %collective-permute-done.refs_1_, bf16[1,4,192,256]{3,2,1,0:T(8,128)(2,1)} %collective-permute-done.1.refs_2_, ...), custom_call_target="tpu_custom_call" | custom-call | flops 5637144576 | bytes 25165824 | tf_op jit(solution)/shard_map/pallas_call | solution.py:102
  188.1 1.7 collective-permute-done.32.received
  189.8 1.3 copy-done.1
  191.1 0.8 shard_map.40
  192.0 0.9 collective-permute-start.33
  192.8 11.7 %collective-permute-done.34.received = f32[384,896]{1,0:T(8,128)S(1)} collective-permute-done((f32[384,896]{1,0:T(8,128)}, f32[384,896]{1,0:T(8,128)S(1)}, u32[]{:S(2)}, u32[]{:S(2)}) %collective-permute-start.34) | collective-permute-done | bytes 1376288 | tf_op jit(solution)/shard_map/ppermute | solution.py:35
  204.5 0.8 shard_map.41
  205.4 3.5 %collective-permute-start.35 = (bf16[192,448]{1,0:T(8,128)(2,1)S(1)}, bf16[192,448]{1,0:T(8,128)(2,1)S(1)}, u32[]{:S(2)}, u32[]{:S(2)}) collective-permute-start(bf16[192,448]{1,0:T(8,128)(2,1)S(1)} %get-tuple-element.39), channel_id=1, source_target_pairs={{0,8},{1,25},{2,10},{3,27},{4,12},{5,29},{6,14},{7,31},{32,40},{33... | collective-permute-start | bytes 516104 | tf_op jit(solution)/shard_map/ppermute | solution.py:35
  209.4 2.5 %collective-permute-done.35.refs_2_ = bf16[192,448]{1,0:T(8,128)(2,1)S(1)} collective-permute-done((bf16[192,448]{1,0:T(8,128)(2,1)S(1)}, bf16[192,448]{1,0:T(8,128)(2,1)S(1)}, u32[]{:S(2)}, u32[]{:S(2)}) %collective-permute-start.35) | collective-permute-done | bytes 172064 | tf_op jit(solution)/shard_map/ppermute | solution.py:35
  211.9 10.9 %collective-permute-done.36.refs_3_ = bf16[192,448]{1,0:T(8,128)(2,1)S(1)} collective-permute-done((bf16[192,448]{1,0:T(8,128)(2,1)S(1)}, bf16[192,448]{1,0:T(8,128)(2,1)S(1)}, u32[]{:S(2)}, u32[]{:S(2)}) %collective-permute-start.36) | collective-permute-done | bytes 172064 | tf_op jit(solution)/shard_map/ppermute | solution.py:35
  222.8 1.5 shard_map.42
  (94 shorter events, 9.7 us)
Async XLA Ops:
  6.5 150.6 %all-gather.3.cloned.1.call-start = ((), (), s32[]{:S(2)}) async-start(), calls=%async_computation | async-start | bytes 4587520 | tf_op jit(solution)/shard_map/all_gather | solution.py:242
  9.9 8.6 %collective-permute-start.24 = (bf16[256,896]{1,0:T(8,128)(2,1)S(1)}, bf16[256,896]{1,0:T(8,128)(2,1)S(1)}, u32[]{:S(2)}, u32[]{:S(2)}) collective-permute-start(bf16[256,896]{1,0:T(8,128)(2,1)S(1)} %get-tuple-element.30), channel_id=1, source_target_pairs={{0,8},{1,25},{2,10},{3,27},{4,12},{5,29},{6,14},{7,31},{32,40},{33... | collective-permute-start | bytes 1376264 | tf_op jit(solution)/shard_map/ppermute | solution.py:35
  19.6 13.5 %collective-permute-start.3 = (bf16[1,4,192,256]{3,2,1,0:T(8,128)(2,1)S(1)}, bf16[1,4,192,256]{3,2,1,0:T(8,128)(2,1)S(1)}, u32[]{:S(2)}, u32[]{:S(2)}) collective-permute-start(bf16[1,4,192,256]{3,2,1,0:T(8,128)(2,1)S(1)} %bitcast.28), channel_id=1, source_target_pairs={{0,38},{1,39},{2,0},{3,1},{4,2},{5,3},{6,4},{7,5},{32,6},{33,7},{3... | collective-permute-start | bytes 1179656 | tf_op jit(solution)/shard_map/ppermute | solution.py:35
  25.3 10.9 %collective-permute-start.4 = (bf16[1,4,192,256]{3,2,1,0:T(8,128)(2,1)S(1)}, bf16[1,4,192,256]{3,2,1,0:T(8,128)(2,1)S(1)}, u32[]{:S(2)}, u32[]{:S(2)}) collective-permute-start(bf16[1,4,192,256]{3,2,1,0:T(8,128)(2,1)S(1)} %bitcast.29), channel_id=1, source_target_pairs={{0,2},{1,3},{2,4},{3,5},{4,6},{5,7},{6,32},{7,33},{32,34},{33,35},... | collective-permute-start | bytes 1179656 | tf_op jit(solution)/shard_map/ppermute | solution.py:35
  25.3 12.1 %collective-permute-start.2 = (bf16[1,4,192,256]{3,2,1,0:T(8,128)(2,1)S(1)}, bf16[1,4,192,256]{3,2,1,0:T(8,128)(2,1)S(1)}, u32[]{:S(2)}, u32[]{:S(2)}) collective-permute-start(bf16[1,4,192,256]{3,2,1,0:T(8,128)(2,1)S(1)} %bitcast.30), channel_id=1, source_target_pairs={{0,25},{1,8},{2,27},{3,10},{4,29},{5,12},{6,31},{7,14},{32,57},{33... | collective-permute-start | bytes 1179656 | tf_op jit(solution)/shard_map/ppermute | solution.py:35
  27.3 11.0 %collective-permute-start.1 = (bf16[1,4,192,256]{3,2,1,0:T(8,128)(2,1)S(1)}, bf16[1,4,192,256]{3,2,1,0:T(8,128)(2,1)}, u32[]{:S(2)}, u32[]{:S(2)}) collective-permute-start(bf16[1,4,192,256]{3,2,1,0:T(8,128)(2,1)S(1)} %bitcast.31), channel_id=1, source_target_pairs={{0,8},{1,25},{2,10},{3,27},{4,12},{5,29},{6,14},{7,31},{32,40},{33... | collective-permute-start | bytes 1179656 | tf_op jit(solution)/shard_map/ppermute | solution.py:35
  29.1 14.7 %collective-permute-start.15 = (bf16[256,896]{1,0:T(8,128)(2,1)S(1)}, bf16[256,896]{1,0:T(8,128)(2,1)S(1)}, u32[]{:S(2)}, u32[]{:S(2)}) collective-permute-start(bf16[256,896]{1,0:T(8,128)(2,1)S(1)} %get-tuple-element.26), channel_id=1, source_target_pairs={{0,8},{1,25},{2,10},{3,27},{4,12},{5,29},{6,14},{7,31},{32,40},{33... | collective-permute-start | bytes 1376264 | tf_op jit(solution)/shard_map/ppermute | solution.py:35
  36.3 39.2 %copy-start.6 = (bf16[2,4,192,256]{3,2,1,0:T(8,128)(2,1)}, bf16[2,4,192,256]{3,2,1,0:T(8,128)(2,1)S(1)}, u32[]{:S(2)}) copy-start(bf16[2,4,192,256]{3,2,1,0:T(8,128)(2,1)S(1)} %constant_dynamic-update-slice_fusion.refs_4_) | copy-start | bytes 2359300
  38.3 40.5 %collective-permute-start.7 = (bf16[2,4,192,256]{3,2,1,0:T(8,128)(2,1)S(1)}, bf16[2,4,192,256]{3,2,1,0:T(8,128)(2,1)S(1)}, u32[]{:S(2)}, u32[]{:S(2)}) collective-permute-start(bf16[2,4,192,256]{3,2,1,0:T(8,128)(2,1)S(1)} %constant_dynamic-update-slice_fusion.refs_4_), channel_id=1, source_target_pairs={{0,25},{1,8},{2,27},{3,10},{4,29},{5,12},{6,31},{7,14},{32,57},{33... | collective-permute-start | bytes 2359304 | tf_op jit(solution)/shard_map/ppermute | solution.py:35
  39.1 39.7 %collective-permute-start.6 = (bf16[2,4,192,256]{3,2,1,0:T(8,128)(2,1)S(1)}, bf16[2,4,192,256]{3,2,1,0:T(8,128)(2,1)S(1)}, u32[]{:S(2)}, u32[]{:S(2)}) collective-permute-start(bf16[2,4,192,256]{3,2,1,0:T(8,128)(2,1)S(1)} %constant_dynamic-update-slice_fusion.refs_4_), channel_id=1, source_target_pairs={{0,8},{1,25},{2,10},{3,27},{4,12},{5,29},{6,14},{7,31},{32,40},{33... | collective-permute-start | bytes 2359304 | tf_op jit(solution)/shard_map/ppermute | solution.py:35
  40.9 33.8 %collective-permute-start.8 = (bf16[1,4,192,256]{3,2,1,0:T(8,128)(2,1)S(1)}, bf16[1,4,192,256]{3,2,1,0:T(8,128)(2,1)S(1)}, u32[]{:S(2)}, u32[]{:S(2)}) collective-permute-start(bf16[1,4,192,256]{3,2,1,0:T(8,128)(2,1)S(1)} %collective-permute-done.3), channel_id=1, source_target_pairs={{0,38},{1,39},{2,0},{3,1},{4,2},{5,3},{6,4},{7,5},{32,6},{33,7},{3... | collective-permute-start | bytes 1179656 | tf_op jit(solution)/shard_map/ppermute | solution.py:35
  43.7 34.3 %collective-permute-start.9 = (bf16[1,4,192,256]{3,2,1,0:T(8,128)(2,1)S(1)}, bf16[1,4,192,256]{3,2,1,0:T(8,128)(2,1)S(1)}, u32[]{:S(2)}, u32[]{:S(2)}) collective-permute-start(bf16[1,4,192,256]{3,2,1,0:T(8,128)(2,1)S(1)} %collective-permute-done.4), channel_id=1, source_target_pairs={{0,2},{1,3},{2,4},{3,5},{4,6},{5,7},{6,32},{7,33},{32,34},{33,35},... | collective-permute-start | bytes 1179656 | tf_op jit(solution)/shard_map/ppermute | solution.py:35
  43.9 39.5 %collective-permute-start.16 = (bf16[2,256,512]{2,1,0:T(8,128)(2,1)S(1)}, bf16[2,256,512]{2,1,0:T(8,128)(2,1)}, u32[]{:S(2)}, u32[]{:S(2)}) collective-permute-start(bf16[2,256,512]{2,1,0:T(8,128)(2,1)S(1)} %pad_maximum_fusion.1), channel_id=1, source_target_pairs={{0,32},{1,33},{2,34},{3,35},{4,36},{5,37},{6,38},{7,39},{32,0},{33... | collective-permute-start | bytes 1572872 | tf_op jit(solution)/shard_map/ppermute | solution.py:35
  78.8 18.1 %collective-permute-start.12 = (bf16[2,4,192,256]{3,2,1,0:T(8,128)(2,1)}, bf16[2,4,192,256]{3,2,1,0:T(8,128)(2,1)}, u32[]{:S(2)}, u32[]{:S(2)}) collective-permute-start(bf16[2,4,192,256]{3,2,1,0:T(8,128)(2,1)} %constant_dynamic-update-slice_fusion.2.refs_8_), channel_id=1, source_target_pairs={{0,25},{1,8},{2,27},{3,10},{4,29},{5,12},{6,31},{7,14},{32,57},{33... | collective-permute-start | bytes 2359304 | tf_op jit(solution)/shard_map/ppermute | solution.py:35
  80.1 12.1 %collective-permute-start.14 = (bf16[1,4,192,256]{3,2,1,0:T(8,128)(2,1)S(1)}, bf16[1,4,192,256]{3,2,1,0:T(8,128)(2,1)S(1)}, u32[]{:S(2)}, u32[]{:S(2)}) collective-permute-start(bf16[1,4,192,256]{3,2,1,0:T(8,128)(2,1)S(1)} %collective-permute-done.9), channel_id=1, source_target_pairs={{0,2},{1,3},{2,4},{3,5},{4,6},{5,7},{6,32},{7,33},{32,34},{33,35},... | collective-permute-start | bytes 1179656 | tf_op jit(solution)/shard_map/ppermute | solution.py:35
  80.1 12.8 %collective-permute-start.13 = (bf16[1,4,192,256]{3,2,1,0:T(8,128)(2,1)S(1)}, bf16[1,4,192,256]{3,2,1,0:T(8,128)(2,1)S(1)}, u32[]{:S(2)}, u32[]{:S(2)}) collective-permute-start(bf16[1,4,192,256]{3,2,1,0:T(8,128)(2,1)S(1)} %collective-permute-done.8), channel_id=1, source_target_pairs={{0,38},{1,39},{2,0},{3,1},{4,2},{5,3},{6,4},{7,5},{32,6},{33,7},{3... | collective-permute-start | bytes 1179656 | tf_op jit(solution)/shard_map/ppermute | solution.py:35
  82.7 17.5 %collective-permute-start.11 = (bf16[2,4,192,256]{3,2,1,0:T(8,128)(2,1)}, bf16[2,4,192,256]{3,2,1,0:T(8,128)(2,1)}, u32[]{:S(2)}, u32[]{:S(2)}) collective-permute-start(bf16[2,4,192,256]{3,2,1,0:T(8,128)(2,1)} %constant_dynamic-update-slice_fusion.2.refs_8_), channel_id=1, source_target_pairs={{0,8},{1,25},{2,10},{3,27},{4,12},{5,29},{6,14},{7,31},{32,40},{33... | collective-permute-start | bytes 2359304 | tf_op jit(solution)/shard_map/ppermute | solution.py:35
  83.4 17.5 %collective-permute-start.5 = (bf16[2,4,192,256]{3,2,1,0:T(8,128)(2,1)}, bf16[2,4,192,256]{3,2,1,0:T(8,128)(2,1)S(1)}, u32[]{:S(2)}, u32[]{:S(2)}) collective-permute-start(bf16[2,4,192,256]{3,2,1,0:T(8,128)(2,1)} %copy-done.6), channel_id=1, source_target_pairs={{0,1},{1,0},{2,3},{3,2},{4,5},{5,4},{6,7},{7,6},{32,33},{33,32},{3... | collective-permute-start | bytes 2359304 | tf_op jit(solution)/shard_map/ppermute | solution.py:35
  92.1 8.1 %collective-permute-start = (bf16[1,4,192,256]{3,2,1,0:T(8,128)(2,1)}, bf16[1,4,192,256]{3,2,1,0:T(8,128)(2,1)}, u32[]{:S(2)}, u32[]{:S(2)}) collective-permute-start(bf16[1,4,192,256]{3,2,1,0:T(8,128)(2,1)} %bitcast.25), channel_id=1, source_target_pairs={{0,1},{1,0},{2,3},{3,2},{4,5},{5,4},{6,7},{7,6},{32,33},{33,32},{3... | collective-permute-start | bytes 1179656 | tf_op jit(solution)/shard_map/ppermute | solution.py:35
  92.9 23.2 %collective-permute-start.28 = (bf16[2,256,384]{2,1,0:T(8,128)(2,1)S(1)}, bf16[2,256,384]{2,1,0:T(8,128)(2,1)S(1)}, u32[]{:S(2)}, u32[]{:S(2)}) collective-permute-start(bf16[2,256,384]{2,1,0:T(8,128)(2,1)S(1)} %pad_maximum_fusion.2), channel_id=1, source_target_pairs={{0,32},{1,33},{2,34},{3,35},{4,36},{5,37},{6,38},{7,39},{32,0},{33... | collective-permute-start | bytes 1179656 | tf_op jit(solution)/shard_map/ppermute | solution.py:35
  96.9 25.1 %collective-permute-start.27 = (bf16[2,256,512]{2,1,0:T(8,128)(2,1)}, bf16[2,256,512]{2,1,0:T(8,128)(2,1)S(1)}, u32[]{:S(2)}, u32[]{:S(2)}) collective-permute-start(bf16[2,256,512]{2,1,0:T(8,128)(2,1)} %collective-permute-done.16.refs_21_), channel_id=1, source_target_pairs={{0,64},{1,65},{2,66},{3,67},{4,68},{5,69},{6,70},{7,71},{32,96},{3... | collective-permute-start | bytes 1572872 | tf_op jit(solution)/shard_map/ppermute | solution.py:35
  98.0 59.1 %copy-start.7 = (bf16[2,4,192,256]{3,2,1,0:T(8,128)(2,1)}, bf16[2,4,192,256]{3,2,1,0:T(8,128)(2,1)S(1)}, u32[]{:S(2)}) copy-start(bf16[2,4,192,256]{3,2,1,0:T(8,128)(2,1)S(1)} %constant_dynamic-update-slice_fusion.4.refs_12_) | copy-start | bytes 2359300
  100.2 31.0 %collective-permute-start.19 = (bf16[2,4,192,256]{3,2,1,0:T(8,128)(2,1)S(1)}, bf16[2,4,192,256]{3,2,1,0:T(8,128)(2,1)S(1)}, u32[]{:S(2)}, u32[]{:S(2)}) collective-permute-start(bf16[2,4,192,256]{3,2,1,0:T(8,128)(2,1)S(1)} %constant_dynamic-update-slice_fusion.4.refs_12_), channel_id=1, source_target_pairs={{0,25},{1,8},{2,27},{3,10},{4,29},{5,12},{6,31},{7,14},{32,57},{33... | collective-permute-start | bytes 2359304 | tf_op jit(solution)/shard_map/ppermute | solution.py:35
  100.2 33.0 %collective-permute-start.18 = (bf16[2,4,192,256]{3,2,1,0:T(8,128)(2,1)S(1)}, bf16[2,4,192,256]{3,2,1,0:T(8,128)(2,1)S(1)}, u32[]{:S(2)}, u32[]{:S(2)}) collective-permute-start(bf16[2,4,192,256]{3,2,1,0:T(8,128)(2,1)S(1)} %constant_dynamic-update-slice_fusion.4.refs_12_), channel_id=1, source_target_pairs={{0,8},{1,25},{2,10},{3,27},{4,12},{5,29},{6,14},{7,31},{32,40},{33... | collective-permute-start | bytes 2359304 | tf_op jit(solution)/shard_map/ppermute | solution.py:35
  100.9 32.3 %copy-start.10 = (bf16[2,4,192,256]{3,2,1,0:T(8,128)(2,1)}, bf16[2,4,192,256]{3,2,1,0:T(8,128)(2,1)S(1)}, u32[]{:S(2)}) copy-start(bf16[2,4,192,256]{3,2,1,0:T(8,128)(2,1)S(1)} %collective-permute-done.5.refs_5_) | copy-start | bytes 2359300
  100.9 22.8 %collective-permute-start.26 = (bf16[2,256,512]{2,1,0:T(8,128)(2,1)}, bf16[2,256,512]{2,1,0:T(8,128)(2,1)S(1)}, u32[]{:S(2)}, u32[]{:S(2)}) collective-permute-start(bf16[2,256,512]{2,1,0:T(8,128)(2,1)} %collective-permute-done.16.refs_21_), channel_id=1, source_target_pairs={{0,128},{1,129},{2,130},{3,131},{4,132},{5,133},{6,134},{7,135},{3... | collective-permute-start | bytes 1572872 | tf_op jit(solution)/shard_map/ppermute | solution.py:35
  116.0 22.1 %copy-start.18 = (bf16[2,256,384]{2,1,0:T(8,128)(2,1)}, bf16[2,256,384]{2,1,0:T(8,128)(2,1)S(1)}, u32[]{:S(2)}) copy-start(bf16[2,256,384]{2,1,0:T(8,128)(2,1)S(1)} %collective-permute-done.28.refs_25_) | copy-start | bytes 1179652
  116.0 13.0 %collective-permute-start.25 = (bf16[2,256,512]{2,1,0:T(8,128)(2,1)}, bf16[2,256,512]{2,1,0:T(8,128)(2,1)S(1)}, u32[]{:S(2)}, u32[]{:S(2)}) collective-permute-start(bf16[2,256,512]{2,1,0:T(8,128)(2,1)} %collective-permute-done.16.refs_21_), channel_id=1, source_target_pairs={{0,192},{1,193},{2,194},{3,195},{4,196},{5,197},{6,198},{7,199},{3... | collective-permute-start | bytes 1572872 | tf_op jit(solution)/shard_map/ppermute | solution.py:35
  122.0 9.2 %collective-permute-start.20 = (bf16[1,4,192,256]{3,2,1,0:T(8,128)(2,1)S(1)}, bf16[1,4,192,256]{3,2,1,0:T(8,128)(2,1)}, u32[]{:S(2)}, u32[]{:S(2)}) collective-permute-start(bf16[1,4,192,256]{3,2,1,0:T(8,128)(2,1)S(1)} %get-tuple-element.41), channel_id=1, source_target_pairs={{0,2},{1,39},{2,4},{3,1},{4,6},{5,3},{6,32},{7,5},{32,34},{33,7},{... | collective-permute-start | bytes 1179656 | tf_op jit(solution)/shard_map/ppermute | solution.py:35
  123.6 33.5 %copy-start.14 = (bf16[2,256,512]{2,1,0:T(8,128)(2,1)}, bf16[2,256,512]{2,1,0:T(8,128)(2,1)S(1)}, u32[]{:S(2)}) copy-start(bf16[2,256,512]{2,1,0:T(8,128)(2,1)S(1)} %collective-permute-done.26.refs_23_) | copy-start | bytes 1572868
  123.6 28.5 %collective-permute-start.10 = (bf16[2,4,192,256]{3,2,1,0:T(8,128)(2,1)}, bf16[2,4,192,256]{3,2,1,0:T(8,128)(2,1)}, u32[]{:S(2)}, u32[]{:S(2)}) collective-permute-start(bf16[2,4,192,256]{3,2,1,0:T(8,128)(2,1)} %constant_dynamic-update-slice_fusion.2.refs_8_), channel_id=1, source_target_pairs={{0,1},{1,0},{2,3},{3,2},{4,5},{5,4},{6,7},{7,6},{32,33},{33,32},{3... | collective-permute-start | bytes 2359304 | tf_op jit(solution)/shard_map/ppermute | solution.py:35
  129.0 28.2 %copy-start.15 = (bf16[2,256,512]{2,1,0:T(8,128)(2,1)}, bf16[2,256,512]{2,1,0:T(8,128)(2,1)S(1)}, u32[]{:S(2)}) copy-start(bf16[2,256,512]{2,1,0:T(8,128)(2,1)S(1)} %collective-permute-done.25.refs_22_) | copy-start | bytes 1572868
  129.0 9.1 %collective-permute-start.31 = (bf16[2,256,384]{2,1,0:T(8,128)(2,1)S(1)}, bf16[2,256,384]{2,1,0:T(8,128)(2,1)S(1)}, u32[]{:S(2)}, u32[]{:S(2)}) collective-permute-start(bf16[2,256,384]{2,1,0:T(8,128)(2,1)S(1)} %collective-permute-done.28.refs_25_), channel_id=1, source_target_pairs={{0,64},{1,65},{2,66},{3,67},{4,68},{5,69},{6,70},{7,71},{32,96},{3... | collective-permute-start | bytes 1179656 | tf_op jit(solution)/shard_map/ppermute | solution.py:35
  131.2 17.2 %collective-permute-start.30 = (bf16[2,256,384]{2,1,0:T(8,128)(2,1)S(1)}, bf16[2,256,384]{2,1,0:T(8,128)(2,1)S(1)}, u32[]{:S(2)}, u32[]{:S(2)}) collective-permute-start(bf16[2,256,384]{2,1,0:T(8,128)(2,1)S(1)} %collective-permute-done.28.refs_25_), channel_id=1, source_target_pairs={{0,128},{1,129},{2,130},{3,131},{4,132},{5,133},{6,134},{7,135},{3... | collective-permute-start | bytes 1179656 | tf_op jit(solution)/shard_map/ppermute | solution.py:35
  131.2 25.9 %copy-start.11 = (bf16[2,4,192,256]{3,2,1,0:T(8,128)(2,1)}, bf16[2,4,192,256]{3,2,1,0:T(8,128)(2,1)S(1)}, u32[]{:S(2)}) copy-start(bf16[2,4,192,256]{3,2,1,0:T(8,128)(2,1)S(1)} %collective-permute-done.19.refs_15_) | copy-start | bytes 2359300
  131.2 20.9 %collective-permute-start.17 = (bf16[2,4,192,256]{3,2,1,0:T(8,128)(2,1)S(1)}, bf16[2,4,192,256]{3,2,1,0:T(8,128)(2,1)}, u32[]{:S(2)}, u32[]{:S(2)}) collective-permute-start(bf16[2,4,192,256]{3,2,1,0:T(8,128)(2,1)S(1)} %constant_dynamic-update-slice_fusion.4.refs_12_), channel_id=1, source_target_pairs={{0,1},{1,0},{2,3},{3,2},{4,5},{5,4},{6,7},{7,6},{32,33},{33,32},{3... | collective-permute-start | bytes 2359304 | tf_op jit(solution)/shard_map/ppermute | solution.py:35
  133.2 24.0 %copy-start.12 = (bf16[2,4,192,256]{3,2,1,0:T(8,128)(2,1)}, bf16[2,4,192,256]{3,2,1,0:T(8,128)(2,1)S(1)}, u32[]{:S(2)}) copy-start(bf16[2,4,192,256]{3,2,1,0:T(8,128)(2,1)S(1)} %collective-permute-done.18.refs_14_) | copy-start | bytes 2359300
  133.2 16.1 %collective-permute-start.29 = (bf16[2,256,384]{2,1,0:T(8,128)(2,1)S(1)}, bf16[2,256,384]{2,1,0:T(8,128)(2,1)S(1)}, u32[]{:S(2)}, u32[]{:S(2)}) collective-permute-start(bf16[2,256,384]{2,1,0:T(8,128)(2,1)S(1)} %collective-permute-done.28.refs_25_), channel_id=1, source_target_pairs={{0,192},{1,193},{2,194},{3,195},{4,196},{5,197},{6,198},{7,199},{3... | collective-permute-start | bytes 1179656 | tf_op jit(solution)/shard_map/ppermute | solution.py:35
  138.1 18.8 %collective-permute-start.23 = (bf16[1,4,192,256]{3,2,1,0:T(8,128)(2,1)}, bf16[1,4,192,256]{3,2,1,0:T(8,128)(2,1)}, u32[]{:S(2)}, u32[]{:S(2)}) collective-permute-start(bf16[1,4,192,256]{3,2,1,0:T(8,128)(2,1)} %collective-permute-done.20.refs_16_), channel_id=1, source_target_pairs={{0,25},{1,8},{2,27},{3,10},{4,29},{5,12},{6,31},{7,14},{32,57},{33... | collective-permute-start | bytes 1179656 | tf_op jit(solution)/shard_map/ppermute | solution.py:35
  148.5 8.7 %collective-permute-start.22 = (bf16[1,4,192,256]{3,2,1,0:T(8,128)(2,1)}, bf16[1,4,192,256]{3,2,1,0:T(8,128)(2,1)}, u32[]{:S(2)}, u32[]{:S(2)}) collective-permute-start(bf16[1,4,192,256]{3,2,1,0:T(8,128)(2,1)} %collective-permute-done.20.refs_16_), channel_id=1, source_target_pairs={{0,8},{1,25},{2,10},{3,27},{4,12},{5,29},{6,14},{7,31},{32,40},{33... | collective-permute-start | bytes 1179656 | tf_op jit(solution)/shard_map/ppermute | solution.py:35
  150.1 7.1 %collective-permute-start.21 = (bf16[1,4,192,256]{3,2,1,0:T(8,128)(2,1)}, bf16[1,4,192,256]{3,2,1,0:T(8,128)(2,1)}, u32[]{:S(2)}, u32[]{:S(2)}) collective-permute-start(bf16[1,4,192,256]{3,2,1,0:T(8,128)(2,1)} %collective-permute-done.20.refs_16_), channel_id=1, source_target_pairs={{0,1},{1,0},{2,3},{3,2},{4,5},{5,4},{6,7},{7,6},{32,33},{33,32},{3... | collective-permute-start | bytes 1179656 | tf_op jit(solution)/shard_map/ppermute | solution.py:35
  171.7 18.1 %collective-permute-start.32 = (f32[384,896]{1,0:T(8,128)}, f32[384,896]{1,0:T(8,128)S(1)}, u32[]{:S(2)}, u32[]{:S(2)}) collective-permute-start(f32[384,896]{1,0:T(8,128)} %get-tuple-element.32), channel_id=1, source_target_pairs={{0,24},{1,9},{2,26},{3,11},{4,28},{5,13},{6,30},{7,15},{32,56},{33... | collective-permute-start | bytes 4128776 | tf_op jit(solution)/shard_map/ppermute | solution.py:35
  173.6 16.2 %copy-start.5 = (s32[7]{0:T(128)S(1)}, s32[7]{0:T(128)}, u32[]{:S(2)}) copy-start(s32[7]{0:T(128)} %copy-done.4) | copy-start | bytes 88
  173.6 30.9 %collective-permute-start.34 = (f32[384,896]{1,0:T(8,128)}, f32[384,896]{1,0:T(8,128)S(1)}, u32[]{:S(2)}, u32[]{:S(2)}) collective-permute-start(f32[384,896]{1,0:T(8,128)} %get-tuple-element.33), channel_id=1, source_target_pairs={{0,24},{1,9},{2,26},{3,11},{4,28},{5,13},{6,30},{7,15},{32,56},{33... | collective-permute-start | bytes 4128776 | tf_op jit(solution)/shard_map/ppermute | solution.py:35
  191.1 13.4 %copy-start = (f32[384,896]{1,0:T(8,128)S(1)}, f32[384,896]{1,0:T(8,128)}, u32[]{:S(2)}) copy-start(f32[384,896]{1,0:T(8,128)} %get-tuple-element.38.kept) | copy-start | bytes 4128772
  192.0 17.5 %collective-permute-start.33 = (bf16[192,448]{1,0:T(8,128)(2,1)S(1)}, bf16[192,448]{1,0:T(8,128)(2,1)S(1)}, u32[]{:S(2)}, u32[]{:S(2)}) collective-permute-start(bf16[192,448]{1,0:T(8,128)(2,1)S(1)} %get-tuple-element.37), channel_id=1, source_target_pairs={{0,32},{1,33},{2,34},{3,35},{4,36},{5,37},{6,38},{7,39},{32,0},{33... | collective-permute-start | bytes 516104 | tf_op jit(solution)/shard_map/ppermute | solution.py:35
  205.4 6.6 %collective-permute-start.35 = (bf16[192,448]{1,0:T(8,128)(2,1)S(1)}, bf16[192,448]{1,0:T(8,128)(2,1)S(1)}, u32[]{:S(2)}, u32[]{:S(2)}) collective-permute-start(bf16[192,448]{1,0:T(8,128)(2,1)S(1)} %get-tuple-element.39), channel_id=1, source_target_pairs={{0,8},{1,25},{2,10},{3,27},{4,12},{5,29},{6,14},{7,31},{32,40},{33... | collective-permute-start | bytes 516104 | tf_op jit(solution)/shard_map/ppermute | solution.py:35
  208.9 13.9 %collective-permute-start.36 = (bf16[192,448]{1,0:T(8,128)(2,1)S(1)}, bf16[192,448]{1,0:T(8,128)(2,1)S(1)}, u32[]{:S(2)}, u32[]{:S(2)}) collective-permute-start(bf16[192,448]{1,0:T(8,128)(2,1)S(1)} %get-tuple-element.40), channel_id=1, source_target_pairs={{0,40},{1,57},{2,42},{3,59},{4,44},{5,61},{6,46},{7,63},{32,8},{33... | collective-permute-start | bytes 516104 | tf_op jit(solution)/shard_map/ppermute | solution.py:35
  (12 other events, 49.9 us)
Sparse Core Ops, SparseCore 0:
  19.7 48.1 all-gather.2

commit v6 on v4

--- a/solution.py
+++ b/solution.py
@@ -54,40 +54,58 @@
     return x - side(x, c), y, z, c
 
 
-def product_kernel(place, own, partner, *refs):
-    near, far, (outs, lhs, rhs) = refs[:4], (refs[4:8], refs[8:12]), (refs[12:14], *refs[14:])
+def product_kernel(u, place, panel, *refs):
+    near, far, refs = refs[:4], (refs[4:8], refs[8:12]), refs[12:]
+    before, (outs, pieces, lhs, rhs, lhs_sem, rhs_sem) = refs[: 2 * u], (refs[2 * u : 2 * u + 2], *refs[2 * u + 2 :])
     y, zh = place[0], place[1]
-    rows = own.shape[3]
+    rows, wide = lhs.shape[0] // 4, rhs.shape[1]
+    tokens = [pltpu.make_async_copy(panel.at[:, :, place[4 + i]], pieces.at[i], lhs_sem.at[i]) for i in range(2)]
+    weights = []
     for d in range(4):
-        for u in range(2):
-            k = u * 8 + lax.rem(y + d, 4) * 2
-            at = pl.ds(pl.multiple_of((k + zh) * 256, 256), 256)
-            rhs[at, :] = near[d][u]
-            at = pl.ds(pl.multiple_of((k + 1 - zh) * 256, 256), 256)
-            for (lo, hi), part in zip(PARTS, far):
-                rhs[at, lo:hi] = part[d][u]
-    for i, out in enumerate(outs):
-        for k in range(16):
-            source = own if k < 8 else partner
-            lhs[:, k * 256 : (k + 1) * 256] = source[:, k % 8, place[4 + i]].reshape(2 * rows, 256)
-        for at in range(0, rhs.shape[1], 256):
-            to = min(at + 256, rhs.shape[1])
-            out[:, at:to] = jnp.dot(lhs[...], rhs[:, at:to], preferred_element_type=jnp.float32)
-
-
-def product(place, own, partner, near, far):
-    rows, depth, wide = own.shape[3], 4096, near[0].shape[2]
-    vmem = pl.BlockSpec(memory_space=pltpu.VMEM)
-    operands = [own, partner, *near, *far[0], *far[1]]
-    return pl.pallas_call(
-        product_kernel,
+        k = lax.rem(y + d, 4) * 2
+        at = pl.multiple_of((k + zh) * 256, 256)
+        weights.append(pltpu.make_async_copy(near[d].at[u], rhs.at[pl.ds(at, 256)], rhs_sem.at[d * 3]))
+        at = pl.multiple_of((k + 1 - zh) * 256, 256)
+        for n, ((lo, hi), part) in enumerate(zip(PARTS, far)):
+            target = rhs.at[pl.ds(at, 256), lo:hi]
+            weights.append(pltpu.make_async_copy(part[d].at[u], target, rhs_sem.at[d * 3 + 1 + n]))
+    for copy in (*tokens, *weights):
+        copy.start()
+    for i in range(2):
+        tokens[i].wait()
+        for b in range(2):
+            at = (i * 2 + b) * rows
+            for k in range(8):
+                lhs[at : at + rows, k * 256 : (k + 1) * 256] = pieces[i, b, k]
+    for copy in weights:
+        copy.wait()
+    for lo in range(0, wide, 256):
+        hi = min(lo + 256, wide)
+        part = jnp.dot(lhs[...], rhs[:, lo:hi], preferred_element_type=jnp.float32)
+        for i, out in enumerate(outs):
+            mine = part[i * 2 * rows : (i + 1) * 2 * rows]
+            out[:, lo:hi] = before[i][:, lo:hi] + mine if u else mine
+
+
+def product(u, place, panel, near, far, before=()):
+    rows, depth, wide = panel.shape[3], 2048, near[0].shape[2]
+    hbm, vmem = pl.BlockSpec(memory_space=pltpu.HBM), pl.BlockSpec(memory_space=pltpu.VMEM)
+    operands = [panel, *near, *far[0], *far[1]]
+    return pl.pallas_call(
+        functools.partial(product_kernel, u),
         out_shape=[jax.ShapeDtypeStruct((2 * rows, wide), jnp.float32)] * 2,
-        in_specs=[pl.BlockSpec(memory_space=pltpu.SMEM)] + [vmem] * len(operands),
+        in_specs=[pl.BlockSpec(memory_space=pltpu.SMEM)] + [hbm] * len(operands) + [vmem] * len(before),
         out_specs=[vmem] * 2,
-        scratch_shapes=[pltpu.VMEM((2 * rows, depth), jnp.bfloat16), pltpu.VMEM((depth, wide), jnp.bfloat16)],
-        compiler_params=pltpu.CompilerParams(vmem_limit_bytes=40 << 20),
-        cost_estimate=pl.CostEstimate(flops=8 * rows * depth * wide, bytes_accessed=24 << 20, transcendentals=0),
-    )(place, *operands)
+        scratch_shapes=[
+            pltpu.VMEM((2, 2, 8, rows, 256), jnp.bfloat16),
+            pltpu.VMEM((4 * rows, depth), jnp.bfloat16),
+            pltpu.VMEM((depth, wide), jnp.bfloat16),
+            pltpu.SemaphoreType.DMA((2,)),
+            pltpu.SemaphoreType.DMA((12,)),
+        ],
+        compiler_params=pltpu.CompilerParams(vmem_limit_bytes=48 << 20),
+        cost_estimate=pl.CostEstimate(flops=8 * rows * depth * wide, bytes_accessed=16 << 20, transcendentals=0),
+    )(place, *operands, *before)
 
 
 def cut_kernel(place, gate, up, near, away, give_near, give_away):
@@ -173,8 +191,8 @@
     )(place, *blocks)
 
 
-def along_y(value):
-    return [value] + [move(value, lambda x, y, z, c, d=d: (x, y - d, z, c)) for d in range(1, 4)]
+def along_y(value, d):
+    return move(value, lambda x, y, z, c: (x, y - d, z, c))
 
 
 def after(value, *others):
@@ -197,20 +215,22 @@
     panel = lax.all_gather(tokens, ("zh", "zl", "c"), axis=0)
     near, away, give_near, give_away = cut(keep_place, gate_weight, up_weight)
     got_near, got_away = move(give_near, to_partner), move(give_away, to_partner)
-    near = along_y(jnp.stack([near, got_near]))
-
-    panel = after(panel, got_away, *near[1:])
-    partner_panel = move(panel, to_partner).reshape(2, 8, NX, rows, 256)
-    own = panel.reshape(2, 8, NX, rows, 256)
-    away, got_away = lax.optimization_barrier((away, got_away, panel))[:2]
+    near = jnp.stack([near, got_near])
+    near = [near, along_y(near, 1), near, along_y(near, 3)]
+
+    panel = after(panel, got_away, near[1], near[3])
+    away, got_away, near[2], panel = lax.optimization_barrier((away, got_away, near[2], panel))
+    own, shared = (p.reshape(2, 8, NX, rows, 256) for p in (panel, move(panel, to_partner)))
     far = [jnp.stack([away[:, lo:hi], got_away[:, lo:hi]]) for lo, hi in PARTS]
     far[0] = move(far[0], to_antipode)
-    far[1] = move(after(far[1], far[0]), to_antipode)
-    far = [along_y(f) for f in far]
-
-    sent = product(send_place, own, partner_panel, near, far)
+    near[2] = along_y(near[2], 2)
+    far[1] = move(after(far[1], far[0], near[2]), to_antipode)
+    far = [[f] + [along_y(f, d) for d in range(1, 4)] for f in far]
+
+    sent = product(1, send_place, shared, near, far, product(0, send_place, own, near, far))
     sums = [move(sent[0], to_summer), move(sent[1], to_summer)]
-    kept = product(after(keep_place, *sent), own, partner_panel, near, far)
+    turn = after(keep_place, *sent)
+    kept = product(1, turn, shared, near, far, product(0, turn, own, near, far))
     mine, over_z = gated(keep_place, kept[0], sums[0])
     over_x, over_both = gated(keep_place, kept[1], sums[1])
     blocks = [mine, move(over_z, to_antipode), move(over_x, to_partner), move(over_both, to_both)]

time: 221 us -> 211 us (0.955)
  the two profiles are of different devices: /device:TPU:24 before, /device:TPU:98 now
where the time goes in v6:
time: 211 us; the launch traced here: 210 us
  waiting for transfers between devices  123 us (58%)
  Pallas kernels  38.7 us (18%)
  starting transfers between devices  29.3 us (14%)
  between operations  13.6 us (6%)
  local copies, waits for them, and re-layouts  5.92 us (3%)
    ppermute x19, waiting for transfers between devices, move(): return lax.ppermute(value, AXES, pairs)  108 us
    pallas_call x4, Pallas kernels, product(): pl.pallas_call(functools.partial(product_kernel, u), out_shape=[jax.Shape...  34.7 us
    ppermute x19, starting transfers between devices, move(): return lax.ppermute(value, AXES, pairs)  29.3 us
    all_gather x1, waiting for transfers between devices, per_device(): panel = lax.all_gather(tokens, ('zh', 'zl', 'c'), axis=0)  13.6 us
    unnamed x16, local copies, waits for them, and re-layouts  4.64 us
  transfers between devices with their start and end apart: 20, of which 11 were waited for; matrix products, arithmetic and copies ran while one was open for 1% of the time, Pallas kernels for 13%

profile of v6, /device:TPU:98, one launch (start us, length us, event | category | flops | bytes accessed | tf_op | source)
XLA Modules:
  0.0 210.4 jit_solution(14776301030021642115)
XLA Ops:
  6.5 0.7 all-gather.3.cloned.1.call-update
  7.3 0.1 stack.72.place
  7.4 1.2 copy-done.2
  8.6 1.2 copy-done.3
  9.8 0.9 shard_map.37
  10.7 0.6 collective-permute-start.1
  11.3 7.9 %collective-permute-done.1 = bf16[256,896]{1,0:T(8,128)(2,1)S(1)} collective-permute-done((bf16[256,896]{1,0:T(8,128)(2,1)S(1)}, bf16[256,896]{1,0:T(8,128)(2,1)S(1)}, u32[]{:S(2)}, u32[]{:S(2)}) %collective-permute-start.1) | collective-permute-done | bytes 458784 | tf_op jit(solution)/shard_map/ppermute | solution.py:34
  19.3 0.1 pad_maximum_fusion.refs_0_
  19.4 1.7 collective-permute-start.3
  21.0 1.7 collective-permute-start.2
  22.7 0.5 collective-permute-start
  23.2 7.9 %collective-permute-done = bf16[256,896]{1,0:T(8,128)(2,1)S(1)} collective-permute-done((bf16[256,896]{1,0:T(8,128)(2,1)S(1)}, bf16[256,896]{1,0:T(8,128)(2,1)S(1)}, u32[]{:S(2)}, u32[]{:S(2)}) %collective-permute-start) | collective-permute-done | bytes 458784 | tf_op jit(solution)/shard_map/ppermute | solution.py:34
  31.2 10.8 %collective-permute-done.3.refs_3_ = bf16[2,256,896]{2,1,0:T(8,128)(2,1)S(1)} collective-permute-done((bf16[2,256,896]{2,1,0:T(8,128)(2,1)S(1)}, bf16[2,256,896]{2,1,0:T(8,128)(2,1)S(1)}, u32[]{:S(2)}, u32[]{:S(2)}) %collective-permute-start.3) | collective-permute-done | bytes 917536 | tf_op jit(solution)/shard_map/ppermute | solution.py:34
  42.0 0.9 copy-done.5
  42.9 13.6 %all-gather.3.cloned.1.call-done = bf16[12288,256]{1,0:T(8,128)(2,1)} async-done(((bf16[768,256]{1,0:T(8,128)(2,1)}), bf16[12288,256]{1,0:T(8,128)(2,1)}) %all-gather.3.cloned.1.call-update) | async-done | bytes 6291472 | tf_op jit(solution)/shard_map/all_gather | solution.py:215
  56.5 0.6 collective-permute-start.4
  57.1 3.0 %collective-permute-start.5 = (bf16[2,256,896]{2,1,0:T(8,128)(2,1)S(1)}, bf16[2,256,896]{2,1,0:T(8,128)(2,1)S(1)}, u32[]{:S(2)}, u32[]{:S(2)}) collective-permute-start(bf16[2,256,896]{2,1,0:T(8,128)(2,1)S(1)} %pad_maximum_fusion.refs_0_), channel_id=1, source_target_pairs={{0,128},{1,129},{2,130},{3,131},{4,132},{5,133},{6,134},{7,135},{3... | collective-permute-start | bytes 2752520 | tf_op jit(solution)/shard_map/ppermute | solution.py:34
  60.2 0.1 pad_maximum_fusion.1
  60.2 2.3 %collective-permute-start.6 = (bf16[2,256,512]{2,1,0:T(8,128)(2,1)S(1)}, bf16[2,256,512]{2,1,0:T(8,128)(2,1)S(1)}, u32[]{:S(2)}, u32[]{:S(2)}) collective-permute-start(bf16[2,256,512]{2,1,0:T(8,128)(2,1)S(1)} %pad_maximum_fusion.1), channel_id=1, source_target_pairs={{0,32},{1,33},{2,34},{3,35},{4,36},{5,37},{6,38},{7,39},{32,0},{33... | collective-permute-start | bytes 1572872 | tf_op jit(solution)/shard_map/ppermute | solution.py:34
  62.5 27.6 %collective-permute-done.6.refs_4_ = bf16[2,256,512]{2,1,0:T(8,128)(2,1)S(1)} collective-permute-done((bf16[2,256,512]{2,1,0:T(8,128)(2,1)S(1)}, bf16[2,256,512]{2,1,0:T(8,128)(2,1)S(1)}, u32[]{:S(2)}, u32[]{:S(2)}) %collective-permute-start.6) | collective-permute-done | bytes 524320 | tf_op jit(solution)/shard_map/ppermute | solution.py:34
  90.1 0.6 collective-permute-start.9
  90.7 2.0 collective-permute-start.8
  92.7 1.1 slice_bitcast_fusion.2
  93.9 2.3 %collective-permute-start.10 = (bf16[2,256,384]{2,1,0:T(8,128)(2,1)S(1)}, bf16[2,256,384]{2,1,0:T(8,128)(2,1)}, u32[]{:S(2)}, u32[]{:S(2)}) collective-permute-start(bf16[2,256,384]{2,1,0:T(8,128)(2,1)S(1)} %pad_maximum_fusion.2), channel_id=1, source_target_pairs={{0,32},{1,33},{2,34},{3,35},{4,36},{5,37},{6,38},{7,39},{32,0},{33... | collective-permute-start | bytes 1179656 | tf_op jit(solution)/shard_map/ppermute | solution.py:34
  96.1 0.6 collective-permute-start.7
  96.8 18.4 %collective-permute-done.10.refs_8_ = bf16[2,256,384]{2,1,0:T(8,128)(2,1)} collective-permute-done((bf16[2,256,384]{2,1,0:T(8,128)(2,1)S(1)}, bf16[2,256,384]{2,1,0:T(8,128)(2,1)}, u32[]{:S(2)}, u32[]{:S(2)}) %collective-permute-start.10) | collective-permute-done | bytes 393248 | tf_op jit(solution)/shard_map/ppermute | solution.py:34
  115.1 1.5 collective-permute-start.13
  116.6 0.9 collective-permute-start.12
  117.5 1.7 collective-permute-start.11
  119.3 0.1 stack.75.place
  119.4 16.7 %collective-permute-done.13.refs_11_ = bf16[2,256,384]{2,1,0:T(8,128)(2,1)} collective-permute-done((bf16[2,256,384]{2,1,0:T(8,128)(2,1)}, bf16[2,256,384]{2,1,0:T(8,128)(2,1)}, u32[]{:S(2)}, u32[]{:S(2)}) %collective-permute-start.13) | collective-permute-done | bytes 393248 | tf_op jit(solution)/shard_map/ppermute | solution.py:34
  136.1 0.6 collective-permute-done.11.refs_9_
  136.7 8.1 %shard_map.38 = (f32[384,896]{1,0:T(8,128)}, f32[384,896]{1,0:T(8,128)}) custom-call(s32[7]{0:T(128)S(1)} %stack.75.place, bf16[2,8,4,192,256]{4,3,2,1,0:T(8,128)(2,1)} %bitcast.24, bf16[2,256,896]{2,1,0:T(8,128)(2,1)S(1)} %pad_maximum_fusion.refs_0_, bf16[2,256,896]{2,1,0:T(8,128)(2,1)S(1)} %collective-permute-done.2.refs_1_, ...), custom_call_target="tpu_custom_call" | custom-call | flops 2818572288 | bytes 16777216 | tf_op jit(solution)/shard_map/pallas_call | solution.py:94
  144.8 9.3 %shard_map.39 = (f32[384,896]{1,0:T(8,128)}, f32[384,896]{1,0:T(8,128)}) custom-call(s32[7]{0:T(128)S(1)} %stack.75.place, bf16[2,8,4,192,256]{4,3,2,1,0:T(8,128)(2,1)} %bitcast.12.panel, bf16[2,256,896]{2,1,0:T(8,128)(2,1)S(1)} %pad_maximum_fusion.refs_0_, bf16[2,256,896]{2,1,0:T(8,128)(2,1)S(1)} %collective-permute-done.2.refs_1_, ...), custom_call_target="tpu_custom_call" | custom-call | flops 2818572288 | bytes 16777216 | tf_op jit(solution)/shard_map/pallas_call | solution.py:94
  154.1 0.1 collective-permute-start.14
  154.2 2.0 collective-permute-start.16
  156.2 8.1 %shard_map.40 = (f32[384,896]{1,0:T(8,128)}, f32[384,896]{1,0:T(8,128)}) custom-call(s32[7]{0:T(128)S(1)} %stack.72.place, bf16[2,8,4,192,256]{4,3,2,1,0:T(8,128)(2,1)} %bitcast.25, bf16[2,256,896]{2,1,0:T(8,128)(2,1)S(1)} %pad_maximum_fusion.refs_0_, bf16[2,256,896]{2,1,0:T(8,128)(2,1)S(1)} %collective-permute-done.2.refs_1_, ...), custom_call_target="tpu_custom_call" | custom-call | flops 2818572288 | bytes 16777216 | tf_op jit(solution)/shard_map/pallas_call | solution.py:94
  164.3 9.3 %shard_map.41 = (f32[384,896]{1,0:T(8,128)}, f32[384,896]{1,0:T(8,128)}) custom-call(s32[7]{0:T(128)S(1)} %stack.72.place, bf16[2,8,4,192,256]{4,3,2,1,0:T(8,128)(2,1)} %bitcast.12.panel, bf16[2,256,896]{2,1,0:T(8,128)(2,1)S(1)} %pad_maximum_fusion.refs_0_, bf16[2,256,896]{2,1,0:T(8,128)(2,1)S(1)} %collective-permute-done.2.refs_1_, ...), custom_call_target="tpu_custom_call" | custom-call | flops 2818572288 | bytes 16777216 | tf_op jit(solution)/shard_map/pallas_call | solution.py:94
  173.6 1.3 copy-done.1
  174.9 0.8 shard_map.42
  175.7 2.2 %collective-permute-start.15 = (bf16[192,448]{1,0:T(8,128)(2,1)S(1)}, bf16[192,448]{1,0:T(8,128)(2,1)S(1)}, u32[]{:S(2)}, u32[]{:S(2)}) collective-permute-start(bf16[192,448]{1,0:T(8,128)(2,1)S(1)} %get-tuple-element.47), channel_id=1, source_target_pairs={{0,32},{1,33},{2,34},{3,35},{4,36},{5,37},{6,38},{7,39},{32,0},{33... | collective-permute-start | bytes 516104 | tf_op jit(solution)/shard_map/ppermute | solution.py:34
  178.0 9.5 %collective-permute-done.16.received = f32[384,896]{1,0:T(8,128)S(1)} collective-permute-done((f32[384,896]{1,0:T(8,128)}, f32[384,896]{1,0:T(8,128)S(1)}, u32[]{:S(2)}, u32[]{:S(2)}) %collective-permute-start.16) | collective-permute-done | bytes 1376288 | tf_op jit(solution)/shard_map/ppermute | solution.py:34
  187.5 0.8 shard_map.43
  188.3 3.3 %collective-permute-start.17 = (bf16[192,448]{1,0:T(8,128)(2,1)S(1)}, bf16[192,448]{1,0:T(8,128)(2,1)S(1)}, u32[]{:S(2)}, u32[]{:S(2)}) collective-permute-start(bf16[192,448]{1,0:T(8,128)(2,1)S(1)} %get-tuple-element.49), channel_id=1, source_target_pairs={{0,8},{1,25},{2,10},{3,27},{4,12},{5,29},{6,14},{7,31},{32,40},{33... | collective-permute-start | bytes 516104 | tf_op jit(solution)/shard_map/ppermute | solution.py:34
  191.6 1.7 collective-permute-start.18
  193.2 2.0 collective-permute-done.17.refs_2_
  195.2 6.8 %collective-permute-done.18.refs_3_ = bf16[192,448]{1,0:T(8,128)(2,1)S(1)} collective-permute-done((bf16[192,448]{1,0:T(8,128)(2,1)S(1)}, bf16[192,448]{1,0:T(8,128)(2,1)S(1)}, u32[]{:S(2)}, u32[]{:S(2)}) %collective-permute-start.18) | collective-permute-done | bytes 172064 | tf_op jit(solution)/shard_map/ppermute | solution.py:34
  202.1 1.5 shard_map.44
  (24 shorter events, 0.1 us)
Async XLA Ops:
  6.5 50.0 %all-gather.3.cloned.1.call-start = ((), (), s32[]{:S(2)}) async-start(), calls=%async_computation | async-start | bytes 6684672 | tf_op jit(solution)/shard_map/all_gather | solution.py:215
  7.4 1.2 copy-start.2
  8.6 1.2 copy-start.3
  10.7 49.4 %copy-start.4 = (bf16[256,896]{1,0:T(8,128)(2,1)}, bf16[256,896]{1,0:T(8,128)(2,1)S(1)}, u32[]{:S(2)}) copy-start(bf16[256,896]{1,0:T(8,128)(2,1)S(1)} %get-tuple-element.35) | copy-start | bytes 1376260
  10.7 8.6 %collective-permute-start.1 = (bf16[256,896]{1,0:T(8,128)(2,1)S(1)}, bf16[256,896]{1,0:T(8,128)(2,1)S(1)}, u32[]{:S(2)}, u32[]{:S(2)}) collective-permute-start(bf16[256,896]{1,0:T(8,128)(2,1)S(1)} %get-tuple-element.31), channel_id=1, source_target_pairs={{0,8},{1,25},{2,10},{3,27},{4,12},{5,29},{6,14},{7,31},{32,40},{33... | collective-permute-start | bytes 1376264 | tf_op jit(solution)/shard_map/ppermute | solution.py:34
  19.4 22.6 %collective-permute-start.3 = (bf16[2,256,896]{2,1,0:T(8,128)(2,1)S(1)}, bf16[2,256,896]{2,1,0:T(8,128)(2,1)S(1)}, u32[]{:S(2)}, u32[]{:S(2)}) collective-permute-start(bf16[2,256,896]{2,1,0:T(8,128)(2,1)S(1)} %pad_maximum_fusion.refs_0_), channel_id=1, source_target_pairs={{0,64},{1,65},{2,66},{3,67},{4,68},{5,69},{6,70},{7,71},{32,96},{3... | collective-permute-start | bytes 2752520 | tf_op jit(solution)/shard_map/ppermute | solution.py:34
  21.0 21.9 %collective-permute-start.2 = (bf16[2,256,896]{2,1,0:T(8,128)(2,1)S(1)}, bf16[2,256,896]{2,1,0:T(8,128)(2,1)S(1)}, u32[]{:S(2)}, u32[]{:S(2)}) collective-permute-start(bf16[2,256,896]{2,1,0:T(8,128)(2,1)S(1)} %pad_maximum_fusion.refs_0_), channel_id=1, source_target_pairs={{0,192},{1,193},{2,194},{3,195},{4,196},{5,197},{6,198},{7,199},{3... | collective-permute-start | bytes 2752520 | tf_op jit(solution)/shard_map/ppermute | solution.py:34
  22.7 8.5 %collective-permute-start = (bf16[256,896]{1,0:T(8,128)(2,1)S(1)}, bf16[256,896]{1,0:T(8,128)(2,1)S(1)}, u32[]{:S(2)}, u32[]{:S(2)}) collective-permute-start(bf16[256,896]{1,0:T(8,128)(2,1)S(1)} %get-tuple-element.29), channel_id=1, source_target_pairs={{0,8},{1,25},{2,10},{3,27},{4,12},{5,29},{6,14},{7,31},{32,40},{33... | collective-permute-start | bytes 1376264 | tf_op jit(solution)/shard_map/ppermute | solution.py:34
  31.2 29.0 %copy-start.7 = (bf16[256,896]{1,0:T(8,128)(2,1)}, bf16[256,896]{1,0:T(8,128)(2,1)S(1)}, u32[]{:S(2)}) copy-start(bf16[256,896]{1,0:T(8,128)(2,1)S(1)} %collective-permute-done) | copy-start | bytes 1376260
  41.9 0.9 copy-start.5
  56.5 88.3 %collective-permute-start.4 = (bf16[16,768,256]{2,1,0:T(8,128)(2,1)}, bf16[16,768,256]{2,1,0:T(8,128)(2,1)}, u32[]{:S(2)}, u32[]{:S(2)}) collective-permute-start(bf16[16,768,256]{2,1,0:T(8,128)(2,1)} %bitcast.23), channel_id=1, source_target_pairs={{0,8},{1,25},{2,10},{3,27},{4,12},{5,29},{6,14},{7,31},{32,40},{33... | collective-permute-start | bytes 18874376 | tf_op jit(solution)/shard_map/ppermute | solution.py:34
  57.1 36.8 %collective-permute-start.5 = (bf16[2,256,896]{2,1,0:T(8,128)(2,1)S(1)}, bf16[2,256,896]{2,1,0:T(8,128)(2,1)S(1)}, u32[]{:S(2)}, u32[]{:S(2)}) collective-permute-start(bf16[2,256,896]{2,1,0:T(8,128)(2,1)S(1)} %pad_maximum_fusion.refs_0_), channel_id=1, source_target_pairs={{0,128},{1,129},{2,130},{3,131},{4,132},{5,133},{6,134},{7,135},{3... | collective-permute-start | bytes 2752520 | tf_op jit(solution)/shard_map/ppermute | solution.py:34
  60.2 29.9 %collective-permute-start.6 = (bf16[2,256,512]{2,1,0:T(8,128)(2,1)S(1)}, bf16[2,256,512]{2,1,0:T(8,128)(2,1)S(1)}, u32[]{:S(2)}, u32[]{:S(2)}) collective-permute-start(bf16[2,256,512]{2,1,0:T(8,128)(2,1)S(1)} %pad_maximum_fusion.1), channel_id=1, source_target_pairs={{0,32},{1,33},{2,34},{3,35},{4,36},{5,37},{6,38},{7,39},{32,0},{33... | collective-permute-start | bytes 1572872 | tf_op jit(solution)/shard_map/ppermute | solution.py:34
  90.1 26.5 %collective-permute-start.9 = (bf16[2,256,512]{2,1,0:T(8,128)(2,1)S(1)}, bf16[2,256,512]{2,1,0:T(8,128)(2,1)S(1)}, u32[]{:S(2)}, u32[]{:S(2)}) collective-permute-start(bf16[2,256,512]{2,1,0:T(8,128)(2,1)S(1)} %collective-permute-done.6.refs_4_), channel_id=1, source_target_pairs={{0,64},{1,65},{2,66},{3,67},{4,68},{5,69},{6,70},{7,71},{32,96},{3... | collective-permute-start | bytes 1572872 | tf_op jit(solution)/shard_map/ppermute | solution.py:34
  90.7 26.8 %collective-permute-start.8 = (bf16[2,256,512]{2,1,0:T(8,128)(2,1)S(1)}, bf16[2,256,512]{2,1,0:T(8,128)(2,1)S(1)}, u32[]{:S(2)}, u32[]{:S(2)}) collective-permute-start(bf16[2,256,512]{2,1,0:T(8,128)(2,1)S(1)} %collective-permute-done.6.refs_4_), channel_id=1, source_target_pairs={{0,128},{1,129},{2,130},{3,131},{4,132},{5,133},{6,134},{7,135},{3... | collective-permute-start | bytes 1572872 | tf_op jit(solution)/shard_map/ppermute | solution.py:34
  93.8 23.7 %copy-start.6 = (bf16[2,256,896]{2,1,0:T(8,128)(2,1)}, bf16[2,256,896]{2,1,0:T(8,128)(2,1)S(1)}, u32[]{:S(2)}) copy-start(bf16[2,256,896]{2,1,0:T(8,128)(2,1)S(1)} %collective-permute-done.5.refs_2_) | copy-start | bytes 2752516
  93.9 21.3 %collective-permute-start.10 = (bf16[2,256,384]{2,1,0:T(8,128)(2,1)S(1)}, bf16[2,256,384]{2,1,0:T(8,128)(2,1)}, u32[]{:S(2)}, u32[]{:S(2)}) collective-permute-start(bf16[2,256,384]{2,1,0:T(8,128)(2,1)S(1)} %pad_maximum_fusion.2), channel_id=1, source_target_pairs={{0,32},{1,33},{2,34},{3,35},{4,36},{5,37},{6,38},{7,39},{32,0},{33... | collective-permute-start | bytes 1179656 | tf_op jit(solution)/shard_map/ppermute | solution.py:34
  96.1 23.3 %collective-permute-start.7 = (bf16[2,256,512]{2,1,0:T(8,128)(2,1)S(1)}, bf16[2,256,512]{2,1,0:T(8,128)(2,1)}, u32[]{:S(2)}, u32[]{:S(2)}) collective-permute-start(bf16[2,256,512]{2,1,0:T(8,128)(2,1)S(1)} %collective-permute-done.6.refs_4_), channel_id=1, source_target_pairs={{0,192},{1,193},{2,194},{3,195},{4,196},{5,197},{6,198},{7,199},{3... | collective-permute-start | bytes 1572872 | tf_op jit(solution)/shard_map/ppermute | solution.py:34
  115.1 21.0 %collective-permute-start.13 = (bf16[2,256,384]{2,1,0:T(8,128)(2,1)}, bf16[2,256,384]{2,1,0:T(8,128)(2,1)}, u32[]{:S(2)}, u32[]{:S(2)}) collective-permute-start(bf16[2,256,384]{2,1,0:T(8,128)(2,1)} %collective-permute-done.10.refs_8_), channel_id=1, source_target_pairs={{0,64},{1,65},{2,66},{3,67},{4,68},{5,69},{6,70},{7,71},{32,96},{3... | collective-permute-start | bytes 1179656 | tf_op jit(solution)/shard_map/ppermute | solution.py:34
  116.6 19.5 %collective-permute-start.12 = (bf16[2,256,384]{2,1,0:T(8,128)(2,1)}, bf16[2,256,384]{2,1,0:T(8,128)(2,1)}, u32[]{:S(2)}, u32[]{:S(2)}) collective-permute-start(bf16[2,256,384]{2,1,0:T(8,128)(2,1)} %collective-permute-done.10.refs_8_), channel_id=1, source_target_pairs={{0,128},{1,129},{2,130},{3,131},{4,132},{5,133},{6,134},{7,135},{3... | collective-permute-start | bytes 1179656 | tf_op jit(solution)/shard_map/ppermute | solution.py:34
  117.5 19.2 %collective-permute-start.11 = (bf16[2,256,384]{2,1,0:T(8,128)(2,1)}, bf16[2,256,384]{2,1,0:T(8,128)(2,1)}, u32[]{:S(2)}, u32[]{:S(2)}) collective-permute-start(bf16[2,256,384]{2,1,0:T(8,128)(2,1)} %collective-permute-done.10.refs_8_), channel_id=1, source_target_pairs={{0,192},{1,193},{2,194},{3,195},{4,196},{5,197},{6,198},{7,199},{3... | collective-permute-start | bytes 1179656 | tf_op jit(solution)/shard_map/ppermute | solution.py:34
  154.1 19.5 %collective-permute-start.14 = (f32[384,896]{1,0:T(8,128)}, f32[384,896]{1,0:T(8,128)S(1)}, u32[]{:S(2)}, u32[]{:S(2)}) collective-permute-start(f32[384,896]{1,0:T(8,128)} %get-tuple-element.40), channel_id=1, source_target_pairs={{0,24},{1,9},{2,26},{3,11},{4,28},{5,13},{6,30},{7,15},{32,56},{33... | collective-permute-start | bytes 4128776 | tf_op jit(solution)/shard_map/ppermute | solution.py:34
  154.2 33.3 %collective-permute-start.16 = (f32[384,896]{1,0:T(8,128)}, f32[384,896]{1,0:T(8,128)S(1)}, u32[]{:S(2)}, u32[]{:S(2)}) collective-permute-start(f32[384,896]{1,0:T(8,128)} %get-tuple-element.41), channel_id=1, source_target_pairs={{0,24},{1,9},{2,26},{3,11},{4,28},{5,13},{6,30},{7,15},{32,56},{33... | collective-permute-start | bytes 4128776 | tf_op jit(solution)/shard_map/ppermute | solution.py:34
  173.6 1.3 copy-start.1
  174.9 12.5 %copy-start = (f32[384,896]{1,0:T(8,128)S(1)}, f32[384,896]{1,0:T(8,128)}, u32[]{:S(2)}) copy-start(f32[384,896]{1,0:T(8,128)} %get-tuple-element.48.kept) | copy-start | bytes 4128772
  175.7 17.5 %collective-permute-start.15 = (bf16[192,448]{1,0:T(8,128)(2,1)S(1)}, bf16[192,448]{1,0:T(8,128)(2,1)S(1)}, u32[]{:S(2)}, u32[]{:S(2)}) collective-permute-start(bf16[192,448]{1,0:T(8,128)(2,1)S(1)} %get-tuple-element.47), channel_id=1, source_target_pairs={{0,32},{1,33},{2,34},{3,35},{4,36},{5,37},{6,38},{7,39},{32,0},{33... | collective-permute-start | bytes 516104 | tf_op jit(solution)/shard_map/ppermute | solution.py:34
  188.3 7.0 %collective-permute-start.17 = (bf16[192,448]{1,0:T(8,128)(2,1)S(1)}, bf16[192,448]{1,0:T(8,128)(2,1)S(1)}, u32[]{:S(2)}, u32[]{:S(2)}) collective-permute-start(bf16[192,448]{1,0:T(8,128)(2,1)S(1)} %get-tuple-element.49), channel_id=1, source_target_pairs={{0,8},{1,25},{2,10},{3,27},{4,12},{5,29},{6,14},{7,31},{32,40},{33... | collective-permute-start | bytes 516104 | tf_op jit(solution)/shard_map/ppermute | solution.py:34
  191.6 10.5 %collective-permute-start.18 = (bf16[192,448]{1,0:T(8,128)(2,1)S(1)}, bf16[192,448]{1,0:T(8,128)(2,1)S(1)}, u32[]{:S(2)}, u32[]{:S(2)}) collective-permute-start(bf16[192,448]{1,0:T(8,128)(2,1)S(1)} %get-tuple-element.50), channel_id=1, source_target_pairs={{0,40},{1,57},{2,42},{3,59},{4,44},{5,61},{6,46},{7,63},{32,8},{33... | collective-permute-start | bytes 516104 | tf_op jit(solution)/shard_map/ppermute | solution.py:34
Sparse Core Ops, SparseCore 0:
  9.2 47.2 all-gather.2

commit v7 on v6

--- a/solution.py
+++ b/solution.py
@@ -12,7 +12,6 @@
 NX, NY, NZ, NC = 4, 4, 8, 2
 AXES = ("y", "zh", "x", "zl", "c")
 TILE = 128
-PARTS = ((0, 512), (512, 896))
 
 
 def device_index(x, y, z, c):
@@ -54,24 +53,22 @@
     return x - side(x, c), y, z, c
 
 
-def product_kernel(u, place, panel, *refs):
-    near, far, refs = refs[:4], (refs[4:8], refs[8:12]), refs[12:]
-    before, (outs, pieces, lhs, rhs, lhs_sem, rhs_sem) = refs[: 2 * u], (refs[2 * u : 2 * u + 2], *refs[2 * u + 2 :])
+def product_kernel(u, slots, place, panel, *refs):
+    near, far, refs = refs[:4], refs[4:8], refs[8:]
+    before, refs = refs[: u * len(slots)], refs[u * len(slots) :]
+    outs, (pieces, lhs, rhs, lhs_sem, rhs_sem) = refs[: len(slots)], refs[len(slots) :]
     y, zh = place[0], place[1]
-    rows, wide = lhs.shape[0] // 4, rhs.shape[1]
-    tokens = [pltpu.make_async_copy(panel.at[:, :, place[4 + i]], pieces.at[i], lhs_sem.at[i]) for i in range(2)]
+    rows, wide = pieces.shape[3], rhs.shape[1]
+    tokens = [pltpu.make_async_copy(panel.at[:, :, place[slot]], pieces.at[i], lhs_sem.at[i]) for i, slot in enumerate(slots)]
     weights = []
     for d in range(4):
         k = lax.rem(y + d, 4) * 2
-        at = pl.multiple_of((k + zh) * 256, 256)
-        weights.append(pltpu.make_async_copy(near[d].at[u], rhs.at[pl.ds(at, 256)], rhs_sem.at[d * 3]))
-        at = pl.multiple_of((k + 1 - zh) * 256, 256)
-        for n, ((lo, hi), part) in enumerate(zip(PARTS, far)):
-            target = rhs.at[pl.ds(at, 256), lo:hi]
-            weights.append(pltpu.make_async_copy(part[d].at[u], target, rhs_sem.at[d * 3 + 1 + n]))
+        for source, at in ((near[d].at[u], k + zh), (far[d], k + 1 - zh)):
+            target = rhs.at[pl.ds(pl.multiple_of(at * 256, 256), 256)]
+            weights.append(pltpu.make_async_copy(source, target, rhs_sem.at[len(weights)]))
     for copy in (*tokens, *weights):
         copy.start()
-    for i in range(2):
+    for i in range(len(slots)):
         tokens[i].wait()
         for b in range(2):
             at = (i * 2 + b) * rows
@@ -87,24 +84,24 @@
             out[:, lo:hi] = before[i][:, lo:hi] + mine if u else mine
 
 
-def product(u, place, panel, near, far, before=()):
-    rows, depth, wide = panel.shape[3], 2048, near[0].shape[2]
+def product(u, slots, place, panel, near, far, before=()):
+    rows, depth, wide, n = panel.shape[3], 2048, far[u][0].shape[1], len(slots)
     hbm, vmem = pl.BlockSpec(memory_space=pltpu.HBM), pl.BlockSpec(memory_space=pltpu.VMEM)
-    operands = [panel, *near, *far[0], *far[1]]
-    return pl.pallas_call(
-        functools.partial(product_kernel, u),
-        out_shape=[jax.ShapeDtypeStruct((2 * rows, wide), jnp.float32)] * 2,
+    operands = [panel, *near, *far[u]]
+    return pl.pallas_call(
+        functools.partial(product_kernel, u, slots),
+        out_shape=[jax.ShapeDtypeStruct((2 * rows, wide), jnp.float32)] * n,
         in_specs=[pl.BlockSpec(memory_space=pltpu.SMEM)] + [hbm] * len(operands) + [vmem] * len(before),
-        out_specs=[vmem] * 2,
+        out_specs=[vmem] * n,
         scratch_shapes=[
-            pltpu.VMEM((2, 2, 8, rows, 256), jnp.bfloat16),
-            pltpu.VMEM((4 * rows, depth), jnp.bfloat16),
+            pltpu.VMEM((n, 2, 8, rows, 256), jnp.bfloat16),
+            pltpu.VMEM((2 * n * rows, depth), jnp.bfloat16),
             pltpu.VMEM((depth, wide), jnp.bfloat16),
-            pltpu.SemaphoreType.DMA((2,)),
-            pltpu.SemaphoreType.DMA((12,)),
+            pltpu.SemaphoreType.DMA((n,)),
+            pltpu.SemaphoreType.DMA((8,)),
         ],
-        compiler_params=pltpu.CompilerParams(vmem_limit_bytes=48 << 20),
-        cost_estimate=pl.CostEstimate(flops=8 * rows * depth * wide, bytes_accessed=16 << 20, transcendentals=0),
+        compiler_params=pltpu.CompilerParams(vmem_limit_bytes=60 << 20),
+        cost_estimate=pl.CostEstimate(flops=4 * n * rows * depth * wide, bytes_accessed=8 * n << 20, transcendentals=0),
     )(place, *operands, *before)
 
 
@@ -221,19 +218,24 @@
     panel = after(panel, got_away, near[1], near[3])
     away, got_away, near[2], panel = lax.optimization_barrier((away, got_away, near[2], panel))
     own, shared = (p.reshape(2, 8, NX, rows, 256) for p in (panel, move(panel, to_partner)))
-    far = [jnp.stack([away[:, lo:hi], got_away[:, lo:hi]]) for lo, hi in PARTS]
-    far[0] = move(far[0], to_antipode)
+    far = [move(away, to_antipode)]
     near[2] = along_y(near[2], 2)
-    far[1] = move(after(far[1], far[0], near[2]), to_antipode)
+    far.append(move(after(got_away, far[0], near[2]), to_antipode))
     far = [[f] + [along_y(f, d) for d in range(1, 4)] for f in far]
 
-    sent = product(1, send_place, shared, near, far, product(0, send_place, own, near, far))
-    sums = [move(sent[0], to_summer), move(sent[1], to_summer)]
-    turn = after(keep_place, *sent)
-    kept = product(1, turn, shared, near, far, product(0, turn, own, near, far))
-    mine, over_z = gated(keep_place, kept[0], sums[0])
-    over_x, over_both = gated(keep_place, kept[1], sums[1])
-    blocks = [mine, move(over_z, to_antipode), move(over_x, to_partner), move(over_both, to_both)]
+    sent = product(0, (4, 5), send_place, own, near, far)
+    kept = product(0, (4, 5), after(keep_place, *sent), own, near, far)
+    sums, turn = [None, None], send_place
+    for i in (1, 0):
+        total = product(1, (4 + i,), turn, shared, near, far, sent[i : i + 1])[0]
+        turn, sums[i] = after(send_place, total), move(total, to_summer)
+    turn = after(keep_place, total)
+    total = product(1, (5,), turn, shared, near, far, kept[1:])[0]
+    over_x, over_both = gated(keep_place, total, sums[1])
+    total = product(1, (4,), after(keep_place, over_x), shared, near, far, kept[:1])[0]
+    over_x, over_both = move(over_x, to_partner), move(over_both, to_both)
+    mine, over_z = gated(keep_place, total, after(sums[0], over_x, over_both))
+    blocks = [mine, move(over_z, to_antipode), over_x, over_both]
     return gather(keep_place, blocks)
 
 

time: 211 us -> 207 us (0.981); the launches traced: 210 us -> 204 us
  waiting for transfers between devices: 123 us -> 104 us
  Pallas kernels: 38.7 us -> 48.1 us
    ppermute x19, waiting for transfers between devices: 108 us -> 89.1 us  [move(): return lax.ppermute(value, AXES, pairs)]
    pallas_call x4 -> x6, Pallas kernels: 34.7 us -> 44.1 us  [product(): pl.pallas_call(functools.partial(product_kernel, u, slots), out_shape=[ja...]
    unnamed x16 -> x30, local copies, waits for them, and re-layouts: 4.64 us -> 6.87 us
  transfers between devices with their start and end apart: 20 -> 20, of which waited for: 11 -> 10; matrix products, arithmetic and copies ran while one was open for 1% -> 0% of each run, Pallas kernels for 13% -> 19%
where the time goes in v7:
time: 207 us; the launch traced here: 204 us
  waiting for transfers between devices  104 us (50%)
  Pallas kernels  48.1 us (23%)
  starting transfers between devices  29.8 us (14%)
  between operations  13.6 us (7%)
  local copies, waits for them, and re-layouts  7.54 us (4%)
    ppermute x19, waiting for transfers between devices, move(): return lax.ppermute(value, AXES, pairs)  89.1 us
    pallas_call x6, Pallas kernels, product(): pl.pallas_call(functools.partial(product_kernel, u, slots), out_shape=[ja...  44.1 us
    ppermute x19, starting transfers between devices, move(): return lax.ppermute(value, AXES, pairs)  29.8 us
    all_gather x1, waiting for transfers between devices, per_device(): panel = lax.all_gather(tokens, ('zh', 'zl', 'c'), axis=0)  14.5 us
    unnamed x30, local copies, waits for them, and re-layouts  6.87 us
  transfers between devices with their start and end apart: 20, of which 10 were waited for; matrix products, arithmetic and copies ran while one was open for 0% of the time, Pallas kernels for 19%

profile of v7, /device:TPU:98, one launch (start us, length us, event | category | flops | bytes accessed | tf_op | source)
XLA Modules:
  0.0 203.5 jit_solution(4457126425911929402)
XLA Ops:
  6.5 0.7 all-gather.3.cloned.1.call-update
  7.3 0.1 stack.54.place
  7.4 1.2 copy-done.2
  8.6 1.2 copy-done.3
  9.8 0.9 shard_map.37
  10.7 0.6 collective-permute-start.1
  11.3 7.9 %collective-permute-done.1 = bf16[256,896]{1,0:T(8,128)(2,1)S(1)} collective-permute-done((bf16[256,896]{1,0:T(8,128)(2,1)S(1)}, bf16[256,896]{1,0:T(8,128)(2,1)S(1)}, u32[]{:S(2)}, u32[]{:S(2)}) %collective-permute-start.1) | collective-permute-done | bytes 458784 | tf_op jit(solution)/shard_map/ppermute | solution.py:33
  19.3 0.1 pad_maximum_fusion.refs_0_
  19.4 1.7 collective-permute-start.3
  21.0 1.7 collective-permute-start.2
  22.7 0.5 collective-permute-start
  23.2 7.9 %collective-permute-done = bf16[256,896]{1,0:T(8,128)(2,1)S(1)} collective-permute-done((bf16[256,896]{1,0:T(8,128)(2,1)S(1)}, bf16[256,896]{1,0:T(8,128)(2,1)S(1)}, u32[]{:S(2)}, u32[]{:S(2)}) %collective-permute-start) | collective-permute-done | bytes 458784 | tf_op jit(solution)/shard_map/ppermute | solution.py:33
  31.2 10.8 %collective-permute-done.3.refs_3_ = bf16[2,256,896]{2,1,0:T(8,128)(2,1)S(1)} collective-permute-done((bf16[2,256,896]{2,1,0:T(8,128)(2,1)S(1)}, bf16[2,256,896]{2,1,0:T(8,128)(2,1)S(1)}, u32[]{:S(2)}, u32[]{:S(2)}) %collective-permute-start.3) | collective-permute-done | bytes 917536 | tf_op jit(solution)/shard_map/ppermute | solution.py:33
  42.0 14.5 %all-gather.3.cloned.1.call-done = bf16[12288,256]{1,0:T(8,128)(2,1)} async-done(((bf16[768,256]{1,0:T(8,128)(2,1)}), bf16[12288,256]{1,0:T(8,128)(2,1)}) %all-gather.3.cloned.1.call-update) | async-done | bytes 6291472 | tf_op jit(solution)/shard_map/all_gather | solution.py:212
  56.5 0.6 collective-permute-start.4
  57.1 3.0 %collective-permute-start.5 = (bf16[2,256,896]{2,1,0:T(8,128)(2,1)S(1)}, bf16[2,256,896]{2,1,0:T(8,128)(2,1)S(1)}, u32[]{:S(2)}, u32[]{:S(2)}) collective-permute-start(bf16[2,256,896]{2,1,0:T(8,128)(2,1)S(1)} %pad_maximum_fusion.refs_0_), channel_id=1, source_target_pairs={{0,128},{1,129},{2,130},{3,131},{4,132},{5,133},{6,134},{7,135},{3... | collective-permute-start | bytes 2752520 | tf_op jit(solution)/shard_map/ppermute | solution.py:33
  60.1 2.2 %collective-permute-start.6 = (bf16[256,896]{1,0:T(8,128)(2,1)S(1)}, bf16[256,896]{1,0:T(8,128)(2,1)}, u32[]{:S(2)}, u32[]{:S(2)}) collective-permute-start(bf16[256,896]{1,0:T(8,128)(2,1)S(1)} %get-tuple-element.36), channel_id=1, source_target_pairs={{0,32},{1,33},{2,34},{3,35},{4,36},{5,37},{6,38},{7,39},{32,0},{33... | collective-permute-start | bytes 1376264 | tf_op jit(solution)/shard_map/ppermute | solution.py:33
  62.3 24.9 %collective-permute-done.6.refs_4_ = bf16[256,896]{1,0:T(8,128)(2,1)} collective-permute-done((bf16[256,896]{1,0:T(8,128)(2,1)S(1)}, bf16[256,896]{1,0:T(8,128)(2,1)}, u32[]{:S(2)}, u32[]{:S(2)}) %collective-permute-start.6) | collective-permute-done | bytes 458784 | tf_op jit(solution)/shard_map/ppermute | solution.py:33
  87.2 1.0 copy-done.10
  88.2 2.2 %collective-permute-start.7 = (bf16[256,896]{1,0:T(8,128)(2,1)}, bf16[256,896]{1,0:T(8,128)(2,1)S(1)}, u32[]{:S(2)}, u32[]{:S(2)}) collective-permute-start(bf16[256,896]{1,0:T(8,128)(2,1)} %copy-done.14), channel_id=1, source_target_pairs={{0,32},{1,33},{2,34},{3,35},{4,36},{5,37},{6,38},{7,39},{32,0},{33... | collective-permute-start | bytes 1376264 | tf_op jit(solution)/shard_map/ppermute | solution.py:33
  90.3 0.6 collective-permute-start.13
  90.9 2.0 collective-permute-start.12
  92.9 0.6 collective-permute-start.11
  93.6 20.2 %collective-permute-done.7.refs_4_ = bf16[256,896]{1,0:T(8,128)(2,1)S(1)} collective-permute-done((bf16[256,896]{1,0:T(8,128)(2,1)}, bf16[256,896]{1,0:T(8,128)(2,1)S(1)}, u32[]{:S(2)}, u32[]{:S(2)}) %collective-permute-start.7) | collective-permute-done | bytes 458784 | tf_op jit(solution)/shard_map/ppermute | solution.py:33
  113.8 0.6 collective-permute-start.10
  114.4 2.0 %collective-permute-start.9 = (bf16[256,896]{1,0:T(8,128)(2,1)S(1)}, bf16[256,896]{1,0:T(8,128)(2,1)}, u32[]{:S(2)}, u32[]{:S(2)}) collective-permute-start(bf16[256,896]{1,0:T(8,128)(2,1)S(1)} %collective-permute-done.7.refs_4_), channel_id=1, source_target_pairs={{0,128},{1,129},{2,130},{3,131},{4,132},{5,133},{6,134},{7,135},{3... | collective-permute-start | bytes 1376264 | tf_op jit(solution)/shard_map/ppermute | solution.py:33
  116.4 0.8 copy-done.13
  117.3 1.4 collective-permute-start.8
  118.7 0.6 stack.57.place
  119.3 8.5 %shard_map.38 = (f32[384,896]{1,0:T(8,128)}, f32[384,896]{1,0:T(8,128)}) custom-call(s32[7]{0:T(128)} %stack.57.place, bf16[2,8,4,192,256]{4,3,2,1,0:T(8,128)(2,1)} %bitcast.16, bf16[2,256,896]{2,1,0:T(8,128)(2,1)} %copy-done.7, bf16[2,256,896]{2,1,0:T(8,128)(2,1)} %copy-done.9, bf16[2,256,896]{2,1,0:T(8,128)(2,1)} %copy-done.10, ...), custom_call_target="tpu_custom_call" | custom-call | flops 2818572288 | bytes 16777216 | tf_op jit(solution)/shard_map/pallas_call | solution.py:91
  127.8 9.2 %collective-permute-done.10.refs_7_ = bf16[256,896]{1,0:T(8,128)(2,1)} collective-permute-done((bf16[256,896]{1,0:T(8,128)(2,1)S(1)}, bf16[256,896]{1,0:T(8,128)(2,1)}, u32[]{:S(2)}, u32[]{:S(2)}) %collective-permute-start.10) | collective-permute-done | bytes 458784 | tf_op jit(solution)/shard_map/ppermute | solution.py:33
  137.0 0.6 collective-permute-done.8.refs_5_
  137.6 6.8 %shard_map.39 = f32[384,896]{1,0:T(8,128)} custom-call(s32[7]{0:T(128)} %stack.57.place, bf16[2,8,4,192,256]{4,3,2,1,0:T(8,128)(2,1)} %bitcast.12.panel, bf16[2,256,896]{2,1,0:T(8,128)(2,1)} %copy-done.7, bf16[2,256,896]{2,1,0:T(8,128)(2,1)} %copy-done.9, bf16[2,256,896]{2,1,0:T(8,128)(2,1)} %copy-done.10, bf16[2,256,896]{2,1,0:T(8,128)(2,1)} %copy-done.8, ...), custom_call_target="tpu_custom_call" | custom-call | flops 1409286144 | bytes 8388608 | tf_op jit(solution)/shard_map/pallas_call | solution.py:91
  144.4 0.1 collective-permute-start.14
  144.5 6.8 %shard_map.40 = f32[384,896]{1,0:T(8,128)} custom-call(s32[7]{0:T(128)} %stack.57.place, bf16[2,8,4,192,256]{4,3,2,1,0:T(8,128)(2,1)} %bitcast.12.panel, bf16[2,256,896]{2,1,0:T(8,128)(2,1)} %copy-done.7, bf16[2,256,896]{2,1,0:T(8,128)(2,1)} %copy-done.9, bf16[2,256,896]{2,1,0:T(8,128)(2,1)} %copy-done.10, bf16[2,256,896]{2,1,0:T(8,128)(2,1)} %copy-done.8, ...), custom_call_target="tpu_custom_call" | custom-call | flops 1409286144 | bytes 8388608 | tf_op jit(solution)/shard_map/pallas_call | solution.py:91
  151.3 2.1 %collective-permute-start.15 = (f32[384,896]{1,0:T(8,128)}, f32[384,896]{1,0:T(8,128)S(1)}, u32[]{:S(2)}, u32[]{:S(2)}) collective-permute-start(f32[384,896]{1,0:T(8,128)} %shard_map.40), channel_id=1, source_target_pairs={{0,24},{1,9},{2,26},{3,11},{4,28},{5,13},{6,30},{7,15},{32,56},{33... | collective-permute-start | bytes 4128776 | tf_op jit(solution)/shard_map/ppermute | solution.py:33
  153.3 8.5 %shard_map.41 = (f32[384,896]{1,0:T(8,128)}, f32[384,896]{1,0:T(8,128)}) custom-call(s32[7]{0:T(128)} %copy-done.4, bf16[2,8,4,192,256]{4,3,2,1,0:T(8,128)(2,1)} %bitcast.17, bf16[2,256,896]{2,1,0:T(8,128)(2,1)} %copy-done.7, bf16[2,256,896]{2,1,0:T(8,128)(2,1)} %copy-done.9, bf16[2,256,896]{2,1,0:T(8,128)(2,1)} %copy-done.10, ...), custom_call_target="tpu_custom_call" | custom-call | flops 2818572288 | bytes 16777216 | tf_op jit(solution)/shard_map/pallas_call | solution.py:91
  161.9 6.8 %shard_map.42.kept = f32[384,896]{1,0:T(8,128)} custom-call(s32[7]{0:T(128)} %copy-done.4, bf16[2,8,4,192,256]{4,3,2,1,0:T(8,128)(2,1)} %bitcast.12.panel, bf16[2,256,896]{2,1,0:T(8,128)(2,1)} %copy-done.7, bf16[2,256,896]{2,1,0:T(8,128)(2,1)} %copy-done.9, bf16[2,256,896]{2,1,0:T(8,128)(2,1)} %copy-done.10, bf16[2,256,896]{2,1,0:T(8,128)(2,1)} %copy-done.8, ...), custom_call_target="tpu_custom_call" | custom-call | flops 1409286144 | bytes 8388608 | tf_op jit(solution)/shard_map/pallas_call | solution.py:91
  168.7 1.3 copy-done.1
  170.0 0.8 shard_map.43
  170.8 4.7 %collective-permute-start.17 = (bf16[192,448]{1,0:T(8,128)(2,1)S(1)}, bf16[192,448]{1,0:T(8,128)(2,1)S(1)}, u32[]{:S(2)}, u32[]{:S(2)}) collective-permute-start(bf16[192,448]{1,0:T(8,128)(2,1)S(1)} %get-tuple-element.47), channel_id=1, source_target_pairs={{0,40},{1,57},{2,42},{3,59},{4,44},{5,61},{6,46},{7,63},{32,8},{33... | collective-permute-start | bytes 516104 | tf_op jit(solution)/shard_map/ppermute | solution.py:33
  175.6 6.8 %shard_map.44.kept = f32[384,896]{1,0:T(8,128)} custom-call(s32[7]{0:T(128)} %copy-done.4, bf16[2,8,4,192,256]{4,3,2,1,0:T(8,128)(2,1)} %bitcast.12.panel, bf16[2,256,896]{2,1,0:T(8,128)(2,1)} %copy-done.7, bf16[2,256,896]{2,1,0:T(8,128)(2,1)} %copy-done.9, bf16[2,256,896]{2,1,0:T(8,128)(2,1)} %copy-done.10, bf16[2,256,896]{2,1,0:T(8,128)(2,1)} %copy-done.8, ...), custom_call_target="tpu_custom_call" | custom-call | flops 1409286144 | bytes 8388608 | tf_op jit(solution)/shard_map/pallas_call | solution.py:91
  182.4 1.0 collective-permute-done.16.refs_2_
  183.4 1.3 copy-done
  184.7 0.8 shard_map.45
  185.5 3.1 %collective-permute-start.18 = (bf16[192,448]{1,0:T(8,128)(2,1)S(1)}, bf16[192,448]{1,0:T(8,128)(2,1)S(1)}, u32[]{:S(2)}, u32[]{:S(2)}) collective-permute-start(bf16[192,448]{1,0:T(8,128)(2,1)S(1)} %get-tuple-element.50), channel_id=1, source_target_pairs={{0,32},{1,33},{2,34},{3,35},{4,36},{5,37},{6,38},{7,39},{32,0},{33... | collective-permute-start | bytes 516104 | tf_op jit(solution)/shard_map/ppermute | solution.py:33
  188.6 6.5 %collective-permute-done.18.refs_1_ = bf16[192,448]{1,0:T(8,128)(2,1)S(1)} collective-permute-done((bf16[192,448]{1,0:T(8,128)(2,1)S(1)}, bf16[192,448]{1,0:T(8,128)(2,1)S(1)}, u32[]{:S(2)}, u32[]{:S(2)}) %collective-permute-start.18) | collective-permute-done | bytes 172064 | tf_op jit(solution)/shard_map/ppermute | solution.py:33
  195.2 1.5 shard_map.46
  (36 shorter events, 0.1 us)
Async XLA Ops:
  6.5 50.0 %all-gather.3.cloned.1.call-start = ((), (), s32[]{:S(2)}) async-start(), calls=%async_computation | async-start | bytes 6684672 | tf_op jit(solution)/shard_map/all_gather | solution.py:212
  7.4 1.2 copy-start.2
  8.6 1.2 copy-start.3
  9.8 9.6 %copy-start.4 = (s32[7]{0:T(128)}, s32[7]{0:T(128)S(1)}, u32[]{:S(2)}) copy-start(s32[7]{0:T(128)S(1)} %stack.54.place) | copy-start | bytes 88
  10.7 8.6 %collective-permute-start.1 = (bf16[256,896]{1,0:T(8,128)(2,1)S(1)}, bf16[256,896]{1,0:T(8,128)(2,1)S(1)}, u32[]{:S(2)}, u32[]{:S(2)}) collective-permute-start(bf16[256,896]{1,0:T(8,128)(2,1)S(1)} %get-tuple-element.31), channel_id=1, source_target_pairs={{0,8},{1,25},{2,10},{3,27},{4,12},{5,29},{6,14},{7,31},{32,40},{33... | collective-permute-start | bytes 1376264 | tf_op jit(solution)/shard_map/ppermute | solution.py:33
  19.4 99.9 %copy-start.7 = (bf16[2,256,896]{2,1,0:T(8,128)(2,1)}, bf16[2,256,896]{2,1,0:T(8,128)(2,1)S(1)}, u32[]{:S(2)}) copy-start(bf16[2,256,896]{2,1,0:T(8,128)(2,1)S(1)} %pad_maximum_fusion.refs_0_) | copy-start | bytes 2752516
  19.4 22.6 %collective-permute-start.3 = (bf16[2,256,896]{2,1,0:T(8,128)(2,1)S(1)}, bf16[2,256,896]{2,1,0:T(8,128)(2,1)S(1)}, u32[]{:S(2)}, u32[]{:S(2)}) collective-permute-start(bf16[2,256,896]{2,1,0:T(8,128)(2,1)S(1)} %pad_maximum_fusion.refs_0_), channel_id=1, source_target_pairs={{0,64},{1,65},{2,66},{3,67},{4,68},{5,69},{6,70},{7,71},{32,96},{3... | collective-permute-start | bytes 2752520 | tf_op jit(solution)/shard_map/ppermute | solution.py:33
  21.0 21.0 %collective-permute-start.2 = (bf16[2,256,896]{2,1,0:T(8,128)(2,1)S(1)}, bf16[2,256,896]{2,1,0:T(8,128)(2,1)S(1)}, u32[]{:S(2)}, u32[]{:S(2)}) collective-permute-start(bf16[2,256,896]{2,1,0:T(8,128)(2,1)S(1)} %pad_maximum_fusion.refs_0_), channel_id=1, source_target_pairs={{0,192},{1,193},{2,194},{3,195},{4,196},{5,197},{6,198},{7,199},{3... | collective-permute-start | bytes 2752520 | tf_op jit(solution)/shard_map/ppermute | solution.py:33
  22.7 8.5 %collective-permute-start = (bf16[256,896]{1,0:T(8,128)(2,1)S(1)}, bf16[256,896]{1,0:T(8,128)(2,1)S(1)}, u32[]{:S(2)}, u32[]{:S(2)}) collective-permute-start(bf16[256,896]{1,0:T(8,128)(2,1)S(1)} %get-tuple-element.29), channel_id=1, source_target_pairs={{0,8},{1,25},{2,10},{3,27},{4,12},{5,29},{6,14},{7,31},{32,40},{33... | collective-permute-start | bytes 1376264 | tf_op jit(solution)/shard_map/ppermute | solution.py:33
  31.2 10.8 %copy-start.14 = (bf16[256,896]{1,0:T(8,128)(2,1)}, bf16[256,896]{1,0:T(8,128)(2,1)S(1)}, u32[]{:S(2)}) copy-start(bf16[256,896]{1,0:T(8,128)(2,1)S(1)} %collective-permute-done) | copy-start | bytes 1376260
  42.0 77.3 %copy-start.8 = (bf16[2,256,896]{2,1,0:T(8,128)(2,1)}, bf16[2,256,896]{2,1,0:T(8,128)(2,1)S(1)}, u32[]{:S(2)}) copy-start(bf16[2,256,896]{2,1,0:T(8,128)(2,1)S(1)} %collective-permute-done.3.refs_3_) | copy-start | bytes 2752516
  42.0 77.3 %copy-start.9 = (bf16[2,256,896]{2,1,0:T(8,128)(2,1)}, bf16[2,256,896]{2,1,0:T(8,128)(2,1)S(1)}, u32[]{:S(2)}) copy-start(bf16[2,256,896]{2,1,0:T(8,128)(2,1)S(1)} %collective-permute-done.2.refs_1_) | copy-start | bytes 2752516
  56.5 81.1 %collective-permute-start.4 = (bf16[16,768,256]{2,1,0:T(8,128)(2,1)}, bf16[16,768,256]{2,1,0:T(8,128)(2,1)}, u32[]{:S(2)}, u32[]{:S(2)}) collective-permute-start(bf16[16,768,256]{2,1,0:T(8,128)(2,1)} %bitcast.15), channel_id=1, source_target_pairs={{0,8},{1,25},{2,10},{3,27},{4,12},{5,29},{6,14},{7,31},{32,40},{33... | collective-permute-start | bytes 18874376 | tf_op jit(solution)/shard_map/ppermute | solution.py:33
  57.1 30.1 %collective-permute-start.5 = (bf16[2,256,896]{2,1,0:T(8,128)(2,1)S(1)}, bf16[2,256,896]{2,1,0:T(8,128)(2,1)S(1)}, u32[]{:S(2)}, u32[]{:S(2)}) collective-permute-start(bf16[2,256,896]{2,1,0:T(8,128)(2,1)S(1)} %pad_maximum_fusion.refs_0_), channel_id=1, source_target_pairs={{0,128},{1,129},{2,130},{3,131},{4,132},{5,133},{6,134},{7,135},{3... | collective-permute-start | bytes 2752520 | tf_op jit(solution)/shard_map/ppermute | solution.py:33
  60.1 27.1 %collective-permute-start.6 = (bf16[256,896]{1,0:T(8,128)(2,1)S(1)}, bf16[256,896]{1,0:T(8,128)(2,1)}, u32[]{:S(2)}, u32[]{:S(2)}) collective-permute-start(bf16[256,896]{1,0:T(8,128)(2,1)S(1)} %get-tuple-element.36), channel_id=1, source_target_pairs={{0,32},{1,33},{2,34},{3,35},{4,36},{5,37},{6,38},{7,39},{32,0},{33... | collective-permute-start | bytes 1376264 | tf_op jit(solution)/shard_map/ppermute | solution.py:33
  87.2 1.0 copy-start.10
  88.2 25.6 %collective-permute-start.7 = (bf16[256,896]{1,0:T(8,128)(2,1)}, bf16[256,896]{1,0:T(8,128)(2,1)S(1)}, u32[]{:S(2)}, u32[]{:S(2)}) collective-permute-start(bf16[256,896]{1,0:T(8,128)(2,1)} %copy-done.14), channel_id=1, source_target_pairs={{0,32},{1,33},{2,34},{3,35},{4,36},{5,37},{6,38},{7,39},{32,0},{33... | collective-permute-start | bytes 1376264 | tf_op jit(solution)/shard_map/ppermute | solution.py:33
  90.3 24.0 %collective-permute-start.13 = (bf16[256,896]{1,0:T(8,128)(2,1)}, bf16[256,896]{1,0:T(8,128)(2,1)S(1)}, u32[]{:S(2)}, u32[]{:S(2)}) collective-permute-start(bf16[256,896]{1,0:T(8,128)(2,1)} %collective-permute-done.6.refs_4_), channel_id=1, source_target_pairs={{0,64},{1,65},{2,66},{3,67},{4,68},{5,69},{6,70},{7,71},{32,96},{3... | collective-permute-start | bytes 1376264 | tf_op jit(solution)/shard_map/ppermute | solution.py:33
  90.9 25.5 %collective-permute-start.12 = (bf16[256,896]{1,0:T(8,128)(2,1)}, bf16[256,896]{1,0:T(8,128)(2,1)S(1)}, u32[]{:S(2)}, u32[]{:S(2)}) collective-permute-start(bf16[256,896]{1,0:T(8,128)(2,1)} %collective-permute-done.6.refs_4_), channel_id=1, source_target_pairs={{0,128},{1,129},{2,130},{3,131},{4,132},{5,133},{6,134},{7,135},{3... | collective-permute-start | bytes 1376264 | tf_op jit(solution)/shard_map/ppermute | solution.py:33
  92.9 26.3 %collective-permute-start.11 = (bf16[256,896]{1,0:T(8,128)(2,1)}, bf16[256,896]{1,0:T(8,128)(2,1)}, u32[]{:S(2)}, u32[]{:S(2)}) collective-permute-start(bf16[256,896]{1,0:T(8,128)(2,1)} %collective-permute-done.6.refs_4_), channel_id=1, source_target_pairs={{0,192},{1,193},{2,194},{3,195},{4,196},{5,197},{6,198},{7,199},{3... | collective-permute-start | bytes 1376264 | tf_op jit(solution)/shard_map/ppermute | solution.py:33
  113.8 14.0 %copy-start.11 = (bf16[256,896]{1,0:T(8,128)(2,1)}, bf16[256,896]{1,0:T(8,128)(2,1)S(1)}, u32[]{:S(2)}) copy-start(bf16[256,896]{1,0:T(8,128)(2,1)S(1)} %collective-permute-done.7.refs_4_) | copy-start | bytes 1376260
  113.8 23.2 %collective-permute-start.10 = (bf16[256,896]{1,0:T(8,128)(2,1)S(1)}, bf16[256,896]{1,0:T(8,128)(2,1)}, u32[]{:S(2)}, u32[]{:S(2)}) collective-permute-start(bf16[256,896]{1,0:T(8,128)(2,1)S(1)} %collective-permute-done.7.refs_4_), channel_id=1, source_target_pairs={{0,64},{1,65},{2,66},{3,67},{4,68},{5,69},{6,70},{7,71},{32,96},{3... | collective-permute-start | bytes 1376264 | tf_op jit(solution)/shard_map/ppermute | solution.py:33
  114.4 2.0 %copy-start.12 = (bf16[256,896]{1,0:T(8,128)(2,1)}, bf16[256,896]{1,0:T(8,128)(2,1)S(1)}, u32[]{:S(2)}) copy-start(bf16[256,896]{1,0:T(8,128)(2,1)S(1)} %collective-permute-done.13.refs_7_) | copy-start | bytes 1376260
  114.4 22.6 %collective-permute-start.9 = (bf16[256,896]{1,0:T(8,128)(2,1)S(1)}, bf16[256,896]{1,0:T(8,128)(2,1)}, u32[]{:S(2)}, u32[]{:S(2)}) collective-permute-start(bf16[256,896]{1,0:T(8,128)(2,1)S(1)} %collective-permute-done.7.refs_4_), channel_id=1, source_target_pairs={{0,128},{1,129},{2,130},{3,131},{4,132},{5,133},{6,134},{7,135},{3... | collective-permute-start | bytes 1376264 | tf_op jit(solution)/shard_map/ppermute | solution.py:33
  116.4 0.8 copy-start.13
  117.3 20.3 %collective-permute-start.8 = (bf16[256,896]{1,0:T(8,128)(2,1)S(1)}, bf16[256,896]{1,0:T(8,128)(2,1)}, u32[]{:S(2)}, u32[]{:S(2)}) collective-permute-start(bf16[256,896]{1,0:T(8,128)(2,1)S(1)} %collective-permute-done.7.refs_4_), channel_id=1, source_target_pairs={{0,192},{1,193},{2,194},{3,195},{4,196},{5,197},{6,198},{7,199},{3... | collective-permute-start | bytes 1376264 | tf_op jit(solution)/shard_map/ppermute | solution.py:33
  144.4 24.3 %collective-permute-start.14 = (f32[384,896]{1,0:T(8,128)}, f32[384,896]{1,0:T(8,128)S(1)}, u32[]{:S(2)}, u32[]{:S(2)}) collective-permute-start(f32[384,896]{1,0:T(8,128)} %shard_map.39), channel_id=1, source_target_pairs={{0,24},{1,9},{2,26},{3,11},{4,28},{5,13},{6,30},{7,15},{32,56},{33... | collective-permute-start | bytes 4128776 | tf_op jit(solution)/shard_map/ppermute | solution.py:33
  151.3 31.1 %collective-permute-start.15 = (f32[384,896]{1,0:T(8,128)}, f32[384,896]{1,0:T(8,128)S(1)}, u32[]{:S(2)}, u32[]{:S(2)}) collective-permute-start(f32[384,896]{1,0:T(8,128)} %shard_map.40), channel_id=1, source_target_pairs={{0,24},{1,9},{2,26},{3,11},{4,28},{5,13},{6,30},{7,15},{32,56},{33... | collective-permute-start | bytes 4128776 | tf_op jit(solution)/shard_map/ppermute | solution.py:33
  161.9 6.8 %copy-start.5 = (s32[7]{0:T(128)S(1)}, s32[7]{0:T(128)}, u32[]{:S(2)}) copy-start(s32[7]{0:T(128)} %copy-done.4) | copy-start | bytes 88
  168.7 1.3 copy-start.1
  170.8 11.6 %collective-permute-start.17 = (bf16[192,448]{1,0:T(8,128)(2,1)S(1)}, bf16[192,448]{1,0:T(8,128)(2,1)S(1)}, u32[]{:S(2)}, u32[]{:S(2)}) collective-permute-start(bf16[192,448]{1,0:T(8,128)(2,1)S(1)} %get-tuple-element.47), channel_id=1, source_target_pairs={{0,40},{1,57},{2,42},{3,59},{4,44},{5,61},{6,46},{7,63},{32,8},{33... | collective-permute-start | bytes 516104 | tf_op jit(solution)/shard_map/ppermute | solution.py:33
  175.6 7.8 %collective-permute-start.16 = (bf16[192,448]{1,0:T(8,128)(2,1)S(1)}, bf16[192,448]{1,0:T(8,128)(2,1)S(1)}, u32[]{:S(2)}, u32[]{:S(2)}) collective-permute-start(bf16[192,448]{1,0:T(8,128)(2,1)S(1)} %get-tuple-element.44), channel_id=1, source_target_pairs={{0,8},{1,25},{2,10},{3,27},{4,12},{5,29},{6,14},{7,31},{32,40},{33... | collective-permute-start | bytes 516104 | tf_op jit(solution)/shard_map/ppermute | solution.py:33
  175.6 7.8 %copy-start.6 = (s32[7]{0:T(128)S(1)}, s32[7]{0:T(128)}, u32[]{:S(2)}) copy-start(s32[7]{0:T(128)} %copy-done.4) | copy-start | bytes 88
  183.4 1.3 copy-start
  185.5 9.7 %collective-permute-start.18 = (bf16[192,448]{1,0:T(8,128)(2,1)S(1)}, bf16[192,448]{1,0:T(8,128)(2,1)S(1)}, u32[]{:S(2)}, u32[]{:S(2)}) collective-permute-start(bf16[192,448]{1,0:T(8,128)(2,1)S(1)} %get-tuple-element.50), channel_id=1, source_target_pairs={{0,32},{1,33},{2,34},{3,35},{4,36},{5,37},{6,38},{7,39},{32,0},{33... | collective-permute-start | bytes 516104 | tf_op jit(solution)/shard_map/ppermute | solution.py:33
Sparse Core Ops, SparseCore 0:
  9.2 47.2 all-gather.2

commit v8 on v7

--- a/solution.py
+++ b/solution.py
@@ -53,13 +53,17 @@
     return x - side(x, c), y, z, c
 
 
-def product_kernel(u, slots, place, panel, *refs):
+def product_kernel(u, halves, place, panel, *refs):
     near, far, refs = refs[:4], refs[4:8], refs[8:]
-    before, refs = refs[: u * len(slots)], refs[u * len(slots) :]
-    outs, (pieces, lhs, rhs, lhs_sem, rhs_sem) = refs[: len(slots)], refs[len(slots) :]
+    n = len(halves)
+    before, outs, (pieces, lhs, rhs, lhs_sem, rhs_sem) = refs[: u * n], refs[u * n : u * n + n], refs[u * n + n :]
     y, zh = place[0], place[1]
     rows, wide = pieces.shape[3], rhs.shape[1]
-    tokens = [pltpu.make_async_copy(panel.at[:, :, place[slot]], pieces.at[i], lhs_sem.at[i]) for i, slot in enumerate(slots)]
+    tokens = []
+    for i, half in enumerate(halves):
+        for j in range(2):
+            source = panel.at[lax.rem(zh + half, 2), :, place[4 + j]]
+            tokens.append(pltpu.make_async_copy(source, pieces.at[i, j], lhs_sem.at[2 * i + j]))
     weights = []
     for d in range(4):
         k = lax.rem(y + d, 4) * 2
@@ -68,12 +72,12 @@
             weights.append(pltpu.make_async_copy(source, target, rhs_sem.at[len(weights)]))
     for copy in (*tokens, *weights):
         copy.start()
-    for i in range(len(slots)):
-        tokens[i].wait()
-        for b in range(2):
-            at = (i * 2 + b) * rows
+    for i in range(n):
+        for j in range(2):
+            tokens[2 * i + j].wait()
+            at = (i * 2 + j) * rows
             for k in range(8):
-                lhs[at : at + rows, k * 256 : (k + 1) * 256] = pieces[i, b, k]
+                lhs[at : at + rows, k * 256 : (k + 1) * 256] = pieces[i, j, k]
     for copy in weights:
         copy.wait()
     for lo in range(0, wide, 256):
@@ -84,12 +88,12 @@
             out[:, lo:hi] = before[i][:, lo:hi] + mine if u else mine
 
 
-def product(u, slots, place, panel, near, far, before=()):
-    rows, depth, wide, n = panel.shape[3], 2048, far[u][0].shape[1], len(slots)
+def product(u, halves, place, panel, near, far, before=()):
+    rows, depth, wide, n = panel.shape[3], 2048, far[u][0].shape[1], len(halves)
     hbm, vmem = pl.BlockSpec(memory_space=pltpu.HBM), pl.BlockSpec(memory_space=pltpu.VMEM)
     operands = [panel, *near, *far[u]]
     return pl.pallas_call(
-        functools.partial(product_kernel, u, slots),
+        functools.partial(product_kernel, u, halves),
         out_shape=[jax.ShapeDtypeStruct((2 * rows, wide), jnp.float32)] * n,
         in_specs=[pl.BlockSpec(memory_space=pltpu.SMEM)] + [hbm] * len(operands) + [vmem] * len(before),
         out_specs=[vmem] * n,
@@ -97,7 +101,7 @@
             pltpu.VMEM((n, 2, 8, rows, 256), jnp.bfloat16),
             pltpu.VMEM((2 * n * rows, depth), jnp.bfloat16),
             pltpu.VMEM((depth, wide), jnp.bfloat16),
-            pltpu.SemaphoreType.DMA((n,)),
+            pltpu.SemaphoreType.DMA((2 * n,)),
             pltpu.SemaphoreType.DMA((8,)),
         ],
         compiler_params=pltpu.CompilerParams(vmem_limit_bytes=60 << 20),
@@ -134,11 +138,10 @@
     )(place, gate, up)
 
 
-def gated_kernel(place, kept, received, *outs):
-    zh = place[1]
+def gated_kernel(kept, received, *outs):
     rows, whole = outs[0].shape[0], kept.shape[1] // (2 * TILE)
     for n, out in enumerate(outs):
-        at = pl.ds(pl.multiple_of(lax.rem(zh + n, 2) * rows, rows), rows)
+        at = slice(n * rows, (n + 1) * rows)
         total = kept[at, :] + received[at, :]
         for t in range(whole):
             gate, up = total[:, 2 * t * TILE : (2 * t + 1) * TILE], total[:, (2 * t + 1) * TILE : (2 * t + 2) * TILE]
@@ -148,17 +151,17 @@
         out[:, whole * TILE :] = (jax.nn.silu(last) * up).astype(jnp.bfloat16)[:, : TILE // 2]
 
 
-def gated(place, kept, received):
+def gated(kept, received):
     rows, wide = kept.shape
     vmem = pl.BlockSpec(memory_space=pltpu.VMEM)
     return pl.pallas_call(
         gated_kernel,
         out_shape=[jax.ShapeDtypeStruct((rows // 2, wide // 2), jnp.bfloat16)] * 2,
-        in_specs=[pl.BlockSpec(memory_space=pltpu.SMEM), vmem, vmem],
+        in_specs=[vmem, vmem],
         out_specs=[vmem] * 2,
         compiler_params=pltpu.CompilerParams(vmem_limit_bytes=16 << 20),
         cost_estimate=pl.CostEstimate(flops=8 * rows * wide, bytes_accessed=4 << 20, transcendentals=rows * wide // 2),
-    )(place, kept, received)
+    )(kept, received)
 
 
 def gather_kernel(place, *refs):
@@ -223,19 +226,18 @@
     far.append(move(after(got_away, far[0], near[2]), to_antipode))
     far = [[f] + [along_y(f, d) for d in range(1, 4)] for f in far]
 
-    sent = product(0, (4, 5), send_place, own, near, far)
-    kept = product(0, (4, 5), after(keep_place, *sent), own, near, far)
-    sums, turn = [None, None], send_place
-    for i in (1, 0):
-        total = product(1, (4 + i,), turn, shared, near, far, sent[i : i + 1])[0]
-        turn, sums[i] = after(send_place, total), move(total, to_summer)
-    turn = after(keep_place, total)
-    total = product(1, (5,), turn, shared, near, far, kept[1:])[0]
-    over_x, over_both = gated(keep_place, total, sums[1])
-    total = product(1, (4,), after(keep_place, over_x), shared, near, far, kept[:1])[0]
-    over_x, over_both = move(over_x, to_partner), move(over_both, to_both)
-    mine, over_z = gated(keep_place, total, after(sums[0], over_x, over_both))
-    blocks = [mine, move(over_z, to_antipode), over_x, over_both]
+    sent = product(0, (0, 1), send_place, own, near, far)
+    kept = product(0, (0, 1), after(keep_place, *sent), own, near, far)
+    sums, turn = [None, None], after(send_place, kept[0])
+    for half in (1, 0):
+        total = product(1, (half,), turn, shared, near, far, sent[half : half + 1])[0]
+        turn, sums[half] = after(send_place, total), move(total, to_summer)
+    total = product(1, (1,), after(keep_place, total), shared, near, far, kept[1:])[0]
+    over_z, over_both = gated(total, sums[1])
+    total = product(1, (0,), after(keep_place, over_z), shared, near, far, kept[:1])[0]
+    over_z, over_both = move(over_z, to_antipode), move(over_both, to_both)
+    mine, over_x = gated(total, after(sums[0], over_z, over_both))
+    blocks = [mine, over_z, move(over_x, to_partner), over_both]
     return gather(keep_place, blocks)
 
 

time: 207 us -> 202 us (0.976); the launches traced: 204 us -> 201 us
    ppermute x19, waiting for transfers between devices: 89.1 us -> 92.4 us  [move(): return lax.ppermute(value, AXES, pairs)]
    all_gather x1, waiting for transfers between devices: 14.5 us -> 11.9 us  [per_device(): panel = lax.all_gather(tokens, ('zh', 'zl', 'c'), axis=0)]
    unnamed x30 -> x26, local copies, waits for them, and re-layouts: 6.87 us -> 6.02 us
  transfers between devices with their start and end apart: 20 -> 20, of which waited for: 10 -> 11; matrix products, arithmetic and copies ran while one was open for 0% -> 0% of each run, Pallas kernels for 19% -> 19%
where the time goes in v8:
time: 202 us; the launch traced here: 201 us
  waiting for transfers between devices  105 us (52%)
  Pallas kernels  47.4 us (23%)
  starting transfers between devices  28.4 us (14%)
  between operations  13.7 us (7%)
  local copies, waits for them, and re-layouts  6.69 us (3%)
    ppermute x19, waiting for transfers between devices, move(): return lax.ppermute(value, AXES, pairs)  92.4 us
    pallas_call x6, Pallas kernels, product(): pl.pallas_call(functools.partial(product_kernel, u, halves), out_shape=[j...  44.4 us
    ppermute x19, starting transfers between devices, move(): return lax.ppermute(value, AXES, pairs)  28.4 us
    all_gather x1, waiting for transfers between devices, per_device(): panel = lax.all_gather(tokens, ('zh', 'zl', 'c'), axis=0)  11.9 us
    unnamed x26, local copies, waits for them, and re-layouts  6.02 us
  transfers between devices with their start and end apart: 20, of which 11 were waited for; matrix products, arithmetic and copies ran while one was open for 0% of the time, Pallas kernels for 19%

profile of v8, /device:TPU:98, one launch (start us, length us, event | category | flops | bytes accessed | tf_op | source)
XLA Modules:
  0.0 201.3 jit_solution(11469228543370136002)
XLA Ops:
  6.5 0.7 all-gather.3.cloned.1.call-update
  7.3 0.1 stack.54.place
  7.4 1.2 copy-done.2
  8.6 1.2 copy-done.3
  9.8 0.9 shard_map.37
  10.7 0.6 collective-permute-start.1
  11.3 7.9 %collective-permute-done.1 = bf16[256,896]{1,0:T(8,128)(2,1)S(1)} collective-permute-done((bf16[256,896]{1,0:T(8,128)(2,1)S(1)}, bf16[256,896]{1,0:T(8,128)(2,1)S(1)}, u32[]{:S(2)}, u32[]{:S(2)}) %collective-permute-start.1) | collective-permute-done | bytes 458784 | tf_op jit(solution)/shard_map/ppermute | solution.py:33
  19.3 0.1 pad_maximum_fusion.refs_0_
  19.4 3.1 %collective-permute-start.2 = (bf16[2,256,896]{2,1,0:T(8,128)(2,1)S(1)}, bf16[2,256,896]{2,1,0:T(8,128)(2,1)S(1)}, u32[]{:S(2)}, u32[]{:S(2)}) collective-permute-start(bf16[2,256,896]{2,1,0:T(8,128)(2,1)S(1)} %pad_maximum_fusion.refs_0_), channel_id=1, source_target_pairs={{0,192},{1,193},{2,194},{3,195},{4,196},{5,197},{6,198},{7,199},{3... | collective-permute-start | bytes 2752520 | tf_op jit(solution)/shard_map/ppermute | solution.py:33
  22.5 0.0 collective-permute-start.3
  22.5 0.5 collective-permute-start
  23.0 7.9 %collective-permute-done = bf16[256,896]{1,0:T(8,128)(2,1)S(1)} collective-permute-done((bf16[256,896]{1,0:T(8,128)(2,1)S(1)}, bf16[256,896]{1,0:T(8,128)(2,1)S(1)}, u32[]{:S(2)}, u32[]{:S(2)}) %collective-permute-start) | collective-permute-done | bytes 458784 | tf_op jit(solution)/shard_map/ppermute | solution.py:33
  31.0 10.3 %collective-permute-done.2.refs_1_ = bf16[2,256,896]{2,1,0:T(8,128)(2,1)S(1)} collective-permute-done((bf16[2,256,896]{2,1,0:T(8,128)(2,1)S(1)}, bf16[2,256,896]{2,1,0:T(8,128)(2,1)S(1)}, u32[]{:S(2)}, u32[]{:S(2)}) %collective-permute-start.2) | collective-permute-done | bytes 917536 | tf_op jit(solution)/shard_map/ppermute | solution.py:33
  41.2 3.4 %collective-permute-done.3.refs_3_ = bf16[2,256,896]{2,1,0:T(8,128)(2,1)S(1)} collective-permute-done((bf16[2,256,896]{2,1,0:T(8,128)(2,1)S(1)}, bf16[2,256,896]{2,1,0:T(8,128)(2,1)S(1)}, u32[]{:S(2)}, u32[]{:S(2)}) %collective-permute-start.3) | collective-permute-done | bytes 917536 | tf_op jit(solution)/shard_map/ppermute | solution.py:33
  44.6 11.9 %all-gather.3.cloned.1.call-done = bf16[12288,256]{1,0:T(8,128)(2,1)} async-done(((bf16[768,256]{1,0:T(8,128)(2,1)}), bf16[12288,256]{1,0:T(8,128)(2,1)}) %all-gather.3.cloned.1.call-update) | async-done | bytes 6291472 | tf_op jit(solution)/shard_map/all_gather | solution.py:215
  56.5 0.6 collective-permute-start.9
  57.1 3.0 %collective-permute-start.4 = (bf16[2,256,896]{2,1,0:T(8,128)(2,1)S(1)}, bf16[2,256,896]{2,1,0:T(8,128)(2,1)S(1)}, u32[]{:S(2)}, u32[]{:S(2)}) collective-permute-start(bf16[2,256,896]{2,1,0:T(8,128)(2,1)S(1)} %pad_maximum_fusion.refs_0_), channel_id=1, source_target_pairs={{0,128},{1,129},{2,130},{3,131},{4,132},{5,133},{6,134},{7,135},{3... | collective-permute-start | bytes 2752520 | tf_op jit(solution)/shard_map/ppermute | solution.py:33
  60.1 2.2 %collective-permute-start.5 = (bf16[256,896]{1,0:T(8,128)(2,1)S(1)}, bf16[256,896]{1,0:T(8,128)(2,1)}, u32[]{:S(2)}, u32[]{:S(2)}) collective-permute-start(bf16[256,896]{1,0:T(8,128)(2,1)S(1)} %get-tuple-element.36), channel_id=1, source_target_pairs={{0,32},{1,33},{2,34},{3,35},{4,36},{5,37},{6,38},{7,39},{32,0},{33... | collective-permute-start | bytes 1376264 | tf_op jit(solution)/shard_map/ppermute | solution.py:33
  62.3 24.9 %collective-permute-done.5.refs_4_ = bf16[256,896]{1,0:T(8,128)(2,1)} collective-permute-done((bf16[256,896]{1,0:T(8,128)(2,1)S(1)}, bf16[256,896]{1,0:T(8,128)(2,1)}, u32[]{:S(2)}, u32[]{:S(2)}) %collective-permute-start.5) | collective-permute-done | bytes 458784 | tf_op jit(solution)/shard_map/ppermute | solution.py:33
  87.2 0.9 copy-done.9
  88.1 2.2 %collective-permute-start.10 = (bf16[256,896]{1,0:T(8,128)(2,1)}, bf16[256,896]{1,0:T(8,128)(2,1)S(1)}, u32[]{:S(2)}, u32[]{:S(2)}) collective-permute-start(bf16[256,896]{1,0:T(8,128)(2,1)} %copy-done.12), channel_id=1, source_target_pairs={{0,32},{1,33},{2,34},{3,35},{4,36},{5,37},{6,38},{7,39},{32,0},{33... | collective-permute-start | bytes 1376264 | tf_op jit(solution)/shard_map/ppermute | solution.py:33
  90.3 1.1 collective-permute-start.6
  91.5 1.5 collective-permute-start.7
  93.0 0.6 stack.57.place
  93.6 20.2 %collective-permute-done.10.refs_4_ = bf16[256,896]{1,0:T(8,128)(2,1)S(1)} collective-permute-done((bf16[256,896]{1,0:T(8,128)(2,1)}, bf16[256,896]{1,0:T(8,128)(2,1)S(1)}, u32[]{:S(2)}, u32[]{:S(2)}) %collective-permute-start.10) | collective-permute-done | bytes 458784 | tf_op jit(solution)/shard_map/ppermute | solution.py:33
  113.8 1.1 collective-permute-start.11
  114.9 1.5 collective-permute-start.12
  116.4 0.0 collective-permute-start.13
  116.5 8.5 %shard_map.38 = (f32[384,896]{1,0:T(8,128)}, f32[384,896]{1,0:T(8,128)}) custom-call(s32[7]{0:T(128)} %stack.57.place, bf16[2,8,4,192,256]{4,3,2,1,0:T(8,128)(2,1)} %bitcast.16, bf16[2,256,896]{2,1,0:T(8,128)(2,1)} %copy-done.6, bf16[2,256,896]{2,1,0:T(8,128)(2,1)} %copy-done.7, bf16[2,256,896]{2,1,0:T(8,128)(2,1)} %copy-done.9, ...), custom_call_target="tpu_custom_call" | custom-call | flops 2818572288 | bytes 16777216 | tf_op jit(solution)/shard_map/pallas_call | solution.py:95
  125.0 8.5 %shard_map.39 = (f32[384,896]{1,0:T(8,128)}, f32[384,896]{1,0:T(8,128)}) custom-call(s32[7]{0:T(128)} %copy-done.4, bf16[2,8,4,192,256]{4,3,2,1,0:T(8,128)(2,1)} %bitcast.17, bf16[2,256,896]{2,1,0:T(8,128)(2,1)} %copy-done.6, bf16[2,256,896]{2,1,0:T(8,128)(2,1)} %copy-done.7, bf16[2,256,896]{2,1,0:T(8,128)(2,1)} %copy-done.9, ...), custom_call_target="tpu_custom_call" | custom-call | flops 2818572288 | bytes 16777216 | tf_op jit(solution)/shard_map/pallas_call | solution.py:95
  133.6 4.5 %collective-permute-done.13.refs_7_ = bf16[256,896]{1,0:T(8,128)(2,1)} collective-permute-done((bf16[256,896]{1,0:T(8,128)(2,1)S(1)}, bf16[256,896]{1,0:T(8,128)(2,1)}, u32[]{:S(2)}, u32[]{:S(2)}) %collective-permute-start.13) | collective-permute-done | bytes 458784 | tf_op jit(solution)/shard_map/ppermute | solution.py:33
  138.1 6.9 %shard_map.40 = f32[384,896]{1,0:T(8,128)} custom-call(s32[7]{0:T(128)} %stack.57.place, bf16[2,8,4,192,256]{4,3,2,1,0:T(8,128)(2,1)} %bitcast.13.panel, bf16[2,256,896]{2,1,0:T(8,128)(2,1)} %copy-done.6, bf16[2,256,896]{2,1,0:T(8,128)(2,1)} %copy-done.7, bf16[2,256,896]{2,1,0:T(8,128)(2,1)} %copy-done.9, bf16[2,256,896]{2,1,0:T(8,128)(2,1)} %copy-done.8, ...), custom_call_target="tpu_custom_call" | custom-call | flops 1409286144 | bytes 8388608 | tf_op jit(solution)/shard_map/pallas_call | solution.py:95
  145.0 0.1 collective-permute-start.14
  145.1 6.8 %shard_map.41 = f32[384,896]{1,0:T(8,128)} custom-call(s32[7]{0:T(128)} %stack.57.place, bf16[2,8,4,192,256]{4,3,2,1,0:T(8,128)(2,1)} %bitcast.13.panel, bf16[2,256,896]{2,1,0:T(8,128)(2,1)} %copy-done.6, bf16[2,256,896]{2,1,0:T(8,128)(2,1)} %copy-done.7, bf16[2,256,896]{2,1,0:T(8,128)(2,1)} %copy-done.9, bf16[2,256,896]{2,1,0:T(8,128)(2,1)} %copy-done.8, ...), custom_call_target="tpu_custom_call" | custom-call | flops 1409286144 | bytes 8388608 | tf_op jit(solution)/shard_map/pallas_call | solution.py:95
  151.9 2.1 %collective-permute-start.15 = (f32[384,896]{1,0:T(8,128)}, f32[384,896]{1,0:T(8,128)S(1)}, u32[]{:S(2)}, u32[]{:S(2)}) collective-permute-start(f32[384,896]{1,0:T(8,128)} %shard_map.41), channel_id=1, source_target_pairs={{0,24},{1,9},{2,26},{3,11},{4,28},{5,13},{6,30},{7,15},{32,56},{33... | collective-permute-start | bytes 4128776 | tf_op jit(solution)/shard_map/ppermute | solution.py:33
  154.0 6.8 %shard_map.42.kept = f32[384,896]{1,0:T(8,128)} custom-call(s32[7]{0:T(128)} %copy-done.4, bf16[2,8,4,192,256]{4,3,2,1,0:T(8,128)(2,1)} %bitcast.13.panel, bf16[2,256,896]{2,1,0:T(8,128)(2,1)} %copy-done.6, bf16[2,256,896]{2,1,0:T(8,128)(2,1)} %copy-done.7, bf16[2,256,896]{2,1,0:T(8,128)(2,1)} %copy-done.9, bf16[2,256,896]{2,1,0:T(8,128)(2,1)} %copy-done.8, ...), custom_call_target="tpu_custom_call" | custom-call | flops 1409286144 | bytes 8388608 | tf_op jit(solution)/shard_map/pallas_call | solution.py:95
  160.8 2.8 %collective-permute-done.14.received = f32[384,896]{1,0:T(8,128)S(1)} collective-permute-done((f32[384,896]{1,0:T(8,128)}, f32[384,896]{1,0:T(8,128)S(1)}, u32[]{:S(2)}, u32[]{:S(2)}) %collective-permute-start.14) | collective-permute-done | bytes 1376288 | tf_op jit(solution)/shard_map/ppermute | solution.py:33
  163.6 1.3 copy-done.1
  165.0 0.3 shard_map.43
  165.3 2.1 %collective-permute-start.16 = (bf16[192,448]{1,0:T(8,128)(2,1)S(1)}, bf16[192,448]{1,0:T(8,128)(2,1)S(1)}, u32[]{:S(2)}, u32[]{:S(2)}) collective-permute-start(bf16[192,448]{1,0:T(8,128)(2,1)S(1)} %get-tuple-element.47), channel_id=1, source_target_pairs={{0,32},{1,33},{2,34},{3,35},{4,36},{5,37},{6,38},{7,39},{32,0},{33... | collective-permute-start | bytes 516104 | tf_op jit(solution)/shard_map/ppermute | solution.py:33
  167.4 6.5 %collective-permute-start.17 = (bf16[192,448]{1,0:T(8,128)(2,1)S(1)}, bf16[192,448]{1,0:T(8,128)(2,1)S(1)}, u32[]{:S(2)}, u32[]{:S(2)}) collective-permute-start(bf16[192,448]{1,0:T(8,128)(2,1)S(1)} %get-tuple-element.49), channel_id=1, source_target_pairs={{0,40},{1,57},{2,42},{3,59},{4,44},{5,61},{6,46},{7,63},{32,8},{33... | collective-permute-start | bytes 516104 | tf_op jit(solution)/shard_map/ppermute | solution.py:33
  173.9 6.9 %shard_map.44.kept = f32[384,896]{1,0:T(8,128)} custom-call(s32[7]{0:T(128)} %copy-done.4, bf16[2,8,4,192,256]{4,3,2,1,0:T(8,128)(2,1)} %bitcast.13.panel, bf16[2,256,896]{2,1,0:T(8,128)(2,1)} %copy-done.6, bf16[2,256,896]{2,1,0:T(8,128)(2,1)} %copy-done.7, bf16[2,256,896]{2,1,0:T(8,128)(2,1)} %copy-done.9, bf16[2,256,896]{2,1,0:T(8,128)(2,1)} %copy-done.8, ...), custom_call_target="tpu_custom_call" | custom-call | flops 1409286144 | bytes 8388608 | tf_op jit(solution)/shard_map/pallas_call | solution.py:95
  180.8 4.7 %collective-permute-done.17.refs_3_ = bf16[192,448]{1,0:T(8,128)(2,1)S(1)} collective-permute-done((bf16[192,448]{1,0:T(8,128)(2,1)S(1)}, bf16[192,448]{1,0:T(8,128)(2,1)S(1)}, u32[]{:S(2)}, u32[]{:S(2)}) %collective-permute-start.17) | collective-permute-done | bytes 172064 | tf_op jit(solution)/shard_map/ppermute | solution.py:33
  185.6 1.3 copy-done
  186.9 0.2 shard_map.45
  187.2 0.1 collective-permute-start.18
  187.3 5.7 %collective-permute-done.18.refs_2_ = bf16[192,448]{1,0:T(8,128)(2,1)S(1)} collective-permute-done((bf16[192,448]{1,0:T(8,128)(2,1)S(1)}, bf16[192,448]{1,0:T(8,128)(2,1)S(1)}, u32[]{:S(2)}, u32[]{:S(2)}) %collective-permute-start.18) | collective-permute-done | bytes 172064 | tf_op jit(solution)/shard_map/ppermute | solution.py:33
  192.9 1.5 shard_map.46
  (32 shorter events, 0.1 us)
Async XLA Ops:
  6.5 50.0 %all-gather.3.cloned.1.call-start = ((), (), s32[]{:S(2)}) async-start(), calls=%async_computation | async-start | bytes 6684672 | tf_op jit(solution)/shard_map/all_gather | solution.py:215
  7.4 1.2 copy-start.2
  8.6 1.2 copy-start.3
  9.8 9.6 %copy-start.4 = (s32[7]{0:T(128)}, s32[7]{0:T(128)S(1)}, u32[]{:S(2)}) copy-start(s32[7]{0:T(128)S(1)} %stack.54.place) | copy-start | bytes 88
  10.7 8.6 %collective-permute-start.1 = (bf16[256,896]{1,0:T(8,128)(2,1)S(1)}, bf16[256,896]{1,0:T(8,128)(2,1)S(1)}, u32[]{:S(2)}, u32[]{:S(2)}) collective-permute-start(bf16[256,896]{1,0:T(8,128)(2,1)S(1)} %get-tuple-element.32), channel_id=1, source_target_pairs={{0,8},{1,25},{2,10},{3,27},{4,12},{5,29},{6,14},{7,31},{32,40},{33... | collective-permute-start | bytes 1376264 | tf_op jit(solution)/shard_map/ppermute | solution.py:33
  19.4 97.1 %copy-start.6 = (bf16[2,256,896]{2,1,0:T(8,128)(2,1)}, bf16[2,256,896]{2,1,0:T(8,128)(2,1)S(1)}, u32[]{:S(2)}) copy-start(bf16[2,256,896]{2,1,0:T(8,128)(2,1)S(1)} %pad_maximum_fusion.refs_0_) | copy-start | bytes 2752516
  19.4 21.8 %collective-permute-start.2 = (bf16[2,256,896]{2,1,0:T(8,128)(2,1)S(1)}, bf16[2,256,896]{2,1,0:T(8,128)(2,1)S(1)}, u32[]{:S(2)}, u32[]{:S(2)}) collective-permute-start(bf16[2,256,896]{2,1,0:T(8,128)(2,1)S(1)} %pad_maximum_fusion.refs_0_), channel_id=1, source_target_pairs={{0,192},{1,193},{2,194},{3,195},{4,196},{5,197},{6,198},{7,199},{3... | collective-permute-start | bytes 2752520 | tf_op jit(solution)/shard_map/ppermute | solution.py:33
  22.5 22.2 %collective-permute-start.3 = (bf16[2,256,896]{2,1,0:T(8,128)(2,1)S(1)}, bf16[2,256,896]{2,1,0:T(8,128)(2,1)S(1)}, u32[]{:S(2)}, u32[]{:S(2)}) collective-permute-start(bf16[2,256,896]{2,1,0:T(8,128)(2,1)S(1)} %pad_maximum_fusion.refs_0_), channel_id=1, source_target_pairs={{0,64},{1,65},{2,66},{3,67},{4,68},{5,69},{6,70},{7,71},{32,96},{3... | collective-permute-start | bytes 2752520 | tf_op jit(solution)/shard_map/ppermute | solution.py:33
  22.5 8.5 %collective-permute-start = (bf16[256,896]{1,0:T(8,128)(2,1)S(1)}, bf16[256,896]{1,0:T(8,128)(2,1)S(1)}, u32[]{:S(2)}, u32[]{:S(2)}) collective-permute-start(bf16[256,896]{1,0:T(8,128)(2,1)S(1)} %get-tuple-element.30), channel_id=1, source_target_pairs={{0,8},{1,25},{2,10},{3,27},{4,12},{5,29},{6,14},{7,31},{32,40},{33... | collective-permute-start | bytes 1376264 | tf_op jit(solution)/shard_map/ppermute | solution.py:33
  30.9 10.3 %copy-start.12 = (bf16[256,896]{1,0:T(8,128)(2,1)}, bf16[256,896]{1,0:T(8,128)(2,1)S(1)}, u32[]{:S(2)}) copy-start(bf16[256,896]{1,0:T(8,128)(2,1)S(1)} %collective-permute-done) | copy-start | bytes 1376260
  41.2 75.2 %copy-start.7 = (bf16[2,256,896]{2,1,0:T(8,128)(2,1)}, bf16[2,256,896]{2,1,0:T(8,128)(2,1)S(1)}, u32[]{:S(2)}) copy-start(bf16[2,256,896]{2,1,0:T(8,128)(2,1)S(1)} %collective-permute-done.2.refs_1_) | copy-start | bytes 2752516
  44.6 71.8 %copy-start.8 = (bf16[2,256,896]{2,1,0:T(8,128)(2,1)}, bf16[2,256,896]{2,1,0:T(8,128)(2,1)S(1)}, u32[]{:S(2)}) copy-start(bf16[2,256,896]{2,1,0:T(8,128)(2,1)S(1)} %collective-permute-done.3.refs_3_) | copy-start | bytes 2752516
  56.5 81.6 %collective-permute-start.9 = (bf16[16,768,256]{2,1,0:T(8,128)(2,1)}, bf16[16,768,256]{2,1,0:T(8,128)(2,1)}, u32[]{:S(2)}, u32[]{:S(2)}) collective-permute-start(bf16[16,768,256]{2,1,0:T(8,128)(2,1)} %bitcast.15), channel_id=1, source_target_pairs={{0,8},{1,25},{2,10},{3,27},{4,12},{5,29},{6,14},{7,31},{32,40},{33... | collective-permute-start | bytes 18874376 | tf_op jit(solution)/shard_map/ppermute | solution.py:33
  57.1 30.1 %collective-permute-start.4 = (bf16[2,256,896]{2,1,0:T(8,128)(2,1)S(1)}, bf16[2,256,896]{2,1,0:T(8,128)(2,1)S(1)}, u32[]{:S(2)}, u32[]{:S(2)}) collective-permute-start(bf16[2,256,896]{2,1,0:T(8,128)(2,1)S(1)} %pad_maximum_fusion.refs_0_), channel_id=1, source_target_pairs={{0,128},{1,129},{2,130},{3,131},{4,132},{5,133},{6,134},{7,135},{3... | collective-permute-start | bytes 2752520 | tf_op jit(solution)/shard_map/ppermute | solution.py:33
  60.1 27.1 %collective-permute-start.5 = (bf16[256,896]{1,0:T(8,128)(2,1)S(1)}, bf16[256,896]{1,0:T(8,128)(2,1)}, u32[]{:S(2)}, u32[]{:S(2)}) collective-permute-start(bf16[256,896]{1,0:T(8,128)(2,1)S(1)} %get-tuple-element.36), channel_id=1, source_target_pairs={{0,32},{1,33},{2,34},{3,35},{4,36},{5,37},{6,38},{7,39},{32,0},{33... | collective-permute-start | bytes 1376264 | tf_op jit(solution)/shard_map/ppermute | solution.py:33
  87.2 0.9 copy-start.9
  88.1 25.6 %collective-permute-start.10 = (bf16[256,896]{1,0:T(8,128)(2,1)}, bf16[256,896]{1,0:T(8,128)(2,1)S(1)}, u32[]{:S(2)}, u32[]{:S(2)}) collective-permute-start(bf16[256,896]{1,0:T(8,128)(2,1)} %copy-done.12), channel_id=1, source_target_pairs={{0,32},{1,33},{2,34},{3,35},{4,36},{5,37},{6,38},{7,39},{32,0},{33... | collective-permute-start | bytes 1376264 | tf_op jit(solution)/shard_map/ppermute | solution.py:33
  90.3 24.6 %collective-permute-start.6 = (bf16[256,896]{1,0:T(8,128)(2,1)}, bf16[256,896]{1,0:T(8,128)(2,1)}, u32[]{:S(2)}, u32[]{:S(2)}) collective-permute-start(bf16[256,896]{1,0:T(8,128)(2,1)} %collective-permute-done.5.refs_4_), channel_id=1, source_target_pairs={{0,192},{1,193},{2,194},{3,195},{4,196},{5,197},{6,198},{7,199},{3... | collective-permute-start | bytes 1376264 | tf_op jit(solution)/shard_map/ppermute | solution.py:33
  91.5 25.0 %collective-permute-start.7 = (bf16[256,896]{1,0:T(8,128)(2,1)}, bf16[256,896]{1,0:T(8,128)(2,1)}, u32[]{:S(2)}, u32[]{:S(2)}) collective-permute-start(bf16[256,896]{1,0:T(8,128)(2,1)} %collective-permute-done.5.refs_4_), channel_id=1, source_target_pairs={{0,128},{1,129},{2,130},{3,131},{4,132},{5,133},{6,134},{7,135},{3... | collective-permute-start | bytes 1376264 | tf_op jit(solution)/shard_map/ppermute | solution.py:33
  93.0 23.5 %collective-permute-start.8 = (bf16[256,896]{1,0:T(8,128)(2,1)}, bf16[256,896]{1,0:T(8,128)(2,1)}, u32[]{:S(2)}, u32[]{:S(2)}) collective-permute-start(bf16[256,896]{1,0:T(8,128)(2,1)} %collective-permute-done.5.refs_4_), channel_id=1, source_target_pairs={{0,64},{1,65},{2,66},{3,67},{4,68},{5,69},{6,70},{7,71},{32,96},{3... | collective-permute-start | bytes 1376264 | tf_op jit(solution)/shard_map/ppermute | solution.py:33
  113.8 11.2 %copy-start.10 = (bf16[256,896]{1,0:T(8,128)(2,1)}, bf16[256,896]{1,0:T(8,128)(2,1)S(1)}, u32[]{:S(2)}) copy-start(bf16[256,896]{1,0:T(8,128)(2,1)S(1)} %collective-permute-done.10.refs_4_) | copy-start | bytes 1376260
  113.8 19.8 %collective-permute-start.11 = (bf16[256,896]{1,0:T(8,128)(2,1)S(1)}, bf16[256,896]{1,0:T(8,128)(2,1)S(1)}, u32[]{:S(2)}, u32[]{:S(2)}) collective-permute-start(bf16[256,896]{1,0:T(8,128)(2,1)S(1)} %collective-permute-done.10.refs_4_), channel_id=1, source_target_pairs={{0,192},{1,193},{2,194},{3,195},{4,196},{5,197},{6,198},{7,199},{3... | collective-permute-start | bytes 1376264 | tf_op jit(solution)/shard_map/ppermute | solution.py:33
  114.9 18.6 %collective-permute-start.12 = (bf16[256,896]{1,0:T(8,128)(2,1)S(1)}, bf16[256,896]{1,0:T(8,128)(2,1)}, u32[]{:S(2)}, u32[]{:S(2)}) collective-permute-start(bf16[256,896]{1,0:T(8,128)(2,1)S(1)} %collective-permute-done.10.refs_4_), channel_id=1, source_target_pairs={{0,128},{1,129},{2,130},{3,131},{4,132},{5,133},{6,134},{7,135},{3... | collective-permute-start | bytes 1376264 | tf_op jit(solution)/shard_map/ppermute | solution.py:33
  116.4 21.7 %collective-permute-start.13 = (bf16[256,896]{1,0:T(8,128)(2,1)S(1)}, bf16[256,896]{1,0:T(8,128)(2,1)}, u32[]{:S(2)}, u32[]{:S(2)}) collective-permute-start(bf16[256,896]{1,0:T(8,128)(2,1)S(1)} %collective-permute-done.10.refs_4_), channel_id=1, source_target_pairs={{0,64},{1,65},{2,66},{3,67},{4,68},{5,69},{6,70},{7,71},{32,96},{3... | collective-permute-start | bytes 1376264 | tf_op jit(solution)/shard_map/ppermute | solution.py:33
  133.5 4.6 %copy-start.11 = (bf16[256,896]{1,0:T(8,128)(2,1)}, bf16[256,896]{1,0:T(8,128)(2,1)S(1)}, u32[]{:S(2)}) copy-start(bf16[256,896]{1,0:T(8,128)(2,1)S(1)} %collective-permute-done.11.refs_5_) | copy-start | bytes 1376260
  145.0 18.6 %collective-permute-start.14 = (f32[384,896]{1,0:T(8,128)}, f32[384,896]{1,0:T(8,128)S(1)}, u32[]{:S(2)}, u32[]{:S(2)}) collective-permute-start(f32[384,896]{1,0:T(8,128)} %shard_map.40), channel_id=1, source_target_pairs={{0,24},{1,9},{2,26},{3,11},{4,28},{5,13},{6,30},{7,15},{32,56},{33... | collective-permute-start | bytes 4128776 | tf_op jit(solution)/shard_map/ppermute | solution.py:33
  151.9 28.9 %collective-permute-start.15 = (f32[384,896]{1,0:T(8,128)}, f32[384,896]{1,0:T(8,128)S(1)}, u32[]{:S(2)}, u32[]{:S(2)}) collective-permute-start(f32[384,896]{1,0:T(8,128)} %shard_map.41), channel_id=1, source_target_pairs={{0,24},{1,9},{2,26},{3,11},{4,28},{5,13},{6,30},{7,15},{32,56},{33... | collective-permute-start | bytes 4128776 | tf_op jit(solution)/shard_map/ppermute | solution.py:33
  163.6 1.3 copy-start.1
  165.3 15.6 %collective-permute-start.16 = (bf16[192,448]{1,0:T(8,128)(2,1)S(1)}, bf16[192,448]{1,0:T(8,128)(2,1)S(1)}, u32[]{:S(2)}, u32[]{:S(2)}) collective-permute-start(bf16[192,448]{1,0:T(8,128)(2,1)S(1)} %get-tuple-element.47), channel_id=1, source_target_pairs={{0,32},{1,33},{2,34},{3,35},{4,36},{5,37},{6,38},{7,39},{32,0},{33... | collective-permute-start | bytes 516104 | tf_op jit(solution)/shard_map/ppermute | solution.py:33
  167.4 18.2 %collective-permute-start.17 = (bf16[192,448]{1,0:T(8,128)(2,1)S(1)}, bf16[192,448]{1,0:T(8,128)(2,1)S(1)}, u32[]{:S(2)}, u32[]{:S(2)}) collective-permute-start(bf16[192,448]{1,0:T(8,128)(2,1)S(1)} %get-tuple-element.49), channel_id=1, source_target_pairs={{0,40},{1,57},{2,42},{3,59},{4,44},{5,61},{6,46},{7,63},{32,8},{33... | collective-permute-start | bytes 516104 | tf_op jit(solution)/shard_map/ppermute | solution.py:33
  173.9 19.0 %copy-start.5 = (s32[7]{0:T(128)S(1)}, s32[7]{0:T(128)}, u32[]{:S(2)}) copy-start(s32[7]{0:T(128)} %copy-done.4) | copy-start | bytes 88
  185.6 1.3 copy-start
  187.2 5.8 %collective-permute-start.18 = (bf16[192,448]{1,0:T(8,128)(2,1)S(1)}, bf16[192,448]{1,0:T(8,128)(2,1)S(1)}, u32[]{:S(2)}, u32[]{:S(2)}) collective-permute-start(bf16[192,448]{1,0:T(8,128)(2,1)S(1)} %get-tuple-element.52), channel_id=1, source_target_pairs={{0,8},{1,25},{2,10},{3,27},{4,12},{5,29},{6,14},{7,31},{32,40},{33... | collective-permute-start | bytes 516104 | tf_op jit(solution)/shard_map/ppermute | solution.py:33
Sparse Core Ops, SparseCore 0:
  9.2 47.2 all-gather.2

commit v9 on v8

--- a/solution.py
+++ b/solution.py
@@ -66,7 +66,7 @@
             tokens.append(pltpu.make_async_copy(source, pieces.at[i, j], lhs_sem.at[2 * i + j]))
     weights = []
     for d in range(4):
-        k = lax.rem(y + d, 4) * 2
+        k = lax.rem(y + d + d % 2 * 2 * place[3], 4) * 2
         for source, at in ((near[d].at[u], k + zh), (far[d], k + 1 - zh)):
             target = rhs.at[pl.ds(pl.multiple_of(at * 256, 256), 256)]
             weights.append(pltpu.make_async_copy(source, target, rhs_sem.at[len(weights)]))
@@ -192,7 +192,7 @@
 
 
 def along_y(value, d):
-    return move(value, lambda x, y, z, c: (x, y - d, z, c))
+    return move(value, lambda x, y, z, c: (x, y - d - 2 * c, z, c))
 
 
 def after(value, *others):
@@ -219,12 +219,15 @@
     near = [near, along_y(near, 1), near, along_y(near, 3)]
 
     panel = after(panel, got_away, near[1], near[3])
-    away, got_away, near[2], panel = lax.optimization_barrier((away, got_away, near[2], panel))
+    away, got_away, near[2], panel = lax.optimization_barrier((away, got_away, near[1], panel))
     own, shared = (p.reshape(2, 8, NX, rows, 256) for p in (panel, move(panel, to_partner)))
     far = [move(away, to_antipode)]
-    near[2] = along_y(near[2], 2)
-    far.append(move(after(got_away, far[0], near[2]), to_antipode))
-    far = [[f] + [along_y(f, d) for d in range(1, 4)] for f in far]
+    near[2] = along_y(near[2], 1)
+    far.append(move(after(got_away, far[0]), to_antipode))
+    for u in range(2):
+        block = after(far[u], *far[0][1:]) if u else far[u]
+        one, three = along_y(block, 1), along_y(block, 3)
+        far[u] = [block, one, along_y(one, 1), three]
 
     sent = product(0, (0, 1), send_place, own, near, far)
     kept = product(0, (0, 1), after(keep_place, *sent), own, near, far)

time: 202 us -> 210 us (1.040)
  starting transfers between devices: 28.4 us -> 32.8 us
    ppermute x19, starting transfers between devices: 28.4 us -> 32.8 us  [move(): return lax.ppermute(value, AXES, pairs)]
    unnamed x26 -> x32, local copies, waits for them, and re-layouts: 6.02 us -> 7.37 us
where the time goes in v9:
time: 210 us; the launch traced here: 208 us
  waiting for transfers between devices  106 us (50%)
  Pallas kernels  47.4 us (23%)
  starting transfers between devices  32.8 us (16%)
  between operations  13.7 us (7%)
  local copies, waits for them, and re-layouts  8.12 us (4%)
    ppermute x19, waiting for transfers between devices, move(): return lax.ppermute(value, AXES, pairs)  92.1 us
    pallas_call x6, Pallas kernels, product(): pl.pallas_call(functools.partial(product_kernel, u, halves), out_shape=[j...  44.4 us
    ppermute x19, starting transfers between devices, move(): return lax.ppermute(value, AXES, pairs)  32.8 us
    all_gather x1, waiting for transfers between devices, per_device(): panel = lax.all_gather(tokens, ('zh', 'zl', 'c'), axis=0)  13.3 us
    unnamed x32, local copies, waits for them, and re-layouts  7.37 us
  transfers between devices with their start and end apart: 20, of which 11 were waited for; matrix products, arithmetic and copies ran while one was open for 0% of the time, Pallas kernels for 19%

profile of v9, /device:TPU:98, one launch (start us, length us, event | category | flops | bytes accessed | tf_op | source)
XLA Modules:
  0.0 208.2 jit_solution(11832712891860549798)
XLA Ops:
  6.5 0.7 all-gather.3.cloned.1.call-update
  7.4 1.2 copy-done.2
  8.6 1.2 copy-done.3
  9.8 0.9 shard_map.37
  10.7 0.6 collective-permute-start.1
  11.3 7.9 %collective-permute-done.1 = bf16[256,896]{1,0:T(8,128)(2,1)S(1)} collective-permute-done((bf16[256,896]{1,0:T(8,128)(2,1)S(1)}, bf16[256,896]{1,0:T(8,128)(2,1)S(1)}, u32[]{:S(2)}, u32[]{:S(2)}) %collective-permute-start.1) | collective-permute-done | bytes 458784 | tf_op jit(solution)/shard_map/ppermute | solution.py:33
  19.3 0.1 pad_maximum_fusion.refs_0_
  19.4 1.7 collective-permute-start.3
  21.0 1.7 collective-permute-start.2
  22.7 0.5 collective-permute-start
  23.2 7.9 %collective-permute-done = bf16[256,896]{1,0:T(8,128)(2,1)S(1)} collective-permute-done((bf16[256,896]{1,0:T(8,128)(2,1)S(1)}, bf16[256,896]{1,0:T(8,128)(2,1)S(1)}, u32[]{:S(2)}, u32[]{:S(2)}) %collective-permute-start) | collective-permute-done | bytes 458784 | tf_op jit(solution)/shard_map/ppermute | solution.py:33
  31.2 12.0 %collective-permute-done.3.refs_3_ = bf16[2,256,896]{2,1,0:T(8,128)(2,1)S(1)} collective-permute-done((bf16[2,256,896]{2,1,0:T(8,128)(2,1)S(1)}, bf16[2,256,896]{2,1,0:T(8,128)(2,1)S(1)}, u32[]{:S(2)}, u32[]{:S(2)}) %collective-permute-start.3) | collective-permute-done | bytes 917536 | tf_op jit(solution)/shard_map/ppermute | solution.py:33
  43.2 13.3 %all-gather.3.cloned.1.call-done = bf16[12288,256]{1,0:T(8,128)(2,1)} async-done(((bf16[768,256]{1,0:T(8,128)(2,1)}), bf16[12288,256]{1,0:T(8,128)(2,1)}) %all-gather.3.cloned.1.call-update) | async-done | bytes 6291472 | tf_op jit(solution)/shard_map/all_gather | solution.py:215
  56.5 0.6 collective-permute-start.9
  57.1 2.2 %collective-permute-start.5 = (bf16[256,896]{1,0:T(8,128)(2,1)S(1)}, bf16[256,896]{1,0:T(8,128)(2,1)S(1)}, u32[]{:S(2)}, u32[]{:S(2)}) collective-permute-start(bf16[256,896]{1,0:T(8,128)(2,1)S(1)} %get-tuple-element.37), channel_id=1, source_target_pairs={{0,32},{1,33},{2,34},{3,35},{4,36},{5,37},{6,38},{7,39},{32,0},{33... | collective-permute-start | bytes 1376264 | tf_op jit(solution)/shard_map/ppermute | solution.py:33
  59.3 24.6 %collective-permute-done.5.refs_4_ = bf16[256,896]{1,0:T(8,128)(2,1)S(1)} collective-permute-done((bf16[256,896]{1,0:T(8,128)(2,1)S(1)}, bf16[256,896]{1,0:T(8,128)(2,1)S(1)}, u32[]{:S(2)}, u32[]{:S(2)}) %collective-permute-start.5) | collective-permute-done | bytes 458784 | tf_op jit(solution)/shard_map/ppermute | solution.py:33
  83.8 3.3 %collective-permute-start.6 = (bf16[256,896]{1,0:T(8,128)(2,1)S(1)}, bf16[256,896]{1,0:T(8,128)(2,1)S(1)}, u32[]{:S(2)}, u32[]{:S(2)}) collective-permute-start(bf16[256,896]{1,0:T(8,128)(2,1)S(1)} %collective-permute-done.5.refs_4_), channel_id=1, source_target_pairs={{0,192},{1,65},{2,194},{3,67},{4,196},{5,69},{6,198},{7,71},{32,22... | collective-permute-start | bytes 1376264 | tf_op jit(solution)/shard_map/ppermute | solution.py:33
  87.1 2.2 %collective-permute-start.10 = (bf16[256,896]{1,0:T(8,128)(2,1)}, bf16[256,896]{1,0:T(8,128)(2,1)S(1)}, u32[]{:S(2)}, u32[]{:S(2)}) collective-permute-start(bf16[256,896]{1,0:T(8,128)(2,1)} %copy-done.15), channel_id=1, source_target_pairs={{0,32},{1,33},{2,34},{3,35},{4,36},{5,37},{6,38},{7,39},{32,0},{33... | collective-permute-start | bytes 1376264 | tf_op jit(solution)/shard_map/ppermute | solution.py:33
  89.3 7.7 %collective-permute-done.6.refs_5_ = bf16[256,896]{1,0:T(8,128)(2,1)S(1)} collective-permute-done((bf16[256,896]{1,0:T(8,128)(2,1)S(1)}, bf16[256,896]{1,0:T(8,128)(2,1)S(1)}, u32[]{:S(2)}, u32[]{:S(2)}) %collective-permute-start.6) | collective-permute-done | bytes 458784 | tf_op jit(solution)/shard_map/ppermute | solution.py:33
  97.0 3.7 %collective-permute-start.7 = (bf16[256,896]{1,0:T(8,128)(2,1)S(1)}, bf16[256,896]{1,0:T(8,128)(2,1)S(1)}, u32[]{:S(2)}, u32[]{:S(2)}) collective-permute-start(bf16[256,896]{1,0:T(8,128)(2,1)S(1)} %collective-permute-done.6.refs_5_), channel_id=1, source_target_pairs={{0,192},{1,65},{2,194},{3,67},{4,196},{5,69},{6,198},{7,71},{32,22... | collective-permute-start | bytes 1376264 | tf_op jit(solution)/shard_map/ppermute | solution.py:33
  100.7 10.7 %collective-permute-done.10.refs_4_ = bf16[256,896]{1,0:T(8,128)(2,1)S(1)} collective-permute-done((bf16[256,896]{1,0:T(8,128)(2,1)}, bf16[256,896]{1,0:T(8,128)(2,1)S(1)}, u32[]{:S(2)}, u32[]{:S(2)}) %collective-permute-start.10) | collective-permute-done | bytes 458784 | tf_op jit(solution)/shard_map/ppermute | solution.py:33
  111.5 0.8 copy-done.13
  112.3 0.8 copy-done.14
  113.0 1.7 collective-permute-start.11
  114.7 0.7 stack.57.place
  115.4 0.3 collective-permute-start.13
  115.7 10.6 %collective-permute-done.11.refs_5_ = bf16[256,896]{1,0:T(8,128)(2,1)} collective-permute-done((bf16[256,896]{1,0:T(8,128)(2,1)S(1)}, bf16[256,896]{1,0:T(8,128)(2,1)}, u32[]{:S(2)}, u32[]{:S(2)}) %collective-permute-start.11) | collective-permute-done | bytes 458784 | tf_op jit(solution)/shard_map/ppermute | solution.py:33
  126.3 3.8 %collective-permute-start.12 = (bf16[256,896]{1,0:T(8,128)(2,1)}, bf16[256,896]{1,0:T(8,128)(2,1)}, u32[]{:S(2)}, u32[]{:S(2)}) collective-permute-start(bf16[256,896]{1,0:T(8,128)(2,1)} %collective-permute-done.11.refs_5_), channel_id=1, source_target_pairs={{0,192},{1,65},{2,194},{3,67},{4,196},{5,69},{6,198},{7,71},{32,22... | collective-permute-start | bytes 1376264 | tf_op jit(solution)/shard_map/ppermute | solution.py:33
  130.1 8.5 %shard_map.38 = (f32[384,896]{1,0:T(8,128)}, f32[384,896]{1,0:T(8,128)}) custom-call(s32[7]{0:T(128)} %stack.57.place, bf16[2,8,4,192,256]{4,3,2,1,0:T(8,128)(2,1)} %bitcast.16, bf16[2,256,896]{2,1,0:T(8,128)(2,1)} %copy-done.6, bf16[2,256,896]{2,1,0:T(8,128)(2,1)} %copy-done.8, bf16[2,256,896]{2,1,0:T(8,128)(2,1)} %collective-permute-done.4.refs_2_, ...), custom_call_target="tpu_custom_call" | custom-call | flops 2818572288 | bytes 16777216 | tf_op jit(solution)/shard_map/pallas_call | solution.py:95
  138.7 8.5 %shard_map.39 = (f32[384,896]{1,0:T(8,128)}, f32[384,896]{1,0:T(8,128)}) custom-call(s32[7]{0:T(128)} %copy-done.4, bf16[2,8,4,192,256]{4,3,2,1,0:T(8,128)(2,1)} %bitcast.17, bf16[2,256,896]{2,1,0:T(8,128)(2,1)} %copy-done.6, bf16[2,256,896]{2,1,0:T(8,128)(2,1)} %copy-done.8, bf16[2,256,896]{2,1,0:T(8,128)(2,1)} %collective-permute-done.4.refs_2_, ...), custom_call_target="tpu_custom_call" | custom-call | flops 2818572288 | bytes 16777216 | tf_op jit(solution)/shard_map/pallas_call | solution.py:95
  147.3 0.7 copy-done.10
  148.0 6.9 %shard_map.40 = f32[384,896]{1,0:T(8,128)} custom-call(s32[7]{0:T(128)} %stack.57.place, bf16[2,8,4,192,256]{4,3,2,1,0:T(8,128)(2,1)} %bitcast.13.panel, bf16[2,256,896]{2,1,0:T(8,128)(2,1)} %copy-done.6, bf16[2,256,896]{2,1,0:T(8,128)(2,1)} %copy-done.8, bf16[2,256,896]{2,1,0:T(8,128)(2,1)} %collective-permute-done.4.refs_2_, ...), custom_call_target="tpu_custom_call" | custom-call | flops 1409286144 | bytes 8388608 | tf_op jit(solution)/shard_map/pallas_call | solution.py:95
  154.9 0.1 collective-permute-start.14
  155.0 6.8 %shard_map.41 = f32[384,896]{1,0:T(8,128)} custom-call(s32[7]{0:T(128)} %stack.57.place, bf16[2,8,4,192,256]{4,3,2,1,0:T(8,128)(2,1)} %bitcast.13.panel, bf16[2,256,896]{2,1,0:T(8,128)(2,1)} %copy-done.6, bf16[2,256,896]{2,1,0:T(8,128)(2,1)} %copy-done.8, bf16[2,256,896]{2,1,0:T(8,128)(2,1)} %collective-permute-done.4.refs_2_, ...), custom_call_target="tpu_custom_call" | custom-call | flops 1409286144 | bytes 8388608 | tf_op jit(solution)/shard_map/pallas_call | solution.py:95
  161.8 2.1 %collective-permute-start.15 = (f32[384,896]{1,0:T(8,128)}, f32[384,896]{1,0:T(8,128)S(1)}, u32[]{:S(2)}, u32[]{:S(2)}) collective-permute-start(f32[384,896]{1,0:T(8,128)} %shard_map.41), channel_id=1, source_target_pairs={{0,24},{1,9},{2,26},{3,11},{4,28},{5,13},{6,30},{7,15},{32,56},{33... | collective-permute-start | bytes 4128776 | tf_op jit(solution)/shard_map/ppermute | solution.py:33
  163.9 6.8 %shard_map.42.kept = f32[384,896]{1,0:T(8,128)} custom-call(s32[7]{0:T(128)} %copy-done.4, bf16[2,8,4,192,256]{4,3,2,1,0:T(8,128)(2,1)} %bitcast.13.panel, bf16[2,256,896]{2,1,0:T(8,128)(2,1)} %copy-done.6, bf16[2,256,896]{2,1,0:T(8,128)(2,1)} %copy-done.8, bf16[2,256,896]{2,1,0:T(8,128)(2,1)} %collective-permute-done.4.refs_2_, ...), custom_call_target="tpu_custom_call" | custom-call | flops 1409286144 | bytes 8388608 | tf_op jit(solution)/shard_map/pallas_call | solution.py:95
  170.7 2.8 %collective-permute-done.14.received = f32[384,896]{1,0:T(8,128)S(1)} collective-permute-done((f32[384,896]{1,0:T(8,128)}, f32[384,896]{1,0:T(8,128)S(1)}, u32[]{:S(2)}, u32[]{:S(2)}) %collective-permute-start.14) | collective-permute-done | bytes 1376288 | tf_op jit(solution)/shard_map/ppermute | solution.py:33
  173.5 1.3 copy-done.1
  174.8 0.3 shard_map.43
  175.1 2.3 %collective-permute-start.17 = (bf16[192,448]{1,0:T(8,128)(2,1)S(1)}, bf16[192,448]{1,0:T(8,128)(2,1)S(1)}, u32[]{:S(2)}, u32[]{:S(2)}) collective-permute-start(bf16[192,448]{1,0:T(8,128)(2,1)S(1)} %get-tuple-element.51), channel_id=1, source_target_pairs={{0,40},{1,57},{2,42},{3,59},{4,44},{5,61},{6,46},{7,63},{32,8},{33... | collective-permute-start | bytes 516104 | tf_op jit(solution)/shard_map/ppermute | solution.py:33
  177.5 4.6 %collective-permute-start.16 = (bf16[192,448]{1,0:T(8,128)(2,1)S(1)}, bf16[192,448]{1,0:T(8,128)(2,1)S(1)}, u32[]{:S(2)}, u32[]{:S(2)}) collective-permute-start(bf16[192,448]{1,0:T(8,128)(2,1)S(1)} %get-tuple-element.49), channel_id=1, source_target_pairs={{0,32},{1,33},{2,34},{3,35},{4,36},{5,37},{6,38},{7,39},{32,0},{33... | collective-permute-start | bytes 516104 | tf_op jit(solution)/shard_map/ppermute | solution.py:33
  182.1 6.9 %shard_map.44.kept = f32[384,896]{1,0:T(8,128)} custom-call(s32[7]{0:T(128)} %copy-done.4, bf16[2,8,4,192,256]{4,3,2,1,0:T(8,128)(2,1)} %bitcast.13.panel, bf16[2,256,896]{2,1,0:T(8,128)(2,1)} %copy-done.6, bf16[2,256,896]{2,1,0:T(8,128)(2,1)} %copy-done.8, bf16[2,256,896]{2,1,0:T(8,128)(2,1)} %collective-permute-done.4.refs_2_, ...), custom_call_target="tpu_custom_call" | custom-call | flops 1409286144 | bytes 8388608 | tf_op jit(solution)/shard_map/pallas_call | solution.py:95
  188.9 3.5 %collective-permute-done.15.received = f32[384,896]{1,0:T(8,128)S(1)} collective-permute-done((f32[384,896]{1,0:T(8,128)}, f32[384,896]{1,0:T(8,128)S(1)}, u32[]{:S(2)}, u32[]{:S(2)}) %collective-permute-start.15) | collective-permute-done | bytes 1376288 | tf_op jit(solution)/shard_map/ppermute | solution.py:33
  192.5 1.3 copy-done
  193.8 0.2 shard_map.45
  194.1 1.5 collective-permute-start.18
  195.6 4.2 %collective-permute-done.18.refs_2_ = bf16[192,448]{1,0:T(8,128)(2,1)S(1)} collective-permute-done((bf16[192,448]{1,0:T(8,128)(2,1)S(1)}, bf16[192,448]{1,0:T(8,128)(2,1)S(1)}, u32[]{:S(2)}, u32[]{:S(2)}) %collective-permute-start.18) | collective-permute-done | bytes 172064 | tf_op jit(solution)/shard_map/ppermute | solution.py:33
  199.8 1.5 shard_map.46
  (38 shorter events, 0.2 us)
Async XLA Ops:
  6.5 50.0 %all-gather.3.cloned.1.call-start = ((), (), s32[]{:S(2)}) async-start(), calls=%async_computation | async-start | bytes 6684672 | tf_op jit(solution)/shard_map/all_gather | solution.py:215
  7.4 1.2 copy-start.2
  8.6 1.2 copy-start.3
  9.8 9.6 %copy-start.4 = (s32[7]{0:T(128)}, s32[7]{0:T(128)S(1)}, u32[]{:S(2)}) copy-start(s32[7]{0:T(128)S(1)} %stack.54.place) | copy-start | bytes 88
  10.7 8.6 %collective-permute-start.1 = (bf16[256,896]{1,0:T(8,128)(2,1)S(1)}, bf16[256,896]{1,0:T(8,128)(2,1)S(1)}, u32[]{:S(2)}, u32[]{:S(2)}) collective-permute-start(bf16[256,896]{1,0:T(8,128)(2,1)S(1)} %get-tuple-element.33), channel_id=1, source_target_pairs={{0,8},{1,25},{2,10},{3,27},{4,12},{5,29},{6,14},{7,31},{32,40},{33... | collective-permute-start | bytes 1376264 | tf_op jit(solution)/shard_map/ppermute | solution.py:33
  19.4 110.8 %copy-start.6 = (bf16[2,256,896]{2,1,0:T(8,128)(2,1)}, bf16[2,256,896]{2,1,0:T(8,128)(2,1)S(1)}, u32[]{:S(2)}) copy-start(bf16[2,256,896]{2,1,0:T(8,128)(2,1)S(1)} %pad_maximum_fusion.refs_0_) | copy-start | bytes 2752516
  19.4 23.8 %collective-permute-start.3 = (bf16[2,256,896]{2,1,0:T(8,128)(2,1)S(1)}, bf16[2,256,896]{2,1,0:T(8,128)(2,1)S(1)}, u32[]{:S(2)}, u32[]{:S(2)}) collective-permute-start(bf16[2,256,896]{2,1,0:T(8,128)(2,1)S(1)} %pad_maximum_fusion.refs_0_), channel_id=1, source_target_pairs={{0,64},{1,193},{2,66},{3,195},{4,68},{5,197},{6,70},{7,199},{32,96... | collective-permute-start | bytes 2752520 | tf_op jit(solution)/shard_map/ppermute | solution.py:33
  21.0 22.2 %collective-permute-start.2 = (bf16[2,256,896]{2,1,0:T(8,128)(2,1)S(1)}, bf16[2,256,896]{2,1,0:T(8,128)(2,1)S(1)}, u32[]{:S(2)}, u32[]{:S(2)}) collective-permute-start(bf16[2,256,896]{2,1,0:T(8,128)(2,1)S(1)} %pad_maximum_fusion.refs_0_), channel_id=1, source_target_pairs={{0,192},{1,65},{2,194},{3,67},{4,196},{5,69},{6,198},{7,71},{32,22... | collective-permute-start | bytes 2752520 | tf_op jit(solution)/shard_map/ppermute | solution.py:33
  22.7 8.5 %collective-permute-start = (bf16[256,896]{1,0:T(8,128)(2,1)S(1)}, bf16[256,896]{1,0:T(8,128)(2,1)S(1)}, u32[]{:S(2)}, u32[]{:S(2)}) collective-permute-start(bf16[256,896]{1,0:T(8,128)(2,1)S(1)} %get-tuple-element.31), channel_id=1, source_target_pairs={{0,8},{1,25},{2,10},{3,27},{4,12},{5,29},{6,14},{7,31},{32,40},{33... | collective-permute-start | bytes 1376264 | tf_op jit(solution)/shard_map/ppermute | solution.py:33
  31.2 12.0 %copy-start.15 = (bf16[256,896]{1,0:T(8,128)(2,1)}, bf16[256,896]{1,0:T(8,128)(2,1)S(1)}, u32[]{:S(2)}) copy-start(bf16[256,896]{1,0:T(8,128)(2,1)S(1)} %collective-permute-done) | copy-start | bytes 1376260
  43.2 87.0 %copy-start.7 = (bf16[2,256,896]{2,1,0:T(8,128)(2,1)}, bf16[2,256,896]{2,1,0:T(8,128)(2,1)S(1)}, u32[]{:S(2)}) copy-start(bf16[2,256,896]{2,1,0:T(8,128)(2,1)S(1)} %collective-permute-done.3.refs_3_) | copy-start | bytes 2752516
  43.2 86.9 %copy-start.8 = (bf16[2,256,896]{2,1,0:T(8,128)(2,1)}, bf16[2,256,896]{2,1,0:T(8,128)(2,1)S(1)}, u32[]{:S(2)}) copy-start(bf16[2,256,896]{2,1,0:T(8,128)(2,1)S(1)} %collective-permute-done.2.refs_1_) | copy-start | bytes 2752516
  56.5 90.8 %collective-permute-start.9 = (bf16[16,768,256]{2,1,0:T(8,128)(2,1)}, bf16[16,768,256]{2,1,0:T(8,128)(2,1)}, u32[]{:S(2)}, u32[]{:S(2)}) collective-permute-start(bf16[16,768,256]{2,1,0:T(8,128)(2,1)} %bitcast.15), channel_id=1, source_target_pairs={{0,8},{1,25},{2,10},{3,27},{4,12},{5,29},{6,14},{7,31},{32,40},{33... | collective-permute-start | bytes 18874376 | tf_op jit(solution)/shard_map/ppermute | solution.py:33
  57.1 26.8 %collective-permute-start.5 = (bf16[256,896]{1,0:T(8,128)(2,1)S(1)}, bf16[256,896]{1,0:T(8,128)(2,1)S(1)}, u32[]{:S(2)}, u32[]{:S(2)}) collective-permute-start(bf16[256,896]{1,0:T(8,128)(2,1)S(1)} %get-tuple-element.37), channel_id=1, source_target_pairs={{0,32},{1,33},{2,34},{3,35},{4,36},{5,37},{6,38},{7,39},{32,0},{33... | collective-permute-start | bytes 1376264 | tf_op jit(solution)/shard_map/ppermute | solution.py:33
  83.8 27.6 %copy-start.11 = (bf16[256,896]{1,0:T(8,128)(2,1)}, bf16[256,896]{1,0:T(8,128)(2,1)S(1)}, u32[]{:S(2)}) copy-start(bf16[256,896]{1,0:T(8,128)(2,1)S(1)} %collective-permute-done.5.refs_4_) | copy-start | bytes 1376260
  83.8 13.1 %collective-permute-start.6 = (bf16[256,896]{1,0:T(8,128)(2,1)S(1)}, bf16[256,896]{1,0:T(8,128)(2,1)S(1)}, u32[]{:S(2)}, u32[]{:S(2)}) collective-permute-start(bf16[256,896]{1,0:T(8,128)(2,1)S(1)} %collective-permute-done.5.refs_4_), channel_id=1, source_target_pairs={{0,192},{1,65},{2,194},{3,67},{4,196},{5,69},{6,198},{7,71},{32,22... | collective-permute-start | bytes 1376264 | tf_op jit(solution)/shard_map/ppermute | solution.py:33
  87.1 24.3 %collective-permute-start.10 = (bf16[256,896]{1,0:T(8,128)(2,1)}, bf16[256,896]{1,0:T(8,128)(2,1)S(1)}, u32[]{:S(2)}, u32[]{:S(2)}) collective-permute-start(bf16[256,896]{1,0:T(8,128)(2,1)} %copy-done.15), channel_id=1, source_target_pairs={{0,32},{1,33},{2,34},{3,35},{4,36},{5,37},{6,38},{7,39},{32,0},{33... | collective-permute-start | bytes 1376264 | tf_op jit(solution)/shard_map/ppermute | solution.py:33
  89.3 22.2 %collective-permute-start.8 = (bf16[256,896]{1,0:T(8,128)(2,1)S(1)}, bf16[256,896]{1,0:T(8,128)(2,1)S(1)}, u32[]{:S(2)}, u32[]{:S(2)}) collective-permute-start(bf16[256,896]{1,0:T(8,128)(2,1)S(1)} %collective-permute-done.5.refs_4_), channel_id=1, source_target_pairs={{0,64},{1,193},{2,66},{3,195},{4,68},{5,197},{6,70},{7,199},{32,96... | collective-permute-start | bytes 1376264 | tf_op jit(solution)/shard_map/ppermute | solution.py:33
  97.0 14.5 %copy-start.12 = (bf16[256,896]{1,0:T(8,128)(2,1)}, bf16[256,896]{1,0:T(8,128)(2,1)S(1)}, u32[]{:S(2)}) copy-start(bf16[256,896]{1,0:T(8,128)(2,1)S(1)} %collective-permute-done.6.refs_5_) | copy-start | bytes 1376260
  97.0 14.5 %collective-permute-start.7 = (bf16[256,896]{1,0:T(8,128)(2,1)S(1)}, bf16[256,896]{1,0:T(8,128)(2,1)S(1)}, u32[]{:S(2)}, u32[]{:S(2)}) collective-permute-start(bf16[256,896]{1,0:T(8,128)(2,1)S(1)} %collective-permute-done.6.refs_5_), channel_id=1, source_target_pairs={{0,192},{1,65},{2,194},{3,67},{4,196},{5,69},{6,198},{7,71},{32,22... | collective-permute-start | bytes 1376264 | tf_op jit(solution)/shard_map/ppermute | solution.py:33
  100.7 29.5 %collective-permute-start.4 = (bf16[2,256,896]{2,1,0:T(8,128)(2,1)S(1)}, bf16[2,256,896]{2,1,0:T(8,128)(2,1)}, u32[]{:S(2)}, u32[]{:S(2)}) collective-permute-start(bf16[2,256,896]{2,1,0:T(8,128)(2,1)S(1)} %collective-permute-done.2.refs_1_), channel_id=1, source_target_pairs={{0,192},{1,65},{2,194},{3,67},{4,196},{5,69},{6,198},{7,71},{32,22... | collective-permute-start | bytes 2752520 | tf_op jit(solution)/shard_map/ppermute | solution.py:33
  111.4 27.3 %copy-start.9 = (bf16[256,896]{1,0:T(8,128)(2,1)}, bf16[256,896]{1,0:T(8,128)(2,1)S(1)}, u32[]{:S(2)}) copy-start(bf16[256,896]{1,0:T(8,128)(2,1)S(1)} %collective-permute-done.10.refs_4_) | copy-start | bytes 1376260
  111.4 0.8 copy-start.13
  112.3 0.8 copy-start.14
  113.0 13.3 %collective-permute-start.11 = (bf16[256,896]{1,0:T(8,128)(2,1)S(1)}, bf16[256,896]{1,0:T(8,128)(2,1)}, u32[]{:S(2)}, u32[]{:S(2)}) collective-permute-start(bf16[256,896]{1,0:T(8,128)(2,1)S(1)} %collective-permute-done.10.refs_4_), channel_id=1, source_target_pairs={{0,192},{1,65},{2,194},{3,67},{4,196},{5,69},{6,198},{7,71},{32,22... | collective-permute-start | bytes 1376264 | tf_op jit(solution)/shard_map/ppermute | solution.py:33
  115.4 31.9 %collective-permute-start.13 = (bf16[256,896]{1,0:T(8,128)(2,1)S(1)}, bf16[256,896]{1,0:T(8,128)(2,1)S(1)}, u32[]{:S(2)}, u32[]{:S(2)}) collective-permute-start(bf16[256,896]{1,0:T(8,128)(2,1)S(1)} %collective-permute-done.10.refs_4_), channel_id=1, source_target_pairs={{0,64},{1,193},{2,66},{3,195},{4,68},{5,197},{6,70},{7,199},{32,96... | collective-permute-start | bytes 1376264 | tf_op jit(solution)/shard_map/ppermute | solution.py:33
  126.3 20.9 %collective-permute-start.12 = (bf16[256,896]{1,0:T(8,128)(2,1)}, bf16[256,896]{1,0:T(8,128)(2,1)}, u32[]{:S(2)}, u32[]{:S(2)}) collective-permute-start(bf16[256,896]{1,0:T(8,128)(2,1)} %collective-permute-done.11.refs_5_), channel_id=1, source_target_pairs={{0,192},{1,65},{2,194},{3,67},{4,196},{5,69},{6,198},{7,71},{32,22... | collective-permute-start | bytes 1376264 | tf_op jit(solution)/shard_map/ppermute | solution.py:33
  147.2 0.8 copy-start.10
  154.9 18.6 %collective-permute-start.14 = (f32[384,896]{1,0:T(8,128)}, f32[384,896]{1,0:T(8,128)S(1)}, u32[]{:S(2)}, u32[]{:S(2)}) collective-permute-start(f32[384,896]{1,0:T(8,128)} %shard_map.40), channel_id=1, source_target_pairs={{0,24},{1,9},{2,26},{3,11},{4,28},{5,13},{6,30},{7,15},{32,56},{33... | collective-permute-start | bytes 4128776 | tf_op jit(solution)/shard_map/ppermute | solution.py:33
  161.8 30.7 %collective-permute-start.15 = (f32[384,896]{1,0:T(8,128)}, f32[384,896]{1,0:T(8,128)S(1)}, u32[]{:S(2)}, u32[]{:S(2)}) collective-permute-start(f32[384,896]{1,0:T(8,128)} %shard_map.41), channel_id=1, source_target_pairs={{0,24},{1,9},{2,26},{3,11},{4,28},{5,13},{6,30},{7,15},{32,56},{33... | collective-permute-start | bytes 4128776 | tf_op jit(solution)/shard_map/ppermute | solution.py:33
  173.5 1.3 copy-start.1
  175.1 17.3 %collective-permute-start.17 = (bf16[192,448]{1,0:T(8,128)(2,1)S(1)}, bf16[192,448]{1,0:T(8,128)(2,1)S(1)}, u32[]{:S(2)}, u32[]{:S(2)}) collective-permute-start(bf16[192,448]{1,0:T(8,128)(2,1)S(1)} %get-tuple-element.51), channel_id=1, source_target_pairs={{0,40},{1,57},{2,42},{3,59},{4,44},{5,61},{6,46},{7,63},{32,8},{33... | collective-permute-start | bytes 516104 | tf_op jit(solution)/shard_map/ppermute | solution.py:33
  177.5 15.0 %collective-permute-start.16 = (bf16[192,448]{1,0:T(8,128)(2,1)S(1)}, bf16[192,448]{1,0:T(8,128)(2,1)S(1)}, u32[]{:S(2)}, u32[]{:S(2)}) collective-permute-start(bf16[192,448]{1,0:T(8,128)(2,1)S(1)} %get-tuple-element.49), channel_id=1, source_target_pairs={{0,32},{1,33},{2,34},{3,35},{4,36},{5,37},{6,38},{7,39},{32,0},{33... | collective-permute-start | bytes 516104 | tf_op jit(solution)/shard_map/ppermute | solution.py:33
  182.1 17.8 %copy-start.5 = (s32[7]{0:T(128)S(1)}, s32[7]{0:T(128)}, u32[]{:S(2)}) copy-start(s32[7]{0:T(128)} %copy-done.4) | copy-start | bytes 88
  192.5 1.3 copy-start
  194.1 5.8 %collective-permute-start.18 = (bf16[192,448]{1,0:T(8,128)(2,1)S(1)}, bf16[192,448]{1,0:T(8,128)(2,1)S(1)}, u32[]{:S(2)}, u32[]{:S(2)}) collective-permute-start(bf16[192,448]{1,0:T(8,128)(2,1)S(1)} %get-tuple-element.54), channel_id=1, source_target_pairs={{0,8},{1,25},{2,10},{3,27},{4,12},{5,29},{6,14},{7,31},{32,40},{33... | collective-permute-start | bytes 516104 | tf_op jit(solution)/shard_map/ppermute | solution.py:33
Sparse Core Ops, SparseCore 0:
  9.2 47.2 all-gather.2

commit v10 on v9

--- a/solution.py
+++ b/solution.py
@@ -224,12 +224,13 @@
     far = [move(away, to_antipode)]
     near[2] = along_y(near[2], 1)
     far.append(move(after(got_away, far[0]), to_antipode))
-    for u in range(2):
-        block = after(far[u], *far[0][1:]) if u else far[u]
-        one, three = along_y(block, 1), along_y(block, 3)
-        far[u] = [block, one, along_y(one, 1), three]
-
+    one, three = along_y(far[0], 1), along_y(far[0], 3)
+    far[0] = [far[0], one, along_y(one, 1), three]
     sent = product(0, (0, 1), send_place, own, near, far)
+    block = after(far[1], *far[0][1:])
+    one, three = along_y(block, 1), along_y(block, 3)
+    far[1] = [block, one, along_y(after(one, sent[0]), 1), three]
+
     kept = product(0, (0, 1), after(keep_place, *sent), own, near, far)
     sums, turn = [None, None], after(send_place, kept[0])
     for half in (1, 0):

time: 210 us -> 202 us (0.962)
  waiting for transfers between devices: 106 us -> 96.2 us
  starting transfers between devices: 32.8 us -> 35.4 us
    ppermute x19, waiting for transfers between devices: 92.1 us -> 82.2 us  [move(): return lax.ppermute(value, AXES, pairs)]
    ppermute x19, starting transfers between devices: 32.8 us -> 35.4 us  [move(): return lax.ppermute(value, AXES, pairs)]
    unnamed x32 -> x34, local copies, waits for them, and re-layouts: 7.37 us -> 7.41 us
  transfers between devices with their start and end apart: 20 -> 20, of which waited for: 11 -> 13; matrix products, arithmetic and copies ran while one was open for 0% -> 0% of each run, Pallas kernels for 19% -> 19%
where the time goes in v10:
time: 202 us; the launch traced here: 201 us
  waiting for transfers between devices  96.2 us (48%)
  Pallas kernels  47.4 us (23%)
  starting transfers between devices  35.4 us (18%)
  between operations  13.7 us (7%)
  local copies, waits for them, and re-layouts  8.06 us (4%)
    ppermute x19, waiting for transfers between devices, move(): return lax.ppermute(value, AXES, pairs)  82.2 us
    pallas_call x6, Pallas kernels, product(): pl.pallas_call(functools.partial(product_kernel, u, halves), out_shape=[j...  44.4 us
    ppermute x19, starting transfers between devices, move(): return lax.ppermute(value, AXES, pairs)  35.4 us
    all_gather x1, waiting for transfers between devices, per_device(): panel = lax.all_gather(tokens, ('zh', 'zl', 'c'), axis=0)  13.3 us
    unnamed x34, local copies, waits for them, and re-layouts  7.41 us
  transfers between devices with their start and end apart: 20, of which 13 were waited for; matrix products, arithmetic and copies ran while one was open for 0% of the time, Pallas kernels for 19%

profile of v10, /device:TPU:98, one launch (start us, length us, event | category | flops | bytes accessed | tf_op | source)
XLA Modules:
  0.0 200.9 jit_solution(5832682665592671879)
XLA Ops:
  6.5 0.7 all-gather.3.cloned.1.call-update
  7.4 1.2 copy-done.2
  8.6 1.2 copy-done.3
  9.8 0.9 shard_map.37
  10.7 0.6 collective-permute-start.1
  11.3 7.9 %collective-permute-done.1 = bf16[256,896]{1,0:T(8,128)(2,1)S(1)} collective-permute-done((bf16[256,896]{1,0:T(8,128)(2,1)S(1)}, bf16[256,896]{1,0:T(8,128)(2,1)S(1)}, u32[]{:S(2)}, u32[]{:S(2)}) %collective-permute-start.1) | collective-permute-done | bytes 458784 | tf_op jit(solution)/shard_map/ppermute | solution.py:33
  19.4 1.7 collective-permute-start.3
  21.0 1.7 collective-permute-start.2
  22.7 0.5 collective-permute-start
  23.2 7.9 %collective-permute-done = bf16[256,896]{1,0:T(8,128)(2,1)S(1)} collective-permute-done((bf16[256,896]{1,0:T(8,128)(2,1)S(1)}, bf16[256,896]{1,0:T(8,128)(2,1)S(1)}, u32[]{:S(2)}, u32[]{:S(2)}) %collective-permute-start) | collective-permute-done | bytes 458784 | tf_op jit(solution)/shard_map/ppermute | solution.py:33
  31.2 12.0 %collective-permute-done.3.refs_3_ = bf16[2,256,896]{2,1,0:T(8,128)(2,1)S(1)} collective-permute-done((bf16[2,256,896]{2,1,0:T(8,128)(2,1)S(1)}, bf16[2,256,896]{2,1,0:T(8,128)(2,1)S(1)}, u32[]{:S(2)}, u32[]{:S(2)}) %collective-permute-start.3) | collective-permute-done | bytes 917536 | tf_op jit(solution)/shard_map/ppermute | solution.py:33
  43.2 13.3 %all-gather.3.cloned.1.call-done = bf16[12288,256]{1,0:T(8,128)(2,1)} async-done(((bf16[768,256]{1,0:T(8,128)(2,1)}), bf16[12288,256]{1,0:T(8,128)(2,1)}) %all-gather.3.cloned.1.call-update) | async-done | bytes 6291472 | tf_op jit(solution)/shard_map/all_gather | solution.py:215
  56.5 0.6 collective-permute-start.9
  57.1 2.2 %collective-permute-start.5 = (bf16[256,896]{1,0:T(8,128)(2,1)S(1)}, bf16[256,896]{1,0:T(8,128)(2,1)S(1)}, u32[]{:S(2)}, u32[]{:S(2)}) collective-permute-start(bf16[256,896]{1,0:T(8,128)(2,1)S(1)} %get-tuple-element.38), channel_id=1, source_target_pairs={{0,32},{1,33},{2,34},{3,35},{4,36},{5,37},{6,38},{7,39},{32,0},{33... | collective-permute-start | bytes 1376264 | tf_op jit(solution)/shard_map/ppermute | solution.py:33
  59.3 24.6 %collective-permute-done.5.refs_4_ = bf16[256,896]{1,0:T(8,128)(2,1)S(1)} collective-permute-done((bf16[256,896]{1,0:T(8,128)(2,1)S(1)}, bf16[256,896]{1,0:T(8,128)(2,1)S(1)}, u32[]{:S(2)}, u32[]{:S(2)}) %collective-permute-start.5) | collective-permute-done | bytes 458784 | tf_op jit(solution)/shard_map/ppermute | solution.py:33
  83.8 3.3 %collective-permute-start.6 = (bf16[256,896]{1,0:T(8,128)(2,1)S(1)}, bf16[256,896]{1,0:T(8,128)(2,1)S(1)}, u32[]{:S(2)}, u32[]{:S(2)}) collective-permute-start(bf16[256,896]{1,0:T(8,128)(2,1)S(1)} %collective-permute-done.5.refs_4_), channel_id=1, source_target_pairs={{0,192},{1,65},{2,194},{3,67},{4,196},{5,69},{6,198},{7,71},{32,22... | collective-permute-start | bytes 1376264 | tf_op jit(solution)/shard_map/ppermute | solution.py:33
  87.1 0.8 collective-permute-start.4
  87.9 2.2 %collective-permute-start.10 = (bf16[256,896]{1,0:T(8,128)(2,1)}, bf16[256,896]{1,0:T(8,128)(2,1)S(1)}, u32[]{:S(2)}, u32[]{:S(2)}) collective-permute-start(bf16[256,896]{1,0:T(8,128)(2,1)} %copy-done.16), channel_id=1, source_target_pairs={{0,32},{1,33},{2,34},{3,35},{4,36},{5,37},{6,38},{7,39},{32,0},{33... | collective-permute-start | bytes 1376264 | tf_op jit(solution)/shard_map/ppermute | solution.py:33
  90.1 1.2 collective-permute-start.8
  91.3 4.4 %collective-permute-done.6.refs_5_ = bf16[256,896]{1,0:T(8,128)(2,1)S(1)} collective-permute-done((bf16[256,896]{1,0:T(8,128)(2,1)S(1)}, bf16[256,896]{1,0:T(8,128)(2,1)S(1)}, u32[]{:S(2)}, u32[]{:S(2)}) %collective-permute-start.6) | collective-permute-done | bytes 458784 | tf_op jit(solution)/shard_map/ppermute | solution.py:33
  95.7 3.7 %collective-permute-start.7 = (bf16[256,896]{1,0:T(8,128)(2,1)S(1)}, bf16[256,896]{1,0:T(8,128)(2,1)S(1)}, u32[]{:S(2)}, u32[]{:S(2)}) collective-permute-start(bf16[256,896]{1,0:T(8,128)(2,1)S(1)} %collective-permute-done.6.refs_5_), channel_id=1, source_target_pairs={{0,192},{1,65},{2,194},{3,67},{4,196},{5,69},{6,198},{7,71},{32,22... | collective-permute-start | bytes 1376264 | tf_op jit(solution)/shard_map/ppermute | solution.py:33
  99.4 13.2 %collective-permute-done.10.refs_4_ = bf16[256,896]{1,0:T(8,128)(2,1)S(1)} collective-permute-done((bf16[256,896]{1,0:T(8,128)(2,1)}, bf16[256,896]{1,0:T(8,128)(2,1)S(1)}, u32[]{:S(2)}, u32[]{:S(2)}) %collective-permute-start.10) | collective-permute-done | bytes 458784 | tf_op jit(solution)/shard_map/ppermute | solution.py:33
  112.8 0.7 copy-done.14
  113.4 0.8 copy-done.15
  114.2 3.0 %collective-permute-start.11 = (bf16[256,896]{1,0:T(8,128)(2,1)S(1)}, bf16[256,896]{1,0:T(8,128)(2,1)}, u32[]{:S(2)}, u32[]{:S(2)}) collective-permute-start(bf16[256,896]{1,0:T(8,128)(2,1)S(1)} %collective-permute-done.10.refs_4_), channel_id=1, source_target_pairs={{0,192},{1,65},{2,194},{3,67},{4,196},{5,69},{6,198},{7,71},{32,22... | collective-permute-start | bytes 1376264 | tf_op jit(solution)/shard_map/ppermute | solution.py:33
  117.2 0.6 stack.57.place
  117.8 8.5 %shard_map.38 = (f32[384,896]{1,0:T(8,128)}, f32[384,896]{1,0:T(8,128)}) custom-call(s32[7]{0:T(128)} %stack.57.place, bf16[2,8,4,192,256]{4,3,2,1,0:T(8,128)(2,1)} %bitcast.16, bf16[2,256,896]{2,1,0:T(8,128)(2,1)} %copy-done.6, bf16[2,256,896]{2,1,0:T(8,128)(2,1)} %copy-done.8, bf16[2,256,896]{2,1,0:T(8,128)(2,1)} %collective-permute-done.4.refs_2_, ...), custom_call_target="tpu_custom_call" | custom-call | flops 2818572288 | bytes 16777216 | tf_op jit(solution)/shard_map/pallas_call | solution.py:95
  126.4 1.3 collective-permute-done.11.refs_5_
  127.6 3.4 %collective-permute-start.12 = (bf16[256,896]{1,0:T(8,128)(2,1)}, bf16[256,896]{1,0:T(8,128)(2,1)S(1)}, u32[]{:S(2)}, u32[]{:S(2)}) collective-permute-start(bf16[256,896]{1,0:T(8,128)(2,1)} %collective-permute-done.11.refs_5_), channel_id=1, source_target_pairs={{0,192},{1,65},{2,194},{3,67},{4,196},{5,69},{6,198},{7,71},{32,22... | collective-permute-start | bytes 1376264 | tf_op jit(solution)/shard_map/ppermute | solution.py:33
  131.1 8.5 %shard_map.39 = (f32[384,896]{1,0:T(8,128)}, f32[384,896]{1,0:T(8,128)}) custom-call(s32[7]{0:T(128)} %copy-done.4, bf16[2,8,4,192,256]{4,3,2,1,0:T(8,128)(2,1)} %bitcast.17, bf16[2,256,896]{2,1,0:T(8,128)(2,1)} %copy-done.6, bf16[2,256,896]{2,1,0:T(8,128)(2,1)} %copy-done.8, bf16[2,256,896]{2,1,0:T(8,128)(2,1)} %collective-permute-done.4.refs_2_, ...), custom_call_target="tpu_custom_call" | custom-call | flops 2818572288 | bytes 16777216 | tf_op jit(solution)/shard_map/pallas_call | solution.py:95
  139.6 0.7 copy-done.10
  140.5 6.9 %shard_map.40 = f32[384,896]{1,0:T(8,128)} custom-call(s32[7]{0:T(128)} %stack.57.place, bf16[2,8,4,192,256]{4,3,2,1,0:T(8,128)(2,1)} %bitcast.13.panel, bf16[2,256,896]{2,1,0:T(8,128)(2,1)} %copy-done.6, bf16[2,256,896]{2,1,0:T(8,128)(2,1)} %copy-done.8, bf16[2,256,896]{2,1,0:T(8,128)(2,1)} %collective-permute-done.4.refs_2_, ...), custom_call_target="tpu_custom_call" | custom-call | flops 1409286144 | bytes 8388608 | tf_op jit(solution)/shard_map/pallas_call | solution.py:95
  147.5 6.8 %shard_map.41 = f32[384,896]{1,0:T(8,128)} custom-call(s32[7]{0:T(128)} %stack.57.place, bf16[2,8,4,192,256]{4,3,2,1,0:T(8,128)(2,1)} %bitcast.13.panel, bf16[2,256,896]{2,1,0:T(8,128)(2,1)} %copy-done.6, bf16[2,256,896]{2,1,0:T(8,128)(2,1)} %copy-done.8, bf16[2,256,896]{2,1,0:T(8,128)(2,1)} %collective-permute-done.4.refs_2_, ...), custom_call_target="tpu_custom_call" | custom-call | flops 1409286144 | bytes 8388608 | tf_op jit(solution)/shard_map/pallas_call | solution.py:95
  154.3 2.1 %collective-permute-start.15 = (f32[384,896]{1,0:T(8,128)}, f32[384,896]{1,0:T(8,128)S(1)}, u32[]{:S(2)}, u32[]{:S(2)}) collective-permute-start(f32[384,896]{1,0:T(8,128)} %shard_map.41), channel_id=1, source_target_pairs={{0,24},{1,9},{2,26},{3,11},{4,28},{5,13},{6,30},{7,15},{32,56},{33... | collective-permute-start | bytes 4128776 | tf_op jit(solution)/shard_map/ppermute | solution.py:33
  156.4 6.8 %shard_map.42.kept = f32[384,896]{1,0:T(8,128)} custom-call(s32[7]{0:T(128)} %copy-done.4, bf16[2,8,4,192,256]{4,3,2,1,0:T(8,128)(2,1)} %bitcast.13.panel, bf16[2,256,896]{2,1,0:T(8,128)(2,1)} %copy-done.6, bf16[2,256,896]{2,1,0:T(8,128)(2,1)} %copy-done.8, bf16[2,256,896]{2,1,0:T(8,128)(2,1)} %collective-permute-done.4.refs_2_, ...), custom_call_target="tpu_custom_call" | custom-call | flops 1409286144 | bytes 8388608 | tf_op jit(solution)/shard_map/pallas_call | solution.py:95
  163.2 2.8 %collective-permute-done.14.received = f32[384,896]{1,0:T(8,128)S(1)} collective-permute-done((f32[384,896]{1,0:T(8,128)}, f32[384,896]{1,0:T(8,128)S(1)}, u32[]{:S(2)}, u32[]{:S(2)}) %collective-permute-start.14) | collective-permute-done | bytes 1376288 | tf_op jit(solution)/shard_map/ppermute | solution.py:33
  166.0 1.3 copy-done.1
  167.4 0.3 shard_map.43
  167.7 4.3 %collective-permute-start.17 = (bf16[192,448]{1,0:T(8,128)(2,1)S(1)}, bf16[192,448]{1,0:T(8,128)(2,1)S(1)}, u32[]{:S(2)}, u32[]{:S(2)}) collective-permute-start(bf16[192,448]{1,0:T(8,128)(2,1)S(1)} %get-tuple-element.53), channel_id=1, source_target_pairs={{0,40},{1,57},{2,42},{3,59},{4,44},{5,61},{6,46},{7,63},{32,8},{33... | collective-permute-start | bytes 516104 | tf_op jit(solution)/shard_map/ppermute | solution.py:33
  172.0 3.7 %collective-permute-start.16 = (bf16[192,448]{1,0:T(8,128)(2,1)S(1)}, bf16[192,448]{1,0:T(8,128)(2,1)S(1)}, u32[]{:S(2)}, u32[]{:S(2)}) collective-permute-start(bf16[192,448]{1,0:T(8,128)(2,1)S(1)} %get-tuple-element.51), channel_id=1, source_target_pairs={{0,32},{1,33},{2,34},{3,35},{4,36},{5,37},{6,38},{7,39},{32,0},{33... | collective-permute-start | bytes 516104 | tf_op jit(solution)/shard_map/ppermute | solution.py:33
  175.7 6.9 %shard_map.44.kept = f32[384,896]{1,0:T(8,128)} custom-call(s32[7]{0:T(128)} %copy-done.4, bf16[2,8,4,192,256]{4,3,2,1,0:T(8,128)(2,1)} %bitcast.13.panel, bf16[2,256,896]{2,1,0:T(8,128)(2,1)} %copy-done.6, bf16[2,256,896]{2,1,0:T(8,128)(2,1)} %copy-done.8, bf16[2,256,896]{2,1,0:T(8,128)(2,1)} %collective-permute-done.4.refs_2_, ...), custom_call_target="tpu_custom_call" | custom-call | flops 1409286144 | bytes 8388608 | tf_op jit(solution)/shard_map/pallas_call | solution.py:95
  182.6 2.1 %collective-permute-done.15.received = f32[384,896]{1,0:T(8,128)S(1)} collective-permute-done((f32[384,896]{1,0:T(8,128)}, f32[384,896]{1,0:T(8,128)S(1)}, u32[]{:S(2)}, u32[]{:S(2)}) %collective-permute-start.15) | collective-permute-done | bytes 1376288 | tf_op jit(solution)/shard_map/ppermute | solution.py:33
  184.6 0.5 collective-permute-done.16.refs_1_
  185.1 1.3 copy-done
  186.5 0.2 shard_map.45
  186.7 0.4 collective-permute-start.18
  187.1 5.4 %collective-permute-done.18.refs_2_ = bf16[192,448]{1,0:T(8,128)(2,1)S(1)} collective-permute-done((bf16[192,448]{1,0:T(8,128)(2,1)S(1)}, bf16[192,448]{1,0:T(8,128)(2,1)S(1)}, u32[]{:S(2)}, u32[]{:S(2)}) %collective-permute-start.18) | collective-permute-done | bytes 172064 | tf_op jit(solution)/shard_map/ppermute | solution.py:33
  192.5 1.5 shard_map.46
  (40 shorter events, 0.6 us)
Async XLA Ops:
  6.5 50.0 %all-gather.3.cloned.1.call-start = ((), (), s32[]{:S(2)}) async-start(), calls=%async_computation | async-start | bytes 6684672 | tf_op jit(solution)/shard_map/all_gather | solution.py:215
  7.4 1.2 copy-start.2
  8.6 1.2 copy-start.3
  9.8 9.6 %copy-start.4 = (s32[7]{0:T(128)}, s32[7]{0:T(128)S(1)}, u32[]{:S(2)}) copy-start(s32[7]{0:T(128)S(1)} %stack.54.place) | copy-start | bytes 88
  10.7 8.6 %collective-permute-start.1 = (bf16[256,896]{1,0:T(8,128)(2,1)S(1)}, bf16[256,896]{1,0:T(8,128)(2,1)S(1)}, u32[]{:S(2)}, u32[]{:S(2)}) collective-permute-start(bf16[256,896]{1,0:T(8,128)(2,1)S(1)} %get-tuple-element.34), channel_id=1, source_target_pairs={{0,8},{1,25},{2,10},{3,27},{4,12},{5,29},{6,14},{7,31},{32,40},{33... | collective-permute-start | bytes 1376264 | tf_op jit(solution)/shard_map/ppermute | solution.py:33
  19.4 98.4 %copy-start.6 = (bf16[2,256,896]{2,1,0:T(8,128)(2,1)}, bf16[2,256,896]{2,1,0:T(8,128)(2,1)S(1)}, u32[]{:S(2)}) copy-start(bf16[2,256,896]{2,1,0:T(8,128)(2,1)S(1)} %pad_maximum_fusion.refs_0_) | copy-start | bytes 2752516
  19.4 23.8 %collective-permute-start.3 = (bf16[2,256,896]{2,1,0:T(8,128)(2,1)S(1)}, bf16[2,256,896]{2,1,0:T(8,128)(2,1)S(1)}, u32[]{:S(2)}, u32[]{:S(2)}) collective-permute-start(bf16[2,256,896]{2,1,0:T(8,128)(2,1)S(1)} %pad_maximum_fusion.refs_0_), channel_id=1, source_target_pairs={{0,64},{1,193},{2,66},{3,195},{4,68},{5,197},{6,70},{7,199},{32,96... | collective-permute-start | bytes 2752520 | tf_op jit(solution)/shard_map/ppermute | solution.py:33
  21.0 22.2 %collective-permute-start.2 = (bf16[2,256,896]{2,1,0:T(8,128)(2,1)S(1)}, bf16[2,256,896]{2,1,0:T(8,128)(2,1)S(1)}, u32[]{:S(2)}, u32[]{:S(2)}) collective-permute-start(bf16[2,256,896]{2,1,0:T(8,128)(2,1)S(1)} %pad_maximum_fusion.refs_0_), channel_id=1, source_target_pairs={{0,192},{1,65},{2,194},{3,67},{4,196},{5,69},{6,198},{7,71},{32,22... | collective-permute-start | bytes 2752520 | tf_op jit(solution)/shard_map/ppermute | solution.py:33
  22.7 8.5 %collective-permute-start = (bf16[256,896]{1,0:T(8,128)(2,1)S(1)}, bf16[256,896]{1,0:T(8,128)(2,1)S(1)}, u32[]{:S(2)}, u32[]{:S(2)}) collective-permute-start(bf16[256,896]{1,0:T(8,128)(2,1)S(1)} %get-tuple-element.32), channel_id=1, source_target_pairs={{0,8},{1,25},{2,10},{3,27},{4,12},{5,29},{6,14},{7,31},{32,40},{33... | collective-permute-start | bytes 1376264 | tf_op jit(solution)/shard_map/ppermute | solution.py:33
  31.2 12.0 %copy-start.16 = (bf16[256,896]{1,0:T(8,128)(2,1)}, bf16[256,896]{1,0:T(8,128)(2,1)S(1)}, u32[]{:S(2)}) copy-start(bf16[256,896]{1,0:T(8,128)(2,1)S(1)} %collective-permute-done) | copy-start | bytes 1376260
  43.2 74.6 %copy-start.7 = (bf16[2,256,896]{2,1,0:T(8,128)(2,1)}, bf16[2,256,896]{2,1,0:T(8,128)(2,1)S(1)}, u32[]{:S(2)}) copy-start(bf16[2,256,896]{2,1,0:T(8,128)(2,1)S(1)} %collective-permute-done.3.refs_3_) | copy-start | bytes 2752516
  43.2 74.6 %copy-start.8 = (bf16[2,256,896]{2,1,0:T(8,128)(2,1)}, bf16[2,256,896]{2,1,0:T(8,128)(2,1)S(1)}, u32[]{:S(2)}) copy-start(bf16[2,256,896]{2,1,0:T(8,128)(2,1)S(1)} %collective-permute-done.2.refs_1_) | copy-start | bytes 2752516
  56.5 83.1 %collective-permute-start.9 = (bf16[16,768,256]{2,1,0:T(8,128)(2,1)}, bf16[16,768,256]{2,1,0:T(8,128)(2,1)}, u32[]{:S(2)}, u32[]{:S(2)}) collective-permute-start(bf16[16,768,256]{2,1,0:T(8,128)(2,1)} %bitcast.15), channel_id=1, source_target_pairs={{0,8},{1,25},{2,10},{3,27},{4,12},{5,29},{6,14},{7,31},{32,40},{33... | collective-permute-start | bytes 18874376 | tf_op jit(solution)/shard_map/ppermute | solution.py:33
  57.1 26.8 %collective-permute-start.5 = (bf16[256,896]{1,0:T(8,128)(2,1)S(1)}, bf16[256,896]{1,0:T(8,128)(2,1)S(1)}, u32[]{:S(2)}, u32[]{:S(2)}) collective-permute-start(bf16[256,896]{1,0:T(8,128)(2,1)S(1)} %get-tuple-element.38), channel_id=1, source_target_pairs={{0,32},{1,33},{2,34},{3,35},{4,36},{5,37},{6,38},{7,39},{32,0},{33... | collective-permute-start | bytes 1376264 | tf_op jit(solution)/shard_map/ppermute | solution.py:33
  83.8 28.8 %copy-start.12 = (bf16[256,896]{1,0:T(8,128)(2,1)}, bf16[256,896]{1,0:T(8,128)(2,1)S(1)}, u32[]{:S(2)}) copy-start(bf16[256,896]{1,0:T(8,128)(2,1)S(1)} %collective-permute-done.5.refs_4_) | copy-start | bytes 1376260
  83.8 11.8 %collective-permute-start.6 = (bf16[256,896]{1,0:T(8,128)(2,1)S(1)}, bf16[256,896]{1,0:T(8,128)(2,1)S(1)}, u32[]{:S(2)}, u32[]{:S(2)}) collective-permute-start(bf16[256,896]{1,0:T(8,128)(2,1)S(1)} %collective-permute-done.5.refs_4_), channel_id=1, source_target_pairs={{0,192},{1,65},{2,194},{3,67},{4,196},{5,69},{6,198},{7,71},{32,22... | collective-permute-start | bytes 1376264 | tf_op jit(solution)/shard_map/ppermute | solution.py:33
  87.1 30.7 %collective-permute-start.4 = (bf16[2,256,896]{2,1,0:T(8,128)(2,1)S(1)}, bf16[2,256,896]{2,1,0:T(8,128)(2,1)}, u32[]{:S(2)}, u32[]{:S(2)}) collective-permute-start(bf16[2,256,896]{2,1,0:T(8,128)(2,1)S(1)} %collective-permute-done.2.refs_1_), channel_id=1, source_target_pairs={{0,192},{1,65},{2,194},{3,67},{4,196},{5,69},{6,198},{7,71},{32,22... | collective-permute-start | bytes 2752520 | tf_op jit(solution)/shard_map/ppermute | solution.py:33
  87.9 24.7 %collective-permute-start.10 = (bf16[256,896]{1,0:T(8,128)(2,1)}, bf16[256,896]{1,0:T(8,128)(2,1)S(1)}, u32[]{:S(2)}, u32[]{:S(2)}) collective-permute-start(bf16[256,896]{1,0:T(8,128)(2,1)} %copy-done.16), channel_id=1, source_target_pairs={{0,32},{1,33},{2,34},{3,35},{4,36},{5,37},{6,38},{7,39},{32,0},{33... | collective-permute-start | bytes 1376264 | tf_op jit(solution)/shard_map/ppermute | solution.py:33
  90.1 22.5 %collective-permute-start.8 = (bf16[256,896]{1,0:T(8,128)(2,1)S(1)}, bf16[256,896]{1,0:T(8,128)(2,1)S(1)}, u32[]{:S(2)}, u32[]{:S(2)}) collective-permute-start(bf16[256,896]{1,0:T(8,128)(2,1)S(1)} %collective-permute-done.5.refs_4_), channel_id=1, source_target_pairs={{0,64},{1,193},{2,66},{3,195},{4,68},{5,197},{6,70},{7,199},{32,96... | collective-permute-start | bytes 1376264 | tf_op jit(solution)/shard_map/ppermute | solution.py:33
  95.7 17.1 %copy-start.13 = (bf16[256,896]{1,0:T(8,128)(2,1)}, bf16[256,896]{1,0:T(8,128)(2,1)S(1)}, u32[]{:S(2)}) copy-start(bf16[256,896]{1,0:T(8,128)(2,1)S(1)} %collective-permute-done.6.refs_5_) | copy-start | bytes 1376260
  95.7 17.1 %collective-permute-start.7 = (bf16[256,896]{1,0:T(8,128)(2,1)S(1)}, bf16[256,896]{1,0:T(8,128)(2,1)S(1)}, u32[]{:S(2)}, u32[]{:S(2)}) collective-permute-start(bf16[256,896]{1,0:T(8,128)(2,1)S(1)} %collective-permute-done.6.refs_5_), channel_id=1, source_target_pairs={{0,192},{1,65},{2,194},{3,67},{4,196},{5,69},{6,198},{7,71},{32,22... | collective-permute-start | bytes 1376264 | tf_op jit(solution)/shard_map/ppermute | solution.py:33
  112.6 13.8 %copy-start.9 = (bf16[256,896]{1,0:T(8,128)(2,1)}, bf16[256,896]{1,0:T(8,128)(2,1)S(1)}, u32[]{:S(2)}) copy-start(bf16[256,896]{1,0:T(8,128)(2,1)S(1)} %collective-permute-done.10.refs_4_) | copy-start | bytes 1376260
  112.6 0.8 copy-start.14
  113.4 0.8 copy-start.15
  114.2 13.4 %collective-permute-start.11 = (bf16[256,896]{1,0:T(8,128)(2,1)S(1)}, bf16[256,896]{1,0:T(8,128)(2,1)}, u32[]{:S(2)}, u32[]{:S(2)}) collective-permute-start(bf16[256,896]{1,0:T(8,128)(2,1)S(1)} %collective-permute-done.10.refs_4_), channel_id=1, source_target_pairs={{0,192},{1,65},{2,194},{3,67},{4,196},{5,69},{6,198},{7,71},{32,22... | collective-permute-start | bytes 1376264 | tf_op jit(solution)/shard_map/ppermute | solution.py:33
  117.8 21.8 %collective-permute-start.13 = (bf16[256,896]{1,0:T(8,128)(2,1)S(1)}, bf16[256,896]{1,0:T(8,128)(2,1)S(1)}, u32[]{:S(2)}, u32[]{:S(2)}) collective-permute-start(bf16[256,896]{1,0:T(8,128)(2,1)S(1)} %collective-permute-done.10.refs_4_), channel_id=1, source_target_pairs={{0,64},{1,193},{2,66},{3,195},{4,68},{5,197},{6,70},{7,199},{32,96... | collective-permute-start | bytes 1376264 | tf_op jit(solution)/shard_map/ppermute | solution.py:33
  127.6 12.0 %collective-permute-start.12 = (bf16[256,896]{1,0:T(8,128)(2,1)}, bf16[256,896]{1,0:T(8,128)(2,1)S(1)}, u32[]{:S(2)}, u32[]{:S(2)}) collective-permute-start(bf16[256,896]{1,0:T(8,128)(2,1)} %collective-permute-done.11.refs_5_), channel_id=1, source_target_pairs={{0,192},{1,65},{2,194},{3,67},{4,196},{5,69},{6,198},{7,71},{32,22... | collective-permute-start | bytes 1376264 | tf_op jit(solution)/shard_map/ppermute | solution.py:33
  139.6 0.8 copy-start.10
  139.6 0.9 copy-start.11
  147.4 18.6 %collective-permute-start.14 = (f32[384,896]{1,0:T(8,128)}, f32[384,896]{1,0:T(8,128)S(1)}, u32[]{:S(2)}, u32[]{:S(2)}) collective-permute-start(f32[384,896]{1,0:T(8,128)} %shard_map.40), channel_id=1, source_target_pairs={{0,24},{1,9},{2,26},{3,11},{4,28},{5,13},{6,30},{7,15},{32,56},{33... | collective-permute-start | bytes 4128776 | tf_op jit(solution)/shard_map/ppermute | solution.py:33
  154.3 30.3 %collective-permute-start.15 = (f32[384,896]{1,0:T(8,128)}, f32[384,896]{1,0:T(8,128)S(1)}, u32[]{:S(2)}, u32[]{:S(2)}) collective-permute-start(f32[384,896]{1,0:T(8,128)} %shard_map.41), channel_id=1, source_target_pairs={{0,24},{1,9},{2,26},{3,11},{4,28},{5,13},{6,30},{7,15},{32,56},{33... | collective-permute-start | bytes 4128776 | tf_op jit(solution)/shard_map/ppermute | solution.py:33
  166.0 1.3 copy-start.1
  167.7 17.0 %collective-permute-start.17 = (bf16[192,448]{1,0:T(8,128)(2,1)S(1)}, bf16[192,448]{1,0:T(8,128)(2,1)S(1)}, u32[]{:S(2)}, u32[]{:S(2)}) collective-permute-start(bf16[192,448]{1,0:T(8,128)(2,1)S(1)} %get-tuple-element.53), channel_id=1, source_target_pairs={{0,40},{1,57},{2,42},{3,59},{4,44},{5,61},{6,46},{7,63},{32,8},{33... | collective-permute-start | bytes 516104 | tf_op jit(solution)/shard_map/ppermute | solution.py:33
  172.0 13.1 %collective-permute-start.16 = (bf16[192,448]{1,0:T(8,128)(2,1)S(1)}, bf16[192,448]{1,0:T(8,128)(2,1)S(1)}, u32[]{:S(2)}, u32[]{:S(2)}) collective-permute-start(bf16[192,448]{1,0:T(8,128)(2,1)S(1)} %get-tuple-element.51), channel_id=1, source_target_pairs={{0,32},{1,33},{2,34},{3,35},{4,36},{5,37},{6,38},{7,39},{32,0},{33... | collective-permute-start | bytes 516104 | tf_op jit(solution)/shard_map/ppermute | solution.py:33
  175.7 16.8 %copy-start.5 = (s32[7]{0:T(128)S(1)}, s32[7]{0:T(128)}, u32[]{:S(2)}) copy-start(s32[7]{0:T(128)} %copy-done.4) | copy-start | bytes 88
  185.1 1.3 copy-start
  186.7 5.8 %collective-permute-start.18 = (bf16[192,448]{1,0:T(8,128)(2,1)S(1)}, bf16[192,448]{1,0:T(8,128)(2,1)S(1)}, u32[]{:S(2)}, u32[]{:S(2)}) collective-permute-start(bf16[192,448]{1,0:T(8,128)(2,1)S(1)} %get-tuple-element.56), channel_id=1, source_target_pairs={{0,8},{1,25},{2,10},{3,27},{4,12},{5,29},{6,14},{7,31},{32,40},{33... | collective-permute-start | bytes 516104 | tf_op jit(solution)/shard_map/ppermute | solution.py:33
Sparse Core Ops, SparseCore 0:
  9.2 47.2 all-gather.2

commit v11 on v10

--- a/solution.py
+++ b/solution.py
@@ -104,7 +104,7 @@
             pltpu.SemaphoreType.DMA((2 * n,)),
             pltpu.SemaphoreType.DMA((8,)),
         ],
-        compiler_params=pltpu.CompilerParams(vmem_limit_bytes=60 << 20),
+        compiler_params=pltpu.CompilerParams(vmem_limit_bytes=(40 if u else 60) << 20),
         cost_estimate=pl.CostEstimate(flops=4 * n * rows * depth * wide, bytes_accessed=8 * n << 20, transcendentals=0),
     )(place, *operands, *before)
 

time: 202 us -> 200 us (0.990)
  Pallas kernels: 47.4 us -> 40.2 us
  waiting for transfers between devices: 96.2 us -> 103 us
  local copies, waits for them, and re-layouts: 8.06 us -> 5.89 us
    pallas_call x6, Pallas kernels: 44.4 us -> 37.3 us  [product(): pl.pallas_call(functools.partial(product_kernel, u, halves), out_shape=[j...]
    ppermute x19, waiting for transfers between devices: 82.2 us -> 88.6 us  [move(): return lax.ppermute(value, AXES, pairs)]
    unnamed x34 -> x40, local copies, waits for them, and re-layouts: 7.41 us -> 5.17 us
  transfers between devices with their start and end apart: 20 -> 20, of which waited for: 13 -> 12; matrix products, arithmetic and copies ran while one was open for 0% -> 0% of each run, Pallas kernels for 19% -> 17%
where the time goes in v11:
time: 200 us; the launch traced here: 198 us
  waiting for transfers between devices  103 us (52%)
  Pallas kernels  40.2 us (20%)
  starting transfers between devices  35.4 us (18%)
  between operations  13.7 us (7%)
  local copies, waits for them, and re-layouts  5.89 us (3%)
    ppermute x19, waiting for transfers between devices, move(): return lax.ppermute(value, AXES, pairs)  88.6 us
    pallas_call x6, Pallas kernels, product(): pl.pallas_call(functools.partial(product_kernel, u, halves), out_shape=[j...  37.3 us
    ppermute x19, starting transfers between devices, move(): return lax.ppermute(value, AXES, pairs)  35.4 us
    all_gather x1, waiting for transfers between devices, per_device(): panel = lax.all_gather(tokens, ('zh', 'zl', 'c'), axis=0)  13.3 us
    unnamed x40, local copies, waits for them, and re-layouts  5.17 us
  transfers between devices with their start and end apart: 20, of which 12 were waited for; matrix products, arithmetic and copies ran while one was open for 0% of the time, Pallas kernels for 17%

profile of v11, /device:TPU:98, one launch (start us, length us, event | category | flops | bytes accessed | tf_op | source)
XLA Modules:
  0.0 198.0 jit_solution(6839767626088706083)
XLA Ops:
  6.5 0.7 all-gather.3.cloned.1.call-update
  7.4 1.2 copy-done.10
  8.6 1.2 copy-done.11
  9.8 0.9 shard_map.37
  10.7 0.6 collective-permute-start.1
  11.3 7.9 %collective-permute-done.1 = bf16[256,896]{1,0:T(8,128)(2,1)S(1)} collective-permute-done((bf16[256,896]{1,0:T(8,128)(2,1)S(1)}, bf16[256,896]{1,0:T(8,128)(2,1)S(1)}, u32[]{:S(2)}, u32[]{:S(2)}) %collective-permute-start.1) | collective-permute-done | bytes 458784 | tf_op jit(solution)/shard_map/ppermute | solution.py:33
  19.3 0.1 pad_maximum_fusion.refs_0_
  19.4 1.7 collective-permute-start.3
  21.0 1.7 collective-permute-start.2
  22.7 0.5 collective-permute-start
  23.2 7.9 %collective-permute-done = bf16[256,896]{1,0:T(8,128)(2,1)S(1)} collective-permute-done((bf16[256,896]{1,0:T(8,128)(2,1)S(1)}, bf16[256,896]{1,0:T(8,128)(2,1)S(1)}, u32[]{:S(2)}, u32[]{:S(2)}) %collective-permute-start) | collective-permute-done | bytes 458784 | tf_op jit(solution)/shard_map/ppermute | solution.py:33
  31.2 12.0 %collective-permute-done.3.refs_3_ = bf16[2,256,896]{2,1,0:T(8,128)(2,1)S(1)} collective-permute-done((bf16[2,256,896]{2,1,0:T(8,128)(2,1)S(1)}, bf16[2,256,896]{2,1,0:T(8,128)(2,1)S(1)}, u32[]{:S(2)}, u32[]{:S(2)}) %collective-permute-start.3) | collective-permute-done | bytes 917536 | tf_op jit(solution)/shard_map/ppermute | solution.py:33
  43.2 13.3 %all-gather.3.cloned.1.call-done = bf16[12288,256]{1,0:T(8,128)(2,1)} async-done(((bf16[768,256]{1,0:T(8,128)(2,1)}), bf16[12288,256]{1,0:T(8,128)(2,1)}) %all-gather.3.cloned.1.call-update) | async-done | bytes 6291472 | tf_op jit(solution)/shard_map/all_gather | solution.py:215
  56.5 0.6 collective-permute-start.9
  57.1 2.2 %collective-permute-start.5 = (bf16[256,896]{1,0:T(8,128)(2,1)S(1)}, bf16[256,896]{1,0:T(8,128)(2,1)S(1)}, u32[]{:S(2)}, u32[]{:S(2)}) collective-permute-start(bf16[256,896]{1,0:T(8,128)(2,1)S(1)} %get-tuple-element.38), channel_id=1, source_target_pairs={{0,32},{1,33},{2,34},{3,35},{4,36},{5,37},{6,38},{7,39},{32,0},{33... | collective-permute-start | bytes 1376264 | tf_op jit(solution)/shard_map/ppermute | solution.py:33
  59.3 24.6 %collective-permute-done.5.refs_4_ = bf16[256,896]{1,0:T(8,128)(2,1)S(1)} collective-permute-done((bf16[256,896]{1,0:T(8,128)(2,1)S(1)}, bf16[256,896]{1,0:T(8,128)(2,1)S(1)}, u32[]{:S(2)}, u32[]{:S(2)}) %collective-permute-start.5) | collective-permute-done | bytes 458784 | tf_op jit(solution)/shard_map/ppermute | solution.py:33
  83.8 3.3 %collective-permute-start.6 = (bf16[256,896]{1,0:T(8,128)(2,1)S(1)}, bf16[256,896]{1,0:T(8,128)(2,1)S(1)}, u32[]{:S(2)}, u32[]{:S(2)}) collective-permute-start(bf16[256,896]{1,0:T(8,128)(2,1)S(1)} %collective-permute-done.5.refs_4_), channel_id=1, source_target_pairs={{0,192},{1,65},{2,194},{3,67},{4,196},{5,69},{6,198},{7,71},{32,22... | collective-permute-start | bytes 1376264 | tf_op jit(solution)/shard_map/ppermute | solution.py:33
  87.1 0.8 collective-permute-start.4
  87.9 2.2 %collective-permute-start.10 = (bf16[256,896]{1,0:T(8,128)(2,1)}, bf16[256,896]{1,0:T(8,128)(2,1)S(1)}, u32[]{:S(2)}, u32[]{:S(2)}) collective-permute-start(bf16[256,896]{1,0:T(8,128)(2,1)} %copy-done.19), channel_id=1, source_target_pairs={{0,32},{1,33},{2,34},{3,35},{4,36},{5,37},{6,38},{7,39},{32,0},{33... | collective-permute-start | bytes 1376264 | tf_op jit(solution)/shard_map/ppermute | solution.py:33
  90.1 1.2 collective-permute-start.8
  91.3 4.4 %collective-permute-done.6.refs_5_ = bf16[256,896]{1,0:T(8,128)(2,1)S(1)} collective-permute-done((bf16[256,896]{1,0:T(8,128)(2,1)S(1)}, bf16[256,896]{1,0:T(8,128)(2,1)S(1)}, u32[]{:S(2)}, u32[]{:S(2)}) %collective-permute-start.6) | collective-permute-done | bytes 458784 | tf_op jit(solution)/shard_map/ppermute | solution.py:33
  95.7 3.7 %collective-permute-start.7 = (bf16[256,896]{1,0:T(8,128)(2,1)S(1)}, bf16[256,896]{1,0:T(8,128)(2,1)S(1)}, u32[]{:S(2)}, u32[]{:S(2)}) collective-permute-start(bf16[256,896]{1,0:T(8,128)(2,1)S(1)} %collective-permute-done.6.refs_5_), channel_id=1, source_target_pairs={{0,192},{1,65},{2,194},{3,67},{4,196},{5,69},{6,198},{7,71},{32,22... | collective-permute-start | bytes 1376264 | tf_op jit(solution)/shard_map/ppermute | solution.py:33
  99.4 13.2 %collective-permute-done.10.refs_4_ = bf16[256,896]{1,0:T(8,128)(2,1)S(1)} collective-permute-done((bf16[256,896]{1,0:T(8,128)(2,1)}, bf16[256,896]{1,0:T(8,128)(2,1)S(1)}, u32[]{:S(2)}, u32[]{:S(2)}) %collective-permute-start.10) | collective-permute-done | bytes 458784 | tf_op jit(solution)/shard_map/ppermute | solution.py:33
  112.6 0.1 collective-permute-done.7.refs_6_
  112.8 0.7 copy-done.17
  113.4 0.8 copy-done.18
  114.2 3.0 %collective-permute-start.11 = (bf16[256,896]{1,0:T(8,128)(2,1)S(1)}, bf16[256,896]{1,0:T(8,128)(2,1)}, u32[]{:S(2)}, u32[]{:S(2)}) collective-permute-start(bf16[256,896]{1,0:T(8,128)(2,1)S(1)} %collective-permute-done.10.refs_4_), channel_id=1, source_target_pairs={{0,192},{1,65},{2,194},{3,67},{4,196},{5,69},{6,198},{7,71},{32,22... | collective-permute-start | bytes 1376264 | tf_op jit(solution)/shard_map/ppermute | solution.py:33
  117.2 0.6 stack.57.place
  117.9 8.6 %shard_map.38 = (f32[384,896]{1,0:T(8,128)}, f32[384,896]{1,0:T(8,128)}) custom-call(s32[7]{0:T(128)} %stack.57.place, bf16[2,8,4,192,256]{4,3,2,1,0:T(8,128)(2,1)} %bitcast.16, bf16[2,256,896]{2,1,0:T(8,128)(2,1)} %copy-done, bf16[2,256,896]{2,1,0:T(8,128)(2,1)} %copy-done.4, bf16[2,256,896]{2,1,0:T(8,128)(2,1)} %collective-permute-done.4.refs_2_, ...), custom_call_target="tpu_custom_call" | custom-call | flops 2818572288 | bytes 16777216 | tf_op jit(solution)/shard_map/pallas_call | solution.py:95
  126.5 1.1 collective-permute-done.11.refs_5_
  127.6 3.6 %collective-permute-start.12 = (bf16[256,896]{1,0:T(8,128)(2,1)}, bf16[256,896]{1,0:T(8,128)(2,1)S(1)}, u32[]{:S(2)}, u32[]{:S(2)}) collective-permute-start(bf16[256,896]{1,0:T(8,128)(2,1)} %collective-permute-done.11.refs_5_), channel_id=1, source_target_pairs={{0,192},{1,65},{2,194},{3,67},{4,196},{5,69},{6,198},{7,71},{32,22... | collective-permute-start | bytes 1376264 | tf_op jit(solution)/shard_map/ppermute | solution.py:33
  131.1 8.7 %shard_map.39 = (f32[384,896]{1,0:T(8,128)}, f32[384,896]{1,0:T(8,128)}) custom-call(s32[7]{0:T(128)} %copy-done.12, bf16[2,8,4,192,256]{4,3,2,1,0:T(8,128)(2,1)} %bitcast.17, bf16[2,256,896]{2,1,0:T(8,128)(2,1)} %copy-done, bf16[2,256,896]{2,1,0:T(8,128)(2,1)} %copy-done.4, bf16[2,256,896]{2,1,0:T(8,128)(2,1)} %collective-permute-done.4.refs_2_, ...), custom_call_target="tpu_custom_call" | custom-call | flops 2818572288 | bytes 16777216 | tf_op jit(solution)/shard_map/pallas_call | solution.py:95
  139.9 1.3 copy-done.9
  141.2 5.0 %shard_map.40 = f32[384,896]{1,0:T(8,128)S(1)} custom-call(s32[7]{0:T(128)S(1)} %copy-done.14, bf16[2,8,4,192,256]{4,3,2,1,0:T(8,128)(2,1)} %bitcast.13.panel, bf16[2,256,896]{2,1,0:T(8,128)(2,1)S(1)} %copy-done.1, bf16[2,256,896]{2,1,0:T(8,128)(2,1)S(1)} %copy-done.5, bf16[2,256,896]{2,1,0:T(8,128)(2,1)} %collective-permute-done.4.refs_2_, ...), custom_call_target="tpu_custom_call" | custom-call | flops 1409286144 | bytes 8388608 | tf_op jit(solution)/shard_map/pallas_call | solution.py:95
  146.3 0.1 collective-permute-start.14
  146.4 5.0 %shard_map.41 = f32[384,896]{1,0:T(8,128)S(1)} custom-call(s32[7]{0:T(128)S(1)} %copy-done.14, bf16[2,8,4,192,256]{4,3,2,1,0:T(8,128)(2,1)} %bitcast.13.panel, bf16[2,256,896]{2,1,0:T(8,128)(2,1)S(1)} %copy-done.1, bf16[2,256,896]{2,1,0:T(8,128)(2,1)S(1)} %copy-done.5, bf16[2,256,896]{2,1,0:T(8,128)(2,1)} %collective-permute-done.4.refs_2_, ...), custom_call_target="tpu_custom_call" | custom-call | flops 1409286144 | bytes 8388608 | tf_op jit(solution)/shard_map/pallas_call | solution.py:95
  151.4 2.1 %collective-permute-start.15 = (f32[384,896]{1,0:T(8,128)S(1)}, f32[384,896]{1,0:T(8,128)S(1)}, u32[]{:S(2)}, u32[]{:S(2)}) collective-permute-start(f32[384,896]{1,0:T(8,128)S(1)} %shard_map.41), channel_id=1, source_target_pairs={{0,24},{1,9},{2,26},{3,11},{4,28},{5,13},{6,30},{7,15},{32,56},{33... | collective-permute-start | bytes 4128776 | tf_op jit(solution)/shard_map/ppermute | solution.py:33
  153.5 5.0 %shard_map.42.kept = f32[384,896]{1,0:T(8,128)S(1)} custom-call(s32[7]{0:T(128)S(1)} %copy-done.13, bf16[2,8,4,192,256]{4,3,2,1,0:T(8,128)(2,1)} %bitcast.13.panel, bf16[2,256,896]{2,1,0:T(8,128)(2,1)S(1)} %copy-done.1, bf16[2,256,896]{2,1,0:T(8,128)(2,1)S(1)} %copy-done.5, bf16[2,256,896]{2,1,0:T(8,128)(2,1)} %collective-permute-done.4.refs_2_, ...), custom_call_target="tpu_custom_call" | custom-call | flops 1409286144 | bytes 8388608 | tf_op jit(solution)/shard_map/pallas_call | solution.py:95
  158.5 6.2 %collective-permute-done.14.received = f32[384,896]{1,0:T(8,128)S(1)} collective-permute-done((f32[384,896]{1,0:T(8,128)S(1)}, f32[384,896]{1,0:T(8,128)S(1)}, u32[]{:S(2)}, u32[]{:S(2)}) %collective-permute-start.14) | collective-permute-done | bytes 1376288 | tf_op jit(solution)/shard_map/ppermute | solution.py:33
  164.7 0.2 shard_map.43
  164.9 4.3 %collective-permute-start.17 = (bf16[192,448]{1,0:T(8,128)(2,1)S(1)}, bf16[192,448]{1,0:T(8,128)(2,1)S(1)}, u32[]{:S(2)}, u32[]{:S(2)}) collective-permute-start(bf16[192,448]{1,0:T(8,128)(2,1)S(1)} %get-tuple-element.53), channel_id=1, source_target_pairs={{0,40},{1,57},{2,42},{3,59},{4,44},{5,61},{6,46},{7,63},{32,8},{33... | collective-permute-start | bytes 516104 | tf_op jit(solution)/shard_map/ppermute | solution.py:33
  169.2 3.6 %collective-permute-start.16 = (bf16[192,448]{1,0:T(8,128)(2,1)S(1)}, bf16[192,448]{1,0:T(8,128)(2,1)S(1)}, u32[]{:S(2)}, u32[]{:S(2)}) collective-permute-start(bf16[192,448]{1,0:T(8,128)(2,1)S(1)} %get-tuple-element.51), channel_id=1, source_target_pairs={{0,32},{1,33},{2,34},{3,35},{4,36},{5,37},{6,38},{7,39},{32,0},{33... | collective-permute-start | bytes 516104 | tf_op jit(solution)/shard_map/ppermute | solution.py:33
  172.8 5.0 %shard_map.44.kept = f32[384,896]{1,0:T(8,128)S(1)} custom-call(s32[7]{0:T(128)S(1)} %copy-done.13, bf16[2,8,4,192,256]{4,3,2,1,0:T(8,128)(2,1)} %bitcast.13.panel, bf16[2,256,896]{2,1,0:T(8,128)(2,1)S(1)} %copy-done.1, bf16[2,256,896]{2,1,0:T(8,128)(2,1)S(1)} %copy-done.5, bf16[2,256,896]{2,1,0:T(8,128)(2,1)} %collective-permute-done.4.refs_2_, ...), custom_call_target="tpu_custom_call" | custom-call | flops 1409286144 | bytes 8388608 | tf_op jit(solution)/shard_map/pallas_call | solution.py:95
  177.8 5.8 %collective-permute-done.15.received = f32[384,896]{1,0:T(8,128)S(1)} collective-permute-done((f32[384,896]{1,0:T(8,128)S(1)}, f32[384,896]{1,0:T(8,128)S(1)}, u32[]{:S(2)}, u32[]{:S(2)}) %collective-permute-start.15) | collective-permute-done | bytes 1376288 | tf_op jit(solution)/shard_map/ppermute | solution.py:33
  183.6 0.2 shard_map.45
  183.9 0.4 collective-permute-start.18
  184.3 5.3 %collective-permute-done.18.refs_2_ = bf16[192,448]{1,0:T(8,128)(2,1)S(1)} collective-permute-done((bf16[192,448]{1,0:T(8,128)(2,1)S(1)}, bf16[192,448]{1,0:T(8,128)(2,1)S(1)}, u32[]{:S(2)}, u32[]{:S(2)}) %collective-permute-start.18) | collective-permute-done | bytes 172064 | tf_op jit(solution)/shard_map/ppermute | solution.py:33
  189.6 1.5 shard_map.46
  (46 shorter events, 0.2 us)
Async XLA Ops:
  6.5 50.0 %all-gather.3.cloned.1.call-start = ((), (), s32[]{:S(2)}) async-start(), calls=%async_computation | async-start | bytes 6684672 | tf_op jit(solution)/shard_map/all_gather | solution.py:215
  7.4 1.2 copy-start.10
  8.6 1.2 copy-start.11
  9.8 9.6 %copy-start.12 = (s32[7]{0:T(128)}, s32[7]{0:T(128)S(1)}, u32[]{:S(2)}) copy-start(s32[7]{0:T(128)S(1)} %stack.54.place) | copy-start | bytes 88
  10.7 8.6 %collective-permute-start.1 = (bf16[256,896]{1,0:T(8,128)(2,1)S(1)}, bf16[256,896]{1,0:T(8,128)(2,1)S(1)}, u32[]{:S(2)}, u32[]{:S(2)}) collective-permute-start(bf16[256,896]{1,0:T(8,128)(2,1)S(1)} %get-tuple-element.34), channel_id=1, source_target_pairs={{0,8},{1,25},{2,10},{3,27},{4,12},{5,29},{6,14},{7,31},{32,40},{33... | collective-permute-start | bytes 1376264 | tf_op jit(solution)/shard_map/ppermute | solution.py:33
  19.4 98.5 %copy-start = (bf16[2,256,896]{2,1,0:T(8,128)(2,1)}, bf16[2,256,896]{2,1,0:T(8,128)(2,1)S(1)}, u32[]{:S(2)}) copy-start(bf16[2,256,896]{2,1,0:T(8,128)(2,1)S(1)} %pad_maximum_fusion.refs_0_) | copy-start | bytes 2752516
  19.4 23.8 %collective-permute-start.3 = (bf16[2,256,896]{2,1,0:T(8,128)(2,1)S(1)}, bf16[2,256,896]{2,1,0:T(8,128)(2,1)S(1)}, u32[]{:S(2)}, u32[]{:S(2)}) collective-permute-start(bf16[2,256,896]{2,1,0:T(8,128)(2,1)S(1)} %pad_maximum_fusion.refs_0_), channel_id=1, source_target_pairs={{0,64},{1,193},{2,66},{3,195},{4,68},{5,197},{6,70},{7,199},{32,96... | collective-permute-start | bytes 2752520 | tf_op jit(solution)/shard_map/ppermute | solution.py:33
  21.0 22.2 %collective-permute-start.2 = (bf16[2,256,896]{2,1,0:T(8,128)(2,1)S(1)}, bf16[2,256,896]{2,1,0:T(8,128)(2,1)S(1)}, u32[]{:S(2)}, u32[]{:S(2)}) collective-permute-start(bf16[2,256,896]{2,1,0:T(8,128)(2,1)S(1)} %pad_maximum_fusion.refs_0_), channel_id=1, source_target_pairs={{0,192},{1,65},{2,194},{3,67},{4,196},{5,69},{6,198},{7,71},{32,22... | collective-permute-start | bytes 2752520 | tf_op jit(solution)/shard_map/ppermute | solution.py:33
  22.7 8.5 %collective-permute-start = (bf16[256,896]{1,0:T(8,128)(2,1)S(1)}, bf16[256,896]{1,0:T(8,128)(2,1)S(1)}, u32[]{:S(2)}, u32[]{:S(2)}) collective-permute-start(bf16[256,896]{1,0:T(8,128)(2,1)S(1)} %get-tuple-element.32), channel_id=1, source_target_pairs={{0,8},{1,25},{2,10},{3,27},{4,12},{5,29},{6,14},{7,31},{32,40},{33... | collective-permute-start | bytes 1376264 | tf_op jit(solution)/shard_map/ppermute | solution.py:33
  31.2 12.0 %copy-start.19 = (bf16[256,896]{1,0:T(8,128)(2,1)}, bf16[256,896]{1,0:T(8,128)(2,1)S(1)}, u32[]{:S(2)}) copy-start(bf16[256,896]{1,0:T(8,128)(2,1)S(1)} %collective-permute-done) | copy-start | bytes 1376260
  43.2 74.7 %copy-start.2 = (bf16[2,256,896]{2,1,0:T(8,128)(2,1)}, bf16[2,256,896]{2,1,0:T(8,128)(2,1)S(1)}, u32[]{:S(2)}) copy-start(bf16[2,256,896]{2,1,0:T(8,128)(2,1)S(1)} %collective-permute-done.3.refs_3_) | copy-start | bytes 2752516
  43.2 74.7 %copy-start.4 = (bf16[2,256,896]{2,1,0:T(8,128)(2,1)}, bf16[2,256,896]{2,1,0:T(8,128)(2,1)S(1)}, u32[]{:S(2)}) copy-start(bf16[2,256,896]{2,1,0:T(8,128)(2,1)S(1)} %collective-permute-done.2.refs_1_) | copy-start | bytes 2752516
  56.5 83.3 %collective-permute-start.9 = (bf16[16,768,256]{2,1,0:T(8,128)(2,1)}, bf16[16,768,256]{2,1,0:T(8,128)(2,1)}, u32[]{:S(2)}, u32[]{:S(2)}) collective-permute-start(bf16[16,768,256]{2,1,0:T(8,128)(2,1)} %bitcast.15), channel_id=1, source_target_pairs={{0,8},{1,25},{2,10},{3,27},{4,12},{5,29},{6,14},{7,31},{32,40},{33... | collective-permute-start | bytes 18874376 | tf_op jit(solution)/shard_map/ppermute | solution.py:33
  57.1 26.8 %collective-permute-start.5 = (bf16[256,896]{1,0:T(8,128)(2,1)S(1)}, bf16[256,896]{1,0:T(8,128)(2,1)S(1)}, u32[]{:S(2)}, u32[]{:S(2)}) collective-permute-start(bf16[256,896]{1,0:T(8,128)(2,1)S(1)} %get-tuple-element.38), channel_id=1, source_target_pairs={{0,32},{1,33},{2,34},{3,35},{4,36},{5,37},{6,38},{7,39},{32,0},{33... | collective-permute-start | bytes 1376264 | tf_op jit(solution)/shard_map/ppermute | solution.py:33
  83.8 28.8 %copy-start.15 = (bf16[256,896]{1,0:T(8,128)(2,1)}, bf16[256,896]{1,0:T(8,128)(2,1)S(1)}, u32[]{:S(2)}) copy-start(bf16[256,896]{1,0:T(8,128)(2,1)S(1)} %collective-permute-done.5.refs_4_) | copy-start | bytes 1376260
  83.8 11.8 %collective-permute-start.6 = (bf16[256,896]{1,0:T(8,128)(2,1)S(1)}, bf16[256,896]{1,0:T(8,128)(2,1)S(1)}, u32[]{:S(2)}, u32[]{:S(2)}) collective-permute-start(bf16[256,896]{1,0:T(8,128)(2,1)S(1)} %collective-permute-done.5.refs_4_), channel_id=1, source_target_pairs={{0,192},{1,65},{2,194},{3,67},{4,196},{5,69},{6,198},{7,71},{32,22... | collective-permute-start | bytes 1376264 | tf_op jit(solution)/shard_map/ppermute | solution.py:33
  87.1 30.8 %collective-permute-start.4 = (bf16[2,256,896]{2,1,0:T(8,128)(2,1)S(1)}, bf16[2,256,896]{2,1,0:T(8,128)(2,1)}, u32[]{:S(2)}, u32[]{:S(2)}) collective-permute-start(bf16[2,256,896]{2,1,0:T(8,128)(2,1)S(1)} %collective-permute-done.2.refs_1_), channel_id=1, source_target_pairs={{0,192},{1,65},{2,194},{3,67},{4,196},{5,69},{6,198},{7,71},{32,22... | collective-permute-start | bytes 2752520 | tf_op jit(solution)/shard_map/ppermute | solution.py:33
  87.9 24.7 %collective-permute-start.10 = (bf16[256,896]{1,0:T(8,128)(2,1)}, bf16[256,896]{1,0:T(8,128)(2,1)S(1)}, u32[]{:S(2)}, u32[]{:S(2)}) collective-permute-start(bf16[256,896]{1,0:T(8,128)(2,1)} %copy-done.19), channel_id=1, source_target_pairs={{0,32},{1,33},{2,34},{3,35},{4,36},{5,37},{6,38},{7,39},{32,0},{33... | collective-permute-start | bytes 1376264 | tf_op jit(solution)/shard_map/ppermute | solution.py:33
  90.1 22.5 %collective-permute-start.8 = (bf16[256,896]{1,0:T(8,128)(2,1)S(1)}, bf16[256,896]{1,0:T(8,128)(2,1)S(1)}, u32[]{:S(2)}, u32[]{:S(2)}) collective-permute-start(bf16[256,896]{1,0:T(8,128)(2,1)S(1)} %collective-permute-done.5.refs_4_), channel_id=1, source_target_pairs={{0,64},{1,193},{2,66},{3,195},{4,68},{5,197},{6,70},{7,199},{32,96... | collective-permute-start | bytes 1376264 | tf_op jit(solution)/shard_map/ppermute | solution.py:33
  95.7 17.1 %copy-start.16 = (bf16[256,896]{1,0:T(8,128)(2,1)}, bf16[256,896]{1,0:T(8,128)(2,1)S(1)}, u32[]{:S(2)}) copy-start(bf16[256,896]{1,0:T(8,128)(2,1)S(1)} %collective-permute-done.6.refs_5_) | copy-start | bytes 1376260
  95.7 17.1 %collective-permute-start.7 = (bf16[256,896]{1,0:T(8,128)(2,1)S(1)}, bf16[256,896]{1,0:T(8,128)(2,1)S(1)}, u32[]{:S(2)}, u32[]{:S(2)}) collective-permute-start(bf16[256,896]{1,0:T(8,128)(2,1)S(1)} %collective-permute-done.6.refs_5_), channel_id=1, source_target_pairs={{0,192},{1,65},{2,194},{3,67},{4,196},{5,69},{6,198},{7,71},{32,22... | collective-permute-start | bytes 1376264 | tf_op jit(solution)/shard_map/ppermute | solution.py:33
  112.6 0.8 copy-start.17
  113.4 0.8 copy-start.18
  114.2 13.4 %collective-permute-start.11 = (bf16[256,896]{1,0:T(8,128)(2,1)S(1)}, bf16[256,896]{1,0:T(8,128)(2,1)}, u32[]{:S(2)}, u32[]{:S(2)}) collective-permute-start(bf16[256,896]{1,0:T(8,128)(2,1)S(1)} %collective-permute-done.10.refs_4_), channel_id=1, source_target_pairs={{0,192},{1,65},{2,194},{3,67},{4,196},{5,69},{6,198},{7,71},{32,22... | collective-permute-start | bytes 1376264 | tf_op jit(solution)/shard_map/ppermute | solution.py:33
  117.8 22.0 %collective-permute-start.13 = (bf16[256,896]{1,0:T(8,128)(2,1)S(1)}, bf16[256,896]{1,0:T(8,128)(2,1)}, u32[]{:S(2)}, u32[]{:S(2)}) collective-permute-start(bf16[256,896]{1,0:T(8,128)(2,1)S(1)} %collective-permute-done.10.refs_4_), channel_id=1, source_target_pairs={{0,64},{1,193},{2,66},{3,195},{4,68},{5,197},{6,70},{7,199},{32,96... | collective-permute-start | bytes 1376264 | tf_op jit(solution)/shard_map/ppermute | solution.py:33
  127.6 12.3 %collective-permute-start.12 = (bf16[256,896]{1,0:T(8,128)(2,1)}, bf16[256,896]{1,0:T(8,128)(2,1)S(1)}, u32[]{:S(2)}, u32[]{:S(2)}) collective-permute-start(bf16[256,896]{1,0:T(8,128)(2,1)} %collective-permute-done.11.refs_5_), channel_id=1, source_target_pairs={{0,192},{1,65},{2,194},{3,67},{4,196},{5,69},{6,198},{7,71},{32,22... | collective-permute-start | bytes 1376264 | tf_op jit(solution)/shard_map/ppermute | solution.py:33
  131.1 8.7 %copy-start.1 = (bf16[2,256,896]{2,1,0:T(8,128)(2,1)S(1)}, bf16[2,256,896]{2,1,0:T(8,128)(2,1)}, u32[]{:S(2)}) copy-start(bf16[2,256,896]{2,1,0:T(8,128)(2,1)} %copy-done) | copy-start | bytes 2752516
  131.1 8.7 %copy-start.3 = (bf16[2,256,896]{2,1,0:T(8,128)(2,1)S(1)}, bf16[2,256,896]{2,1,0:T(8,128)(2,1)}, u32[]{:S(2)}) copy-start(bf16[2,256,896]{2,1,0:T(8,128)(2,1)} %copy-done.2) | copy-start | bytes 2752516
  131.1 8.7 %copy-start.5 = (bf16[2,256,896]{2,1,0:T(8,128)(2,1)S(1)}, bf16[2,256,896]{2,1,0:T(8,128)(2,1)}, u32[]{:S(2)}) copy-start(bf16[2,256,896]{2,1,0:T(8,128)(2,1)} %copy-done.4) | copy-start | bytes 2752516
  131.1 8.7 %copy-start.14 = (s32[7]{0:T(128)S(1)}, s32[7]{0:T(128)}, u32[]{:S(2)}) copy-start(s32[7]{0:T(128)} %stack.57.place) | copy-start | bytes 88
  139.9 1.3 copy-start.9
  141.2 5.1 %copy-start.7 = (f32[384,896]{1,0:T(8,128)S(1)}, f32[384,896]{1,0:T(8,128)}, u32[]{:S(2)}) copy-start(f32[384,896]{1,0:T(8,128)} %get-tuple-element.39.refs_8_) | copy-start | bytes 4128772
  146.2 7.2 %copy-start.8 = (f32[384,896]{1,0:T(8,128)S(1)}, f32[384,896]{1,0:T(8,128)}, u32[]{:S(2)}) copy-start(f32[384,896]{1,0:T(8,128)} %get-tuple-element.50.refs_8_) | copy-start | bytes 4128772
  146.2 7.2 %copy-start.13 = (s32[7]{0:T(128)S(1)}, s32[7]{0:T(128)}, u32[]{:S(2)}) copy-start(s32[7]{0:T(128)} %copy-done.12) | copy-start | bytes 88
  146.3 18.4 %collective-permute-start.14 = (f32[384,896]{1,0:T(8,128)S(1)}, f32[384,896]{1,0:T(8,128)S(1)}, u32[]{:S(2)}, u32[]{:S(2)}) collective-permute-start(f32[384,896]{1,0:T(8,128)S(1)} %shard_map.40), channel_id=1, source_target_pairs={{0,24},{1,9},{2,26},{3,11},{4,28},{5,13},{6,30},{7,15},{32,56},{33... | collective-permute-start | bytes 4128776 | tf_op jit(solution)/shard_map/ppermute | solution.py:33
  151.4 32.2 %collective-permute-start.15 = (f32[384,896]{1,0:T(8,128)S(1)}, f32[384,896]{1,0:T(8,128)S(1)}, u32[]{:S(2)}, u32[]{:S(2)}) collective-permute-start(f32[384,896]{1,0:T(8,128)S(1)} %shard_map.41), channel_id=1, source_target_pairs={{0,24},{1,9},{2,26},{3,11},{4,28},{5,13},{6,30},{7,15},{32,56},{33... | collective-permute-start | bytes 4128776 | tf_op jit(solution)/shard_map/ppermute | solution.py:33
  158.5 14.3 %copy-start.6 = (f32[384,896]{1,0:T(8,128)S(1)}, f32[384,896]{1,0:T(8,128)}, u32[]{:S(2)}) copy-start(f32[384,896]{1,0:T(8,128)} %get-tuple-element.42.refs_8_) | copy-start | bytes 4128772
  164.9 18.7 %collective-permute-start.17 = (bf16[192,448]{1,0:T(8,128)(2,1)S(1)}, bf16[192,448]{1,0:T(8,128)(2,1)S(1)}, u32[]{:S(2)}, u32[]{:S(2)}) collective-permute-start(bf16[192,448]{1,0:T(8,128)(2,1)S(1)} %get-tuple-element.53), channel_id=1, source_target_pairs={{0,40},{1,57},{2,42},{3,59},{4,44},{5,61},{6,46},{7,63},{32,8},{33... | collective-permute-start | bytes 516104 | tf_op jit(solution)/shard_map/ppermute | solution.py:33
  169.2 14.4 %collective-permute-start.16 = (bf16[192,448]{1,0:T(8,128)(2,1)S(1)}, bf16[192,448]{1,0:T(8,128)(2,1)S(1)}, u32[]{:S(2)}, u32[]{:S(2)}) collective-permute-start(bf16[192,448]{1,0:T(8,128)(2,1)S(1)} %get-tuple-element.51), channel_id=1, source_target_pairs={{0,32},{1,33},{2,34},{3,35},{4,36},{5,37},{6,38},{7,39},{32,0},{33... | collective-permute-start | bytes 516104 | tf_op jit(solution)/shard_map/ppermute | solution.py:33
  183.9 5.8 %collective-permute-start.18 = (bf16[192,448]{1,0:T(8,128)(2,1)S(1)}, bf16[192,448]{1,0:T(8,128)(2,1)S(1)}, u32[]{:S(2)}, u32[]{:S(2)}) collective-permute-start(bf16[192,448]{1,0:T(8,128)(2,1)S(1)} %get-tuple-element.56), channel_id=1, source_target_pairs={{0,8},{1,25},{2,10},{3,27},{4,12},{5,29},{6,14},{7,31},{32,40},{33... | collective-permute-start | bytes 516104 | tf_op jit(solution)/shard_map/ppermute | solution.py:33
Sparse Core Ops, SparseCore 0:
  9.2 47.2 all-gather.2
